TPU v7x, 32 devices: a whole 2x2x4 slice. The times are simulated.
32 devices in a mesh: dp: 8 (over y, x, core), fsdp: 4 (over z).
Axes of the slice: x: 2, y: 2, z: 4, core: 2. Of those that a mesh axis runs over, the one named last changes fastest.
Arguments:
- tokens_in: bfloat16 [4096, 2048], P(('dp', 'fsdp')), may hold values from -6 to 6
- text_in: bfloat16 [1024, 4096], P(('dp', 'fsdp')), may hold values from -6 to 6
- seg_ids: int32 [32, 128], P(('dp', 'fsdp')), may hold values from 0 to 2, never falling along the last dimension, each value on 1 to 64 neighbouring positions
- capt_ids: int32 [32, 32], P(('dp', 'fsdp')), may hold values from 0 to 2, never falling along the last dimension, each value on 1 to 21 neighbouring positions
- grad_out: bfloat16 [4096, 2048], P(('dp', 'fsdp')), may hold values from -6 to 6
- owner_query: int32 [64, 1], replicated, may hold values from 0 to 7; in each aligned block of 64 rows (0 to 63, 64 to 127, ...) at most 16 rows name the same one
- owner_up: int32 [64, 1], replicated, may hold values from 0 to 7; in each aligned block of 64 rows (0 to 63, 64 to 127, ...) at most 16 rows name the same one
- owner_outs: int32 [32, 1], replicated, may hold values from 0 to 7; in each aligned block of 32 rows (0 to 31, 32 to 63, ...) at most 8 rows name the same one
- owner_text: int32 [64, 1], replicated, may hold values from 0 to 7; in each aligned block of 64 rows (0 to 63, 64 to 127, ...) at most 16 rows name the same one
- owner_down: int32 [64, 1], replicated, may hold values from 0 to 7; in each aligned block of 64 rows (0 to 63, 64 to 127, ...) at most 16 rows name the same one
- w_query: float32 [2048, 16384], P('fsdp', 'dp'), may hold values from -0.125 to 0.125
- m_query: float32 [2048, 16384], P('fsdp', 'dp'), may hold values from -48 to 48
- v_query: float32 [2048, 16384], P('fsdp', 'dp'), may hold values from 5.89824 to 23.59296
- w_up: float32 [2048, 16384], P('fsdp', 'dp'), may hold values from -0.125 to 0.125
- m_up: float32 [2048, 16384], P('fsdp', 'dp'), may hold values from -20 to 20
- v_up: float32 [2048, 16384], P('fsdp', 'dp'), may hold values from 1.024 to 4.096
- w_outs: float32 [2048, 8192], P('fsdp', 'dp'), may hold values from -0.375 to 0.375
- m_outs: float32 [2048, 8192], P('fsdp', 'dp'), may hold values from -16 to 16
- v_outs: float32 [2048, 8192], P('fsdp', 'dp'), may hold values from 0.65536 to 2.62144
- w_text: float32 [2048, 16384], P('fsdp', 'dp'), may hold values from -0.09375 to 0.09375
- m_text: float32 [2048, 16384], P('fsdp', 'dp'), may hold values from -32 to 32
- v_text: float32 [2048, 16384], P('fsdp', 'dp'), may hold values from 2.9696 to 11.8784
- w_down: float32 [2048, 16384], P('fsdp', 'dp'), may hold values from -0.09375 to 0.09375
- m_down: float32 [2048, 16384], P('fsdp', 'dp'), may hold values from -28 to 28
- v_down: float32 [2048, 16384], P('fsdp', 'dp'), may hold values from 1.72032 to 6.9632
- norm_weight: float32 [6, 2048], P(None, 'dp'), may hold values from -1 to 2, as said below
- m_norm: float32 [6, 2048], P(None, 'dp'), may hold values from -64 to 64
- v_norm: float32 [6, 2048], P(None, 'dp'), may hold values from 9.216 to 36.864
Outputs:
- result: bfloat16 [4096, 2048], P(('dp', 'fsdp'))
- grad_in: bfloat16 [4096, 2048], P(('dp', 'fsdp'))
- query_first: float32 [2048, 16384], P('fsdp', 'dp')
- query_second: float32 [2048, 16384], P('fsdp', 'dp')
- query_weight: float32 [2048, 16384], P('fsdp', 'dp')
- up_first: float32 [2048, 16384], P('fsdp', 'dp')
- up_second: float32 [2048, 16384], P('fsdp', 'dp')
- up_weight: float32 [2048, 16384], P('fsdp', 'dp')
- outs_first: float32 [2048, 8192], P('fsdp', 'dp')
- outs_second: float32 [2048, 8192], P('fsdp', 'dp')
- outs_weight: float32 [2048, 8192], P('fsdp', 'dp')
- text_first: float32 [2048, 16384], P('fsdp', 'dp')
- text_second: float32 [2048, 16384], P('fsdp', 'dp')
- text_weight: float32 [2048, 16384], P('fsdp', 'dp')
- down_first: float32 [2048, 16384], P('fsdp', 'dp')
- down_second: float32 [2048, 16384], P('fsdp', 'dp')
- down_weight: float32 [2048, 16384], P('fsdp', 'dp')
- norm_first: float32 [6, 2048], P(None, 'dp')
- norm_second: float32 [6, 2048], P(None, 'dp')
- norm_new: float32 [6, 2048], P(None, 'dp')
Inputs may be any that keep to these rules, and one draw needn't show every extreme that they name: `seg_ids`: within one packed row the image numbers never fall; each image holds 1 to 64 tokens, one holds exactly 64, and every image number appears. `capt_ids`: within one packed row the caption numbers never fall; caption n belongs to image n of the same row; each caption holds 1 to 21 text tokens, one holds exactly 21, and every caption number appears. `owner_query`: no dp index owns more than 16 blocks, one owns exactly 16, every index owns at least one. `owner_up`: no dp index owns more than 16 blocks, one owns exactly 16, every index owns at least one. `owner_outs`: no dp index owns more than 8 blocks, one owns exactly 8, every index owns at least one. `owner_text`: no dp index owns more than 16 blocks, one owns exactly 16, every index owns at least one. `owner_down`: no dp index owns more than 16 blocks, one owns exactly 16, every index owns at least one. `norm_weight`: rows 0, 2 and 4 are positive gains, rows 1, 3 and 5 biases.
All inputs are finite; a program needn't handle non-finite values.
Results may differ from a plain program's by a relative error of at most 0.022.
Values may be sent and summed in bfloat16 or wider, within the bound.
A program may use at most 512 MiB of HBM per device.

v0:
```python
import jax
import jax.numpy as jnp
from jax import lax
from jax.sharding import PartitionSpec as P

HEADS = 16
HEAD = 128
STEP = 10
BLK = 128


beta_first = 0.9
beta_second = 0.999
adam_eps = 1e-08
decay_rate = 0.01
rate_query = 0.04
rate_up = 0.04
rate_outs = 0.12
rate_text = 0.03
rate_down = 0.03
rate_norm = 0.5
norm_eps = 1e-05
score_floor = -1e30


def normalize(values):
    centered = values - jnp.mean(values, axis=-1, keepdims=True)
    inverse_std = lax.rsqrt(jnp.mean(centered * centered, axis=-1, keepdims=True) + norm_eps)
    return (centered * inverse_std, inverse_std)


def norm_back(back_hidden, normed, inverse_std, gain_row):
    back_normed = back_hidden * gain_row
    return inverse_std * (
        back_normed
        - jnp.mean(back_normed, axis=-1, keepdims=True)
        - normed * jnp.mean(back_normed * normed, axis=-1, keepdims=True)
    )


def exact_gelu(values):
    return jax.nn.gelu(values, approximate=False)


def slot_index(owner_list, capacity):
    owner_column = owner_list[:, 0]
    block_count = owner_column.shape[0]
    same_owner = owner_column[:, None] == owner_column[None, :]
    earlier = lax.broadcasted_iota(jnp.int32, (block_count, block_count), 1) < lax.broadcasted_iota(
        jnp.int32, (block_count, block_count), 0
    )
    position = jnp.sum(jnp.logical_and(same_owner, earlier).astype(jnp.int32), axis=1)
    return owner_column * capacity + position


def unslot(slot_array, slot_list):
    row_count = slot_array.shape[0]
    return jnp.take(slot_array.reshape(row_count, -1, BLK), slot_list, axis=1).reshape(
        row_count, -1
    )


def to_slots(grad_rows, slot_list, slot_total):
    row_count = grad_rows.shape[0]
    block_count = slot_list.shape[0]
    slot_hits = (
        slot_list[None, :] == lax.broadcasted_iota(jnp.int32, (slot_total, block_count), 0)
    ).astype(jnp.int32)
    live_mask = jnp.sum(slot_hits, axis=1)
    block_of = jnp.sum(
        slot_hits * lax.broadcasted_iota(jnp.int32, (slot_total, block_count), 1), axis=1
    )
    taken = jnp.take(grad_rows.reshape(row_count, block_count, BLK), block_of, axis=1)
    return (taken * live_mask.astype(jnp.float32)[None, :, None]).reshape(row_count, -1)


def head_split(values):
    return values.reshape(values.shape[0], HEADS, HEAD)


def block_scores(query_heads, key_heads, allowed):
    raw_scores = jnp.einsum(
        "qhd,khd->hqk", query_heads, key_heads, preferred_element_type=jnp.float32
    ) * HEAD ** (-0.5)
    return (query_heads, jnp.where(allowed[None], raw_scores, score_floor))


def attend_forward(queries, keys, values, allowed):
    row_count = queries.shape[0]
    query_heads = head_split(queries)
    key_heads = head_split(keys)
    value_heads = head_split(values)
    query_block, scores = block_scores(query_heads, key_heads, allowed)
    row_peak = jnp.max(scores, axis=-1, keepdims=True)
    powers = jnp.exp(scores - row_peak)
    exp_total = jnp.sum(powers, axis=-1, keepdims=True)
    shares_low = (powers / exp_total).astype(jnp.bfloat16)
    logsum_parts = [row_peak + jnp.log(exp_total)]
    attended_parts = jnp.einsum(
        "hqk,khd->qhd", shares_low, value_heads, preferred_element_type=jnp.float32
    )
    attended = attended_parts.reshape(row_count, -1).astype(jnp.bfloat16)
    return (attended, logsum_parts)


def attend_backward(queries, keys, values, allowed, logsum_parts, back_attended):
    row_count = queries.shape[0]
    key_count = keys.shape[0]
    query_heads = head_split(queries)
    key_heads = head_split(keys)
    value_heads = head_split(values)
    back_heads = head_split(back_attended)
    score_scale = HEAD ** (-0.5)
    query_grads = []
    key_grad = jnp.zeros(key_heads.shape, jnp.float32)
    value_grad = jnp.zeros(value_heads.shape, jnp.float32)
    for block_index, first_row in enumerate(range(0, row_count, row_count)):
        query_block, scores = block_scores(query_heads, key_heads, allowed)
        shares = jnp.exp(scores - logsum_parts[block_index])
        shares_low = shares.astype(jnp.bfloat16)
        back_shares = jnp.einsum(
            "qhd,khd->hqk", back_heads, value_heads, preferred_element_type=jnp.float32
        )
        inner_sum = jnp.sum(shares * back_shares, axis=-1, keepdims=True)
        back_scores = (shares * (back_shares - inner_sum)).astype(jnp.bfloat16)
        query_grads.append(
            jnp.einsum("hqk,khd->qhd", back_scores, key_heads, preferred_element_type=jnp.float32)
            * score_scale
        )
        key_grad = (
            jnp.einsum("hqk,qhd->khd", back_scores, query_block, preferred_element_type=jnp.float32)
            * score_scale
        )
        value_grad = jnp.einsum(
            "hqk,qhd->khd", shares_low, back_heads, preferred_element_type=jnp.float32
        )
    query_grad = query_grads[0].reshape(row_count, -1)
    return (query_grad, key_grad.reshape(key_count, -1), value_grad.reshape(key_count, -1))


def adamw_update(weight, first, second, gradient, rate, decay):
    first_new = beta_first * first + (1.0 - beta_first) * gradient
    second_new = beta_second * second + (1.0 - beta_second) * gradient * gradient
    first_hat = first_new / (1.0 - beta_first**STEP)
    second_hat = second_new / (1.0 - beta_second**STEP)
    weight_new = weight - rate * (first_hat / (jnp.sqrt(second_hat) + adam_eps) + decay * weight)
    return (first_new, second_new, weight_new)


def body(
    tokens_in,
    text_in,
    seg_ids,
    capt_ids,
    grad_out,
    owner_query,
    owner_up,
    owner_outs,
    owner_text,
    owner_down,
    w_query,
    m_query,
    v_query,
    w_up,
    m_up,
    v_up,
    w_outs,
    m_outs,
    v_outs,
    w_text,
    m_text,
    v_text,
    w_down,
    m_down,
    v_down,
    norm_weight,
    m_norm,
    v_norm,
):
    dp_count = lax.axis_size("dp")
    cap_big = w_query.shape[1] // BLK
    cap_out = w_outs.shape[1] // BLK
    slot_query = slot_index(owner_query, cap_big)
    slot_up = slot_index(owner_up, cap_big)
    slot_outs = slot_index(owner_outs, cap_out)
    slot_text = slot_index(owner_text, cap_big)
    slot_down = slot_index(owner_down, cap_big)
    gathered = (
        lax.all_gather(w_query, "dp", axis=1, tiled=True),
        lax.all_gather(w_up, "dp", axis=1, tiled=True),
        lax.all_gather(w_outs, "dp", axis=1, tiled=True),
        lax.all_gather(w_text, "dp", axis=1, tiled=True),
        lax.all_gather(w_down, "dp", axis=1, tiled=True),
        lax.all_gather(norm_weight, "dp", axis=1, tiled=True),
    )
    query_low = unslot(gathered[0], slot_query).astype(jnp.bfloat16)
    up_low = unslot(gathered[1], slot_up).astype(jnp.bfloat16)
    outs_low = unslot(gathered[2], slot_outs).astype(jnp.bfloat16)
    text_low = unslot(gathered[3], slot_text).astype(jnp.bfloat16)
    down_low = unslot(gathered[4], slot_down).astype(jnp.bfloat16)
    norm_full = gathered[5]
    row_count = tokens_in.shape[0]
    model_width = tokens_in.shape[1]
    text_count = text_in.shape[0]
    own_rows = query_low.shape[0]
    segment = seg_ids[0]
    caption = capt_ids[0]
    self_mask = segment[:, None] == segment[None, :]
    cross_mask = segment[:, None] == caption[None, :]
    text_folded = text_in.reshape(text_count, 2, model_width)
    query_full, outs_full, text_full = (
        lax.all_gather(query_low, "fsdp", axis=0, tiled=True),
        lax.all_gather(outs_low, "fsdp", axis=0, tiled=True),
        lax.all_gather(text_low, "fsdp", axis=0, tiled=True),
    )
    inputs = tokens_in.astype(jnp.float32)
    normed1, inverse1 = normalize(inputs)
    hidden1 = (normed1 * norm_full[0] + norm_full[1]).astype(jnp.bfloat16)
    projected = jnp.dot(
        hidden1, query_full[:, : 3 * model_width], preferred_element_type=jnp.float32
    ).astype(jnp.bfloat16)
    self_query = projected[:, :model_width]
    self_key = projected[:, model_width : 2 * model_width]
    self_value = projected[:, 2 * model_width :]
    attended1, logsum1 = attend_forward(self_query, self_key, self_value, self_mask)
    middle1 = inputs + jnp.dot(
        attended1, outs_full[:, :model_width], preferred_element_type=jnp.float32
    )
    normed2, inverse2 = normalize(middle1)
    hidden2 = (normed2 * norm_full[2] + norm_full[3]).astype(jnp.bfloat16)
    cross_query = jnp.dot(
        hidden2, query_full[:, 3 * model_width :], preferred_element_type=jnp.float32
    ).astype(jnp.bfloat16)
    text_pairs = jnp.einsum(
        "tfr,rfc->tc",
        text_folded,
        text_full.reshape(model_width, 2, 2 * model_width),
        preferred_element_type=jnp.float32,
    ).astype(jnp.bfloat16)
    text_key = text_pairs[:, :model_width]
    text_value = text_pairs[:, model_width:]
    attended2, logsum2 = attend_forward(cross_query, text_key, text_value, cross_mask)
    middle2 = middle1 + jnp.dot(
        attended2, outs_full[:, model_width:], preferred_element_type=jnp.float32
    )
    up_full, down_full = (
        lax.all_gather(up_low, "fsdp", axis=0, tiled=True),
        lax.all_gather(down_low, "fsdp", axis=0, tiled=True),
    )
    normed3, inverse3 = normalize(middle2)
    hidden3 = (normed3 * norm_full[4] + norm_full[5]).astype(jnp.bfloat16)
    up_values = jnp.dot(hidden3, up_full, preferred_element_type=jnp.float32)
    gelu_values, gelu_pull = jax.vjp(exact_gelu, up_values)
    activated = gelu_values.astype(jnp.bfloat16)
    branch3 = jnp.einsum(
        "tfr,rfc->tc",
        activated.reshape(row_count, 4, model_width),
        down_full.reshape(model_width, 4, model_width),
        preferred_element_type=jnp.float32,
    )
    result = (middle2 + branch3).astype(jnp.bfloat16)
    up_back, down_back = (
        lax.all_gather(up_low, "fsdp", axis=0, tiled=True),
        lax.all_gather(down_low, "fsdp", axis=0, tiled=True),
    )
    back_act = jnp.einsum(
        "tc,rfc->tfr",
        grad_out,
        down_back.reshape(model_width, 4, model_width),
        preferred_element_type=jnp.float32,
    ).reshape(row_count, 4 * model_width)
    back_up = gelu_pull(back_act)[0].astype(jnp.bfloat16)
    back_hidden3 = jnp.einsum("tk,rk->tr", back_up, up_back, preferred_element_type=jnp.float32)
    at_middle2 = grad_out.astype(jnp.float32) + norm_back(
        back_hidden3, normed3, inverse3, norm_full[4]
    )
    middle2_low = at_middle2.astype(jnp.bfloat16)
    query_back, outs_back = (
        lax.all_gather(query_low, "fsdp", axis=0, tiled=True),
        lax.all_gather(outs_low, "fsdp", axis=0, tiled=True),
    )
    back_att2 = jnp.einsum(
        "tc,rc->tr", middle2_low, outs_back[:, model_width:], preferred_element_type=jnp.float32
    ).astype(jnp.bfloat16)
    cross_qgrad, text_kgrad, text_vgrad = attend_backward(
        cross_query, text_key, text_value, cross_mask, logsum2, back_att2
    )
    back_cross = cross_qgrad.astype(jnp.bfloat16)
    back_pairs = jnp.concatenate([text_kgrad, text_vgrad], axis=1).astype(jnp.bfloat16)
    back_hidden2 = jnp.einsum(
        "tc,rc->tr",
        back_cross,
        query_back[:, 3 * model_width :],
        preferred_element_type=jnp.float32,
    )
    at_middle1 = at_middle2 + norm_back(back_hidden2, normed2, inverse2, norm_full[2])
    middle1_low = at_middle1.astype(jnp.bfloat16)
    back_att1 = jnp.einsum(
        "tc,rc->tr", middle1_low, outs_back[:, :model_width], preferred_element_type=jnp.float32
    ).astype(jnp.bfloat16)
    self_qgrad, self_kgrad, self_vgrad = attend_backward(
        self_query, self_key, self_value, self_mask, logsum1, back_att1
    )
    back_projected = jnp.concatenate([self_qgrad, self_kgrad, self_vgrad], axis=1).astype(
        jnp.bfloat16
    )
    back_hidden1 = jnp.einsum(
        "tc,rc->tr",
        back_projected,
        query_back[:, : 3 * model_width],
        preferred_element_type=jnp.float32,
    )
    grad_in = (at_middle1 + norm_back(back_hidden1, normed1, inverse1, norm_full[0])).astype(
        jnp.bfloat16
    )
    norm_term = jnp.stack(
        [
            jnp.sum(back_hidden1 * normed1, axis=0),
            jnp.sum(back_hidden1, axis=0),
            jnp.sum(back_hidden2 * normed2, axis=0),
            jnp.sum(back_hidden2, axis=0),
            jnp.sum(back_hidden3 * normed3, axis=0),
            jnp.sum(back_hidden3, axis=0),
        ]
    )
    own_first = lax.axis_index("fsdp") * own_rows
    hidden_piece = lax.all_gather(hidden3, "fsdp", axis=0, tiled=True)
    back_piece = lax.all_gather(back_up, "fsdp", axis=0, tiled=True)
    act_piece = lax.all_gather(activated, "fsdp", axis=0, tiled=True)
    grad_piece = lax.all_gather(grad_out, "fsdp", axis=0, tiled=True)
    hidden_cols = lax.dynamic_slice_in_dim(hidden_piece, own_first, own_rows, 1)
    act_cols = lax.dynamic_slice_in_dim(
        act_piece.reshape(act_piece.shape[0], 4, model_width), own_first, own_rows, 2
    )
    up_part = jnp.einsum("tr,tk->rk", hidden_cols, back_piece, preferred_element_type=jnp.float32)
    down_part = jnp.einsum(
        "tfr,tc->rfc", act_cols, grad_piece, preferred_element_type=jnp.float32
    ).reshape(own_rows, 4 * model_width)
    hidden_piece = lax.all_gather(hidden2, "fsdp", axis=0, tiled=True)
    back_piece = lax.all_gather(back_cross, "fsdp", axis=0, tiled=True)
    attended_piece = lax.all_gather(attended2, "fsdp", axis=0, tiled=True)
    carry_piece = lax.all_gather(middle2_low, "fsdp", axis=0, tiled=True)
    hidden_cols = lax.dynamic_slice_in_dim(hidden_piece, own_first, own_rows, 1)
    attended_cols = lax.dynamic_slice_in_dim(attended_piece, own_first, own_rows, 1)
    query_part = jnp.einsum(
        "tr,tc->rc", hidden_cols, back_piece, preferred_element_type=jnp.float32
    )
    outs_part = jnp.einsum(
        "tr,tc->rc", attended_cols, carry_piece, preferred_element_type=jnp.float32
    )
    text_piece = lax.all_gather(text_in, "fsdp", axis=0, tiled=True)
    back_piece = lax.all_gather(back_pairs, "fsdp", axis=0, tiled=True)
    text_cols = lax.dynamic_slice_in_dim(
        text_piece.reshape(text_piece.shape[0], 2, model_width), own_first, own_rows, 2
    )
    text_part = jnp.einsum(
        "tfr,tc->rfc", text_cols, back_piece, preferred_element_type=jnp.float32
    ).reshape(own_rows, 4 * model_width)
    hidden_piece = lax.all_gather(hidden1, "fsdp", axis=0, tiled=True)
    back_piece = lax.all_gather(back_projected, "fsdp", axis=0, tiled=True)
    attended_piece = lax.all_gather(attended1, "fsdp", axis=0, tiled=True)
    carry_piece = lax.all_gather(middle1_low, "fsdp", axis=0, tiled=True)
    hidden_cols = lax.dynamic_slice_in_dim(hidden_piece, own_first, own_rows, 1)
    attended_cols = lax.dynamic_slice_in_dim(attended_piece, own_first, own_rows, 1)
    fold_query_part = jnp.einsum(
        "tr,tc->rc", hidden_cols, back_piece, preferred_element_type=jnp.float32
    )
    fold_outs_part = jnp.einsum(
        "tr,tc->rc", attended_cols, carry_piece, preferred_element_type=jnp.float32
    )
    query_rows = jnp.concatenate([fold_query_part, query_part], axis=1)
    outs_rows = jnp.concatenate([fold_outs_part, outs_part], axis=1)
    query_slots = to_slots(query_rows, slot_query, cap_big * dp_count)
    up_slots = to_slots(up_part, slot_up, cap_big * dp_count)
    outs_slots = to_slots(outs_rows, slot_outs, cap_out * dp_count)
    text_slots = to_slots(text_part, slot_text, cap_big * dp_count)
    down_slots = to_slots(down_part, slot_down, cap_big * dp_count)
    query_grad, up_grad, outs_grad, text_grad, down_grad = (
        lax.psum_scatter(
            query_slots.astype(jnp.bfloat16), "dp", scatter_dimension=1, tiled=True
        ).astype(jnp.float32),
        lax.psum_scatter(
            up_slots.astype(jnp.bfloat16), "dp", scatter_dimension=1, tiled=True
        ).astype(jnp.float32),
        lax.psum_scatter(
            outs_slots.astype(jnp.bfloat16), "dp", scatter_dimension=1, tiled=True
        ).astype(jnp.float32),
        lax.psum_scatter(
            text_slots.astype(jnp.bfloat16), "dp", scatter_dimension=1, tiled=True
        ).astype(jnp.float32),
        lax.psum_scatter(
            down_slots.astype(jnp.bfloat16), "dp", scatter_dimension=1, tiled=True
        ).astype(jnp.float32),
    )
    norm_total = lax.psum(norm_term, ("dp", "fsdp"))
    norm_share = model_width // dp_count
    norm_grad = lax.dynamic_slice_in_dim(
        norm_total, lax.axis_index("dp") * norm_share, norm_share, 1
    )
    query_first, query_second, query_weight = adamw_update(
        w_query, m_query, v_query, query_grad, rate_query, decay_rate
    )
    up_first, up_second, up_weight = adamw_update(w_up, m_up, v_up, up_grad, rate_up, decay_rate)
    outs_first, outs_second, outs_weight = adamw_update(
        w_outs, m_outs, v_outs, outs_grad, rate_outs, decay_rate
    )
    text_first, text_second, text_weight = adamw_update(
        w_text, m_text, v_text, text_grad, rate_text, decay_rate
    )
    down_first, down_second, down_weight = adamw_update(
        w_down, m_down, v_down, down_grad, rate_down, decay_rate
    )
    norm_first, norm_second, norm_new = adamw_update(
        norm_weight, m_norm, v_norm, norm_grad, rate_norm, 0.0
    )
    return (
        result,
        grad_in,
        query_first,
        query_second,
        query_weight,
        up_first,
        up_second,
        up_weight,
        outs_first,
        outs_second,
        outs_weight,
        text_first,
        text_second,
        text_weight,
        down_first,
        down_second,
        down_weight,
        norm_first,
        norm_second,
        norm_new,
    )


def solution(mesh):
    in_specs = (
        P(("dp", "fsdp"), None),
        P(("dp", "fsdp"), None),
        P(("dp", "fsdp"), None),
        P(("dp", "fsdp"), None),
        P(("dp", "fsdp"), None),
        P(),
        P(),
        P(),
        P(),
        P(),
        P("fsdp", "dp"),
        P("fsdp", "dp"),
        P("fsdp", "dp"),
        P("fsdp", "dp"),
        P("fsdp", "dp"),
        P("fsdp", "dp"),
        P("fsdp", "dp"),
        P("fsdp", "dp"),
        P("fsdp", "dp"),
        P("fsdp", "dp"),
        P("fsdp", "dp"),
        P("fsdp", "dp"),
        P("fsdp", "dp"),
        P("fsdp", "dp"),
        P("fsdp", "dp"),
        P(None, "dp"),
        P(None, "dp"),
        P(None, "dp"),
    )
    out_specs = (
        P(("dp", "fsdp"), None),
        P(("dp", "fsdp"), None),
        P("fsdp", "dp"),
        P("fsdp", "dp"),
        P("fsdp", "dp"),
        P("fsdp", "dp"),
        P("fsdp", "dp"),
        P("fsdp", "dp"),
        P("fsdp", "dp"),
        P("fsdp", "dp"),
        P("fsdp", "dp"),
        P("fsdp", "dp"),
        P("fsdp", "dp"),
        P("fsdp", "dp"),
        P("fsdp", "dp"),
        P("fsdp", "dp"),
        P("fsdp", "dp"),
        P(None, "dp"),
        P(None, "dp"),
        P(None, "dp"),
    )
    return jax.shard_map(body, mesh=mesh, in_specs=in_specs, out_specs=out_specs, check_vma=False)
```

profile of v0, /device:TPU:0, one launch (start us, length us, event | category | flops | bytes accessed | tf_op | source)
XLA Modules:
  0.0 4494.9 jit_solution(15797088008939239209)
XLA Ops:
  48.8 60.3 %all-gather.25.cloned.1.call-done = bf16[512,16384]{0,1:T(8,128)(2,1)} async-done(((bf16[512,2048]{0,1:T(8,128)(2,1)}), bf16[512,16384]{0,1:T(8,128)(2,1)}) %all-gather.25.cloned.1.call-update) | async-done | bytes 16777232 | tf_op jit(solution)/shard_map/all_gather | solution.py:189
  166.9 34.6 all-gather.41.cloned.1.call-done
  289.9 60.7 %all-gather.33.cloned.1.call-done = bf16[512,16384]{0,1:T(8,128)(2,1)} async-done(((bf16[512,2048]{0,1:T(8,128)(2,1)}), bf16[512,16384]{0,1:T(8,128)(2,1)}) %all-gather.33.cloned.1.call-update) | async-done | bytes 16777232 | tf_op jit(solution)/shard_map/all_gather | solution.py:192
  408.1 34.7 all-gather.37.cloned.1.call-done
  512.2 493.4 %all-gather.27.cloned.1.call-done = bf16[2048,8192]{0,1:T(8,128)(2,1)} async-done(((bf16[512,8192]{0,1:T(8,128)(2,1)}), bf16[2048,8192]{0,1:T(8,128)(2,1)}) %all-gather.27.cloned.1.call-update) | async-done | bytes 33554448 | tf_op jit(solution)/shard_map/all_gather | solution.py:212
  1022.9 544.0 %all-gather.43.cloned.1.call-done = bf16[2048,8192]{0,1:T(8,128)(2,1)} async-done(((bf16[512,8192]{0,1:T(8,128)(2,1)}), bf16[2048,8192]{0,1:T(8,128)(2,1)}) %all-gather.43.cloned.1.call-update) | async-done | bytes 33554448 | tf_op jit(solution)/shard_map/all_gather | solution.py:248
  1593.8 260.1 %all-gather.31.cloned.1.call-done = bf16[2048,4096]{0,1:T(8,128)(2,1)} async-done(((bf16[512,4096]{0,1:T(8,128)(2,1)}), bf16[2048,4096]{0,1:T(8,128)(2,1)}) %all-gather.31.cloned.1.call-update) | async-done | bytes 16777232 | tf_op jit(solution)/shard_map/all_gather | solution.py:213
  1860.8 554.4 %all-gather.35.cloned.1.call-done = bf16[2048,8192]{0,1:T(8,128)(2,1)} async-done(((bf16[512,8192]{0,1:T(8,128)(2,1)}), bf16[2048,8192]{0,1:T(8,128)(2,1)}) %all-gather.35.cloned.1.call-update) | async-done | bytes 33554448 | tf_op jit(solution)/shard_map/all_gather | solution.py:214
  2454.3 522.0 %all-gather.39.cloned.1.call-done = bf16[2048,8192]{0,1:T(8,128)(2,1)} async-done(((bf16[512,8192]{0,1:T(8,128)(2,1)}), bf16[2048,8192]{0,1:T(8,128)(2,1)}) %all-gather.39.cloned.1.call-update) | async-done | bytes 33554448 | tf_op jit(solution)/shard_map/all_gather | solution.py:247
  2976.2 27.7 add_convert_fusion
  3064.8 46.7 %all-gather.61.cloned.1.call-done = bf16[512,2048]{0,1:T(8,128)(2,1)} async-done(((bf16[128,2048]{0,1:T(8,128)(2,1)}), bf16[512,2048]{0,1:T(8,128)(2,1)}) %all-gather.61.cloned.1.call-update) | async-done | bytes 2097168 | tf_op jit(solution)/shard_map/all_gather | solution.py:341
  3116.5 41.3 all-gather.59.cloned.1.call-done
  3157.8 47.0 %all-gather.57.cloned.1.call-done = bf16[512,2048]{0,1:T(8,128)(2,1)} async-done(((bf16[128,2048]{0,1:T(8,128)(2,1)}), bf16[512,2048]{0,1:T(8,128)(2,1)}) %all-gather.57.cloned.1.call-update) | async-done | bytes 2097168 | tf_op jit(solution)/shard_map/all_gather | solution.py:361
  3310.8 43.2 all-gather.49.cloned.1.call-done
  3359.1 41.2 all-gather.45.cloned.1.call-done
  3400.3 115.6 %all-gather.47.cloned.1.call-done = bf16[512,6144]{0,1:T(8,128)(2,1)} async-done(((bf16[128,6144]{0,1:T(8,128)(2,1)}), bf16[512,6144]{0,1:T(8,128)(2,1)}) %all-gather.47.cloned.1.call-update) | async-done | bytes 6291472 | tf_op jit(solution)/shard_map/all_gather | solution.py:360
  3589.4 123.3 %all-gather.55.cloned.1.call-done = bf16[512,8192]{1,0:T(8,128)(2,1)} async-done(((bf16[128,8192]{1,0:T(8,128)(2,1)}), bf16[512,8192]{1,0:T(8,128)(2,1)}) %all-gather.55.cloned.1.call-update) | async-done | bytes 8388624 | tf_op jit(solution)/shard_map/all_gather | solution.py:328
  3788.6 74.1 %all-gather.69.cloned.1.call-done = bf16[512,8192]{1,0:T(8,128)(2,1)} async-done(((bf16[128,8192]{1,0:T(8,128)(2,1)}), bf16[512,8192]{1,0:T(8,128)(2,1)}) %all-gather.69.cloned.1.call-update) | async-done | bytes 8388624 | tf_op jit(solution)/shard_map/all_gather | solution.py:329
  3874.8 33.6 all-gather.71.cloned.1.call-done
  3998.9 23.3 copy.388
  4087.2 39.5 psum.7
  4190.2 31.9 reduce-scatter.6.cloned.1.call-done
  4249.3 92.8 %reduce-scatter.8.cloned.1.call-done = bf16[512,2048]{0,1:T(8,128)(2,1)} async-done(((bf16[512,16384]{0,1:T(8,128)(2,1)}), bf16[512,2048]{0,1:T(8,128)(2,1)}) %reduce-scatter.8.cloned.1.call-update) | async-done | bytes 2097168 | tf_op jit(solution)/shard_map/reduce_scatter | solution.py:382
  4369.6 92.5 %reduce-scatter.14.cloned.1.call-done = bf16[512,2048]{0,1:T(8,128)(2,1)} async-done(((bf16[512,16384]{0,1:T(8,128)(2,1)}), bf16[512,2048]{0,1:T(8,128)(2,1)}) %reduce-scatter.14.cloned.1.call-update) | async-done | bytes 2097168 | tf_op jit(solution)/shard_map/reduce_scatter | solution.py:391
  (432 shorter events, 1041.4 us)
Async XLA Ops:
  25.6 233.3 %all-gather.29.cloned.1.call-start = ((), (), s32[]{:S(2)}) async-start(), calls=%async_computation.7 | async-start | bytes 9437184 | tf_op jit(solution)/shard_map/all_gather | solution.py:191
  29.2 321.3 %all-gather.33.cloned.1.call-start = ((), (), s32[]{:S(2)}) async-start(), calls=%async_computation.9 | async-start | bytes 18874368 | tf_op jit(solution)/shard_map/all_gather | solution.py:192
  38.8 403.9 %all-gather.37.cloned.1.call-start = ((), (), s32[]{:S(2)}) async-start(), calls=%async_computation.11 | async-start | bytes 18874368 | tf_op jit(solution)/shard_map/all_gather | solution.py:190
  48.0 957.6 %all-gather.27.cloned.1.call-start = ((), (), s32[]{:S(2)}) async-start(), calls=%async_computation.6 | async-start | bytes 41943040 | tf_op jit(solution)/shard_map/all_gather | solution.py:212
  165.5 1401.4 %all-gather.43.cloned.1.call-start = ((), (), s32[]{:S(2)}) async-start(), calls=%async_computation.14 | async-start | bytes 41943040 | tf_op jit(solution)/shard_map/all_gather | solution.py:248
  257.4 1596.6 %all-gather.31.cloned.1.call-start = ((), (), s32[]{:S(2)}) async-start(), calls=%async_computation.8 | async-start | bytes 20971520 | tf_op jit(solution)/shard_map/all_gather | solution.py:213
  288.5 2126.7 %all-gather.35.cloned.1.call-start = ((), (), s32[]{:S(2)}) async-start(), calls=%async_computation.10 | async-start | bytes 41943040 | tf_op jit(solution)/shard_map/all_gather | solution.py:214
  406.7 2569.5 %all-gather.39.cloned.1.call-start = ((), (), s32[]{:S(2)}) async-start(), calls=%async_computation.12 | async-start | bytes 41943040 | tf_op jit(solution)/shard_map/all_gather | solution.py:247
  500.8 2564.0 %all-gather.63.cloned.1.call-start = ((), (), s32[]{:S(2)}) async-start(), calls=%async_computation.26 | async-start | bytes 2621440 | tf_op jit(solution)/shard_map/all_gather | solution.py:342
  3038.0 215.3 %all-gather.67.cloned.1.call-start = ((), (), s32[]{:S(2)}) async-start(), calls=%async_computation.29 | async-start | bytes 1310720 | tf_op jit(solution)/shard_map/all_gather | solution.py:351
  3038.5 222.7 %all-gather.65.cloned.1.call-start = ((), (), s32[]{:S(2)}) async-start(), calls=%async_computation.28 | async-start | bytes 1310720 | tf_op jit(solution)/shard_map/all_gather | solution.py:352
  3041.0 269.9 %all-gather.51.cloned.1.call-start = ((), (), s32[]{:S(2)}) async-start(), calls=%async_computation.18 | async-start | bytes 2621440 | tf_op jit(solution)/shard_map/all_gather | solution.py:340
  3041.5 312.5 %all-gather.49.cloned.1.call-start = ((), (), s32[]{:S(2)}) async-start(), calls=%async_computation.17 | async-start | bytes 2621440 | tf_op jit(solution)/shard_map/all_gather | solution.py:339
  3042.1 358.2 %all-gather.45.cloned.1.call-start = ((), (), s32[]{:S(2)}) async-start(), calls=%async_computation.15 | async-start | bytes 2621440 | tf_op jit(solution)/shard_map/all_gather | solution.py:359
  3042.9 473.0 %all-gather.47.cloned.1.call-start = ((), (), s32[]{:S(2)}) async-start(), calls=%async_computation.16 | async-start | bytes 7864320 | tf_op jit(solution)/shard_map/all_gather | solution.py:360
  3056.8 532.6 %all-gather.53.cloned.1.call-start = ((), (), s32[]{:S(2)}) async-start(), calls=%async_computation.20 | async-start | bytes 2621440 | tf_op jit(solution)/shard_map/all_gather | solution.py:327
  3057.5 655.2 %all-gather.55.cloned.1.call-start = ((), (), s32[]{:S(2)}) async-start(), calls=%async_computation.21 | async-start | bytes 10485760 | tf_op jit(solution)/shard_map/all_gather | solution.py:328
  3058.3 804.5 %all-gather.69.cloned.1.call-start = ((), (), s32[]{:S(2)}) async-start(), calls=%async_computation.31 | async-start | bytes 10485760 | tf_op jit(solution)/shard_map/all_gather | solution.py:329
  3063.6 844.7 %all-gather.71.cloned.1.call-start = ((), (), s32[]{:S(2)}) async-start(), calls=%async_computation.32 | async-start | bytes 2621440 | tf_op jit(solution)/shard_map/all_gather | solution.py:330
  3064.2 1084.4 %reduce-scatter.10.cloned.1.call-start = ((), (), s32[]{:S(2)}) async-start(), calls=%async_computation.27 | async-start | bytes 9437184 | tf_op jit(solution)/shard_map/reduce_scatter | solution.py:385
  3251.4 911.6 %reduce-scatter.12.cloned.1.call-start = ((), (), s32[]{:S(2)}) async-start(), calls=%async_computation.30 | async-start | bytes 18874368 | tf_op jit(solution)/shard_map/reduce_scatter | solution.py:388
  3310.0 912.1 %reduce-scatter.6.cloned.1.call-start = ((), (), s32[]{:S(2)}) async-start(), calls=%async_computation.19 | async-start | bytes 18874368 | tf_op jit(solution)/shard_map/reduce_scatter | solution.py:379
  3589.3 752.9 %reduce-scatter.8.cloned.1.call-start = ((), (), s32[]{:S(2)}) async-start(), calls=%async_computation.22 | async-start | bytes 18874368 | tf_op jit(solution)/shard_map/reduce_scatter | solution.py:382
  3788.0 674.1 %reduce-scatter.14.cloned.1.call-start = ((), (), s32[]{:S(2)}) async-start(), calls=%async_computation.33 | async-start | bytes 18874368 | tf_op jit(solution)/shard_map/reduce_scatter | solution.py:391
  (86 other events, 9486.9 us)
Sparse Core Ops, SparseCore 0:
  16.5 92.5 all-gather.24
  111.6 89.8 all-gather.40
  203.9 54.3 all-gather.28
  260.7 89.8 all-gather.32
  352.9 89.8 all-gather.36
  444.2 561.3 all-gather.26
  1007.2 559.6 all-gather.42
  1569.0 284.9 all-gather.30
  1855.6 559.5 all-gather.34
  2416.6 559.5 all-gather.38
  3066.4 44.9 all-gather.60
  3113.6 44.1 all-gather.58
  3159.8 44.9 all-gather.56
  3262.6 45.7 all-gather.50
  3309.8 44.1 all-gather.48
  3355.6 44.6 all-gather.44
  3402.3 113.5 all-gather.46
  3564.3 148.3 all-gather.54
  3714.9 147.8 all-gather.68
  3911.8 69.9 reduce-scatter.9
  3985.7 116.5 reduce-scatter.11
  4106.1 115.9 reduce-scatter.5
  4226.1 115.9 reduce-scatter.7
  4346.1 115.9 reduce-scatter.13
  (5 shorter events, 185.7 us)
where the time goes:
time: 4510 us; the launch traced here: 4490 us
  waiting for transfers between devices  3360 us (75%)
  local copies, waits for them, and re-layouts  611 us (14%)
  other arithmetic  230 us (5%)
  matrix products  228 us (5%)
  blocking collectives  48 us (1%)
    all_gather x1, waiting for transfers between devices, body(): lax.all_gather(text_low, 'fsdp', axis=0, tiled=True)  554 us
    all_gather x1, waiting for transfers between devices, body(): lax.all_gather(down_low, 'fsdp', axis=0, tiled=True)  544 us
    all_gather x1, waiting for transfers between devices, body(): lax.all_gather(up_low, 'fsdp', axis=0, tiled=True)  522 us
    all_gather x1, waiting for transfers between devices, body(): lax.all_gather(query_low, 'fsdp', axis=0, tiled=True)  493 us
    all_gather x1, waiting for transfers between devices, body(): lax.all_gather(outs_low, 'fsdp', axis=0, tiled=True)  260 us
    unnamed x194, local copies, waits for them, and re-layouts  157 us
    all_gather x1, waiting for transfers between devices, body(): back_piece = lax.all_gather(back_up, 'fsdp', axis=0, tiled=True)  123 us
    all_gather x1, waiting for transfers between devices, body(): back_piece = lax.all_gather(back_projected, 'fsdp', axis=0, tiled=True)  116 us
  transfers between devices with their start and end apart: 29, of which 22 were waited for; matrix products, arithmetic and copies ran while one was open for 22% of the time, Pallas kernels for 0%

commit v1 on v0

v1 whole, which is shorter than its diff:
```python
import functools

import jax
import jax.numpy as jnp
from jax import lax
from jax.experimental import pallas as pl
from jax.experimental.pallas import tpu as pltpu
from jax.sharding import PartitionSpec as P

HEADS = 16
HEAD = 128
STEP = 10
BLK = 128


beta_first = 0.9
beta_second = 0.999
adam_eps = 1e-08
decay_rate = 0.01
rate_query = 0.04
rate_up = 0.04
rate_outs = 0.12
rate_text = 0.03
rate_down = 0.03
rate_norm = 0.5
norm_eps = 1e-05
score_floor = -1e30
bf16 = jnp.bfloat16
f32 = jnp.float32


def normalize(values):
    centered = values - jnp.mean(values, axis=-1, keepdims=True)
    inverse_std = lax.rsqrt(jnp.mean(centered * centered, axis=-1, keepdims=True) + norm_eps)
    return (centered * inverse_std, inverse_std)


def norm_back(back_hidden, normed, inverse_std, gain_row):
    back_normed = back_hidden * gain_row
    return inverse_std * (
        back_normed
        - jnp.mean(back_normed, axis=-1, keepdims=True)
        - normed * jnp.mean(back_normed * normed, axis=-1, keepdims=True)
    )


def exact_gelu(values):
    return jax.nn.gelu(values, approximate=False)


def adamw_update(weight, first, second, gradient, rate, decay):
    first_new = beta_first * first + (1.0 - beta_first) * gradient
    second_new = beta_second * second + (1.0 - beta_second) * gradient * gradient
    first_hat = first_new / (1.0 - beta_first**STEP)
    second_hat = second_new / (1.0 - beta_second**STEP)
    weight_new = weight - rate * (first_hat / (jnp.sqrt(second_hat) + adam_eps) + decay * weight)
    return (first_new, second_new, weight_new)


def dot(left, right):
    return jnp.dot(left, right, preferred_element_type=f32)


def dot_nt(left, right):
    return lax.dot_general(left, right, (((1,), (1,)), ((), ())), preferred_element_type=f32)


def dot_tn(left, right):
    return lax.dot_general(left, right, (((0,), (0,)), ((), ())), preferred_element_type=f32)


def split_place(block, per_part, parts):
    group, rest = divmod(block, per_part * parts)
    part, inner = divmod(rest, per_part)
    return part, group * per_part + inner


def flat_place(block):
    return 0, block


def compact_kernel(places, n_dp, owner_ref, slots_ref, out_ref, count_ref):
    for index in range(n_dp):
        count_ref[index] = 0
    for block, (part, column) in enumerate(places):
        owner = owner_ref[block]
        position = count_ref[owner]
        count_ref[owner] = position + 1
        start = pl.multiple_of(position * BLK, BLK)
        out_ref[part, :, column * BLK : (column + 1) * BLK] = slots_ref[
            owner, :, pl.ds(start, BLK)
        ]


def compact(slots, owner, places, parts):
    n_dp, rows, _ = slots.shape
    columns = len(places) // parts * BLK
    return pl.pallas_call(
        functools.partial(compact_kernel, places, n_dp),
        out_shape=jax.ShapeDtypeStruct((parts, rows, columns), slots.dtype),
        in_specs=[
            pl.BlockSpec(memory_space=pltpu.SMEM),
            pl.BlockSpec(memory_space=pltpu.VMEM),
        ],
        out_specs=pl.BlockSpec(memory_space=pltpu.VMEM),
        scratch_shapes=[pltpu.SMEM((n_dp,), jnp.int32)],
        compiler_params=pltpu.CompilerParams(vmem_limit_bytes=32 * 1024 * 1024),
        cost_estimate=pl.CostEstimate(
            flops=0, bytes_accessed=2 * (slots.size + len(places) * BLK * rows), transcendentals=0
        ),
    )(owner, slots)


def expand_kernel(places, n_dp, owner_ref, grad_ref, out_ref, count_ref):
    for index in range(n_dp):
        count_ref[index] = 0
    out_ref[...] = jnp.zeros_like(out_ref)
    for block, (part, column) in enumerate(places):
        owner = owner_ref[block]
        position = count_ref[owner]
        count_ref[owner] = position + 1
        start = pl.multiple_of(position * BLK, BLK)
        out_ref[owner, :, pl.ds(start, BLK)] = grad_ref[
            part, :, column * BLK : (column + 1) * BLK
        ]


def expand(grad, owner, places, n_dp, capacity):
    rows = grad.shape[1]
    return pl.pallas_call(
        functools.partial(expand_kernel, places, n_dp),
        out_shape=jax.ShapeDtypeStruct((n_dp, rows, capacity * BLK), grad.dtype),
        in_specs=[
            pl.BlockSpec(memory_space=pltpu.SMEM),
            pl.BlockSpec(memory_space=pltpu.VMEM),
        ],
        out_specs=pl.BlockSpec(memory_space=pltpu.VMEM),
        scratch_shapes=[pltpu.SMEM((n_dp,), jnp.int32)],
        compiler_params=pltpu.CompilerParams(vmem_limit_bytes=32 * 1024 * 1024),
        cost_estimate=pl.CostEstimate(
            flops=0,
            bytes_accessed=2 * (grad.size + n_dp * capacity * BLK * rows),
            transcendentals=0,
        ),
    )(owner, grad)


def swap(values, axis):
    return lax.all_to_all(values, axis, 0, 0, tiled=True)


def z_gather(values):
    return lax.all_gather(values, "fsdp", axis=0, tiled=True)


def z_reduce(values):
    return lax.psum_scatter(values.astype(bf16), "fsdp", scatter_dimension=0, tiled=True).astype(
        f32
    )


def attend_forward(queries, keys, values, allowed):
    packed = allowed.shape[0]
    heads = queries.shape[1] // HEAD
    query_heads = queries.reshape(packed, -1, heads, HEAD)
    key_heads = keys.reshape(packed, -1, heads, HEAD)
    value_heads = values.reshape(packed, -1, heads, HEAD)
    scores = jnp.einsum(
        "pqhd,pkhd->phqk", query_heads, key_heads, preferred_element_type=f32
    ) * HEAD ** (-0.5)
    scores = jnp.where(allowed[:, None], scores, score_floor)
    powers = jnp.exp(scores - jnp.max(scores, axis=-1, keepdims=True))
    shares = powers / jnp.sum(powers, axis=-1, keepdims=True)
    attended = jnp.einsum(
        "phqk,pkhd->pqhd", shares.astype(bf16), value_heads, preferred_element_type=f32
    )
    return attended.reshape(queries.shape).astype(bf16), shares


def attend_backward(queries, keys, values, shares, back_attended):
    packed = shares.shape[0]
    heads = queries.shape[1] // HEAD
    query_heads = queries.reshape(packed, -1, heads, HEAD)
    key_heads = keys.reshape(packed, -1, heads, HEAD)
    value_heads = values.reshape(packed, -1, heads, HEAD)
    back_heads = back_attended.reshape(packed, -1, heads, HEAD)
    score_scale = HEAD ** (-0.5)
    back_shares = jnp.einsum(
        "pqhd,pkhd->phqk", back_heads, value_heads, preferred_element_type=f32
    )
    inner_sum = jnp.sum(shares * back_shares, axis=-1, keepdims=True)
    back_scores = (shares * (back_shares - inner_sum)).astype(bf16)
    query_grad = (
        jnp.einsum("phqk,pkhd->pqhd", back_scores, key_heads, preferred_element_type=f32)
        * score_scale
    )
    key_grad = (
        jnp.einsum("phqk,pqhd->pkhd", back_scores, query_heads, preferred_element_type=f32)
        * score_scale
    )
    value_grad = jnp.einsum(
        "phqk,pqhd->pkhd", shares.astype(bf16), back_heads, preferred_element_type=f32
    )
    return (
        query_grad.reshape(queries.shape).astype(bf16),
        key_grad.reshape(keys.shape).astype(bf16),
        value_grad.reshape(values.shape).astype(bf16),
    )


def body(
    tokens_in,
    text_in,
    seg_ids,
    capt_ids,
    grad_out,
    owner_query,
    owner_up,
    owner_outs,
    owner_text,
    owner_down,
    w_query,
    m_query,
    v_query,
    w_up,
    m_up,
    v_up,
    w_outs,
    m_outs,
    v_outs,
    w_text,
    m_text,
    v_text,
    w_down,
    m_down,
    v_down,
    norm_weight,
    m_norm,
    v_norm,
):
    n_dp = lax.axis_size("dp")
    n_z = lax.axis_size("fsdp")
    width = tokens_in.shape[1]
    own_rows = w_query.shape[0]
    chunk = own_rows // n_dp
    cap_big = w_query.shape[1] // BLK
    cap_out = w_outs.shape[1] // BLK
    heads_z = HEADS // n_z
    share = width // n_z
    owner_query, owner_up, owner_outs, owner_text, owner_down = (
        owner[:, 0] for owner in (owner_query, owner_up, owner_outs, owner_text, owner_down)
    )
    split_places = [split_place(b, heads_z, n_z) for b in range(owner_query.shape[0])]
    big_places = [flat_place(b) for b in range(owner_down.shape[0])]
    out_places = [flat_place(b) for b in range(owner_outs.shape[0])]

    def shuffled(values):
        lead = values.shape[:-1]
        folds = values.shape[-1] // width
        cut = values.reshape(lead[0], folds, n_z, n_dp, chunk)
        return cut.transpose(0, 1, 3, 2, 4).reshape(values.shape)

    def unshuffled(values):
        cut = values.reshape(values.shape[0], n_dp, n_z, chunk)
        return cut.transpose(0, 2, 1, 3).reshape(values.shape)

    def fetch(weight, owner, places, parts):
        slots = swap(weight.astype(bf16), "dp").reshape(n_dp, chunk, -1)
        rows = compact(slots, owner, places, parts)
        if parts > 1:
            rows = swap(rows, "fsdp")
        rows = rows.reshape(parts * chunk, -1)
        return lax.all_gather(rows, "dp", axis=0, tiled=True)

    def settle(pieces, owner, places, parts, capacity):
        summed = [
            lax.psum_scatter(piece, "dp", scatter_dimension=0, tiled=True) for piece in pieces
        ]
        summed = summed[0] if len(summed) == 1 else jnp.concatenate(summed, axis=1)
        rows = summed.reshape(parts, chunk, -1)
        if parts > 1:
            rows = swap(rows, "fsdp")
        slots = expand(rows, owner, places, n_dp, capacity)
        return swap(slots, "dp").reshape(n_dp * chunk, -1).astype(f32)

    norm_full = lax.all_gather(norm_weight, "dp", axis=1, tiled=True)
    marks = lax.all_gather(jnp.concatenate([seg_ids, capt_ids], axis=1), "fsdp", axis=0, tiled=True)
    token_count = tokens_in.shape[0]
    segment = marks[:, :token_count]
    caption = marks[:, token_count:]
    self_mask = segment[:, :, None] == segment[:, None, :]
    cross_mask = segment[:, :, None] == caption[:, None, :]

    query_z = fetch(w_query, owner_query, split_places, n_z)
    outs_z = fetch(w_outs, owner_outs, out_places, 1)
    text_z = fetch(w_text, owner_text, split_places, n_z)
    up_z = fetch(w_up, owner_up, split_places, n_z)
    down_z = fetch(w_down, owner_down, big_places, 1)

    inputs = tokens_in.astype(f32)
    normed1, inverse1 = normalize(inputs)
    hidden1 = z_gather(shuffled((normed1 * norm_full[0] + norm_full[1]).astype(bf16)))
    text_all = z_gather(shuffled(text_in))
    grad_all = z_gather(grad_out)

    projected = dot(hidden1, query_z[:, : 3 * share]).astype(bf16)
    self_query = projected[:, :share]
    self_key = projected[:, share : 2 * share]
    self_value = projected[:, 2 * share :]
    attended1, shares1 = attend_forward(self_query, self_key, self_value, self_mask)
    middle1 = inputs + z_reduce(dot(attended1, outs_z[:, :width]))
    normed2, inverse2 = normalize(middle1)
    hidden2 = z_gather(shuffled((normed2 * norm_full[2] + norm_full[3]).astype(bf16)))
    cross_query = dot(hidden2, query_z[:, 3 * share :]).astype(bf16)
    text_pairs = (
        dot(text_all[:, :width], text_z[:, : 2 * share])
        + dot(text_all[:, width:], text_z[:, 2 * share :])
    ).astype(bf16)
    text_key = text_pairs[:, :share]
    text_value = text_pairs[:, share:]
    attended2, shares2 = attend_forward(cross_query, text_key, text_value, cross_mask)
    middle2 = middle1 + z_reduce(dot(attended2, outs_z[:, width:]))
    normed3, inverse3 = normalize(middle2)
    hidden3 = z_gather(shuffled((normed3 * norm_full[4] + norm_full[5]).astype(bf16)))
    up_values = dot(hidden3, up_z)
    gelu_values, gelu_pull = jax.vjp(exact_gelu, up_values)
    activated = gelu_values.astype(bf16)
    branch3 = sum(
        dot(activated[:, f * share : (f + 1) * share], down_z[:, f * width : (f + 1) * width])
        for f in range(4)
    )
    result = (middle2 + z_reduce(branch3)).astype(bf16)

    down_part = jnp.concatenate(
        [dot_tn(activated[:, f * share : (f + 1) * share], grad_all).astype(bf16) for f in range(4)],
        axis=1,
    )
    down_grad = settle([down_part], owner_down, big_places, 1, cap_big)
    back_act = jnp.concatenate(
        [dot_nt(grad_all, down_z[:, f * width : (f + 1) * width]) for f in range(4)], axis=1
    )
    back_up = gelu_pull(back_act)[0].astype(bf16)
    back_hidden3 = unshuffled(z_reduce(dot_nt(back_up, up_z)))
    up_part = dot_tn(hidden3, back_up).astype(bf16)
    up_grad = settle([up_part], owner_up, split_places, n_z, cap_big)
    at_middle2 = grad_out.astype(f32) + norm_back(back_hidden3, normed3, inverse3, norm_full[4])
    carry2 = z_gather(at_middle2.astype(bf16))
    back_att2 = dot_nt(carry2, outs_z[:, width:]).astype(bf16)
    outs_part2 = dot_tn(attended2, carry2).astype(bf16)
    back_cross, text_kgrad, text_vgrad = attend_backward(
        cross_query, text_key, text_value, shares2, back_att2
    )
    back_pairs = jnp.concatenate([text_kgrad, text_vgrad], axis=1)
    back_hidden2 = unshuffled(z_reduce(dot_nt(back_cross, query_z[:, 3 * share :])))
    text_part = jnp.concatenate(
        [dot_tn(text_all[:, f * width : (f + 1) * width], back_pairs).astype(bf16) for f in range(2)],
        axis=1,
    )
    text_grad = settle([text_part], owner_text, split_places, n_z, cap_big)
    query_part2 = dot_tn(hidden2, back_cross).astype(bf16)
    at_middle1 = at_middle2 + norm_back(back_hidden2, normed2, inverse2, norm_full[2])
    carry1 = z_gather(at_middle1.astype(bf16))
    back_att1 = dot_nt(carry1, outs_z[:, :width]).astype(bf16)
    outs_part1 = dot_tn(attended1, carry1).astype(bf16)
    outs_grad = settle([outs_part1, outs_part2], owner_outs, out_places, 1, cap_out)
    back_projected = jnp.concatenate(
        attend_backward(self_query, self_key, self_value, shares1, back_att1), axis=1
    )
    query_part1 = dot_tn(hidden1, back_projected).astype(bf16)
    query_grad = settle([query_part1, query_part2], owner_query, split_places, n_z, cap_big)
    back_hidden1 = unshuffled(z_reduce(dot_nt(back_projected, query_z[:, : 3 * share])))
    grad_in = (at_middle1 + norm_back(back_hidden1, normed1, inverse1, norm_full[0])).astype(bf16)

    norm_term = jnp.stack(
        [
            jnp.sum(back_hidden1 * normed1, axis=0),
            jnp.sum(back_hidden1, axis=0),
            jnp.sum(back_hidden2 * normed2, axis=0),
            jnp.sum(back_hidden2, axis=0),
            jnp.sum(back_hidden3 * normed3, axis=0),
            jnp.sum(back_hidden3, axis=0),
        ]
    )
    norm_total = lax.psum(norm_term, ("dp", "fsdp"))
    norm_share = width // n_dp
    norm_grad = lax.dynamic_slice_in_dim(
        norm_total, lax.axis_index("dp") * norm_share, norm_share, 1
    )
    query_new = adamw_update(w_query, m_query, v_query, query_grad, rate_query, decay_rate)
    up_new = adamw_update(w_up, m_up, v_up, up_grad, rate_up, decay_rate)
    outs_new = adamw_update(w_outs, m_outs, v_outs, outs_grad, rate_outs, decay_rate)
    text_new = adamw_update(w_text, m_text, v_text, text_grad, rate_text, decay_rate)
    down_new = adamw_update(w_down, m_down, v_down, down_grad, rate_down, decay_rate)
    norm_new = adamw_update(norm_weight, m_norm, v_norm, norm_grad, rate_norm, 0.0)
    return (
        result,
        grad_in,
        *query_new,
        *up_new,
        *outs_new,
        *text_new,
        *down_new,
        *norm_new,
    )


def solution(mesh):
    rows = P(("dp", "fsdp"), None)
    slots = P("fsdp", "dp")
    norms = P(None, "dp")
    in_specs = (rows,) * 5 + (P(),) * 5 + (slots,) * 15 + (norms,) * 3
    out_specs = (rows,) * 2 + (slots,) * 15 + (norms,) * 3
    return jax.shard_map(body, mesh=mesh, in_specs=in_specs, out_specs=out_specs, check_vma=False)
```

time: 4510 us -> 1580 us (0.35)
  waiting for transfers between devices: 3360 us -> 932 us
  local copies, waits for them, and re-layouts: 611 us -> 45.2 us
  blocking collectives: 48 us -> 256 us
  other arithmetic: 230 us -> 107 us
  matrix products: 228 us -> 145 us
  starting transfers between devices: 3.02 us -> 51.3 us
    all_gather x24 -> x12, waiting for transfers between devices: 3140 us -> 357 us  [the longest x5 205 us: fetch(): return lax.all_gather(rows, 'dp', axis=0, tiled=True)]
    reduce_scatter x5 -> x13, waiting for transfers between devices: 217 us -> 429 us  [the longest x7 321 us: settle(): lax.psum_scatter(piece, 'dp', scatter_dimension=0, tiled=True)]
    all_to_all x0 -> x5, blocking collectives: none -> 179 us  [swap(): return lax.all_to_all(values, axis, 0, 0, tiled=True)]
    gather x12 -> x0, local copies, waits for them, and re-layouts: 169 us -> none  [the longest x6 108 us: to_slots(): jnp.take(grad_rows.reshape(row_count, block_count, BLK), block_of, axis=1)]
    unnamed x194 -> x168, local copies, waits for them, and re-layouts: 157 us -> 11.8 us
    all_to_all x0 -> x11, waiting for transfers between devices: none -> 145 us  [swap(): return lax.all_to_all(values, axis, 0, 0, tiled=True)]
    convert_element_type x23 -> x13, other arithmetic: 144 us -> 27 us  [the longest x5 12.9 us: fetch(): slots = swap(weight.astype(bf16), 'dp').reshape(n_dp, chunk, -1)]
    reshape x13 -> x17, local copies, waits for them, and re-layouts: 128 us -> 12.2 us  [the longest x3 6.61 us: unshuffled(): return cut.transpose(0, 2, 1, 3).reshape(values.shape)]
  transfers between devices with their start and end apart: 29 -> 36, of which waited for: 22 -> 24; matrix products, arithmetic and copies ran while one was open for 22% -> 13% of each run, Pallas kernels for 0% -> 1%
where the time goes in v1:
time: 1580 us; the launch traced here: 1570 us
  waiting for transfers between devices  932 us (59%)
  blocking collectives  256 us (16%)
  matrix products  145 us (9%)
  other arithmetic  107 us (7%)
  starting transfers between devices  51.3 us (3%)
  local copies, waits for them, and re-layouts  45.2 us (3%)
  Pallas kernels  17.6 us (1%)
  between operations  16 us (1%)
    reduce_scatter x7, waiting for transfers between devices, settle(): lax.psum_scatter(piece, 'dp', scatter_dimension=0, tiled=True)  321 us
    all_gather x5, waiting for transfers between devices, fetch(): return lax.all_gather(rows, 'dp', axis=0, tiled=True)  205 us
    all_to_all x5, blocking collectives, swap(): return lax.all_to_all(values, axis, 0, 0, tiled=True)  179 us
    all_gather x7, waiting for transfers between devices, z_gather(): return lax.all_gather(values, 'fsdp', axis=0, tiled=True)  152 us
    all_to_all x11, waiting for transfers between devices, swap(): return lax.all_to_all(values, axis, 0, 0, tiled=True)  145 us
    reduce_scatter x6, waiting for transfers between devices, z_reduce(): lax.psum_scatter(values.astype(bf16), 'fsdp', scatter_dimension=0, tiled=...  107 us
    dot_general x11, matrix products, dot(): return jnp.dot(left, right, preferred_element_type=f32)  56.7 us
    all_to_all x11, starting transfers between devices, swap(): return lax.all_to_all(values, axis, 0, 0, tiled=True)  49 us
  transfers between devices with their start and end apart: 36, of which 24 were waited for; matrix products, arithmetic and copies ran while one was open for 13% of the time, Pallas kernels for 1%

profile of v1, /device:TPU:0, one launch (start us, length us, event | category | flops | bytes accessed | tf_op | source)
XLA Modules:
  0.0 1570.4 jit_solution(1758838662662371260)
XLA Ops:
  16.9 29.5 %all_gather.42 = f32[6,2048]{1,0:T(8,128)S(1)} all-gather(f32[6,256]{1,0:T(8,128)S(1)} %copy-done.58), channel_id=1, replica_groups=mesh['dp'=8,'fsdp'=4] {'dp'}, dimensions={1}, use_global_device_ids=true | all-gather | bytes 55296 | tf_op jit(solution)/shard_map/all_gather | solution.py:286
  51.9 58.8 %all_to_all.100 = bf16[4,64,2048]{2,1,0:T(8,128)(2,1)} all-to-all(bf16[4,64,2048]{2,1,0:T(8,128)(2,1)S(1)} %shard_map.419), channel_id=1, replica_groups=mesh['dp'=8,'fsdp'=4] {'fsdp'}, dimensions={0} | all-to-all | bytes 2097152 | tf_op jit(solution)/shard_map/all_to_all | solution.py:149
  139.6 33.6 %all-gather.18.cloned.1.call-done = bf16[2048,2048]{1,0:T(8,128)(2,1)} async-done(((bf16[256,2048]{1,0:T(8,128)(2,1)}), bf16[2048,2048]{1,0:T(8,128)(2,1)}) %all-gather.18.cloned.1.call-update) | async-done | bytes 8388624 | tf_op jit(solution)/shard_map/all_gather | solution.py:273
  258.7 37.2 %all-to-all-done.4 = bf16[4,64,2048]{2,1,0:T(8,128)(2,1)S(1)} async-done(((bf16[4,64,2048]{2,1,0:T(8,128)(2,1)}), bf16[4,64,2048]{2,1,0:T(8,128)(2,1)S(1)}, u32[]{:S(2)}, u32[]{:S(2)}) %all-to-all-start.4) | async-done | bytes 1048608 | tf_op jit(solution)/shard_map/all_to_all | solution.py:149
  302.8 52.8 %all-gather.20.cloned.1.call-done = bf16[2048,2048]{1,0:T(8,128)(2,1)} async-done(((bf16[256,2048]{1,0:T(8,128)(2,1)}), bf16[2048,2048]{1,0:T(8,128)(2,1)}) %all-gather.20.cloned.1.call-update) | async-done | bytes 8388624 | tf_op jit(solution)/shard_map/all_gather | solution.py:273
  363.1 41.0 %all-gather.24.cloned.1.call-done = bf16[512,2048]{0,1:T(8,128)(2,1)} async-done(((bf16[128,2048]{0,1:T(8,128)(2,1)}), bf16[512,2048]{0,1:T(8,128)(2,1)}) %all-gather.24.cloned.1.call-update) | async-done | bytes 2097168 | tf_op jit(solution)/shard_map/all_gather | solution.py:153
  417.3 30.1 %all_to_all.102.slots_ref = bf16[8,64,2048]{2,1,0:T(8,128)(2,1)S(1)} all-to-all(bf16[8,64,2048]{2,1,0:T(8,128)(2,1)S(1)} %bitcast.227), channel_id=1, replica_groups=mesh['dp'=8,'fsdp'=4] {'dp'}, dimensions={0} | all-to-all | bytes 4194304 | tf_op jit(solution)/shard_map/all_to_all | solution.py:149
  451.8 29.0 %all_to_all.103.slots_ref = bf16[8,64,2048]{2,1,0:T(8,128)(2,1)S(1)} all-to-all(bf16[8,64,2048]{2,1,0:T(8,128)(2,1)S(1)} %bitcast.228), channel_id=1, replica_groups=mesh['dp'=8,'fsdp'=4] {'dp'}, dimensions={0} | all-to-all | bytes 4194304 | tf_op jit(solution)/shard_map/all_to_all | solution.py:149
  481.7 43.5 %all_to_all.104 = bf16[4,64,2048]{2,1,0:T(8,128)(2,1)} all-to-all(bf16[4,64,2048]{2,1,0:T(8,128)(2,1)S(1)} %shard_map.422), channel_id=1, replica_groups=mesh['dp'=8,'fsdp'=4] {'fsdp'}, dimensions={0} | all-to-all | bytes 2097152 | tf_op jit(solution)/shard_map/all_to_all | solution.py:149
  528.6 49.3 %all-gather.38.cloned.1.call-done = bf16[1,512,8192]{2,1,0:T(8,128)(2,1)} async-done(((bf16[1,64,8192]{2,1,0:T(8,128)(2,1)}), bf16[1,512,8192]{2,1,0:T(8,128)(2,1)}) %all-gather.38.cloned.1.call-update) | async-done | bytes 8388624 | tf_op jit(solution)/shard_map/all_gather | solution.py:273
  590.6 43.7 %all-gather.28.cloned.1.call-done = bf16[2048,2048]{1,0:T(8,128)(2,1)} async-done(((bf16[256,2048]{1,0:T(8,128)(2,1)}), bf16[2048,2048]{1,0:T(8,128)(2,1)}) %all-gather.28.cloned.1.call-update) | async-done | bytes 8388624 | tf_op jit(solution)/shard_map/all_gather | solution.py:273
  634.2 48.3 %all-gather.26.cloned.1.call-done = bf16[512,2048]{0,1:T(8,128)(2,1)} async-done(((bf16[128,2048]{0,1:T(8,128)(2,1)}), bf16[512,2048]{0,1:T(8,128)(2,1)}) %all-gather.26.cloned.1.call-update) | async-done | bytes 2097168 | tf_op jit(solution)/shard_map/all_gather | solution.py:153
  759.3 38.6 %reduce-scatter.18.cloned.1.call-done = bf16[128,2048]{1,0:T(8,128)(2,1)} async-done(((bf16[512,2048]{1,0:T(8,128)(2,1)}), bf16[128,2048]{1,0:T(8,128)(2,1)}) %reduce-scatter.18.cloned.1.call-update) | async-done | bytes 524304 | tf_op jit(solution)/shard_map/reduce_scatter | solution.py:157
  801.5 45.3 %all-gather.32.cloned.1.call-done = bf16[512,2048]{1,0:T(8,128)(2,1)} async-done(((bf16[128,2048]{1,0:T(8,128)(2,1)}), bf16[512,2048]{1,0:T(8,128)(2,1)}) %all-gather.32.cloned.1.call-update) | async-done | bytes 2097168 | tf_op jit(solution)/shard_map/all_gather | solution.py:153
  857.4 42.2 %reduce-scatter.22.cloned.1.call-done = bf16[128,2048]{1,0:T(8,128)(2,1)} async-done(((bf16[512,2048]{1,0:T(8,128)(2,1)}), bf16[128,2048]{1,0:T(8,128)(2,1)}) %reduce-scatter.22.cloned.1.call-update) | async-done | bytes 524304 | tf_op jit(solution)/shard_map/reduce_scatter | solution.py:157
  999.6 26.9 %reduce-scatter.30.cloned.1.call-done = bf16[256,2048]{1,0:T(8,128)(2,1)} async-done(((bf16[2048,2048]{1,0:T(8,128)(2,1)}), bf16[256,2048]{1,0:T(8,128)(2,1)}) %reduce-scatter.30.cloned.1.call-update) | async-done | bytes 1048592 | tf_op jit(solution)/shard_map/reduce_scatter | solution.py:277
  1031.4 69.9 %reduce-scatter.38.cloned.1.call-done = bf16[64,8192]{1,0:T(8,128)(2,1)} async-done(((bf16[512,8192]{1,0:T(8,128)(2,1)}), bf16[64,8192]{1,0:T(8,128)(2,1)}) %reduce-scatter.38.cloned.1.call-update) | async-done | bytes 1048592 | tf_op jit(solution)/shard_map/reduce_scatter | solution.py:277
  1111.5 30.0 %all-to-all-done.15 = bf16[8,64,2048]{2,1,0:T(8,128)(2,1)} async-done(((bf16[8,64,2048]{2,1,0:T(8,128)(2,1)}), bf16[8,64,2048]{2,1,0:T(8,128)(2,1)}, u32[]{:S(2)}, u32[]{:S(2)}) %all-to-all-start.15) | async-done | bytes 2097184 | tf_op jit(solution)/shard_map/all_to_all | solution.py:149
  1155.4 50.2 %reduce-scatter.32.cloned.1.call-done = bf16[64,2048]{1,0:T(8,128)(2,1)} async-done(((bf16[512,2048]{1,0:T(8,128)(2,1)}), bf16[64,2048]{1,0:T(8,128)(2,1)}) %reduce-scatter.32.cloned.1.call-update) | async-done | bytes 262160 | tf_op jit(solution)/shard_map/reduce_scatter | solution.py:277
  1212.7 68.1 %reduce-scatter.36.cloned.1.call-done = bf16[256,2048]{0,1:T(8,128)(2,1)} async-done(((bf16[2048,2048]{0,1:T(8,128)(2,1)}), bf16[256,2048]{0,1:T(8,128)(2,1)}) %reduce-scatter.36.cloned.1.call-update) | async-done | bytes 1048592 | tf_op jit(solution)/shard_map/reduce_scatter | solution.py:277
  1295.9 30.0 %reduce-scatter.28.cloned.1.call-done = bf16[256,512]{1,0:T(8,128)(2,1)} async-done(((bf16[2048,512]{1,0:T(8,128)(2,1)}), bf16[256,512]{1,0:T(8,128)(2,1)}) %reduce-scatter.28.cloned.1.call-update) | async-done | bytes 262160 | tf_op jit(solution)/shard_map/reduce_scatter | solution.py:277
  1326.0 65.4 %reduce-scatter.26.cloned.1.call-done = bf16[256,1536]{1,0:T(8,128)(2,1)} async-done(((bf16[2048,1536]{1,0:T(8,128)(2,1)}), bf16[256,1536]{1,0:T(8,128)(2,1)}) %reduce-scatter.26.cloned.1.call-update) | async-done | bytes 786448 | tf_op jit(solution)/shard_map/reduce_scatter | solution.py:277
  1414.0 38.1 %all-to-all-done.8.grad_ref = bf16[4,64,2048]{2,1,0:T(8,128)(2,1)S(1)} async-done(((bf16[4,64,2048]{2,1,0:T(8,128)(2,1)}), bf16[4,64,2048]{2,1,0:T(8,128)(2,1)S(1)}, u32[]{:S(2)}, u32[]{:S(2)}) %all-to-all-start.8) | async-done | bytes 1048608 | tf_op jit(solution)/shard_map/all_to_all | solution.py:149
  1480.4 38.6 %psum.7 = f32[6,2048]{1,0:T(8,128)S(1)} all-reduce(f32[6,2048]{1,0:T(8,128)S(1)} %stack.27), channel_id=1, replica_groups=mesh['dp'=8,'fsdp'=4] {'dp','fsdp'}, use_global_device_ids=true, to_apply=%region_37.38 | all-reduce | flops 12288 | bytes 98304 | tf_op jit(solution)/shard_map/psum | solution.py:384
  (418 shorter events, 514.1 us)
Async XLA Ops:
  16.4 123.2 %all-gather.16.cloned.1.call-start = ((), (), s32[]{:S(2)}) async-start(), calls=%async_computation.29 | async-start | bytes 2621440 | tf_op jit(solution)/shard_map/all_gather | solution.py:153
  51.0 122.2 %all-gather.18.cloned.1.call-start = ((), (), s32[]{:S(2)}) async-start(), calls=%async_computation.30 | async-start | bytes 9437184 | tf_op jit(solution)/shard_map/all_gather | solution.py:273
  110.8 101.6 %all-gather.36.cloned.1.call-start = ((), (), s32[]{:S(2)}) async-start(), calls=%async_computation.52 | async-start | bytes 4718592 | tf_op jit(solution)/shard_map/all_gather | solution.py:273
  130.3 167.2 %reduce-scatter.14.cloned.1.call-start = ((), (), s32[]{:S(2)}) async-start(), calls=%async_computation.31 | async-start | bytes 2621440 | tf_op jit(solution)/shard_map/reduce_scatter | solution.py:157
  258.7 96.9 %all-gather.20.cloned.1.call-start = ((), (), s32[]{:S(2)}) async-start(), calls=%async_computation.32 | async-start | bytes 9437184 | tf_op jit(solution)/shard_map/all_gather | solution.py:273
  296.9 107.1 %all-gather.24.cloned.1.call-start = ((), (), s32[]{:S(2)}) async-start(), calls=%async_computation.34 | async-start | bytes 2621440 | tf_op jit(solution)/shard_map/all_gather | solution.py:153
  302.6 222.7 %reduce-scatter.16.cloned.1.call-start = ((), (), s32[]{:S(2)}) async-start(), calls=%async_computation.35 | async-start | bytes 2621440 | tf_op jit(solution)/shard_map/reduce_scatter | solution.py:157
  414.0 114.7 %all-gather.30.cloned.1.call-start = ((), (), s32[]{:S(2)}) async-start(), calls=%async_computation.39 | async-start | bytes 2621440 | tf_op jit(solution)/shard_map/all_gather | solution.py:153
  414.7 163.2 %all-gather.38.cloned.1.call-start = ((), (), s32[]{:S(2)}) async-start(), calls=%async_computation.53 | async-start | bytes 9437184 | tf_op jit(solution)/shard_map/all_gather | solution.py:273
  449.2 185.1 %all-gather.28.cloned.1.call-start = ((), (), s32[]{:S(2)}) async-start(), calls=%async_computation.37 | async-start | bytes 9437184 | tf_op jit(solution)/shard_map/all_gather | solution.py:273
  525.2 157.3 %all-gather.26.cloned.1.call-start = ((), (), s32[]{:S(2)}) async-start(), calls=%async_computation.36 | async-start | bytes 2621440 | tf_op jit(solution)/shard_map/all_gather | solution.py:153
  528.4 223.4 %reduce-scatter.20.cloned.1.call-start = ((), (), s32[]{:S(2)}) async-start(), calls=%async_computation.40 | async-start | bytes 2621440 | tf_op jit(solution)/shard_map/reduce_scatter | solution.py:157
  725.1 121.7 %all-gather.32.cloned.1.call-start = ((), (), s32[]{:S(2)}) async-start(), calls=%async_computation.41 | async-start | bytes 2621440 | tf_op jit(solution)/shard_map/all_gather | solution.py:153
  801.4 98.2 %reduce-scatter.22.cloned.1.call-start = ((), (), s32[]{:S(2)}) async-start(), calls=%async_computation.42 | async-start | bytes 2621440 | tf_op jit(solution)/shard_map/reduce_scatter | solution.py:157
  856.9 95.9 %all-gather.34.cloned.1.call-start = ((), (), s32[]{:S(2)}) async-start(), calls=%async_computation.43 | async-start | bytes 2621440 | tf_op jit(solution)/shard_map/all_gather | solution.py:153
  907.4 119.2 %reduce-scatter.30.cloned.1.call-start = ((), (), s32[]{:S(2)}) async-start(), calls=%async_computation.47 | async-start | bytes 9437184 | tf_op jit(solution)/shard_map/reduce_scatter | solution.py:277
  917.5 183.8 %reduce-scatter.38.cloned.1.call-start = ((), (), s32[]{:S(2)}) async-start(), calls=%async_computation.51 | async-start | bytes 9437184 | tf_op jit(solution)/shard_map/reduce_scatter | solution.py:277
  929.9 225.5 %reduce-scatter.34.cloned.1.call-start = ((), (), s32[]{:S(2)}) async-start(), calls=%async_computation.49 | async-start | bytes 2359296 | tf_op jit(solution)/shard_map/reduce_scatter | solution.py:277
  935.2 270.5 %reduce-scatter.32.cloned.1.call-start = ((), (), s32[]{:S(2)}) async-start(), calls=%async_computation.48 | async-start | bytes 2359296 | tf_op jit(solution)/shard_map/reduce_scatter | solution.py:277
  957.0 323.8 %reduce-scatter.36.cloned.1.call-start = ((), (), s32[]{:S(2)}) async-start(), calls=%async_computation.50 | async-start | bytes 9437184 | tf_op jit(solution)/shard_map/reduce_scatter | solution.py:277
  975.7 350.3 %reduce-scatter.28.cloned.1.call-start = ((), (), s32[]{:S(2)}) async-start(), calls=%async_computation.46 | async-start | bytes 2359296 | tf_op jit(solution)/shard_map/reduce_scatter | solution.py:277
  980.0 411.3 %reduce-scatter.26.cloned.1.call-start = ((), (), s32[]{:S(2)}) async-start(), calls=%async_computation.45 | async-start | bytes 7077888 | tf_op jit(solution)/shard_map/reduce_scatter | solution.py:277
  1283.1 110.6 %all-to-all-start.13 = ((bf16[4,64,2048]{2,1,0:T(8,128)(2,1)}), bf16[4,64,2048]{2,1,0:T(8,128)(2,1)S(1)}, u32[]{:S(2)}, u32[]{:S(2)}) async-start(bf16[4,64,2048]{2,1,0:T(8,128)(2,1)} %bitcast.244), calls=%async_computation.25 | async-start | bytes 2097152 | tf_op jit(solution)/shard_map/all_to_all | solution.py:149
  1287.7 185.7 %reduce-scatter.24.cloned.1.call-start = ((), (), s32[]{:S(2)}) async-start(), calls=%async_computation.44 | async-start | bytes 2621440 | tf_op jit(solution)/shard_map/reduce_scatter | solution.py:157
  (94 other events, 2987.1 us)
Sparse Core Ops, SparseCore 0:
  51.1 66.4 all-gather.15
  119.5 53.6 all-gather.17
  175.7 36.7 all-gather.35
  216.9 44.2 reduce-scatter.13
  301.8 53.7 all-gather.19
  357.8 46.2 all-gather.23
  414.1 42.0 reduce-scatter.15
  457.8 64.0 all-gather.29
  524.1 53.7 all-gather.37
  579.8 54.3 all-gather.27
  636.2 46.2 all-gather.25
  709.7 42.0 reduce-scatter.19
  754.6 43.1 reduce-scatter.17
  801.5 45.2 all-gather.31
  857.0 42.5 reduce-scatter.21
  907.5 45.2 all-gather.33
  956.5 69.9 reduce-scatter.29
  1030.0 71.2 reduce-scatter.37
  1105.4 50.0 reduce-scatter.33
  1159.3 46.3 reduce-scatter.31
  1209.5 71.2 reduce-scatter.35
  1284.7 41.2 reduce-scatter.27
  1329.6 61.7 reduce-scatter.25
  1394.2 62.0 reduce-scatter.23
  (1 shorter events, 35.8 us)

commit v2 on v1

--- a/solution.py
+++ b/solution.py
@@ -149,14 +149,636 @@
     return lax.all_to_all(values, axis, 0, 0, tiled=True)
 
 
-def z_gather(values):
-    return lax.all_gather(values, "fsdp", axis=0, tiled=True)
-
-
-def z_reduce(values):
-    return lax.psum_scatter(values.astype(bf16), "fsdp", scatter_dimension=0, tiled=True).astype(
-        f32
-    )
+SUBS = 4
+
+
+class Line:
+    def __init__(self, n, rows, step):
+        self.n, self.rows, self.step = n, rows, step
+        self.at = lax.axis_index("fsdp")
+
+    def has(self, way):
+        return self.at < self.n - 1 if way == 0 else self.at > 0
+
+    def peer(self, way):
+        index = jnp.clip(self.at + (1 if way == 0 else -1), 0, self.n - 1)
+        return {"fsdp": index}
+
+    def greet(self, others=0):
+        barrier = pltpu.get_barrier_semaphore()
+        for way in (0, 1):
+
+            @pl.when(self.has(way))
+            def _():
+                pl.semaphore_signal(
+                    barrier, inc=1, device_id=self.peer(way), device_id_type=pl.DeviceIdType.MESH
+                )
+
+        pl.semaphore_wait(
+            barrier, others + self.has(0).astype(jnp.int32) + self.has(1).astype(jnp.int32)
+        )
+
+    def copy(self, source, target, send, recv, way):
+        return pltpu.make_async_remote_copy(
+            src_ref=source,
+            dst_ref=target,
+            send_sem=send,
+            recv_sem=recv,
+            device_id=self.peer(way),
+            device_id_type=pl.DeviceIdType.MESH,
+        )
+
+    def part(self, sub):
+        return pl.ds(sub * self.step, self.step)
+
+
+class Sums:
+    def __init__(self, line, part, held, send, recv):
+        self.line, self.part, self.held, self.send, self.recv = line, part, held, send, recv
+
+    def move(self, way, target, sub, source):
+        line = self.line
+        rows = line.part(sub)
+        return line.copy(
+            source,
+            self.held.at[way, target, rows],
+            self.send.at[way, target, sub],
+            self.recv.at[way, target, sub],
+            way,
+        )
+
+    def targets(self, way):
+        n = self.line.n
+        return range(n - 1, 0, -1) if way == 0 else range(n - 1)
+
+    def beyond(self, way, target):
+        return self.line.at < target if way == 0 else self.line.at > target
+
+    def forward(self, sub):
+        line = self.line
+        rows = line.part(sub)
+        for step in range(line.n - 1):
+            for way in (0, 1):
+                target = self.targets(way)[step]
+                inner = jnp.logical_and(self.beyond(way, target), line.has(1 - way))
+                outer = jnp.logical_and(
+                    self.beyond(way, target), jnp.logical_not(line.has(1 - way))
+                )
+
+                @pl.when(outer)
+                def _():
+                    self.move(way, target, sub, self.part.at[target, rows]).start()
+
+                @pl.when(inner)
+                def _():
+                    held = self.held.at[way, target, rows]
+                    self.move(way, target, sub, held).wait_recv()
+                    total = held[...].astype(f32) + self.part[target, rows].astype(f32)
+                    held[...] = total.astype(bf16)
+                    self.move(way, target, sub, held).start()
+
+    def total(self, sub, sum_ref):
+        line = self.line
+        rows = line.part(sub)
+        sum_ref[...] = self.part[line.at, rows].astype(f32)
+        for way in (0, 1):
+
+            @pl.when(line.has(1 - way))
+            def _():
+                held = self.held.at[way, line.at, rows]
+                self.move(way, line.at, sub, held).wait_recv()
+                sum_ref[...] += held[...].astype(f32)
+
+    def finish(self):
+        for way in (0, 1):
+            for target in self.targets(way):
+
+                @pl.when(self.beyond(way, target))
+                def _():
+                    for sub in range(self.line.rows // self.line.step):
+                        held = self.held.at[way, target, self.line.part(sub)]
+                        self.move(way, target, sub, held).wait_send()
+
+
+class Blocks:
+    def __init__(self, line, full, send, recv):
+        self.line, self.full, self.send, self.recv = line, full, send, recv
+
+    def move(self, way, source, sub):
+        line = self.line
+        held = self.full.at[source, line.part(sub)]
+        return line.copy(
+            held, held, self.send.at[way, source, sub], self.recv.at[way, source, sub], way
+        )
+
+    def sources(self, way):
+        n = self.line.n
+        return range(n - 2, -1, -1) if way == 0 else range(1, n)
+
+    def behind(self, way, source):
+        return self.line.at > source if way == 0 else self.line.at < source
+
+    def start(self, sub):
+        for way in (0, 1):
+
+            @pl.when(self.line.has(way))
+            def _():
+                self.move(way, self.line.at, sub).start()
+
+    def forward(self, sub):
+        line = self.line
+        for step in range(line.n - 1):
+            for way in (0, 1):
+                source = self.sources(way)[step]
+
+                @pl.when(self.behind(way, source))
+                def _():
+                    self.move(way, source, sub).wait_recv()
+
+                    @pl.when(line.has(way))
+                    def _():
+                        self.move(way, source, sub).start()
+
+    def finish(self):
+        line = self.line
+        for way in (0, 1):
+            for source in range(line.n):
+                ours = jnp.logical_or(self.behind(way, source), line.at == source)
+
+                @pl.when(jnp.logical_and(ours, line.has(way)))
+                def _():
+                    for sub in range(line.rows // line.step):
+                        self.move(way, source, sub).wait_send()
+
+
+def lane_moves(width, order):
+    moves = []
+    piece = width // len(order)
+    for group in range(width // BLK):
+        parts = []
+        for offset in range(0, BLK, piece):
+            start = order[(group * BLK + offset) // piece] * piece
+            parts.append((offset, start // BLK, start % BLK))
+        moves.append(parts)
+    return piece, moves
+
+
+def reorder(load, store, rows, width, order):
+    piece, moves = lane_moves(width, order)
+    lane = lax.broadcasted_iota(jnp.int32, (rows, BLK), 1)
+    for group, parts in enumerate(moves):
+        value = None
+        for offset, source, start in parts:
+            block = load(source)
+            if start != offset:
+                block = pltpu.roll(block, (offset - start) % BLK, 1)
+            value = block if value is None else jnp.where(lane >= offset, block, value)
+        store(group, value)
+
+
+def shuffle_order(n_z, n_dp):
+    return [z * n_dp + i for i in range(n_dp) for z in range(n_z)]
+
+
+def unshuffle_order(n_z, n_dp):
+    return [i * n_z + z for z in range(n_z) for i in range(n_dp)]
+
+
+def by_tiles(columns, tile, run):
+    def one(index, carry):
+        run(pl.ds(pl.multiple_of(index * tile, tile), tile))
+        return carry
+
+    lax.fori_loop(0, columns // tile, one, 0)
+
+
+def start_kernel(n, n_dp, order, tokens, text, grad, marks, norms, *rest):
+    h_full, text_full, grad_full, marks_full, norm_full = rest[:5]
+    parts, work, n_send, n_recv = rest[5:9]
+    sems = rest[9:]
+    rows, width = tokens.shape
+    step = rows // SUBS
+    me = lax.axis_index("dp")
+    line = Line(n, rows, step)
+    barrier = pltpu.get_barrier_semaphore()
+    for jump in range(1, n_dp):
+        pl.semaphore_signal(
+            barrier,
+            inc=1,
+            device_id={"dp": lax.rem(me + jump, n_dp)},
+            device_id_type=pl.DeviceIdType.MESH,
+        )
+    line.greet(n_dp - 1)
+
+    def norm_copy(jump):
+        return pltpu.make_async_remote_copy(
+            src_ref=norms,
+            dst_ref=parts.at[me],
+            send_sem=n_send.at[jump],
+            recv_sem=n_recv.at[me],
+            device_id={"dp": lax.rem(me + jump, n_dp)},
+            device_id_type=pl.DeviceIdType.MESH,
+        )
+
+    def norm_arrival(jump):
+        source = lax.rem(me + jump, n_dp)
+        return pltpu.make_async_remote_copy(
+            src_ref=norms,
+            dst_ref=parts.at[source],
+            send_sem=n_send.at[jump],
+            recv_sem=n_recv.at[source],
+            device_id={"dp": source},
+            device_id_type=pl.DeviceIdType.MESH,
+        )
+
+    for jump in range(1, n_dp):
+        norm_copy(jump).start()
+    text_rows = text.shape[0]
+    text_line = Line(n, text_rows, text_rows)
+    mark_line = Line(n, marks.shape[0], marks.shape[0])
+    hidden = Blocks(line, h_full, sems[0], sems[1])
+    texts = Blocks(text_line, text_full, sems[2], sems[3])
+    grads = Blocks(line, grad_full, sems[4], sems[5])
+    places = Blocks(mark_line, marks_full, sems[6], sems[7])
+    marks_full[line.at] = marks[...]
+    places.start(0)
+    parts[me] = norms[...]
+    for jump in range(1, n_dp):
+        norm_arrival(jump).wait_recv()
+    share = width // n_dp
+    for index in range(n_dp):
+        norm_full[:, index * share : (index + 1) * share] = parts[index]
+    for sub in range(SUBS):
+        here = line.part(sub)
+        normed, _ = normalize(tokens[here].astype(f32))
+        work[...] = normed * norm_full[0:1] + norm_full[1:2]
+
+        def load(group):
+            return work[:, group * BLK : (group + 1) * BLK]
+
+        def store(group, value):
+            h_full[line.at, here, group * BLK : (group + 1) * BLK] = value.astype(bf16)
+
+        reorder(load, store, step, width, order)
+        hidden.start(sub)
+
+    def load_text(group):
+        return text[:, group * BLK : (group + 1) * BLK].astype(f32)
+
+    def store_text(group, value):
+        text_full[line.at, :, group * BLK : (group + 1) * BLK] = value.astype(bf16)
+
+    folds = text.shape[1] // width
+    text_order = [fold * len(order) + piece for fold in range(folds) for piece in order]
+    reorder(load_text, store_text, text_rows, folds * width, text_order)
+    texts.start(0)
+    for sub in range(SUBS):
+        here = line.part(sub)
+        grad_full[line.at, here] = grad[here]
+        grads.start(sub)
+    places.forward(0)
+    for sub in range(SUBS):
+        hidden.forward(sub)
+    texts.forward(0)
+    for sub in range(SUBS):
+        grads.forward(sub)
+    for blocks in (hidden, texts, grads, places):
+        blocks.finish()
+    for jump in range(1, n_dp):
+        norm_copy(jump).wait_send()
+
+
+def fetch_columns(source, index, target, sem):
+    columns = target.shape[1]
+    return pltpu.make_async_copy(source.at[:, pl.ds(index * columns, columns)], target, sem)
+
+
+def forward_kernel(n, order, half, wide, att_ref, outs_hbm, base_ref, norm_ref, *rest):
+    if wide:
+        next_hbm, middle_ref, full_ref, result_ref = rest[:4]
+        *rest, next_ref, next_sem = rest[4:]
+    else:
+        middle_ref, full_ref = rest[:2]
+        rest = rest[2:]
+    part, held, work, s_send, s_recv, b_send, b_recv, outs_ref, outs_sem = rest
+    rows, width = base_ref.shape
+    step = rows // SUBS
+    load_outs = fetch_columns(outs_hbm, half, outs_ref, outs_sem)
+    load_outs.start()
+    if wide:
+        load_next = fetch_columns(next_hbm, 3, next_ref, next_sem)
+        load_next.start()
+    line = Line(n, rows, step)
+    line.greet()
+    load_outs.wait()
+    sums = Sums(line, part, held, s_send, s_recv)
+    blocks = Blocks(line, full_ref, b_send, b_recv)
+
+    def multiply(columns):
+        product = dot(att_ref[...], outs_ref[:, columns]).astype(bf16)
+        part[:, :, columns] = product.reshape(n, rows, -1)
+
+    by_tiles(width, 256, multiply)
+    for time in range(SUBS + 2):
+        if time < SUBS:
+            sums.forward(time)
+        if 0 <= time - 1 < SUBS:
+            sub = time - 1
+            here = line.part(sub)
+            sums.total(sub, work)
+            middle = base_ref[here].astype(f32) + work[...]
+            middle_ref[here] = middle
+            normed, _ = normalize(middle)
+            work[...] = normed * norm_ref[0:1] + norm_ref[1:2]
+
+            def load(group):
+                return work[:, group * BLK : (group + 1) * BLK]
+
+            def store(group, value):
+                full_ref[line.at, here, group * BLK : (group + 1) * BLK] = value.astype(bf16)
+
+            reorder(load, store, step, width, order)
+            blocks.start(sub)
+        if 0 <= time - 2 < SUBS:
+            blocks.forward(time - 2)
+    sums.finish()
+    blocks.finish()
+    if wide:
+        load_next.wait()
+
+        def multiply_next(columns):
+            whole = full_ref[...].reshape(n * rows, width)
+            result_ref[:, columns] = dot(whole, next_ref[:, columns]).astype(bf16)
+
+        by_tiles(result_ref.shape[1], 256, multiply_next)
+
+
+def carry_back(work, plain, order, step, width, middle, base, gain, term_ref, first):
+    def load(group):
+        return work[:, group * BLK : (group + 1) * BLK]
+
+    def store(group, value):
+        plain[:, group * BLK : (group + 1) * BLK] = value
+
+    reorder(load, store, step, width, order)
+    back_hidden = plain[...]
+    normed, inverse = normalize(middle)
+    gain_term = jnp.sum(back_hidden * normed, axis=0, keepdims=True)
+    bias_term = jnp.sum(back_hidden, axis=0, keepdims=True)
+    if first:
+        term_ref[0:1] = gain_term
+        term_ref[1:2] = bias_term
+    else:
+        term_ref[0:1] += gain_term
+        term_ref[1:2] += bias_term
+    return base + norm_back(back_hidden, normed, inverse, gain)
+
+
+def back_kernel(
+    n, order, column, half, dy_ref, w_hbm, base_ref, middle_ref, norm_ref, outs_hbm, *rest
+):
+    carry_ref, full_ref, att_ref, term_ref = rest[:4]
+    part, held, work, plain, s_send, s_recv, b_send, b_recv = rest[4:12]
+    w_ref, w_sem, outs_ref, outs_sem = rest[12:]
+    rows, width = base_ref.shape
+    step = rows // SUBS
+    load_w = fetch_columns(w_hbm, column, w_ref, w_sem)
+    load_w.start()
+    load_outs = fetch_columns(outs_hbm, half, outs_ref, outs_sem)
+    load_outs.start()
+    line = Line(n, rows, step)
+    line.greet()
+    load_w.wait()
+    sums = Sums(line, part, held, s_send, s_recv)
+    blocks = Blocks(line, full_ref, b_send, b_recv)
+
+    def multiply(columns):
+        product = dot_nt(dy_ref[...], w_ref[columns]).astype(bf16)
+        part[:, :, columns] = product.reshape(n, rows, -1)
+
+    by_tiles(width, 256, multiply)
+    for time in range(SUBS + 2):
+        if time < SUBS:
+            sums.forward(time)
+        if 0 <= time - 1 < SUBS:
+            sub = time - 1
+            here = line.part(sub)
+            sums.total(sub, work)
+            carry = carry_back(
+                work,
+                plain,
+                order,
+                step,
+                width,
+                middle_ref[here].astype(f32),
+                base_ref[here].astype(f32),
+                norm_ref[0:1],
+                term_ref,
+                sub == 0,
+            )
+            carry_ref[here] = carry
+            full_ref[line.at, here] = carry.astype(bf16)
+            blocks.start(sub)
+        if 0 <= time - 2 < SUBS:
+            blocks.forward(time - 2)
+    sums.finish()
+    blocks.finish()
+    load_outs.wait()
+
+    def multiply_next(columns):
+        whole = full_ref[...].reshape(n * rows, width)
+        att_ref[:, columns] = dot_nt(whole, outs_ref[columns]).astype(bf16)
+
+    by_tiles(att_ref.shape[1], 256, multiply_next)
+
+
+def last_kernel(n, order, dy_ref, w_hbm, base_ref, tokens, norm_ref, branch, middle, *rest):
+    grad_ref, result_ref, term_ref = rest[:3]
+    part, held, held2, work, plain, s_send, s_recv, r_send, r_recv, w_ref, w_sem = rest[3:]
+    rows, width = base_ref.shape
+    step = rows // SUBS
+    load_w = fetch_columns(w_hbm, 0, w_ref, w_sem)
+    load_w.start()
+    line = Line(n, rows, step)
+    line.greet()
+    load_w.wait()
+    sums = Sums(line, part, held, s_send, s_recv)
+    results = Sums(line, branch, held2, r_send, r_recv)
+
+    def multiply(columns):
+        product = dot_nt(dy_ref[...], w_ref[columns]).astype(bf16)
+        part[:, :, columns] = product.reshape(n, rows, -1)
+
+    by_tiles(width, 256, multiply)
+    for time in range(SUBS + 1):
+        if time < SUBS:
+            sums.forward(time)
+            results.forward(time)
+        if 0 <= time - 1 < SUBS:
+            sub = time - 1
+            here = line.part(sub)
+            sums.total(sub, work)
+            carry = carry_back(
+                work,
+                plain,
+                order,
+                step,
+                width,
+                tokens[here].astype(f32),
+                base_ref[here],
+                norm_ref[0:1],
+                term_ref,
+                sub == 0,
+            )
+            grad_ref[here] = carry.astype(bf16)
+            results.total(sub, work)
+            result_ref[here] = (middle[here] + work[...]).astype(bf16)
+    sums.finish()
+    results.finish()
+
+
+VMEM_CAP = 52 * 1024 * 1024
+
+
+def in_place():
+    return pl.BlockSpec(memory_space=pl.ANY)
+
+
+def whole_vmem():
+    return pl.BlockSpec(memory_space=pltpu.VMEM)
+
+
+def sem_pair(n, subs):
+    return [pltpu.SemaphoreType.DMA((2, n, subs)), pltpu.SemaphoreType.DMA((2, n, subs))]
+
+
+def line_call(kernel, name, ident, outs, specs, scratch, flops, moved):
+    return pl.pallas_call(
+        kernel,
+        name=name,
+        out_shape=outs,
+        in_specs=specs,
+        out_specs=jax.tree.map(lambda _: whole_vmem(), outs),
+        scratch_shapes=scratch,
+        compiler_params=pltpu.CompilerParams(
+            collective_id=ident, has_side_effects=True, vmem_limit_bytes=VMEM_CAP
+        ),
+        cost_estimate=pl.CostEstimate(flops=flops, bytes_accessed=moved, transcendentals=0),
+    )
+
+
+def shape(dims, kind):
+    return jax.ShapeDtypeStruct(dims, kind)
+
+
+LINK_COST = 120_000_000
+
+
+def start_call(tokens, text, grad, marks, norms, n, n_dp):
+    rows, width = tokens.shape
+    outs = (
+        shape((n, *tokens.shape), bf16),
+        shape((n, *text.shape), bf16),
+        shape((n, *grad.shape), bf16),
+        shape((n, *marks.shape), jnp.int32),
+        shape((norms.shape[0], width), f32),
+    )
+    scratch = [
+        pltpu.VMEM((n_dp, *norms.shape), f32),
+        pltpu.VMEM((rows // SUBS, width), f32),
+        pltpu.SemaphoreType.DMA((n_dp,)),
+        pltpu.SemaphoreType.DMA((n_dp,)),
+        *sem_pair(n, SUBS),
+        *sem_pair(n, 1),
+        *sem_pair(n, SUBS),
+        *sem_pair(n, 1),
+    ]
+    kernel = functools.partial(start_kernel, n, n_dp, shuffle_order(n, n_dp))
+    call = line_call(kernel, "start", 0, outs, [whole_vmem()] * 5, scratch, 0, LINK_COST)
+    return call(tokens, text, grad, marks, norms)
+
+
+def forward_call(attended, outs_z, half, base, norm_rows, after, n, n_dp, ident):
+    rows, width = base.shape
+    share = outs_z.shape[0]
+    outs = [shape((rows, width), f32), shape((n, rows, width), bf16)]
+    specs = [whole_vmem(), in_place(), whole_vmem(), whole_vmem()]
+    args = [attended, outs_z, base, norm_rows]
+    scratch = [
+        pltpu.VMEM((n, rows, width), bf16),
+        pltpu.VMEM((2, n, rows, width), bf16),
+        pltpu.VMEM((rows // SUBS, width), f32),
+        *sem_pair(n, SUBS),
+        *sem_pair(n, SUBS),
+        pltpu.VMEM((share, width), bf16),
+        pltpu.SemaphoreType.DMA,
+    ]
+    if after is not None:
+        outs.append(shape((n * rows, share), bf16))
+        specs.append(in_place())
+        args.append(after)
+        scratch += [pltpu.VMEM((width, share), bf16), pltpu.SemaphoreType.DMA]
+    kernel = functools.partial(forward_kernel, n, shuffle_order(n, n_dp), half, after is not None)
+    call = line_call(kernel, f"forward{half}", ident, outs, specs, scratch, 0, LINK_COST)
+    return call(*args)
+
+
+def back_call(dy, weight, column, base, middle, norm_rows, outs_z, half, n, n_dp, ident):
+    rows, width = base.shape
+    share = outs_z.shape[0]
+    outs = [
+        shape((rows, width), f32),
+        shape((n, rows, width), bf16),
+        shape((n * rows, share), bf16),
+        shape((8, width), f32),
+    ]
+    specs = [
+        whole_vmem(),
+        in_place(),
+        whole_vmem(),
+        whole_vmem(),
+        whole_vmem(),
+        in_place(),
+    ]
+    scratch = [
+        pltpu.VMEM((n, rows, width), bf16),
+        pltpu.VMEM((2, n, rows, width), bf16),
+        pltpu.VMEM((rows // SUBS, width), f32),
+        pltpu.VMEM((rows // SUBS, width), f32),
+        *sem_pair(n, SUBS),
+        *sem_pair(n, SUBS),
+        pltpu.VMEM((width, dy.shape[1]), bf16),
+        pltpu.SemaphoreType.DMA,
+        pltpu.VMEM((share, width), bf16),
+        pltpu.SemaphoreType.DMA,
+    ]
+    kernel = functools.partial(back_kernel, n, unshuffle_order(n, n_dp), column, half)
+    call = line_call(kernel, f"back{half}", ident, outs, specs, scratch, 0, LINK_COST)
+    return call(dy, weight, base, middle, norm_rows, outs_z)
+
+
+def last_call(dy, weight, base, tokens, norm_rows, branch, middle, n, n_dp, ident):
+    rows, width = base.shape
+    outs = [
+        shape((rows, width), bf16),
+        shape((rows, width), bf16),
+        shape((8, width), f32),
+    ]
+    specs = [whole_vmem(), in_place()] + [whole_vmem()] * 5
+    scratch = [
+        pltpu.VMEM((n, rows, width), bf16),
+        pltpu.VMEM((2, n, rows, width), bf16),
+        pltpu.VMEM((2, n, rows, width), bf16),
+        pltpu.VMEM((rows // SUBS, width), f32),
+        pltpu.VMEM((rows // SUBS, width), f32),
+        *sem_pair(n, SUBS),
+        *sem_pair(n, SUBS),
+        pltpu.VMEM((width, dy.shape[1]), bf16),
+        pltpu.SemaphoreType.DMA,
+    ]
+    kernel = functools.partial(last_kernel, n, unshuffle_order(n, n_dp))
+    call = line_call(kernel, "last", ident, outs, specs, scratch, 0, LINK_COST)
+    return call(dy, weight, base, tokens, norm_rows, branch, middle)
 
 
 def attend_forward(queries, keys, values, allowed):
@@ -254,16 +876,6 @@
     big_places = [flat_place(b) for b in range(owner_down.shape[0])]
     out_places = [flat_place(b) for b in range(owner_outs.shape[0])]
 
-    def shuffled(values):
-        lead = values.shape[:-1]
-        folds = values.shape[-1] // width
-        cut = values.reshape(lead[0], folds, n_z, n_dp, chunk)
-        return cut.transpose(0, 1, 3, 2, 4).reshape(values.shape)
-
-    def unshuffled(values):
-        cut = values.reshape(values.shape[0], n_dp, n_z, chunk)
-        return cut.transpose(0, 2, 1, 3).reshape(values.shape)
-
     def fetch(weight, owner, places, parts):
         slots = swap(weight.astype(bf16), "dp").reshape(n_dp, chunk, -1)
         rows = compact(slots, owner, places, parts)
@@ -283,35 +895,36 @@
         slots = expand(rows, owner, places, n_dp, capacity)
         return swap(slots, "dp").reshape(n_dp * chunk, -1).astype(f32)
 
-    norm_full = lax.all_gather(norm_weight, "dp", axis=1, tiled=True)
-    marks = lax.all_gather(jnp.concatenate([seg_ids, capt_ids], axis=1), "fsdp", axis=0, tiled=True)
-    token_count = tokens_in.shape[0]
-    segment = marks[:, :token_count]
-    caption = marks[:, token_count:]
-    self_mask = segment[:, :, None] == segment[:, None, :]
-    cross_mask = segment[:, :, None] == caption[:, None, :]
-
     query_z = fetch(w_query, owner_query, split_places, n_z)
     outs_z = fetch(w_outs, owner_outs, out_places, 1)
     text_z = fetch(w_text, owner_text, split_places, n_z)
     up_z = fetch(w_up, owner_up, split_places, n_z)
     down_z = fetch(w_down, owner_down, big_places, 1)
 
-    inputs = tokens_in.astype(f32)
-    normed1, inverse1 = normalize(inputs)
-    hidden1 = z_gather(shuffled((normed1 * norm_full[0] + norm_full[1]).astype(bf16)))
-    text_all = z_gather(shuffled(text_in))
-    grad_all = z_gather(grad_out)
+    token_count = tokens_in.shape[0]
+    marks = jnp.concatenate([seg_ids, capt_ids], axis=1)
+    marks = jnp.pad(marks, ((0, 7), (0, 256 - marks.shape[1])))
+    norms = jnp.pad(norm_weight, ((0, 2), (0, 0)))
+    hidden1, text_all, grad_all, marks, norm_full = start_call(
+        tokens_in, text_in, grad_out, marks, norms, n_z, n_dp
+    )
+    hidden1, text_all, grad_all = (
+        values.reshape(-1, values.shape[-1]) for values in (hidden1, text_all, grad_all)
+    )
+    segment = marks[:, 0, :token_count]
+    caption = marks[:, 0, token_count : token_count + capt_ids.shape[1]]
+    self_mask = segment[:, :, None] == segment[:, None, :]
+    cross_mask = segment[:, :, None] == caption[:, None, :]
 
     projected = dot(hidden1, query_z[:, : 3 * share]).astype(bf16)
     self_query = projected[:, :share]
     self_key = projected[:, share : 2 * share]
     self_value = projected[:, 2 * share :]
     attended1, shares1 = attend_forward(self_query, self_key, self_value, self_mask)
-    middle1 = inputs + z_reduce(dot(attended1, outs_z[:, :width]))
-    normed2, inverse2 = normalize(middle1)
-    hidden2 = z_gather(shuffled((normed2 * norm_full[2] + norm_full[3]).astype(bf16)))
-    cross_query = dot(hidden2, query_z[:, 3 * share :]).astype(bf16)
+    middle1, hidden2, cross_query = forward_call(
+        attended1, outs_z, 0, tokens_in, norm_full[2:4], query_z, n_z, n_dp, 1
+    )
+    hidden2 = hidden2.reshape(-1, width)
     text_pairs = (
         dot(text_all[:, :width], text_z[:, : 2 * share])
         + dot(text_all[:, width:], text_z[:, 2 * share :])
@@ -319,9 +932,10 @@
     text_key = text_pairs[:, :share]
     text_value = text_pairs[:, share:]
     attended2, shares2 = attend_forward(cross_query, text_key, text_value, cross_mask)
-    middle2 = middle1 + z_reduce(dot(attended2, outs_z[:, width:]))
-    normed3, inverse3 = normalize(middle2)
-    hidden3 = z_gather(shuffled((normed3 * norm_full[4] + norm_full[5]).astype(bf16)))
+    middle2, hidden3 = forward_call(
+        attended2, outs_z, 1, middle1, norm_full[4:6], None, n_z, n_dp, 2
+    )
+    hidden3 = hidden3.reshape(-1, width)
     up_values = dot(hidden3, up_z)
     gelu_values, gelu_pull = jax.vjp(exact_gelu, up_values)
     activated = gelu_values.astype(bf16)
@@ -329,7 +943,7 @@
         dot(activated[:, f * share : (f + 1) * share], down_z[:, f * width : (f + 1) * width])
         for f in range(4)
     )
-    result = (middle2 + z_reduce(branch3)).astype(bf16)
+    branch3 = branch3.astype(bf16).reshape(n_z, token_count, width)
 
     down_part = jnp.concatenate(
         [dot_tn(activated[:, f * share : (f + 1) * share], grad_all).astype(bf16) for f in range(4)],
@@ -340,27 +954,27 @@
         [dot_nt(grad_all, down_z[:, f * width : (f + 1) * width]) for f in range(4)], axis=1
     )
     back_up = gelu_pull(back_act)[0].astype(bf16)
-    back_hidden3 = unshuffled(z_reduce(dot_nt(back_up, up_z)))
     up_part = dot_tn(hidden3, back_up).astype(bf16)
     up_grad = settle([up_part], owner_up, split_places, n_z, cap_big)
-    at_middle2 = grad_out.astype(f32) + norm_back(back_hidden3, normed3, inverse3, norm_full[4])
-    carry2 = z_gather(at_middle2.astype(bf16))
-    back_att2 = dot_nt(carry2, outs_z[:, width:]).astype(bf16)
+    at_middle2, carry2, back_att2, term3 = back_call(
+        back_up, up_z, 0, grad_out, middle2, norm_full[4:6], outs_z, 1, n_z, n_dp, 3
+    )
+    carry2 = carry2.reshape(-1, width)
     outs_part2 = dot_tn(attended2, carry2).astype(bf16)
     back_cross, text_kgrad, text_vgrad = attend_backward(
         cross_query, text_key, text_value, shares2, back_att2
     )
     back_pairs = jnp.concatenate([text_kgrad, text_vgrad], axis=1)
-    back_hidden2 = unshuffled(z_reduce(dot_nt(back_cross, query_z[:, 3 * share :])))
     text_part = jnp.concatenate(
         [dot_tn(text_all[:, f * width : (f + 1) * width], back_pairs).astype(bf16) for f in range(2)],
         axis=1,
     )
     text_grad = settle([text_part], owner_text, split_places, n_z, cap_big)
     query_part2 = dot_tn(hidden2, back_cross).astype(bf16)
-    at_middle1 = at_middle2 + norm_back(back_hidden2, normed2, inverse2, norm_full[2])
-    carry1 = z_gather(at_middle1.astype(bf16))
-    back_att1 = dot_nt(carry1, outs_z[:, :width]).astype(bf16)
+    at_middle1, carry1, back_att1, term2 = back_call(
+        back_cross, query_z, 3, at_middle2, middle1, norm_full[2:4], outs_z, 0, n_z, n_dp, 4
+    )
+    carry1 = carry1.reshape(-1, width)
     outs_part1 = dot_tn(attended1, carry1).astype(bf16)
     outs_grad = settle([outs_part1, outs_part2], owner_outs, out_places, 1, cap_out)
     back_projected = jnp.concatenate(
@@ -368,19 +982,19 @@
     )
     query_part1 = dot_tn(hidden1, back_projected).astype(bf16)
     query_grad = settle([query_part1, query_part2], owner_query, split_places, n_z, cap_big)
-    back_hidden1 = unshuffled(z_reduce(dot_nt(back_projected, query_z[:, : 3 * share])))
-    grad_in = (at_middle1 + norm_back(back_hidden1, normed1, inverse1, norm_full[0])).astype(bf16)
-
-    norm_term = jnp.stack(
-        [
-            jnp.sum(back_hidden1 * normed1, axis=0),
-            jnp.sum(back_hidden1, axis=0),
-            jnp.sum(back_hidden2 * normed2, axis=0),
-            jnp.sum(back_hidden2, axis=0),
-            jnp.sum(back_hidden3 * normed3, axis=0),
-            jnp.sum(back_hidden3, axis=0),
-        ]
-    )
+    grad_in, result, term1 = last_call(
+        back_projected,
+        query_z,
+        at_middle1,
+        tokens_in,
+        norm_full[0:2],
+        branch3,
+        middle2,
+        n_z,
+        n_dp,
+        5,
+    )
+    norm_term = jnp.concatenate([term1[:2], term2[:2], term3[:2]], axis=0)
     norm_total = lax.psum(norm_term, ("dp", "fsdp"))
     norm_share = width // n_dp
     norm_grad = lax.dynamic_slice_in_dim(

time: 1580 us -> 1660 us (1.051)
  Pallas kernels: 17.6 us -> 671 us
  waiting for transfers between devices: 932 us -> 394 us
  blocking collectives: 256 us -> 335 us
  other arithmetic: 107 us -> 71.9 us
  matrix products: 145 us -> 112 us
  starting transfers between devices: 51.3 us -> 30.3 us
    pallas_call x0 -> x6, Pallas kernels: none -> 656 us  [the longest x2 224 us: back_call(): return call(dy, weight, base, middle, norm_rows, outs_z)]
    all_gather x7 -> x0, waiting for transfers between devices: 152 us -> none  [z_gather(): return lax.all_gather(values, 'fsdp', axis=0, tiled=True)]
    all_gather x5, waiting for transfers between devices: 205 us -> 53.6 us  [fetch(): return lax.all_gather(rows, 'dp', axis=0, tiled=True)]
    all_to_all x11 -> x7, waiting for transfers between devices: 145 us -> 27.9 us  [swap(): return lax.all_to_all(values, axis, 0, 0, tiled=True)]
    all_to_all x5 -> x9, blocking collectives: 179 us -> 295 us  [swap(): return lax.all_to_all(values, axis, 0, 0, tiled=True)]
    reduce_scatter x6 -> x0, waiting for transfers between devices: 107 us -> none  [z_reduce(): lax.psum_scatter(values.astype(bf16), 'fsdp', scatter_dimension=0, tiled=...]
    all_gather x2 -> x0, blocking collectives: 38.5 us -> none  [the longest x1 29.5 us: body(): norm_full = lax.all_gather(norm_weight, 'dp', axis=1, tiled=True)]
    dot_general x9 -> x4, matrix products: 38.2 us -> 7.49 us  [dot_nt(): lax.dot_general(left, right, (((1,), (1,)), ((), ())), preferred_element_...]
  transfers between devices with their start and end apart: 36 -> 19, of which waited for: 24 -> 10; matrix products, arithmetic and copies ran while one was open for 13% -> 8% of each run, Pallas kernels for 1% -> 33%
where the time goes in v2:
time: 1660 us
  Pallas kernels  671 us (40%)
  waiting for transfers between devices  394 us (24%)
  blocking collectives  335 us (20%)
  matrix products  112 us (7%)
  other arithmetic  71.9 us (4%)
  starting transfers between devices  30.3 us (2%)
  local copies, waits for them, and re-layouts  29.5 us (2%)
    reduce_scatter x7, waiting for transfers between devices, settle(): lax.psum_scatter(piece, 'dp', scatter_dimension=0, tiled=True)  313 us
    all_to_all x9, blocking collectives, swap(): return lax.all_to_all(values, axis, 0, 0, tiled=True)  295 us
    pallas_call x2, Pallas kernels, back_call(): return call(dy, weight, base, middle, norm_rows, outs_z)  224 us
    pallas_call x2, Pallas kernels, forward_call(): return call(*args)  211 us
    pallas_call x1, Pallas kernels, start_call(): return call(tokens, text, grad, marks, norms)  121 us
    pallas_call x1, Pallas kernels, last_call(): return call(dy, weight, base, tokens, norm_rows, branch, middle)  98.7 us
    dot_general x8, matrix products, dot(): return jnp.dot(left, right, preferred_element_type=f32)  53.9 us
    all_gather x5, waiting for transfers between devices, fetch(): return lax.all_gather(rows, 'dp', axis=0, tiled=True)  53.6 us
  transfers between devices with their start and end apart: 19, of which 10 were waited for; matrix products, arithmetic and copies ran while one was open for 8% of the time, Pallas kernels for 33%

profile of v2, /device:TPU:0, one launch (start us, length us, event | category | flops | bytes accessed | tf_op | source)
XLA Modules:
  0.0 1659.3 jit_solution(6830311518773889490)
XLA Ops:
  9.8 31.6 %all_to_all.100.slots_ref = bf16[8,64,2048]{2,1,0:T(8,128)(2,1)S(1)} all-to-all(bf16[8,64,2048]{2,1,0:T(8,128)(2,1)S(1)} %bitcast.170), channel_id=1, replica_groups=mesh['dp'=8,'fsdp'=4] {'dp'}, dimensions={0} | all-to-all | bytes 4194304 | tf_op jit(solution)/shard_map/all_to_all | solution.py:149
  42.2 29.9 %all_to_all.101 = bf16[4,64,2048]{2,1,0:T(8,128)(2,1)} all-to-all(bf16[4,64,2048]{2,1,0:T(8,128)(2,1)S(1)} %shard_map.419), channel_id=1, replica_groups=mesh['dp'=8,'fsdp'=4] {'fsdp'}, dimensions={0} | all-to-all | bytes 2097152 | tf_op jit(solution)/shard_map/all_to_all | solution.py:149
  72.3 26.6 %all_to_all.102.slots_ref = bf16[8,64,1024]{2,1,0:T(8,128)(2,1)S(1)} all-to-all(bf16[8,64,1024]{2,1,0:T(8,128)(2,1)S(1)} %bitcast.182), channel_id=1, replica_groups=mesh['dp'=8,'fsdp'=4] {'dp'}, dimensions={0} | all-to-all | bytes 2097152 | tf_op jit(solution)/shard_map/all_to_all | solution.py:149
  103.0 49.0 %all_to_all.103.slots_ref = bf16[8,64,2048]{2,1,0:T(8,128)(2,1)S(1)} all-to-all(bf16[8,64,2048]{2,1,0:T(8,128)(2,1)S(1)} %bitcast.171), channel_id=1, replica_groups=mesh['dp'=8,'fsdp'=4] {'dp'}, dimensions={0} | all-to-all | bytes 4194304 | tf_op jit(solution)/shard_map/all_to_all | solution.py:149
  152.9 27.9 %all_to_all.104 = bf16[4,64,2048]{2,1,0:T(8,128)(2,1)} all-to-all(bf16[4,64,2048]{2,1,0:T(8,128)(2,1)S(1)} %shard_map.420), channel_id=1, replica_groups=mesh['dp'=8,'fsdp'=4] {'fsdp'}, dimensions={0} | all-to-all | bytes 2097152 | tf_op jit(solution)/shard_map/all_to_all | solution.py:149
  183.4 32.6 %all_to_all.105.slots_ref = bf16[8,64,2048]{2,1,0:T(8,128)(2,1)S(1)} all-to-all(bf16[8,64,2048]{2,1,0:T(8,128)(2,1)S(1)} %bitcast.172), channel_id=1, replica_groups=mesh['dp'=8,'fsdp'=4] {'dp'}, dimensions={0} | all-to-all | bytes 4194304 | tf_op jit(solution)/shard_map/all_to_all | solution.py:149
  216.9 27.5 %all_to_all.106 = bf16[4,64,2048]{2,1,0:T(8,128)(2,1)} all-to-all(bf16[4,64,2048]{2,1,0:T(8,128)(2,1)S(1)} %shard_map.422), channel_id=1, replica_groups=mesh['dp'=8,'fsdp'=4] {'fsdp'}, dimensions={0} | all-to-all | bytes 2097152 | tf_op jit(solution)/shard_map/all_to_all | solution.py:149
  244.6 121.5 %start.1 = (bf16[4,128,2048]{2,1,0:T(8,128)(2,1)}, bf16[4,32,4096]{2,1,0:T(8,128)(2,1)}, bf16[4,128,2048]{2,1,0:T(8,128)(2,1)}, s32[4,8,256]{2,1,0:T(8,128)S(1)}, f32[8,2048]{1,0:T(8,128)S(1)}) custom-call(bf16[128,2048]{1,0:T(8,128)(2,1)S(1)} %copy-done, bf16[32,4096]{1,0:T(8,128)(2,1)S(1)} %copy-done.4, bf16[128,2048]{1,0:T(8,128)(2,1)S(1)} %copy-done.2, ...), custom_call_target="tpu_custom_call" | custom-call | bytes 120000000 | tf_op jit(solution)/shard_map/start/pallas_call | solution.py:698
  382.5 106.2 %forward0.1 = (f32[128,2048]{1,0:T(8,128)}, bf16[4,128,2048]{2,1,0:T(8,128)(2,1)}, bf16[512,512]{1,0:T(8,128)(2,1)S(1)}) custom-call(bf16[512,512]{1,0:T(8,128)(2,1)S(1)} %bitcast.153, bf16[512,4096]{1,0:T(8,128)(2,1)} %bitcast.165, bf16[128,2048]{1,0:T(8,128)(2,1)S(1)} %copy-done, f32[2,2048]{1,0:T(2,128)S(1)} %get-tuple-element.90.norm_ref, ...), custom_call_target="tpu_custom_call" | custom-call | bytes 120000000 | tf_op jit(solution)/shard_map/forward0/pallas_call | solution.py:723
  498.8 105.2 %forward1.1 = (f32[128,2048]{1,0:T(8,128)S(1)}, bf16[4,128,2048]{2,1,0:T(8,128)(2,1)}) custom-call(bf16[512,512]{1,0:T(8,128)(2,1)S(1)} %bitcast.152, bf16[512,4096]{1,0:T(8,128)(2,1)} %bitcast.166, f32[128,2048]{1,0:T(8,128)} %get-tuple-element.46.base_ref.middle_ref, f32[2,2048]{1,0:T(2,128)S(1)} %get-tuple-element.89.norm_ref), custom_call_target="tpu_custom_call" | custom-call | bytes 120000000 | tf_op jit(solution)/shard_map/forward1/pallas_call | solution.py:723
  604.9 18.0 %multiply_convert_fusion = (bf16[512,2048]{1,0:T(8,128)(2,1)S(1)}, f32[512,2048]{1,0:T(8,128)}, f32[512,2048]{1,0:T(8,128)}) fusion(bf16[512,2048]{1,0:T(8,128)(2,1)} %bitcast.208, bf16[2048,2048]{1,0:T(8,128)(2,1)} %all-gather.12.cloned.1.call-done.w_hbm), kind=kOutput, calls=%fused_computation.40 | convolution fusion | flops 4363124736 | bytes 20971520 | tf_op jit(solution)/shard_map/dot_general | solution.py:61
  632.0 69.1 %reduce-scatter.20.cloned.1.call-done = bf16[64,8192]{1,0:T(8,128)(2,1)} async-done(((bf16[512,8192]{1,0:T(8,128)(2,1)}), bf16[64,8192]{1,0:T(8,128)(2,1)}) %reduce-scatter.20.cloned.1.call-update) | async-done | bytes 1048592 | tf_op jit(solution)/shard_map/reduce_scatter | solution.py:889
  703.3 41.1 %all_to_all.107 = bf16[8,64,2048]{2,1,0:T(8,128)(2,1)S(1)} all-to-all(bf16[8,64,2048]{2,1,0:T(8,128)(2,1)S(1)} %shard_map.428), channel_id=1, replica_groups=mesh['dp'=8,'fsdp'=4] {'dp'}, dimensions={0} | all-to-all | bytes 4194304 | tf_op jit(solution)/shard_map/all_to_all | solution.py:149
  752.5 29.0 %all_to_all.108.slots_ref = bf16[8,64,2048]{2,1,0:T(8,128)(2,1)S(1)} all-to-all(bf16[8,64,2048]{2,1,0:T(8,128)(2,1)S(1)} %bitcast.169), channel_id=1, replica_groups=mesh['dp'=8,'fsdp'=4] {'dp'}, dimensions={0} | all-to-all | bytes 4194304 | tf_op jit(solution)/shard_map/all_to_all | solution.py:149
  783.4 53.6 %all-gather.16.cloned.1.call-done = bf16[1,512,8192]{2,1,0:T(8,128)(2,1)} async-done(((bf16[1,64,8192]{2,1,0:T(8,128)(2,1)}), bf16[1,512,8192]{2,1,0:T(8,128)(2,1)}) %all-gather.16.cloned.1.call-update) | async-done | bytes 8388624 | tf_op jit(solution)/shard_map/all_gather | solution.py:885
  851.0 114.3 %back1.1 = (f32[128,2048]{1,0:T(8,128)}, bf16[4,128,2048]{2,1,0:T(8,128)(2,1)}, bf16[512,512]{1,0:T(8,128)(2,1)S(1)}, f32[8,2048]{1,0:T(8,128)S(1)}) custom-call(bf16[512,2048]{1,0:T(8,128)(2,1)} %add_convert_fusion.1.dy_ref, bf16[2048,2048]{1,0:T(8,128)(2,1)} %all-gather.12.cloned.1.call-done.w_hbm, bf16[128,2048]{1,0:T(8,128)(2,1)S(1)} %copy-done.2, ...), custom_call_target="tpu_custom_call" | custom-call | bytes 120000000 | tf_op jit(solution)/shard_map/back1/pallas_call | solution.py:757
  970.0 109.8 %back0.1 = (f32[128,2048]{1,0:T(8,128)}, bf16[4,128,2048]{2,1,0:T(8,128)(2,1)}, bf16[512,512]{1,0:T(8,128)(2,1)S(1)}, f32[8,2048]{1,0:T(8,128)S(1)}) custom-call(bf16[512,512]{1,0:T(8,128)(2,1)S(1)} %bitcast.151, bf16[2048,2048]{1,0:T(8,128)(2,1)} %all-gather.8.cloned.1.call-done.rest_0_.w_hbm, f32[128,2048]{1,0:T(8,128)} %get-tuple-element.51.base_ref, ...), custom_call_target="tpu_custom_call" | custom-call | bytes 120000000 | tf_op jit(solution)/shard_map/back0/pallas_call | solution.py:757
  1133.7 21.6 %reduce-scatter.8.cloned.1.call-done = bf16[256,1536]{1,0:T(8,128)(2,1)} async-done(((bf16[2048,1536]{1,0:T(8,128)(2,1)}), bf16[256,1536]{1,0:T(8,128)(2,1)}) %reduce-scatter.8.cloned.1.call-update) | async-done | bytes 786448 | tf_op jit(solution)/shard_map/reduce_scatter | solution.py:889
  1162.3 38.6 %reduce-scatter.16.cloned.1.call-done = bf16[64,2048]{1,0:T(8,128)(2,1)} async-done(((bf16[512,2048]{1,0:T(8,128)(2,1)}), bf16[64,2048]{1,0:T(8,128)(2,1)}) %reduce-scatter.16.cloned.1.call-update) | async-done | bytes 262160 | tf_op jit(solution)/shard_map/reduce_scatter | solution.py:889
  1200.9 45.0 %reduce-scatter.14.cloned.1.call-done = bf16[64,2048]{1,0:T(8,128)(2,1)} async-done(((bf16[512,2048]{1,0:T(8,128)(2,1)}), bf16[64,2048]{1,0:T(8,128)(2,1)}) %reduce-scatter.14.cloned.1.call-update) | async-done | bytes 262160 | tf_op jit(solution)/shard_map/reduce_scatter | solution.py:889
  1272.2 69.7 %reduce-scatter.12.cloned.1.call-done = bf16[256,2048]{1,0:T(8,128)(2,1)} async-done(((bf16[2048,2048]{1,0:T(8,128)(2,1)}), bf16[256,2048]{1,0:T(8,128)(2,1)}) %reduce-scatter.12.cloned.1.call-update) | async-done | bytes 1048592 | tf_op jit(solution)/shard_map/reduce_scatter | solution.py:889
  1347.8 68.7 %reduce-scatter.18.cloned.1.call-done = bf16[256,2048]{0,1:T(8,128)(2,1)} async-done(((bf16[2048,2048]{0,1:T(8,128)(2,1)}), bf16[256,2048]{0,1:T(8,128)(2,1)}) %reduce-scatter.18.cloned.1.call-update) | async-done | bytes 1048592 | tf_op jit(solution)/shard_map/reduce_scatter | solution.py:889
  1461.4 98.7 %last.1 = (bf16[128,2048]{1,0:T(8,128)(2,1)S(1)}, bf16[128,2048]{1,0:T(8,128)(2,1)S(1)}, f32[8,2048]{1,0:T(8,128)S(1)}) custom-call(bf16[512,1536]{1,0:T(8,128)(2,1)} %copy-done.29, bf16[2048,2048]{1,0:T(8,128)(2,1)} %all-gather.8.cloned.1.call-done.rest_0_.w_hbm, f32[128,2048]{1,0:T(8,128)} %get-tuple-element.53.base_ref, bf16[128,2048]{1,0:T(8,128)(2,1)S(1)} %copy-done, ...), custom_call_target="tpu_custom_call" | custom-call | bytes 120000000 | tf_op jit(solution)/shard_map/last/pallas_call | solution.py:781
  1560.2 39.3 %psum.7 = f32[6,2048]{1,0:T(8,128)S(1)} all-reduce(f32[6,2048]{1,0:T(8,128)S(1)} %pad_maximum_fusion.4), channel_id=1, replica_groups=mesh['dp'=8,'fsdp'=4] {'dp','fsdp'}, use_global_device_ids=true, to_apply=%region_13.14 | all-reduce | flops 12288 | bytes 98304 | tf_op jit(solution)/shard_map/psum | solution.py:998
  (254 shorter events, 269.4 us)
Async XLA Ops:
  7.2 359.2 %all-gather.8.cloned.1.call-start = ((), (), s32[]{:S(2)}) async-start(), calls=%async_computation.23 | async-start | bytes 9437184 | tf_op jit(solution)/shard_map/all_gather | solution.py:885
  72.1 310.4 %all-gather.14.cloned.1.call-start = ((), (), s32[]{:S(2)}) async-start(), calls=%async_computation.33 | async-start | bytes 4718592 | tf_op jit(solution)/shard_map/all_gather | solution.py:885
  100.4 389.1 %all-gather.10.cloned.1.call-start = ((), (), s32[]{:S(2)}) async-start(), calls=%async_computation.24 | async-start | bytes 9437184 | tf_op jit(solution)/shard_map/all_gather | solution.py:885
  180.8 424.1 %all-gather.12.cloned.1.call-start = ((), (), s32[]{:S(2)}) async-start(), calls=%async_computation.25 | async-start | bytes 9437184 | tf_op jit(solution)/shard_map/all_gather | solution.py:885
  244.5 456.6 %reduce-scatter.20.cloned.1.call-start = ((), (), s32[]{:S(2)}) async-start(), calls=%async_computation.32 | async-start | bytes 9437184 | tf_op jit(solution)/shard_map/reduce_scatter | solution.py:889
  498.7 124.3 %copy-start.32 = (bf16[4,128,4,128]{3,2,1,0:T(4,128)(2,1)}, bf16[4,128,4,128]{3,2,1,0:T(4,128)(2,1)S(1)}, u32[]{:S(2)}) copy-start(bf16[4,128,4,128]{3,2,1,0:T(4,128)(2,1)S(1)} %copy.90) | copy-start | bytes 1572868
  631.9 205.1 %all-gather.16.cloned.1.call-start = ((), (), s32[]{:S(2)}) async-start(), calls=%async_computation.34 | async-start | bytes 9437184 | tf_op jit(solution)/shard_map/all_gather | solution.py:885
  783.4 350.4 %reduce-scatter.10.cloned.1.call-start = ((), (), s32[]{:S(2)}) async-start(), calls=%async_computation.27 | async-start | bytes 2359296 | tf_op jit(solution)/shard_map/reduce_scatter | solution.py:889
  969.9 185.5 %reduce-scatter.8.cloned.1.call-start = ((), (), s32[]{:S(2)}) async-start(), calls=%async_computation.26 | async-start | bytes 7077888 | tf_op jit(solution)/shard_map/reduce_scatter | solution.py:889
  1096.7 104.1 %reduce-scatter.16.cloned.1.call-start = ((), (), s32[]{:S(2)}) async-start(), calls=%async_computation.30 | async-start | bytes 2359296 | tf_op jit(solution)/shard_map/reduce_scatter | solution.py:889
  1102.3 143.6 %reduce-scatter.14.cloned.1.call-start = ((), (), s32[]{:S(2)}) async-start(), calls=%async_computation.29 | async-start | bytes 2359296 | tf_op jit(solution)/shard_map/reduce_scatter | solution.py:889
  1107.0 234.9 %reduce-scatter.12.cloned.1.call-start = ((), (), s32[]{:S(2)}) async-start(), calls=%async_computation.28 | async-start | bytes 9437184 | tf_op jit(solution)/shard_map/reduce_scatter | solution.py:889
  1115.7 300.8 %reduce-scatter.18.cloned.1.call-start = ((), (), s32[]{:S(2)}) async-start(), calls=%async_computation.31 | async-start | bytes 9437184 | tf_op jit(solution)/shard_map/reduce_scatter | solution.py:889
  1133.7 118.5 %copy-start.9 = (s32[64,1]{0,1:T(1,128)S(1)}, s32[64,1]{0,1:T(1,128)}, u32[]{:S(2)}) copy-start(s32[64,1]{0,1:T(1,128)} %param.33) | copy-start | bytes 772
  1157.7 91.0 %all-to-all-start.8 = ((bf16[4,64,2048]{2,1,0:T(8,128)(2,1)}), bf16[4,64,2048]{2,1,0:T(8,128)(2,1)S(1)}, u32[]{:S(2)}, u32[]{:S(2)}) async-start(bf16[4,64,2048]{2,1,0:T(8,128)(2,1)} %bitcast.29), calls=%async_computation.10 | async-start | bytes 2097152 | tf_op jit(solution)/shard_map/all_to_all | solution.py:149
  1248.7 18.9 %all-to-all-start.12 = ((bf16[8,64,1024]{2,1,0:T(8,128)(2,1)}), bf16[8,64,1024]{2,1,0:T(8,128)(2,1)S(1)}, u32[]{:S(2)}, u32[]{:S(2)}) async-start(bf16[8,64,1024]{2,1,0:T(8,128)(2,1)} %shard_map.426), calls=%async_computation.17 | async-start | bytes 2097152 | tf_op jit(solution)/shard_map/all_to_all | solution.py:149
  1268.5 73.3 %all-to-all-start.9 = ((bf16[8,64,2048]{2,1,0:T(8,128)(2,1)}), bf16[8,64,2048]{2,1,0:T(8,128)(2,1)S(1)}, u32[]{:S(2)}, u32[]{:S(2)}) async-start(bf16[8,64,2048]{2,1,0:T(8,128)(2,1)} %shard_map.424), calls=%async_computation.11 | async-start | bytes 4194304 | tf_op jit(solution)/shard_map/all_to_all | solution.py:149
  1343.2 75.5 %all-to-all-start.10 = ((bf16[4,64,2048]{2,1,0:T(8,128)(2,1)}), bf16[4,64,2048]{2,1,0:T(8,128)(2,1)S(1)}, u32[]{:S(2)}, u32[]{:S(2)}) async-start(bf16[4,64,2048]{2,1,0:T(8,128)(2,1)} %bitcast.200), calls=%async_computation.13 | async-start | bytes 2097152 | tf_op jit(solution)/shard_map/all_to_all | solution.py:149
  1418.7 30.3 %all-to-all-start.13 = ((bf16[4,64,2048]{2,1,0:T(8,128)(2,1)}), bf16[4,64,2048]{2,1,0:T(8,128)(2,1)S(1)}, u32[]{:S(2)}, u32[]{:S(2)}) async-start(bf16[4,64,2048]{2,1,0:T(8,128)(2,1)} %bitcast.186), calls=%async_computation.19 | async-start | bytes 2097152 | tf_op jit(solution)/shard_map/all_to_all | solution.py:149
  1449.0 160.6 %all-to-all-start.11 = ((bf16[8,64,2048]{2,1,0:T(8,128)(2,1)}), bf16[8,64,2048]{2,1,0:T(8,128)(2,1)}, u32[]{:S(2)}, u32[]{:S(2)}) async-start(bf16[8,64,2048]{2,1,0:T(8,128)(2,1)} %shard_map.425), calls=%async_computation.14 | async-start | bytes 4194304 | tf_op jit(solution)/shard_map/all_to_all | solution.py:149
  1461.4 138.1 %copy-start.44 = (f32[6,256]{1,0:T(8,128)S(1)}, f32[6,256]{1,0:T(8,128)}, u32[]{:S(2)}) copy-start(f32[6,256]{1,0:T(8,128)} %param.53) | copy-start | bytes 18436
  1461.4 138.1 %copy-start.45 = (f32[6,256]{1,0:T(8,128)S(1)}, f32[6,256]{1,0:T(8,128)}, u32[]{:S(2)}) copy-start(f32[6,256]{1,0:T(8,128)} %param.55) | copy-start | bytes 18436
  1461.4 138.1 %copy-start.46 = (f32[6,256]{1,0:T(8,128)S(1)}, f32[6,256]{1,0:T(8,128)}, u32[]{:S(2)}) copy-start(f32[6,256]{1,0:T(8,128)} %param.54) | copy-start | bytes 18436
  1609.7 31.0 %all-to-all-start.14 = ((bf16[8,64,2048]{2,1,0:T(8,128)(2,1)}), bf16[8,64,2048]{2,1,0:T(8,128)(2,1)}, u32[]{:S(2)}, u32[]{:S(2)}) async-start(bf16[8,64,2048]{2,1,0:T(8,128)(2,1)} %shard_map.427), calls=%async_computation.20 | async-start | bytes 4194304 | tf_op jit(solution)/shard_map/all_to_all | solution.py:149
  (47 other events, 1075.7 us)
Sparse Core Ops, SparseCore 0:
  72.2 79.4 all-gather.7
  154.2 36.9 all-gather.13
  193.1 62.7 all-gather.9
  257.6 54.3 all-gather.11
  632.0 69.0 reduce-scatter.19
  783.5 53.4 all-gather.15
  970.0 38.5 reduce-scatter.9
  1096.8 58.4 reduce-scatter.7
  1159.6 41.2 reduce-scatter.15
  1204.6 41.2 reduce-scatter.13
  1249.7 92.0 reduce-scatter.11
  1345.1 71.2 reduce-scatter.17

commit v3 on v2

--- a/solution.py
+++ b/solution.py
@@ -79,74 +79,7 @@
     return 0, block
 
 
-def compact_kernel(places, n_dp, owner_ref, slots_ref, out_ref, count_ref):
-    for index in range(n_dp):
-        count_ref[index] = 0
-    for block, (part, column) in enumerate(places):
-        owner = owner_ref[block]
-        position = count_ref[owner]
-        count_ref[owner] = position + 1
-        start = pl.multiple_of(position * BLK, BLK)
-        out_ref[part, :, column * BLK : (column + 1) * BLK] = slots_ref[
-            owner, :, pl.ds(start, BLK)
-        ]
-
-
-def compact(slots, owner, places, parts):
-    n_dp, rows, _ = slots.shape
-    columns = len(places) // parts * BLK
-    return pl.pallas_call(
-        functools.partial(compact_kernel, places, n_dp),
-        out_shape=jax.ShapeDtypeStruct((parts, rows, columns), slots.dtype),
-        in_specs=[
-            pl.BlockSpec(memory_space=pltpu.SMEM),
-            pl.BlockSpec(memory_space=pltpu.VMEM),
-        ],
-        out_specs=pl.BlockSpec(memory_space=pltpu.VMEM),
-        scratch_shapes=[pltpu.SMEM((n_dp,), jnp.int32)],
-        compiler_params=pltpu.CompilerParams(vmem_limit_bytes=32 * 1024 * 1024),
-        cost_estimate=pl.CostEstimate(
-            flops=0, bytes_accessed=2 * (slots.size + len(places) * BLK * rows), transcendentals=0
-        ),
-    )(owner, slots)
-
-
-def expand_kernel(places, n_dp, owner_ref, grad_ref, out_ref, count_ref):
-    for index in range(n_dp):
-        count_ref[index] = 0
-    out_ref[...] = jnp.zeros_like(out_ref)
-    for block, (part, column) in enumerate(places):
-        owner = owner_ref[block]
-        position = count_ref[owner]
-        count_ref[owner] = position + 1
-        start = pl.multiple_of(position * BLK, BLK)
-        out_ref[owner, :, pl.ds(start, BLK)] = grad_ref[
-            part, :, column * BLK : (column + 1) * BLK
-        ]
-
-
-def expand(grad, owner, places, n_dp, capacity):
-    rows = grad.shape[1]
-    return pl.pallas_call(
-        functools.partial(expand_kernel, places, n_dp),
-        out_shape=jax.ShapeDtypeStruct((n_dp, rows, capacity * BLK), grad.dtype),
-        in_specs=[
-            pl.BlockSpec(memory_space=pltpu.SMEM),
-            pl.BlockSpec(memory_space=pltpu.VMEM),
-        ],
-        out_specs=pl.BlockSpec(memory_space=pltpu.VMEM),
-        scratch_shapes=[pltpu.SMEM((n_dp,), jnp.int32)],
-        compiler_params=pltpu.CompilerParams(vmem_limit_bytes=32 * 1024 * 1024),
-        cost_estimate=pl.CostEstimate(
-            flops=0,
-            bytes_accessed=2 * (grad.size + n_dp * capacity * BLK * rows),
-            transcendentals=0,
-        ),
-    )(owner, grad)
-
-
-def swap(values, axis):
-    return lax.all_to_all(values, axis, 0, 0, tiled=True)
+MESH = pl.DeviceIdType.MESH
 
 
 SUBS = 4
@@ -207,35 +140,36 @@
             way,
         )
 
-    def targets(self, way):
-        n = self.line.n
-        return range(n - 1, 0, -1) if way == 0 else range(n - 1)
-
-    def beyond(self, way, target):
-        return self.line.at < target if way == 0 else self.line.at > target
-
-    def forward(self, sub):
+    def target(self, way, time):
+        n, at = self.line.n, self.line.at
+        return n - 1 - (time - at) if way == 0 else time - (n - 1 - at)
+
+    def passes(self, way, target):
+        n, at = self.line.n, self.line.at
+        if way == 0:
+            return jnp.logical_and(target > at, target < n)
+        return jnp.logical_and(target < at, target >= 0)
+
+    def forward(self, sub, time):
         line = self.line
         rows = line.part(sub)
-        for step in range(line.n - 1):
-            for way in (0, 1):
-                target = self.targets(way)[step]
-                inner = jnp.logical_and(self.beyond(way, target), line.has(1 - way))
-                outer = jnp.logical_and(
-                    self.beyond(way, target), jnp.logical_not(line.has(1 - way))
-                )
-
-                @pl.when(outer)
-                def _():
-                    self.move(way, target, sub, self.part.at[target, rows]).start()
-
-                @pl.when(inner)
-                def _():
-                    held = self.held.at[way, target, rows]
-                    self.move(way, target, sub, held).wait_recv()
-                    total = held[...].astype(f32) + self.part[target, rows].astype(f32)
-                    held[...] = total.astype(bf16)
-                    self.move(way, target, sub, held).start()
+        for way in (0, 1):
+            target = self.target(way, time)
+            passes = self.passes(way, target)
+            inner = jnp.logical_and(passes, line.has(1 - way))
+            outer = jnp.logical_and(passes, jnp.logical_not(line.has(1 - way)))
+
+            @pl.when(outer)
+            def _():
+                self.move(way, target, sub, self.part.at[target, rows]).start()
+
+            @pl.when(inner)
+            def _():
+                held = self.held.at[way, target, rows]
+                self.move(way, target, sub, held).wait_recv()
+                total = held[...].astype(f32) + self.part[target, rows].astype(f32)
+                held[...] = total.astype(bf16)
+                self.move(way, target, sub, held).start()
 
     def total(self, sub, sum_ref):
         line = self.line
@@ -250,14 +184,35 @@
                 sum_ref[...] += held[...].astype(f32)
 
     def finish(self):
+        line = self.line
         for way in (0, 1):
-            for target in self.targets(way):
-
-                @pl.when(self.beyond(way, target))
+            for time in range(line.n - 1):
+                target = self.target(way, time)
+
+                @pl.when(self.passes(way, target))
                 def _():
-                    for sub in range(self.line.rows // self.line.step):
-                        held = self.held.at[way, target, self.line.part(sub)]
+                    for sub in range(line.rows // line.step):
+                        held = self.held.at[way, target, line.part(sub)]
                         self.move(way, target, sub, held).wait_send()
+
+
+def relay(n, sums, blocks, settle):
+    for slot in range((SUBS + 2) * (n - 1)):
+        sub, time = divmod(slot, n - 1)
+        if sub < SUBS:
+            for one in sums:
+                one.forward(sub, time)
+        if time == 0 and 0 <= sub - 1 < SUBS:
+            settle(sub - 1)
+        if blocks is not None:
+            if time == n - 2 and 0 <= sub - 1 < SUBS:
+                blocks.forward(sub - 1, 1)
+            if time < n - 2 and 0 <= sub - 2 < SUBS:
+                blocks.forward(sub - 2, time + 2)
+    for one in sums:
+        one.finish()
+    if blocks is not None:
+        blocks.finish()
 
 
 class Blocks:
@@ -271,10 +226,6 @@
             held, held, self.send.at[way, source, sub], self.recv.at[way, source, sub], way
         )
 
-    def sources(self, way):
-        n = self.line.n
-        return range(n - 2, -1, -1) if way == 0 else range(1, n)
-
     def behind(self, way, source):
         return self.line.at > source if way == 0 else self.line.at < source
 
@@ -285,19 +236,22 @@
             def _():
                 self.move(way, self.line.at, sub).start()
 
-    def forward(self, sub):
+    def forward(self, sub, step):
         line = self.line
-        for step in range(line.n - 1):
-            for way in (0, 1):
-                source = self.sources(way)[step]
-
-                @pl.when(self.behind(way, source))
+        for way in (0, 1):
+            source = line.at - step if way == 0 else line.at + step
+
+            @pl.when(jnp.logical_and(source >= 0, source < line.n))
+            def _():
+                self.move(way, source, sub).wait_recv()
+
+                @pl.when(line.has(way))
                 def _():
-                    self.move(way, source, sub).wait_recv()
-
-                    @pl.when(line.has(way))
-                    def _():
-                        self.move(way, source, sub).start()
+                    self.move(way, source, sub).start()
+
+    def forward_all(self, sub):
+        for step in range(1, self.line.n):
+            self.forward(sub, step)
 
     def finish(self):
         line = self.line
@@ -352,100 +306,254 @@
     lax.fori_loop(0, columns // tile, one, 0)
 
 
-def start_kernel(n, n_dp, order, tokens, text, grad, marks, norms, *rest):
-    h_full, text_full, grad_full, marks_full, norm_full = rest[:5]
-    parts, work, n_send, n_recv = rest[5:9]
-    sems = rest[9:]
-    rows, width = tokens.shape
-    step = rows // SUBS
-    me = lax.axis_index("dp")
-    line = Line(n, rows, step)
+class Swap:
+    def __init__(self, axis, source, target, send, recv):
+        self.axis, self.source, self.target = axis, source, target
+        self.send, self.recv = send, recv
+        self.n = lax.axis_size(axis)
+        self.me = lax.axis_index(axis)
+
+    def copy(self, jump, arrival=False):
+        peer = lax.rem(self.me + jump, self.n)
+        slot = peer if arrival else self.me
+        return pltpu.make_async_remote_copy(
+            src_ref=self.source.at[peer],
+            dst_ref=self.target.at[slot],
+            send_sem=self.send.at[jump],
+            recv_sem=self.recv.at[slot],
+            device_id={self.axis: peer},
+            device_id_type=MESH,
+        )
+
+    def start(self):
+        for jump in range(1, self.n):
+            self.copy(jump).start()
+
+    def keep(self):
+        self.target[self.me] = self.source[self.me]
+
+    def wait(self):
+        for jump in range(1, self.n):
+            self.copy(jump, True).wait_recv()
+
+    def finish(self):
+        for jump in range(1, self.n):
+            self.copy(jump).wait_send()
+
+
+def greet_all():
     barrier = pltpu.get_barrier_semaphore()
-    for jump in range(1, n_dp):
-        pl.semaphore_signal(
-            barrier,
-            inc=1,
-            device_id={"dp": lax.rem(me + jump, n_dp)},
-            device_id_type=pl.DeviceIdType.MESH,
+    count = 0
+    for axis in ("dp", "fsdp"):
+        n, me = lax.axis_size(axis), lax.axis_index(axis)
+        count += n - 1
+        for jump in range(1, n):
+            pl.semaphore_signal(
+                barrier, inc=1, device_id={axis: lax.rem(me + jump, n)}, device_id_type=MESH
+            )
+    pl.semaphore_wait(barrier, count)
+
+
+class Refs:
+    def __init__(self, refs):
+        self.refs = list(refs)
+
+    def take(self, count=None):
+        taken = self.refs[: 1 if count is None else count]
+        self.refs = self.refs[len(taken) :]
+        return taken[0] if count is None else taken
+
+
+def enter_kernel(weights, gathers, order, normed, hidden, *refs):
+    refs = Refs(refs)
+    n_dp, n_z = lax.axis_size("dp"), lax.axis_size("fsdp")
+    slots_ref = refs.take()
+    w_refs = refs.take(len(weights))
+    in_refs = refs.take(len(gathers))
+    norm_in = refs.take() if normed or hidden else None
+    row_refs = refs.take(len(weights))
+    full_refs = refs.take(len(gathers))
+    norm_out = refs.take() if normed else None
+    loads = []
+    for w_ref in w_refs:
+        stage, sem = refs.take(2)
+        load = pltpu.make_async_copy(w_ref, stage, sem)
+        load.start()
+        loads.append((stage, load))
+    greet_all()
+    if normed:
+        parts, *sems = refs.take(3)
+        norm_swap = Spread("dp", norm_in, parts, *sems)
+        norm_swap.start()
+    lines = []
+    for in_ref, full_ref in zip(in_refs, full_refs):
+        rows = in_ref.shape[0]
+        step = rows // SUBS if rows >= 16 * SUBS else rows
+        lines.append(Blocks(Line(n_z, rows, step), full_ref, *refs.take(2)))
+    swaps = []
+    for (stage, load), (places, split, _) in zip(loads, weights):
+        source, target, *sems = refs.take(4)
+        swap = Swap("dp", source, target, *sems)
+        load.wait()
+        chunk = source.shape[2]
+        for jump in range(n_dp):
+            peer = lax.rem(swap.me + jump, n_dp)
+            into = source if jump else target
+            for slot in range(source.shape[1]):
+                here = pl.ds(pl.multiple_of(peer * chunk, chunk), chunk)
+                piece = stage[here, slot * BLK : (slot + 1) * BLK]
+                into[peer, slot] = piece.astype(bf16)
+            if jump:
+                swap.copy(jump).start()
+        swaps.append(swap)
+    work = refs.take()
+    for index, (in_ref, full_ref, blocks) in enumerate(zip(in_refs, full_refs, lines)):
+        line = blocks.line
+        if hidden and index == 0:
+            for sub in range(line.rows // line.step):
+                here = line.part(sub)
+                values, _ = normalize(in_ref[here].astype(f32))
+                work[...] = values * norm_in[0:1] + norm_in[1:2]
+                store_shuffled(work, full_ref, line, here, order)
+                blocks.start(sub)
+        elif in_ref.dtype == bf16 and gathers[index]:
+            work2 = refs.take()
+            work2[...] = in_ref[...].astype(f32)
+            store_shuffled(work2, full_ref, line, line.part(0), order)
+            blocks.start(0)
+        else:
+            for sub in range(line.rows // line.step):
+                here = line.part(sub)
+                full_ref[line.at, here] = in_ref[here]
+                blocks.start(sub)
+    if normed:
+        parts[norm_swap.me] = norm_in[...]
+        norm_swap.wait()
+        share = norm_in.shape[1]
+        for index in range(n_dp):
+            norm_out[:, index * share : (index + 1) * share] = parts[index]
+    shares = []
+    for swap, row_ref, (places, split, first) in zip(swaps, row_refs, weights):
+        swap.wait()
+        if split:
+            cut, *sems = refs.take(3)
+            share = Swap("fsdp", cut, row_ref, *sems)
+            shares.append(share)
+        else:
+            cut = row_ref
+        for block, (part, column) in enumerate(places):
+            owner, slot = slots_ref[0, first + block], slots_ref[1, first + block]
+            cut[part, :, column * BLK : (column + 1) * BLK] = swap.target[owner, slot]
+        if split:
+            share.start()
+            share.keep()
+    for blocks in lines:
+        for sub in range(blocks.line.rows // blocks.line.step):
+            blocks.forward_all(sub)
+    for share in shares:
+        share.wait()
+    for one in [*swaps, *shares, *lines]:
+        one.finish()
+    if normed:
+        norm_swap.finish()
+
+
+class Spread(Swap):
+    def copy(self, jump, arrival=False):
+        peer = lax.rem(self.me + jump, self.n)
+        slot = peer if arrival else self.me
+        return pltpu.make_async_remote_copy(
+            src_ref=self.source,
+            dst_ref=self.target.at[slot],
+            send_sem=self.send.at[jump],
+            recv_sem=self.recv.at[slot],
+            device_id={self.axis: peer},
+            device_id_type=MESH,
         )
-    line.greet(n_dp - 1)
-
-    def norm_copy(jump):
-        return pltpu.make_async_remote_copy(
-            src_ref=norms,
-            dst_ref=parts.at[me],
-            send_sem=n_send.at[jump],
-            recv_sem=n_recv.at[me],
-            device_id={"dp": lax.rem(me + jump, n_dp)},
-            device_id_type=pl.DeviceIdType.MESH,
-        )
-
-    def norm_arrival(jump):
-        source = lax.rem(me + jump, n_dp)
-        return pltpu.make_async_remote_copy(
-            src_ref=norms,
-            dst_ref=parts.at[source],
-            send_sem=n_send.at[jump],
-            recv_sem=n_recv.at[source],
-            device_id={"dp": source},
-            device_id_type=pl.DeviceIdType.MESH,
-        )
-
-    for jump in range(1, n_dp):
-        norm_copy(jump).start()
-    text_rows = text.shape[0]
-    text_line = Line(n, text_rows, text_rows)
-    mark_line = Line(n, marks.shape[0], marks.shape[0])
-    hidden = Blocks(line, h_full, sems[0], sems[1])
-    texts = Blocks(text_line, text_full, sems[2], sems[3])
-    grads = Blocks(line, grad_full, sems[4], sems[5])
-    places = Blocks(mark_line, marks_full, sems[6], sems[7])
-    marks_full[line.at] = marks[...]
-    places.start(0)
-    parts[me] = norms[...]
-    for jump in range(1, n_dp):
-        norm_arrival(jump).wait_recv()
-    share = width // n_dp
-    for index in range(n_dp):
-        norm_full[:, index * share : (index + 1) * share] = parts[index]
-    for sub in range(SUBS):
-        here = line.part(sub)
-        normed, _ = normalize(tokens[here].astype(f32))
-        work[...] = normed * norm_full[0:1] + norm_full[1:2]
-
-        def load(group):
-            return work[:, group * BLK : (group + 1) * BLK]
-
-        def store(group, value):
-            h_full[line.at, here, group * BLK : (group + 1) * BLK] = value.astype(bf16)
-
-        reorder(load, store, step, width, order)
-        hidden.start(sub)
-
-    def load_text(group):
-        return text[:, group * BLK : (group + 1) * BLK].astype(f32)
-
-    def store_text(group, value):
-        text_full[line.at, :, group * BLK : (group + 1) * BLK] = value.astype(bf16)
-
-    folds = text.shape[1] // width
-    text_order = [fold * len(order) + piece for fold in range(folds) for piece in order]
-    reorder(load_text, store_text, text_rows, folds * width, text_order)
-    texts.start(0)
-    for sub in range(SUBS):
-        here = line.part(sub)
-        grad_full[line.at, here] = grad[here]
-        grads.start(sub)
-    places.forward(0)
-    for sub in range(SUBS):
-        hidden.forward(sub)
-    texts.forward(0)
-    for sub in range(SUBS):
-        grads.forward(sub)
-    for blocks in (hidden, texts, grads, places):
-        blocks.finish()
-    for jump in range(1, n_dp):
-        norm_copy(jump).wait_send()
+
+
+def store_shuffled(work, full_ref, line, here, order):
+    rows, width = work.shape
+    folds = width // order.width
+    pieces = len(order.pieces)
+    orders = [fold * pieces + piece for fold in range(folds) for piece in order.pieces]
+
+    def load(group):
+        return work[:, group * BLK : (group + 1) * BLK]
+
+    def store(group, value):
+        full_ref[line.at, here, group * BLK : (group + 1) * BLK] = value.astype(bf16)
+
+    reorder(load, store, rows, width, orders)
+
+
+def leave_kernel(weights, summed, *refs):
+    refs = Refs(refs)
+    n_dp = lax.axis_size("dp")
+    slots_ref = refs.take()
+    row_refs = refs.take(len(weights))
+    term_ref = refs.take() if summed else None
+    out_refs = refs.take(len(weights))
+    sum_ref = refs.take() if summed else None
+    greet_all()
+    if summed:
+        cut, parts, send, recv, total, others, send2, recv2 = refs.take(8)
+        share = cut.shape[2]
+        for index in range(n_dp):
+            cut[index] = term_ref[:, index * share : (index + 1) * share]
+        term_swap = Swap("dp", cut, parts, send, recv)
+        term_swap.start()
+        term_swap.keep()
+    shares = []
+    for row_ref, (split, _, _) in zip(row_refs, weights):
+        if split:
+            held, *sems = refs.take(3)
+            share = Swap("fsdp", row_ref, held, *sems)
+            share.start()
+            share.keep()
+            shares.append(share)
+        else:
+            shares.append(None)
+    if summed:
+        term_swap.wait()
+        total[...] = jnp.sum(parts[...], axis=0)
+        total_spread = Spread("fsdp", total, others, send2, recv2)
+        total_spread.start()
+        others[total_spread.me] = total[...]
+    swaps = []
+    for row_ref, out_ref, share, (split, capacity, first) in zip(
+        row_refs, out_refs, shares, weights
+    ):
+        if split:
+            share.wait()
+        rows = share.target if split else row_ref
+        cut, *sems, blocks = refs.take(4)
+        columns = rows.shape[2] // BLK
+        for part in range(rows.shape[0]):
+            for column in range(columns):
+                blocks[part * columns + column] = rows[part, :, column * BLK : (column + 1) * BLK]
+        swap = Swap("dp", cut, out_ref, *sems)
+        for owner in range(n_dp):
+
+            for position in range(capacity):
+                slot = first + owner * capacity + position
+                value = blocks[slots_ref[0, slot]].astype(f32)
+                live = slots_ref[1, slot].astype(f32)
+                cut[owner, :, position * BLK : (position + 1) * BLK] = (value * live).astype(bf16)
+        swap.start()
+        swap.keep()
+        swaps.append(swap)
+    if summed:
+        total_spread.wait()
+        sum_ref[...] = jnp.sum(others[...], axis=0)
+    for swap in swaps:
+        swap.wait()
+    for one in [*swaps, *shares]:
+        if one is not None:
+            one.finish()
+    if summed:
+        term_swap.finish()
+        total_spread.finish()
 
 
 def fetch_columns(source, index, target, sem):
@@ -479,30 +587,25 @@
         part[:, :, columns] = product.reshape(n, rows, -1)
 
     by_tiles(width, 256, multiply)
-    for time in range(SUBS + 2):
-        if time < SUBS:
-            sums.forward(time)
-        if 0 <= time - 1 < SUBS:
-            sub = time - 1
-            here = line.part(sub)
-            sums.total(sub, work)
-            middle = base_ref[here].astype(f32) + work[...]
-            middle_ref[here] = middle
-            normed, _ = normalize(middle)
-            work[...] = normed * norm_ref[0:1] + norm_ref[1:2]
-
-            def load(group):
-                return work[:, group * BLK : (group + 1) * BLK]
-
-            def store(group, value):
-                full_ref[line.at, here, group * BLK : (group + 1) * BLK] = value.astype(bf16)
-
-            reorder(load, store, step, width, order)
-            blocks.start(sub)
-        if 0 <= time - 2 < SUBS:
-            blocks.forward(time - 2)
-    sums.finish()
-    blocks.finish()
+
+    def settle(sub):
+        here = line.part(sub)
+        sums.total(sub, work)
+        middle = base_ref[here].astype(f32) + work[...]
+        middle_ref[here] = middle
+        normed, _ = normalize(middle)
+        work[...] = normed * norm_ref[0:1] + norm_ref[1:2]
+
+        def load(group):
+            return work[:, group * BLK : (group + 1) * BLK]
+
+        def store(group, value):
+            full_ref[line.at, here, group * BLK : (group + 1) * BLK] = value.astype(bf16)
+
+        reorder(load, store, step, width, order)
+        blocks.start(sub)
+
+    relay(n, [sums], blocks, settle)
     if wide:
         load_next.wait()
 
@@ -526,6 +629,7 @@
     gain_term = jnp.sum(back_hidden * normed, axis=0, keepdims=True)
     bias_term = jnp.sum(back_hidden, axis=0, keepdims=True)
     if first:
+        term_ref[...] = jnp.zeros_like(term_ref)
         term_ref[0:1] = gain_term
         term_ref[1:2] = bias_term
     else:
@@ -557,32 +661,27 @@
         part[:, :, columns] = product.reshape(n, rows, -1)
 
     by_tiles(width, 256, multiply)
-    for time in range(SUBS + 2):
-        if time < SUBS:
-            sums.forward(time)
-        if 0 <= time - 1 < SUBS:
-            sub = time - 1
-            here = line.part(sub)
-            sums.total(sub, work)
-            carry = carry_back(
-                work,
-                plain,
-                order,
-                step,
-                width,
-                middle_ref[here].astype(f32),
-                base_ref[here].astype(f32),
-                norm_ref[0:1],
-                term_ref,
-                sub == 0,
-            )
-            carry_ref[here] = carry
-            full_ref[line.at, here] = carry.astype(bf16)
-            blocks.start(sub)
-        if 0 <= time - 2 < SUBS:
-            blocks.forward(time - 2)
-    sums.finish()
-    blocks.finish()
+
+    def settle(sub):
+        here = line.part(sub)
+        sums.total(sub, work)
+        carry = carry_back(
+            work,
+            plain,
+            order,
+            step,
+            width,
+            middle_ref[here].astype(f32),
+            base_ref[here].astype(f32),
+            norm_ref[0:1],
+            term_ref,
+            sub == 0,
+        )
+        carry_ref[here] = carry
+        full_ref[line.at, here] = carry.astype(bf16)
+        blocks.start(sub)
+
+    relay(n, [sums], blocks, settle)
     load_outs.wait()
 
     def multiply_next(columns):
@@ -610,31 +709,27 @@
         part[:, :, columns] = product.reshape(n, rows, -1)
 
     by_tiles(width, 256, multiply)
-    for time in range(SUBS + 1):
-        if time < SUBS:
-            sums.forward(time)
-            results.forward(time)
-        if 0 <= time - 1 < SUBS:
-            sub = time - 1
-            here = line.part(sub)
-            sums.total(sub, work)
-            carry = carry_back(
-                work,
-                plain,
-                order,
-                step,
-                width,
-                tokens[here].astype(f32),
-                base_ref[here],
-                norm_ref[0:1],
-                term_ref,
-                sub == 0,
-            )
-            grad_ref[here] = carry.astype(bf16)
-            results.total(sub, work)
-            result_ref[here] = (middle[here] + work[...]).astype(bf16)
-    sums.finish()
-    results.finish()
+
+    def settle(sub):
+        here = line.part(sub)
+        sums.total(sub, work)
+        carry = carry_back(
+            work,
+            plain,
+            order,
+            step,
+            width,
+            tokens[here].astype(f32),
+            base_ref[here],
+            norm_ref[0:1],
+            term_ref,
+            sub == 0,
+        )
+        grad_ref[here] = carry.astype(bf16)
+        results.total(sub, work)
+        result_ref[here] = (middle[here] + work[...]).astype(bf16)
+
+    relay(n, [sums, results], None, settle)
 
 
 VMEM_CAP = 52 * 1024 * 1024
@@ -674,28 +769,84 @@
 LINK_COST = 120_000_000
 
 
-def start_call(tokens, text, grad, marks, norms, n, n_dp):
-    rows, width = tokens.shape
-    outs = (
-        shape((n, *tokens.shape), bf16),
-        shape((n, *text.shape), bf16),
-        shape((n, *grad.shape), bf16),
-        shape((n, *marks.shape), jnp.int32),
-        shape((norms.shape[0], width), f32),
-    )
-    scratch = [
-        pltpu.VMEM((n_dp, *norms.shape), f32),
-        pltpu.VMEM((rows // SUBS, width), f32),
-        pltpu.SemaphoreType.DMA((n_dp,)),
-        pltpu.SemaphoreType.DMA((n_dp,)),
-        *sem_pair(n, SUBS),
-        *sem_pair(n, 1),
-        *sem_pair(n, SUBS),
-        *sem_pair(n, 1),
-    ]
-    kernel = functools.partial(start_kernel, n, n_dp, shuffle_order(n, n_dp))
-    call = line_call(kernel, "start", 0, outs, [whole_vmem()] * 5, scratch, 0, LINK_COST)
-    return call(tokens, text, grad, marks, norms)
+class Order:
+    def __init__(self, pieces, width):
+        self.pieces, self.width = pieces, width
+
+
+def swap_sems(n):
+    return [pltpu.SemaphoreType.DMA((n,)), pltpu.SemaphoreType.DMA((n,))]
+
+
+def enter_call(name, ident, slots, weights, gathers, norms, normed, hidden, n, n_dp, width):
+    chunk = weights[0][0].shape[0] // n_dp
+    outs, scratch = [], []
+    for array, places, split, _ in weights:
+        parts = n if split else 1
+        outs.append(shape((parts, chunk, len(places) // parts * BLK), bf16))
+        scratch += [pltpu.VMEM(array.shape, f32), pltpu.SemaphoreType.DMA]
+    if normed:
+        scratch += [pltpu.VMEM((n_dp, *norms.shape), f32), *swap_sems(n_dp)]
+    for array, _ in gathers:
+        rows = array.shape[0]
+        outs.append(shape((n, *array.shape), array.dtype))
+        scratch += sem_pair(n, SUBS if rows >= 16 * SUBS else 1)
+    if normed:
+        outs.append(shape((norms.shape[0], n_dp * norms.shape[1]), f32))
+    for array, _, _, _ in weights:
+        slots_shape = (n_dp, array.shape[1] // BLK, chunk, BLK)
+        scratch += [pltpu.VMEM(slots_shape, bf16)] * 2 + swap_sems(n_dp)
+    rows = gathers[0][0].shape[0]
+    scratch.append(pltpu.VMEM((rows // SUBS if hidden else 8, width), f32))
+    for array, moved in gathers[1 if hidden else 0 :]:
+        if moved:
+            scratch.append(pltpu.VMEM(array.shape, f32))
+    for index, (_, places, split, _) in enumerate(weights):
+        if split:
+            scratch += [pltpu.VMEM(outs[index].shape, bf16), *swap_sems(n)]
+    args = [slots, *(weight[0] for weight in weights), *(gather[0] for gather in gathers)]
+    specs = [pl.BlockSpec(memory_space=pltpu.SMEM)] + [in_place()] * len(weights)
+    specs += [whole_vmem()] * len(gathers)
+    if normed or hidden:
+        args.append(norms)
+        specs.append(whole_vmem())
+    kernel = functools.partial(
+        enter_kernel,
+        [weight[1:] for weight in weights],
+        [gather[1] for gather in gathers],
+        Order(shuffle_order(n, n_dp), width),
+        normed,
+        hidden,
+    )
+    return line_call(kernel, name, ident, outs, specs, scratch, 0, LINK_COST)(*args)
+
+
+def leave_call(name, ident, slots, weights, term, n, n_dp):
+    outs, scratch = [], []
+    specs = [pl.BlockSpec(memory_space=pltpu.SMEM)] + [whole_vmem()] * len(weights)
+    args = [slots, *(weight[0] for weight in weights)]
+    chunk = weights[0][0].shape[1]
+    if term is not None:
+        args.append(term)
+        specs.append(whole_vmem())
+        block = (term.shape[0], term.shape[1] // n_dp)
+        scratch += [pltpu.VMEM((n_dp, *block), f32)] * 2 + swap_sems(n_dp)
+        scratch += [pltpu.VMEM(block, f32), pltpu.VMEM((n, *block), f32), *swap_sems(n)]
+    for rows, split, _, _ in weights:
+        if split:
+            scratch += [pltpu.VMEM(rows.shape, bf16), *swap_sems(n)]
+    for rows, _, capacity, _ in weights:
+        slots_shape = (n_dp, chunk, capacity * BLK)
+        outs.append(shape(slots_shape, bf16))
+        scratch += [pltpu.VMEM(slots_shape, bf16), *swap_sems(n_dp)]
+        blocks = rows.shape[0] * rows.shape[2] // BLK
+        scratch.append(pltpu.VMEM((blocks, chunk, BLK), bf16))
+    if term is not None:
+        outs.append(shape(block, f32))
+    kernel = functools.partial(
+        leave_kernel, [weight[1:] for weight in weights], term is not None
+    )
+    return line_call(kernel, name, ident, outs, specs, scratch, 0, LINK_COST)(*args)
 
 
 def forward_call(attended, outs_z, half, base, norm_rows, after, n, n_dp, ident):
@@ -828,6 +979,47 @@
         key_grad.reshape(keys.shape).astype(bf16),
         value_grad.reshape(values.shape).astype(bf16),
     )
+
+
+def block_slots(owners):
+    owner = jnp.concatenate(owners)
+    weight = jnp.concatenate([jnp.full(one.shape, at, jnp.int32) for at, one in enumerate(owners)])
+    mark = owner + weight * 1024
+    count = mark.shape[0]
+    earlier = lax.broadcasted_iota(jnp.int32, (count, count), 1) < lax.broadcasted_iota(
+        jnp.int32, (count, count), 0
+    )
+    same = jnp.logical_and(mark[:, None] == mark[None, :], earlier)
+    return jnp.stack([owner, jnp.sum(same.astype(jnp.int32), axis=1)])
+
+
+def slot_contents(owners, slots, places, capacities, firsts, n_dp):
+    rows = []
+    for owner, place, capacity, first in zip(owners, places, capacities, firsts):
+        count = owner.shape[0]
+        at = owner * capacity + slots[1, first : first + count]
+        hit = at[None, :] == lax.broadcasted_iota(jnp.int32, (n_dp * capacity, count), 0)
+        block = lax.broadcasted_iota(jnp.int32, (n_dp * capacity, count), 1)
+        per_group, per_part, split = place_rule(place)
+        part = block % per_group // per_part if split else block * 0
+        column = block // per_group * per_part + block % per_part if split else block
+        index = part * (count // (per_group // per_part)) + column if split else column
+        rows.append(
+            jnp.stack([jnp.sum(jnp.where(hit, value, 0), axis=1) for value in (index, block * 0 + 1)])
+        )
+    return jnp.concatenate(rows, axis=1)
+
+
+def place_rule(place):
+    parts = 1 + max(part for part, _ in place)
+    if parts == 1:
+        return 0, 0, False
+    per_part = sum(1 for part, _ in place[:HEADS] if part == 0)
+    return per_part * parts, per_part, True
+
+
+def after(small, first):
+    return lax.optimization_barrier((small, first))[0]
 
 
 def body(
@@ -875,42 +1067,54 @@
     split_places = [split_place(b, heads_z, n_z) for b in range(owner_query.shape[0])]
     big_places = [flat_place(b) for b in range(owner_down.shape[0])]
     out_places = [flat_place(b) for b in range(owner_outs.shape[0])]
-
-    def fetch(weight, owner, places, parts):
-        slots = swap(weight.astype(bf16), "dp").reshape(n_dp, chunk, -1)
-        rows = compact(slots, owner, places, parts)
-        if parts > 1:
-            rows = swap(rows, "fsdp")
-        rows = rows.reshape(parts * chunk, -1)
-        return lax.all_gather(rows, "dp", axis=0, tiled=True)
-
-    def settle(pieces, owner, places, parts, capacity):
-        summed = [
-            lax.psum_scatter(piece, "dp", scatter_dimension=0, tiled=True) for piece in pieces
-        ]
-        summed = summed[0] if len(summed) == 1 else jnp.concatenate(summed, axis=1)
-        rows = summed.reshape(parts, chunk, -1)
-        if parts > 1:
-            rows = swap(rows, "fsdp")
-        slots = expand(rows, owner, places, n_dp, capacity)
-        return swap(slots, "dp").reshape(n_dp * chunk, -1).astype(f32)
-
-    query_z = fetch(w_query, owner_query, split_places, n_z)
-    outs_z = fetch(w_outs, owner_outs, out_places, 1)
-    text_z = fetch(w_text, owner_text, split_places, n_z)
-    up_z = fetch(w_up, owner_up, split_places, n_z)
-    down_z = fetch(w_down, owner_down, big_places, 1)
+    owners = (owner_query, owner_outs, owner_text, owner_up, owner_down)
+    places = (split_places, out_places, split_places, split_places, big_places)
+    capacities = (cap_big, cap_out, cap_big, cap_big, cap_big)
+    firsts = [sum(len(one) for one in places[:index]) for index in range(5)]
+    slot_firsts = [sum(capacities[:index]) * n_dp for index in range(5)]
+    slots = block_slots(owners)
+    contents = slot_contents(owners, slots, places, capacities, firsts, n_dp)
+
+    def spread(rows):
+        return lax.all_gather(rows.reshape(-1, rows.shape[-1]), "dp", axis=0, tiled=True)
+
+    def gather_sum(piece, parts):
+        summed = lax.psum_scatter(piece, "dp", scatter_dimension=0, tiled=True)
+        return summed.reshape(parts, chunk, -1)
 
     token_count = tokens_in.shape[0]
     marks = jnp.concatenate([seg_ids, capt_ids], axis=1)
     marks = jnp.pad(marks, ((0, 7), (0, 256 - marks.shape[1])))
     norms = jnp.pad(norm_weight, ((0, 2), (0, 0)))
-    hidden1, text_all, grad_all, marks, norm_full = start_call(
-        tokens_in, text_in, grad_out, marks, norms, n_z, n_dp
-    )
-    hidden1, text_all, grad_all = (
-        values.reshape(-1, values.shape[-1]) for values in (hidden1, text_all, grad_all)
-    )
+    query_rows, marks, norm_full = enter_call(
+        "enter_query",
+        0,
+        slots,
+        [(w_query, split_places, True, firsts[0])],
+        [(marks, False)],
+        norms,
+        True,
+        False,
+        n_z,
+        n_dp,
+        width,
+    )
+    outs_rows, text_rows, hidden1, text_all = enter_call(
+        "enter_text",
+        6,
+        slots,
+        [(w_outs, out_places, False, firsts[1]), (w_text, split_places, True, firsts[2])],
+        [(tokens_in, True), (text_in, True)],
+        norm_full[0:2],
+        False,
+        True,
+        n_z,
+        n_dp,
+        width,
+    )
+    query_z, outs_z, text_z = spread(query_rows), spread(outs_rows), spread(text_rows)
+    hidden1 = hidden1.reshape(-1, width)
+    text_all = text_all.reshape(-1, text_in.shape[1])
     segment = marks[:, 0, :token_count]
     caption = marks[:, 0, token_count : token_count + capt_ids.shape[1]]
     self_mask = segment[:, :, None] == segment[:, None, :]
@@ -921,8 +1125,23 @@
     self_key = projected[:, share : 2 * share]
     self_value = projected[:, 2 * share :]
     attended1, shares1 = attend_forward(self_query, self_key, self_value, self_mask)
+    up_rows, down_rows, grad_all = enter_call(
+        "enter_up",
+        7,
+        after(slots, attended1),
+        [(w_up, split_places, True, firsts[3]), (w_down, big_places, False, firsts[4])],
+        [(grad_out, False)],
+        None,
+        False,
+        False,
+        n_z,
+        n_dp,
+        width,
+    )
+    grad_all = grad_all.reshape(-1, width)
+    up_z, down_z = spread(up_rows), spread(down_rows)
     middle1, hidden2, cross_query = forward_call(
-        attended1, outs_z, 0, tokens_in, norm_full[2:4], query_z, n_z, n_dp, 1
+        attended1, outs_z, 0, tokens_in, after(norm_full[2:4], up_rows), query_z, n_z, n_dp, 1
     )
     hidden2 = hidden2.reshape(-1, width)
     text_pairs = (
@@ -949,13 +1168,13 @@
         [dot_tn(activated[:, f * share : (f + 1) * share], grad_all).astype(bf16) for f in range(4)],
         axis=1,
     )
-    down_grad = settle([down_part], owner_down, big_places, 1, cap_big)
+    down_sum = gather_sum(down_part, 1)
     back_act = jnp.concatenate(
         [dot_nt(grad_all, down_z[:, f * width : (f + 1) * width]) for f in range(4)], axis=1
     )
     back_up = gelu_pull(back_act)[0].astype(bf16)
     up_part = dot_tn(hidden3, back_up).astype(bf16)
-    up_grad = settle([up_part], owner_up, split_places, n_z, cap_big)
+    up_sum = gather_sum(up_part, n_z)
     at_middle2, carry2, back_att2, term3 = back_call(
         back_up, up_z, 0, grad_out, middle2, norm_full[4:6], outs_z, 1, n_z, n_dp, 3
     )
@@ -969,36 +1188,61 @@
         [dot_tn(text_all[:, f * width : (f + 1) * width], back_pairs).astype(bf16) for f in range(2)],
         axis=1,
     )
-    text_grad = settle([text_part], owner_text, split_places, n_z, cap_big)
+    text_sum = gather_sum(text_part, n_z)
     query_part2 = dot_tn(hidden2, back_cross).astype(bf16)
     at_middle1, carry1, back_att1, term2 = back_call(
         back_cross, query_z, 3, at_middle2, middle1, norm_full[2:4], outs_z, 0, n_z, n_dp, 4
     )
     carry1 = carry1.reshape(-1, width)
     outs_part1 = dot_tn(attended1, carry1).astype(bf16)
-    outs_grad = settle([outs_part1, outs_part2], owner_outs, out_places, 1, cap_out)
+    outs_sum = gather_sum(jnp.concatenate([outs_part1, outs_part2], axis=1), 1)
     back_projected = jnp.concatenate(
         attend_backward(self_query, self_key, self_value, shares1, back_att1), axis=1
     )
     query_part1 = dot_tn(hidden1, back_projected).astype(bf16)
-    query_grad = settle([query_part1, query_part2], owner_query, split_places, n_z, cap_big)
+    query_sum = gather_sum(jnp.concatenate([query_part1, query_part2], axis=1), n_z)
+    text_grad, up_grad, down_grad = leave_call(
+        "leave_up",
+        8,
+        after(contents, back_projected),
+        [
+            (text_sum, True, cap_big, slot_firsts[2]),
+            (up_sum, True, cap_big, slot_firsts[3]),
+            (down_sum, False, cap_big, slot_firsts[4]),
+        ],
+        None,
+        n_z,
+        n_dp,
+    )
     grad_in, result, term1 = last_call(
         back_projected,
         query_z,
         at_middle1,
         tokens_in,
-        norm_full[0:2],
+        after(norm_full[0:2], text_grad),
         branch3,
         middle2,
         n_z,
         n_dp,
         5,
     )
-    norm_term = jnp.concatenate([term1[:2], term2[:2], term3[:2]], axis=0)
-    norm_total = lax.psum(norm_term, ("dp", "fsdp"))
-    norm_share = width // n_dp
-    norm_grad = lax.dynamic_slice_in_dim(
-        norm_total, lax.axis_index("dp") * norm_share, norm_share, 1
+    norm_term = jnp.concatenate([term1[:2], term2[:2], term3[:4]], axis=0)
+    query_grad, outs_grad, norm_grad = leave_call(
+        "leave_query",
+        9,
+        contents,
+        [
+            (query_sum, True, cap_big, slot_firsts[0]),
+            (outs_sum, False, cap_out, slot_firsts[1]),
+        ],
+        norm_term,
+        n_z,
+        n_dp,
+    )
+    norm_grad = norm_grad[:6]
+    query_grad, outs_grad, text_grad, up_grad, down_grad = (
+        grad.reshape(own_rows, -1).astype(f32)
+        for grad in (query_grad, outs_grad, text_grad, up_grad, down_grad)
     )
     query_new = adamw_update(w_query, m_query, v_query, query_grad, rate_query, decay_rate)
     up_new = adamw_update(w_up, m_up, v_up, up_grad, rate_up, decay_rate)

time: 1660 us -> 1130 us (0.68)
  blocking collectives: 335 us -> 0 us
  waiting for transfers between devices: 394 us -> 64.1 us
  Pallas kernels: 671 us -> 820 us
  starting transfers between devices: 30.3 us -> 0.98 us
    pallas_call x11 -> x5, Pallas kernels: 137 us -> 435 us  [the longest x3 245 us: enter_call(): line_call(kernel, name, ident, outs, specs, scratch, 0, LINK_COST)(*args)]
    all_to_all x9 -> x0, blocking collectives: 295 us -> none  [swap(): return lax.all_to_all(values, axis, 0, 0, tiled=True)]
    reduce_scatter x7 -> x5, waiting for transfers between devices: 313 us -> 62.7 us  [gather_sum(): summed = lax.psum_scatter(piece, 'dp', scatter_dimension=0, tiled=True)]
    pallas_call x2, Pallas kernels: 224 us -> 155 us  [back_call(): return call(dy, weight, base, middle, norm_rows, outs_z)]
    pallas_call x2, Pallas kernels: 211 us -> 148 us  [forward_call(): return call(*args)]
    all_gather x5, waiting for transfers between devices: 53.6 us -> 0.07 us  [spread(): lax.all_gather(rows.reshape(-1, rows.shape[-1]), 'dp', axis=0, tiled=True)]
    psum x1 -> x0, blocking collectives: 39.3 us -> none  [body(): norm_total = lax.psum(norm_term, ('dp', 'fsdp'))]
    all_to_all x7 -> x0, starting transfers between devices: 29.7 us -> none  [swap(): return lax.all_to_all(values, axis, 0, 0, tiled=True)]
  transfers between devices with their start and end apart: 19 -> 10, of which waited for: 10 -> 1; matrix products, arithmetic and copies ran while one was open for 8% -> 11% of each run, Pallas kernels for 33% -> 56%
where the time goes in v3:
time: 1130 us; the launch traced here: 1120 us
  Pallas kernels  820 us (73%)
  matrix products  106 us (9%)
  other arithmetic  68.7 us (6%)
  waiting for transfers between devices  64.1 us (6%)
  local copies, waits for them, and re-layouts  40.6 us (4%)
  between operations  15.5 us (1%)
    pallas_call x3, Pallas kernels, enter_call(): line_call(kernel, name, ident, outs, specs, scratch, 0, LINK_COST)(*args)  245 us
    pallas_call x2, Pallas kernels, leave_call(): line_call(kernel, name, ident, outs, specs, scratch, 0, LINK_COST)(*args)  190 us
    pallas_call x2, Pallas kernels, back_call(): return call(dy, weight, base, middle, norm_rows, outs_z)  155 us
    pallas_call x2, Pallas kernels, forward_call(): return call(*args)  148 us
    pallas_call x1, Pallas kernels, last_call(): return call(dy, weight, base, tokens, norm_rows, branch, middle)  83.2 us
    reduce_scatter x5, waiting for transfers between devices, gather_sum(): summed = lax.psum_scatter(piece, 'dp', scatter_dimension=0, tiled=True)  62.7 us
    dot_general x8, matrix products, dot(): return jnp.dot(left, right, preferred_element_type=f32)  44.3 us
    sub x6, other arithmetic, adamw_update(): weight - rate * (first_hat / (jnp.sqrt(second_hat) + adam_eps) + decay *...  38.2 us
  transfers between devices with their start and end apart: 10, of which 1 were waited for; matrix products, arithmetic and copies ran while one was open for 11% of the time, Pallas kernels for 56%

profile of v3, /device:TPU:0, one launch (start us, length us, event | category | flops | bytes accessed | tf_op | source)
XLA Modules:
  0.0 1115.9 jit_solution(2385920080296515263)
XLA Ops:
  11.0 54.3 %enter_query.1 = (bf16[4,64,2048]{2,1,0:T(8,128)(2,1)}, s32[4,8,256]{2,1,0:T(8,128)S(1)}, f32[8,2048]{1,0:T(8,128)S(1)}) custom-call(s32[2,288]{1,0:T(2,128)S(1)} %pad_add_fusion.refs_0_, f32[512,2048]{1,0:T(8,128)} %refs_1_.3, s32[8,256]{1,0:T(8,128)S(1)} %pad.8.refs_2_, f32[8,256]{1,0:T(8,128)S(1)} %pad.9.refs_3_), custom_call_target="tpu_custom_call" | custom-call | bytes 120000000 | tf_op jit(solution)/shard_map/enter_query/pallas_call | solution.py:821
  65.4 106.9 %enter_text.1 = (bf16[1,64,4096]{2,1,0:T(8,128)(2,1)}, bf16[4,64,2048]{2,1,0:T(8,128)(2,1)}, bf16[4,128,2048]{2,1,0:T(8,128)(2,1)}, bf16[4,32,4096]{2,1,0:T(8,128)(2,1)}) custom-call(s32[2,288]{1,0:T(2,128)S(1)} %pad_add_fusion.refs_0_, f32[512,1024]{1,0:T(8,128)} %refs_1_.4, f32[512,2048]{1,0:T(8,128)} %refs_2_.2, bf16[128,2048]{1,0:T(8,128)(2,1)S(1)} %copy-done, ...), custom_call_target="tpu_custom_call" | custom-call | bytes 120000000 | tf_op jit(solution)/shard_map/enter_text/pallas_call | solution.py:821
  173.3 6.8 fusion.22
  191.1 83.6 %enter_up.1 = (bf16[4,64,2048]{2,1,0:T(8,128)(2,1)}, bf16[1,64,8192]{2,1,0:T(8,128)(2,1)}, bf16[4,128,2048]{2,1,0:T(8,128)(2,1)}) custom-call(s32[2,288]{1,0:T(2,128)S(1)} %pad_add_fusion.refs_0_, f32[512,2048]{1,0:T(8,128)} %refs_1_.5, f32[512,2048]{1,0:T(8,128)} %refs_2_.3, bf16[128,2048]{1,0:T(8,128)(2,1)S(1)} %copy-done.2), custom_call_target="tpu_custom_call" | custom-call | bytes 120000000 | tf_op jit(solution)/shard_map/enter_up/pallas_call | solution.py:821
  275.5 72.0 %forward0.1 = (f32[128,2048]{1,0:T(8,128)}, bf16[4,128,2048]{2,1,0:T(8,128)(2,1)}, bf16[512,512]{1,0:T(8,128)(2,1)S(1)}) custom-call(bf16[512,512]{1,0:T(8,128)(2,1)S(1)} %bitcast.178, bf16[512,4096]{1,0:T(8,128)(2,1)} %bitcast.180, bf16[128,2048]{1,0:T(8,128)(2,1)S(1)} %copy-done, f32[2,2048]{1,0:T(2,128)S(1)} %get-tuple-element.65.norm_ref, ...), custom_call_target="tpu_custom_call" | custom-call | bytes 120000000 | tf_op jit(solution)/shard_map/forward0/pallas_call | solution.py:874
  357.1 76.0 %forward1.1 = (f32[128,2048]{1,0:T(8,128)S(1)}, bf16[4,128,2048]{2,1,0:T(8,128)(2,1)}) custom-call(bf16[512,512]{1,0:T(8,128)(2,1)S(1)} %bitcast.177, bf16[512,4096]{1,0:T(8,128)(2,1)} %bitcast.181, f32[128,2048]{1,0:T(8,128)} %get-tuple-element.67.base_ref.middle_ref, f32[2,2048]{1,0:T(2,128)S(1)} %get-tuple-element.127.norm_ref), custom_call_target="tpu_custom_call" | custom-call | bytes 120000000 | tf_op jit(solution)/shard_map/forward1/pallas_call | solution.py:874
  434.1 4.6 fusion.28
  446.5 17.6 %multiply_convert_fusion = (bf16[512,2048]{1,0:T(8,128)(2,1)}, f32[512,2048]{1,0:T(8,128)S(1)}, f32[512,2048]{1,0:T(8,128)S(1)}) fusion(bf16[512,2048]{1,0:T(8,128)(2,1)} %bitcast.242, bf16[2048,2048]{1,0:T(8,128)(2,1)} %all-gather.12.cloned.1.call-done.w_hbm), kind=kOutput, calls=%fused_computation.42 | convolution fusion | flops 4363124736 | bytes 20971520 | tf_op jit(solution)/shard_map/dot_general | solution.py:61
  466.8 80.8 %back1.1 = (f32[128,2048]{1,0:T(8,128)}, bf16[4,128,2048]{2,1,0:T(8,128)(2,1)}, bf16[512,512]{1,0:T(8,128)(2,1)S(1)}, f32[8,2048]{1,0:T(8,128)S(1)}) custom-call(bf16[512,2048]{1,0:T(8,128)(2,1)} %add_convert_fusion.1.dy_ref, bf16[2048,2048]{1,0:T(8,128)(2,1)} %all-gather.12.cloned.1.call-done.w_hbm, bf16[128,2048]{1,0:T(8,128)(2,1)S(1)} %copy-done.2, ...), custom_call_target="tpu_custom_call" | custom-call | bytes 120000000 | tf_op jit(solution)/shard_map/back1/pallas_call | solution.py:908
  550.0 4.4 convolution_convert_fusion.2
  557.8 8.4 pad_maximum_fusion
  567.7 8.7 convolution_convert_fusion.1
  591.6 73.9 %back0.1 = (f32[128,2048]{1,0:T(8,128)}, bf16[4,128,2048]{2,1,0:T(8,128)(2,1)}, bf16[512,512]{1,0:T(8,128)(2,1)S(1)}, f32[8,2048]{1,0:T(8,128)S(1)}) custom-call(bf16[512,512]{1,0:T(8,128)(2,1)S(1)} %bitcast.176, bf16[2048,2048]{1,0:T(8,128)(2,1)} %all-gather.8.cloned.1.call-done.rest_0_.w_hbm, f32[128,2048]{1,0:T(8,128)} %get-tuple-element.73.base_ref, ...), custom_call_target="tpu_custom_call" | custom-call | bytes 120000000 | tf_op jit(solution)/shard_map/back0/pallas_call | solution.py:908
  680.7 4.8 convolution_convert_fusion.6
  685.5 5.4 convolution_convert_fusion
  690.9 8.5 pad_maximum_fusion.2
  723.7 62.7 %reduce-scatter.10.cloned.1.call-done = bf16[64,8192]{1,0:T(8,128)(2,1)} async-done(((bf16[512,8192]{1,0:T(8,128)(2,1)}), bf16[64,8192]{1,0:T(8,128)(2,1)}) %reduce-scatter.10.cloned.1.call-update) | async-done | bytes 1048592 | tf_op jit(solution)/shard_map/reduce_scatter | solution.py:1082
  786.4 128.3 %leave_up.1 = (bf16[8,64,2048]{2,1,0:T(8,128)(2,1)}, bf16[8,64,2048]{2,1,0:T(8,128)(2,1)}, bf16[8,64,2048]{2,1,0:T(8,128)(2,1)}) custom-call(s32[2,576]{1,0:T(2,128)S(1)} %concatenate.45.refs_0_, bf16[4,64,2048]{2,1,0:T(8,128)(2,1)S(1)} %bitcast.175, bf16[4,64,2048]{2,1,0:T(8,128)(2,1)} %bitcast.207, bf16[1,64,8192]{2,1,0:T(8,128)(2,1)} %bitcast.208), custom_call_target="tpu_custom_call" | custom-call | bytes 120000000 | tf_op jit(solution)/shard_map/leave_up/pallas_call | solution.py:849
  914.7 83.2 %last.1 = (bf16[128,2048]{1,0:T(8,128)(2,1)S(1)}, bf16[128,2048]{1,0:T(8,128)(2,1)S(1)}, f32[8,2048]{1,0:T(8,128)S(1)}) custom-call(bf16[512,1536]{1,0:T(8,128)(2,1)} %copy-done.21, bf16[2048,2048]{1,0:T(8,128)(2,1)} %all-gather.8.cloned.1.call-done.rest_0_.w_hbm, f32[128,2048]{1,0:T(8,128)} %get-tuple-element.75.base_ref, bf16[128,2048]{1,0:T(8,128)(2,1)S(1)} %copy-done, ...), custom_call_target="tpu_custom_call" | custom-call | bytes 120000000 | tf_op jit(solution)/shard_map/last/pallas_call | solution.py:932
  1000.5 10.0 multiply_subtract_fusion.1
  1011.5 61.5 %leave_query.1 = (bf16[8,64,2048]{2,1,0:T(8,128)(2,1)}, bf16[8,64,1024]{2,1,0:T(8,128)(2,1)S(1)}, f32[8,256]{1,0:T(8,128)S(1)}) custom-call(s32[2,576]{1,0:T(2,128)S(1)} %concatenate.45.refs_0_, bf16[4,64,2048]{2,1,0:T(8,128)(2,1)} %bitcast.193, bf16[1,64,4096]{2,1,0:T(8,128)(2,1)S(1)} %bitcast.179, f32[8,2048]{1,0:T(8,128)S(1)} %pad_maximum_fusion.5.refs_3_), custom_call_target="tpu_custom_call" | custom-call | bytes 120000000 | tf_op jit(solution)/shard_map/leave_query/pallas_call | solution.py:849
  1073.0 10.3 multiply_subtract_fusion.3
  1086.3 7.2 multiply_subtract_fusion.2
  1100.5 6.0 multiply_subtract_fusion
  (242 shorter events, 114.6 us)
Async XLA Ops:
  7.2 58.2 %copy-start = (bf16[128,2048]{1,0:T(8,128)(2,1)S(1)}, bf16[128,2048]{1,0:T(8,128)(2,1)}, u32[]{:S(2)}) copy-start(bf16[128,2048]{1,0:T(8,128)(2,1)} %tokens.1) | copy-start | bytes 1572868
  7.2 58.2 %copy-start.4 = (bf16[32,4096]{1,0:T(8,128)(2,1)S(1)}, bf16[32,4096]{1,0:T(8,128)(2,1)}, u32[]{:S(2)}) copy-start(bf16[32,4096]{1,0:T(8,128)(2,1)} %refs_4_.1) | copy-start | bytes 786436
  7.2 166.1 %all-gather.8.cloned.1.call-start = ((), (), s32[]{:S(2)}) async-start(), calls=%async_computation.5 | async-start | bytes 9437184 | tf_op jit(solution)/shard_map/all_gather | solution.py:1079
  65.3 210.2 %all-gather.14.cloned.1.call-start = ((), (), s32[]{:S(2)}) async-start(), calls=%async_computation.13 | async-start | bytes 4718592 | tf_op jit(solution)/shard_map/all_gather | solution.py:1079
  65.4 106.9 %copy-start.5 = (f32[2,2048]{1,0:T(2,128)}, f32[2,2048]{1,0:T(2,128)S(1)}, u32[]{:S(2)}) copy-start(f32[2,2048]{1,0:T(2,128)S(1)} %get-tuple-element.78.refs_5_.norm_ref) | copy-start | bytes 49156
  172.3 175.3 %all-gather.10.cloned.1.call-start = ((), (), s32[]{:S(2)}) async-start(), calls=%async_computation.6 | async-start | bytes 9437184 | tf_op jit(solution)/shard_map/all_gather | solution.py:1079
  173.1 261.0 %all-gather.16.cloned.1.call-start = ((), (), s32[]{:S(2)}) async-start(), calls=%async_computation.14 | async-start | bytes 9437184 | tf_op jit(solution)/shard_map/all_gather | solution.py:1079
  274.7 171.8 %all-gather.12.cloned.1.call-start = ((), (), s32[]{:S(2)}) async-start(), calls=%async_computation.7 | async-start | bytes 9437184 | tf_op jit(solution)/shard_map/all_gather | solution.py:1079
  275.3 446.7 %reduce-scatter.6.cloned.1.call-start = ((), (), s32[]{:S(2)}) async-start(), calls=%async_computation.8 | async-start | bytes 9437184 | tf_op jit(solution)/shard_map/reduce_scatter | solution.py:1082
  357.0 81.7 %copy-start.23 = (bf16[4,128,4,128]{3,2,1,0:T(4,128)(2,1)}, bf16[4,128,4,128]{3,2,1,0:T(4,128)(2,1)S(1)}, u32[]{:S(2)}) copy-start(bf16[4,128,4,128]{3,2,1,0:T(4,128)(2,1)S(1)} %copy.128) | copy-start | bytes 1572868
  446.5 17.6 %copy-start.34 = (f32[512,512]{1,0:T(8,128)S(1)}, f32[512,512]{1,0:T(8,128)}, u32[]{:S(2)}) copy-start(f32[512,512]{1,0:T(8,128)} %fusion.28) | copy-start | bytes 3145732
  446.5 17.6 %copy-start.35 = (f32[512,512]{1,0:T(8,128)S(1)}, f32[512,512]{1,0:T(8,128)}, u32[]{:S(2)}) copy-start(f32[512,512]{1,0:T(8,128)} %fusion.32) | copy-start | bytes 3145732
  446.5 17.6 %copy-start.36 = (f32[512,512]{1,0:T(8,128)S(1)}, f32[512,512]{1,0:T(8,128)}, u32[]{:S(2)}) copy-start(f32[512,512]{1,0:T(8,128)} %fusion.36) | copy-start | bytes 3145732
  446.5 17.6 %copy-start.37 = (f32[512,512]{1,0:T(8,128)S(1)}, f32[512,512]{1,0:T(8,128)}, u32[]{:S(2)}) copy-start(f32[512,512]{1,0:T(8,128)} %fusion.40) | copy-start | bytes 3145732
  566.2 157.5 %reduce-scatter.8.cloned.1.call-start = ((), (), s32[]{:S(2)}) async-start(), calls=%async_computation.9 | async-start | bytes 9437184 | tf_op jit(solution)/shard_map/reduce_scatter | solution.py:1082
  576.4 209.9 %reduce-scatter.10.cloned.1.call-start = ((), (), s32[]{:S(2)}) async-start(), calls=%async_computation.10 | async-start | bytes 9437184 | tf_op jit(solution)/shard_map/reduce_scatter | solution.py:1082
  589.5 408.4 %reduce-scatter.12.cloned.1.call-start = ((), (), s32[]{:S(2)}) async-start(), calls=%async_computation.11 | async-start | bytes 9437184 | tf_op jit(solution)/shard_map/reduce_scatter | solution.py:1082
  591.6 76.8 %copy-start.15 = (f32[4,4,128,128]{2,3,1,0:T(8,128)S(1)}, f32[4,4,128,128]{2,3,1,0:T(8,128)}, u32[]{:S(2)}) copy-start(f32[4,4,128,128]{2,3,1,0:T(8,128)} %get-tuple-element.135) | copy-start | bytes 3145732
  699.4 311.0 %reduce-scatter.14.cloned.1.call-start = ((), (), s32[]{:S(2)}) async-start(), calls=%async_computation.12 | async-start | bytes 4718592 | tf_op jit(solution)/shard_map/reduce_scatter | solution.py:1082
  722.0 192.7 %copy-start.6 = (f32[2,2048]{1,0:T(2,128)S(1)}, f32[2,2048]{1,0:T(2,128)}, u32[]{:S(2)}) copy-start(f32[2,2048]{1,0:T(2,128)} %copy-done.5) | copy-start | bytes 49156
  1073.0 10.4 copy-start.7
  1073.0 12.1 %copy-start.16 = (f32[512,2048]{1,0:T(8,128)S(1)}, f32[512,2048]{1,0:T(8,128)}, u32[]{:S(2)}) copy-start(f32[512,2048]{1,0:T(8,128)} %param.43) | copy-start | bytes 12582916
  1073.0 13.3 %copy-start.17 = (f32[512,2048]{1,0:T(8,128)S(1)}, f32[512,2048]{1,0:T(8,128)}, u32[]{:S(2)}) copy-start(f32[512,2048]{1,0:T(8,128)} %param.42) | copy-start | bytes 12582916
  1086.3 11.4 %copy-start.33 = (bf16[8,64,2048]{2,1,0:T(8,128)(2,1)S(1)}, bf16[8,64,2048]{2,1,0:T(8,128)(2,1)}, u32[]{:S(2)}) copy-start(bf16[8,64,2048]{2,1,0:T(8,128)(2,1)} %get-tuple-element.90) | copy-start | bytes 6291460
  (39 other events, 142.5 us)
Sparse Core Ops, SparseCore 0:
  65.4 75.1 all-gather.7
  172.4 54.9 all-gather.13
  229.3 64.9 all-gather.9
  296.1 54.3 all-gather.15
  352.2 54.4 all-gather.11
  566.3 70.1 reduce-scatter.5
  640.3 71.2 reduce-scatter.7
  715.1 71.2 reduce-scatter.9
  790.2 124.6 reduce-scatter.11
  918.7 53.6 reduce-scatter.13

commit v4 on v3

--- a/solution.py
+++ b/solution.py
@@ -42,10 +42,6 @@
         - jnp.mean(back_normed, axis=-1, keepdims=True)
         - normed * jnp.mean(back_normed * normed, axis=-1, keepdims=True)
     )
-
-
-def exact_gelu(values):
-    return jax.nn.gelu(values, approximate=False)
 
 
 def adamw_update(weight, first, second, gradient, rate, decay):
@@ -932,53 +928,332 @@
     return call(dy, weight, base, tokens, norm_rows, branch, middle)
 
 
-def attend_forward(queries, keys, values, allowed):
-    packed = allowed.shape[0]
-    heads = queries.shape[1] // HEAD
-    query_heads = queries.reshape(packed, -1, heads, HEAD)
-    key_heads = keys.reshape(packed, -1, heads, HEAD)
-    value_heads = values.reshape(packed, -1, heads, HEAD)
-    scores = jnp.einsum(
-        "pqhd,pkhd->phqk", query_heads, key_heads, preferred_element_type=f32
-    ) * HEAD ** (-0.5)
-    scores = jnp.where(allowed[:, None], scores, score_floor)
-    powers = jnp.exp(scores - jnp.max(scores, axis=-1, keepdims=True))
-    shares = powers / jnp.sum(powers, axis=-1, keepdims=True)
-    attended = jnp.einsum(
-        "phqk,pkhd->pqhd", shares.astype(bf16), value_heads, preferred_element_type=f32
-    )
-    return attended.reshape(queries.shape).astype(bf16), shares
-
-
-def attend_backward(queries, keys, values, shares, back_attended):
-    packed = shares.shape[0]
-    heads = queries.shape[1] // HEAD
-    query_heads = queries.reshape(packed, -1, heads, HEAD)
-    key_heads = keys.reshape(packed, -1, heads, HEAD)
-    value_heads = values.reshape(packed, -1, heads, HEAD)
-    back_heads = back_attended.reshape(packed, -1, heads, HEAD)
+def attend_forward(query, keys, values, mask_ref, keyed, att_ref, share_ref):
+    packed, rows, _ = mask_ref.shape
+    heads = att_ref.shape[1] // HEAD
+    for p in range(packed):
+        here = slice(p * rows, (p + 1) * rows)
+        there = here if keyed else slice(None)
+        for h in range(heads):
+            columns = slice(h * HEAD, (h + 1) * HEAD)
+            scores = dot_nt(query[here, columns], keys[there, columns]) * HEAD ** (-0.5)
+            scores = jnp.where(mask_ref[p] > 0, scores, score_floor)
+            powers = jnp.exp(scores - jnp.max(scores, axis=-1, keepdims=True))
+            shares = powers / jnp.sum(powers, axis=-1, keepdims=True)
+            share_ref[p * heads + h] = shares
+            att_ref[here, columns] = dot(shares.astype(bf16), values[there, columns]).astype(bf16)
+
+
+def attend_backward(query, keys, values, share_ref, back_ref, rows, keyed, put_query, put_pair):
+    heads = back_ref.shape[1] // HEAD
+    packed = back_ref.shape[0] // rows
     score_scale = HEAD ** (-0.5)
-    back_shares = jnp.einsum(
-        "pqhd,pkhd->phqk", back_heads, value_heads, preferred_element_type=f32
-    )
-    inner_sum = jnp.sum(shares * back_shares, axis=-1, keepdims=True)
-    back_scores = (shares * (back_shares - inner_sum)).astype(bf16)
-    query_grad = (
-        jnp.einsum("phqk,pkhd->pqhd", back_scores, key_heads, preferred_element_type=f32)
-        * score_scale
-    )
-    key_grad = (
-        jnp.einsum("phqk,pqhd->pkhd", back_scores, query_heads, preferred_element_type=f32)
-        * score_scale
-    )
-    value_grad = jnp.einsum(
-        "phqk,pqhd->pkhd", shares.astype(bf16), back_heads, preferred_element_type=f32
-    )
-    return (
-        query_grad.reshape(queries.shape).astype(bf16),
-        key_grad.reshape(keys.shape).astype(bf16),
-        value_grad.reshape(values.shape).astype(bf16),
-    )
+    for h in range(heads):
+        columns = slice(h * HEAD, (h + 1) * HEAD)
+        key_grad = value_grad = None
+        for p in range(packed):
+            here = slice(p * rows, (p + 1) * rows)
+            there = here if keyed else slice(None)
+            shares = share_ref[p * heads + h]
+            back = back_ref[here, columns]
+            back_shares = dot_nt(back, values[there, columns])
+            inner_sum = jnp.sum(shares * back_shares, axis=-1, keepdims=True)
+            back_scores = (shares * (back_shares - inner_sum)).astype(bf16)
+            put_query(here, columns, dot(back_scores, keys[there, columns]) * score_scale)
+            key_term = dot_tn(back_scores, query[here, columns]) * score_scale
+            value_term = dot_tn(shares.astype(bf16), back)
+            if keyed:
+                put_pair(there, columns, key_term, value_term)
+            else:
+                key_grad = key_term if key_grad is None else key_grad + key_term
+                value_grad = value_term if value_grad is None else value_grad + value_term
+        if not keyed:
+            put_pair(slice(None), columns, key_grad, value_grad)
+
+
+def self_forward_kernel(h_ref, w_ref, mask_ref, proj_ref, att_ref, share_ref):
+    tile = pl.program_id(0)
+    proj_ref[tile] = dot(h_ref[...], w_ref[...]).astype(bf16)
+
+    @pl.when(tile == 2)
+    def _():
+        attend_forward(
+            proj_ref.at[0], proj_ref.at[1], proj_ref.at[2], mask_ref, True, att_ref, share_ref
+        )
+
+
+def cross_forward_kernel(cq_ref, text_ref, w_ref, mask_ref, kv_ref, att_ref, share_ref, total):
+    tile = pl.program_id(0)
+    product = dot(text_ref[...], w_ref[...])
+
+    @pl.when(tile < 2)
+    def _():
+        total[tile] = product
+
+    @pl.when(tile >= 2)
+    def _():
+        kv_ref[tile - 2] = (total[tile - 2] + product).astype(bf16)
+
+    @pl.when(tile == 3)
+    def _():
+        attend_forward(cq_ref, kv_ref.at[0], kv_ref.at[1], mask_ref, False, att_ref, share_ref)
+
+
+def ffn_kernel(h_ref, up_ref, down_ref, grad_ref, du_ref, branch_ref, gup_ref, gdown_ref, total):
+    tile = pl.program_id(0)
+    up_values = dot(h_ref[...], up_ref[...])
+    chance = 0.5 * (1.0 + lax.erf(up_values * 0.5**0.5))
+    density = jnp.exp(-0.5 * up_values * up_values) * 0.3989422804014327
+    activated = (up_values * chance).astype(bf16)
+    back_act = dot_nt(grad_ref[...], down_ref[...])
+    back_up = (back_act * (chance + up_values * density)).astype(bf16)
+    du_ref[...] = back_up
+    gup_ref[...] = dot_tn(h_ref[...], back_up).astype(bf16)
+    gdown_ref[...] = dot_tn(activated, grad_ref[...]).astype(bf16)
+
+    @pl.when(tile == 0)
+    def _():
+        total[...] = dot(activated, down_ref[...])
+
+    @pl.when(tile > 0)
+    def _():
+        total[...] += dot(activated, down_ref[...])
+
+    @pl.when(tile == 3)
+    def _():
+        branch_ref[...] = total[...].astype(bf16)
+
+
+def cross_back_kernel(
+    rows, back_ref, cq_ref, kv_ref, share_ref, text_ref, dcq_ref, grad_ref, pairs
+):
+    share = cq_ref.shape[1]
+
+    @pl.when(pl.program_id(0) == 0)
+    def _():
+        def put_query(here, columns, value):
+            dcq_ref[here, columns] = value.astype(bf16)
+
+        def put_pair(there, columns, key_grad, value_grad):
+            pairs[there, columns] = key_grad.astype(bf16)
+            after_keys = slice(share + columns.start, share + columns.stop)
+            pairs[there, after_keys] = value_grad.astype(bf16)
+
+        attend_backward(
+            cq_ref, kv_ref.at[0], kv_ref.at[1], share_ref, back_ref, rows, False, put_query, put_pair
+        )
+
+    grad_ref[...] = dot_tn(text_ref[...], pairs[...]).astype(bf16)
+
+
+def outs_grad_kernel(att1_ref, carry1_ref, att2_ref, carry2_ref, grad_ref):
+    tile = pl.program_id(0)
+
+    @pl.when(tile == 0)
+    def _():
+        grad_ref[...] = dot_tn(att1_ref[...], carry1_ref[...]).astype(bf16)
+
+    @pl.when(tile == 1)
+    def _():
+        grad_ref[...] = dot_tn(att2_ref[...], carry2_ref[...]).astype(bf16)
+
+
+def self_back_kernel(
+    rows, back_ref, proj_ref, share_ref, h1_ref, h2_ref, dcq_ref, dproj_ref, grad_ref, parts
+):
+    tile = pl.program_id(0)
+    share = dcq_ref.shape[1]
+
+    @pl.when(tile == 0)
+    def _():
+        def put(part, here, columns, value):
+            value = value.astype(bf16)
+            parts[part, here, columns] = value
+            dproj_ref[here, part * share + columns.start : part * share + columns.stop] = value
+
+        def put_query(here, columns, value):
+            put(0, here, columns, value)
+
+        def put_pair(there, columns, key_grad, value_grad):
+            put(1, there, columns, key_grad)
+            put(2, there, columns, value_grad)
+
+        attend_backward(
+            proj_ref.at[0],
+            proj_ref.at[1],
+            proj_ref.at[2],
+            share_ref,
+            back_ref,
+            rows,
+            True,
+            put_query,
+            put_pair,
+        )
+
+    @pl.when(tile < 3)
+    def _():
+        grad_ref[...] = dot_tn(h1_ref[...], parts[tile]).astype(bf16)
+
+    @pl.when(tile == 3)
+    def _():
+        grad_ref[...] = dot_tn(h2_ref[...], dcq_ref[...]).astype(bf16)
+
+
+def fixed(dims):
+    return pl.BlockSpec(dims, lambda t: (0,) * len(dims))
+
+
+def moving(dims, index):
+    return pl.BlockSpec(dims, lambda t: (0, index(t)))
+
+
+def local_call(kernel, name, tiles, outs, specs, out_specs, scratch, flops, moved):
+    return pl.pallas_call(
+        kernel,
+        name=name,
+        grid=(tiles,),
+        out_shape=outs,
+        in_specs=specs,
+        out_specs=out_specs,
+        scratch_shapes=scratch,
+        compiler_params=pltpu.CompilerParams(vmem_limit_bytes=VMEM_CAP),
+        cost_estimate=pl.CostEstimate(flops=flops, bytes_accessed=moved, transcendentals=0),
+    )
+
+
+def self_forward(hidden, query_z, mask):
+    tokens, width = hidden.shape
+    share = query_z.shape[1] // 4
+    packed, rows, _ = mask.shape
+    pairs = (packed * share // HEAD, rows, rows)
+    return local_call(
+        self_forward_kernel,
+        "self_forward",
+        3,
+        (shape((3, tokens, share), bf16), shape((tokens, share), bf16), shape(pairs, f32)),
+        [fixed(hidden.shape), moving((width, share), lambda t: t), fixed(mask.shape)],
+        (fixed((3, tokens, share)), fixed((tokens, share)), fixed(pairs)),
+        [],
+        6 * tokens * width * share,
+        20_000_000,
+    )(hidden, query_z, mask)
+
+
+def cross_forward(cross_query, text_all, text_z, mask):
+    tokens, share = cross_query.shape
+    texts = text_all.shape[0]
+    width = text_z.shape[0]
+    packed, rows, _ = mask.shape
+    pairs = (packed * share // HEAD, rows, texts)
+    return local_call(
+        cross_forward_kernel,
+        "cross_forward",
+        4,
+        (shape((2, texts, share), bf16), shape((tokens, share), bf16), shape(pairs, f32)),
+        [
+            fixed(cross_query.shape),
+            moving((texts, width), lambda t: t // 2),
+            moving((width, share), lambda t: t),
+            fixed(mask.shape),
+        ],
+        (fixed((2, texts, share)), fixed((tokens, share)), fixed(pairs)),
+        [pltpu.VMEM((2, texts, share), f32)],
+        8 * texts * width * share,
+        20_000_000,
+    )(cross_query, text_all, text_z, mask)
+
+
+def ffn(hidden, up_z, down_z, grad_all):
+    tokens, width = hidden.shape
+    share = down_z.shape[0]
+    return local_call(
+        ffn_kernel,
+        "ffn",
+        4,
+        (
+            shape((tokens, 4 * share), bf16),
+            shape((tokens, width), bf16),
+            shape(up_z.shape, bf16),
+            shape(down_z.shape, bf16),
+        ),
+        [
+            fixed(hidden.shape),
+            moving((width, share), lambda t: t),
+            moving((share, width), lambda t: t),
+            fixed(grad_all.shape),
+        ],
+        (
+            moving((tokens, share), lambda t: t),
+            fixed((tokens, width)),
+            moving((width, share), lambda t: t),
+            moving((share, width), lambda t: t),
+        ),
+        [pltpu.VMEM((tokens, width), f32)],
+        40 * tokens * width * share,
+        60_000_000,
+    )(hidden, up_z, down_z, grad_all)
+
+
+def cross_back(back_attended, cross_query, text_pairs, shares, text_all, rows):
+    tokens, share = cross_query.shape
+    texts = text_all.shape[0]
+    width = text_all.shape[1] // 2
+    return local_call(
+        functools.partial(cross_back_kernel, rows),
+        "cross_back",
+        2,
+        (shape((tokens, share), bf16), shape((width, 4 * share), bf16)),
+        [
+            fixed(back_attended.shape),
+            fixed(cross_query.shape),
+            fixed(text_pairs.shape),
+            fixed(shares.shape),
+            moving((texts, width), lambda t: t),
+        ],
+        (fixed((tokens, share)), moving((width, 2 * share), lambda t: t)),
+        [pltpu.VMEM((texts, 2 * share), bf16)],
+        8 * texts * width * share,
+        20_000_000,
+    )(back_attended, cross_query, text_pairs, shares, text_all)
+
+
+def outs_grad(attended1, carry1, attended2, carry2):
+    tokens, share = attended1.shape
+    width = carry1.shape[1]
+    return local_call(
+        outs_grad_kernel,
+        "outs_grad",
+        2,
+        shape((share, 2 * width), bf16),
+        [fixed((tokens, share)), fixed((tokens, width))] * 2,
+        moving((share, width), lambda t: t),
+        [],
+        4 * tokens * width * share,
+        10_000_000,
+    )(attended1, carry1, attended2, carry2)
+
+
+def self_back(back_attended, projected, shares, hidden1, hidden2, back_cross, rows):
+    tokens, width = hidden1.shape
+    share = back_cross.shape[1]
+    return local_call(
+        functools.partial(self_back_kernel, rows),
+        "self_back",
+        4,
+        (shape((tokens, 3 * share), bf16), shape((width, 4 * share), bf16)),
+        [
+            fixed(back_attended.shape),
+            fixed(projected.shape),
+            fixed(shares.shape),
+            fixed(hidden1.shape),
+            fixed(hidden2.shape),
+            fixed(back_cross.shape),
+        ],
+        (fixed((tokens, 3 * share)), moving((width, share), lambda t: t)),
+        [pltpu.VMEM((3, tokens, share), bf16)],
+        8 * tokens * width * share,
+        25_000_000,
+    )(back_attended, projected, shares, hidden1, hidden2, back_cross)
 
 
 def block_slots(owners):
@@ -1117,14 +1392,14 @@
     text_all = text_all.reshape(-1, text_in.shape[1])
     segment = marks[:, 0, :token_count]
     caption = marks[:, 0, token_count : token_count + capt_ids.shape[1]]
-    self_mask = segment[:, :, None] == segment[:, None, :]
-    cross_mask = segment[:, :, None] == caption[:, None, :]
-
-    projected = dot(hidden1, query_z[:, : 3 * share]).astype(bf16)
-    self_query = projected[:, :share]
-    self_key = projected[:, share : 2 * share]
-    self_value = projected[:, 2 * share :]
-    attended1, shares1 = attend_forward(self_query, self_key, self_value, self_mask)
+    self_mask = (segment[:, :, None] == segment[:, None, :]).astype(jnp.int32)
+    text_row = lax.broadcasted_iota(jnp.int32, caption.shape, 0).reshape(1, 1, -1)
+    packed_row = lax.broadcasted_iota(jnp.int32, (n_z, 1, 1), 0)
+    cross_mask = jnp.logical_and(
+        segment[:, :, None] == caption.reshape(1, 1, -1), packed_row == text_row
+    ).astype(jnp.int32)
+
+    projected, attended1, shares1 = self_forward(hidden1, query_z, self_mask)
     up_rows, down_rows, grad_all = enter_call(
         "enter_up",
         7,
@@ -1144,63 +1419,32 @@
         attended1, outs_z, 0, tokens_in, after(norm_full[2:4], up_rows), query_z, n_z, n_dp, 1
     )
     hidden2 = hidden2.reshape(-1, width)
-    text_pairs = (
-        dot(text_all[:, :width], text_z[:, : 2 * share])
-        + dot(text_all[:, width:], text_z[:, 2 * share :])
-    ).astype(bf16)
-    text_key = text_pairs[:, :share]
-    text_value = text_pairs[:, share:]
-    attended2, shares2 = attend_forward(cross_query, text_key, text_value, cross_mask)
+    text_pairs, attended2, shares2 = cross_forward(cross_query, text_all, text_z, cross_mask)
     middle2, hidden3 = forward_call(
         attended2, outs_z, 1, middle1, norm_full[4:6], None, n_z, n_dp, 2
     )
     hidden3 = hidden3.reshape(-1, width)
-    up_values = dot(hidden3, up_z)
-    gelu_values, gelu_pull = jax.vjp(exact_gelu, up_values)
-    activated = gelu_values.astype(bf16)
-    branch3 = sum(
-        dot(activated[:, f * share : (f + 1) * share], down_z[:, f * width : (f + 1) * width])
-        for f in range(4)
-    )
-    branch3 = branch3.astype(bf16).reshape(n_z, token_count, width)
-
-    down_part = jnp.concatenate(
-        [dot_tn(activated[:, f * share : (f + 1) * share], grad_all).astype(bf16) for f in range(4)],
-        axis=1,
-    )
+    back_up, branch3, up_part, down_part = ffn(hidden3, up_z, down_z, grad_all)
+    branch3 = branch3.reshape(n_z, token_count, width)
     down_sum = gather_sum(down_part, 1)
-    back_act = jnp.concatenate(
-        [dot_nt(grad_all, down_z[:, f * width : (f + 1) * width]) for f in range(4)], axis=1
-    )
-    back_up = gelu_pull(back_act)[0].astype(bf16)
-    up_part = dot_tn(hidden3, back_up).astype(bf16)
     up_sum = gather_sum(up_part, n_z)
     at_middle2, carry2, back_att2, term3 = back_call(
         back_up, up_z, 0, grad_out, middle2, norm_full[4:6], outs_z, 1, n_z, n_dp, 3
     )
     carry2 = carry2.reshape(-1, width)
-    outs_part2 = dot_tn(attended2, carry2).astype(bf16)
-    back_cross, text_kgrad, text_vgrad = attend_backward(
-        cross_query, text_key, text_value, shares2, back_att2
-    )
-    back_pairs = jnp.concatenate([text_kgrad, text_vgrad], axis=1)
-    text_part = jnp.concatenate(
-        [dot_tn(text_all[:, f * width : (f + 1) * width], back_pairs).astype(bf16) for f in range(2)],
-        axis=1,
+    back_cross, text_part = cross_back(
+        back_att2, cross_query, text_pairs, shares2, text_all, token_count
     )
     text_sum = gather_sum(text_part, n_z)
-    query_part2 = dot_tn(hidden2, back_cross).astype(bf16)
     at_middle1, carry1, back_att1, term2 = back_call(
         back_cross, query_z, 3, at_middle2, middle1, norm_full[2:4], outs_z, 0, n_z, n_dp, 4
     )
     carry1 = carry1.reshape(-1, width)
-    outs_part1 = dot_tn(attended1, carry1).astype(bf16)
-    outs_sum = gather_sum(jnp.concatenate([outs_part1, outs_part2], axis=1), 1)
-    back_projected = jnp.concatenate(
-        attend_backward(self_query, self_key, self_value, shares1, back_att1), axis=1
-    )
-    query_part1 = dot_tn(hidden1, back_projected).astype(bf16)
-    query_sum = gather_sum(jnp.concatenate([query_part1, query_part2], axis=1), n_z)
+    outs_sum = gather_sum(outs_grad(attended1, carry1, attended2, carry2), 1)
+    back_projected, query_part = self_back(
+        back_att1, projected, shares1, hidden1, hidden2, back_cross, token_count
+    )
+    query_sum = gather_sum(query_part, n_z)
     text_grad, up_grad, down_grad = leave_call(
         "leave_up",
         8,
@@ -1227,7 +1471,7 @@
         5,
     )
     norm_term = jnp.concatenate([term1[:2], term2[:2], term3[:4]], axis=0)
-    query_grad, outs_grad, norm_grad = leave_call(
+    query_grad, outs_slots, norm_grad = leave_call(
         "leave_query",
         9,
         contents,
@@ -1240,13 +1484,13 @@
         n_dp,
     )
     norm_grad = norm_grad[:6]
-    query_grad, outs_grad, text_grad, up_grad, down_grad = (
+    query_grad, outs_slots, text_grad, up_grad, down_grad = (
         grad.reshape(own_rows, -1).astype(f32)
-        for grad in (query_grad, outs_grad, text_grad, up_grad, down_grad)
+        for grad in (query_grad, outs_slots, text_grad, up_grad, down_grad)
     )
     query_new = adamw_update(w_query, m_query, v_query, query_grad, rate_query, decay_rate)
     up_new = adamw_update(w_up, m_up, v_up, up_grad, rate_up, decay_rate)
-    outs_new = adamw_update(w_outs, m_outs, v_outs, outs_grad, rate_outs, decay_rate)
+    outs_new = adamw_update(w_outs, m_outs, v_outs, outs_slots, rate_outs, decay_rate)
     text_new = adamw_update(w_text, m_text, v_text, text_grad, rate_text, decay_rate)
     down_new = adamw_update(w_down, m_down, v_down, down_grad, rate_down, decay_rate)
     norm_new = adamw_update(norm_weight, m_norm, v_norm, norm_grad, rate_norm, 0.0)

time: 1130 us -> 1090 us (0.965)
  matrix products: 106 us -> 0 us
  waiting for transfers between devices: 64.1 us -> 130 us
  Pallas kernels: 820 us -> 881 us
  other arithmetic: 68.7 us -> 40.6 us
  local copies, waits for them, and re-layouts: 40.6 us -> 12.6 us
    dot_general x35 -> x0, matrix products: 106 us -> none  [the longest x8 44.3 us: dot(): return jnp.dot(left, right, preferred_element_type=f32)]
    pallas_call x0 -> x6, Pallas kernels: none -> 85.8 us  [the longest x1 30.3 us: ffn(): local_call(ffn_kernel, 'ffn', 4, (shape((tokens, 4 * share), bf16), shape...]
    reduce_scatter x5, waiting for transfers between devices: 62.7 us -> 128 us  [gather_sum(): summed = lax.psum_scatter(piece, 'dp', scatter_dimension=0, tiled=True)]
    concatenate x4 -> x0, other arithmetic: 23.3 us -> none  [the longest x1 8.51 us: body(): jnp.concatenate([query_part1, query_part2], axis=1)]
    pallas_call x2, Pallas kernels: 190 us -> 172 us  [leave_call(): line_call(kernel, name, ident, outs, specs, scratch, 0, LINK_COST)(*args)]
  transfers between devices with their start and end apart: 10 -> 10, of which waited for: 1 -> 2; matrix products, arithmetic and copies ran while one was open for 11% -> 1% of each run, Pallas kernels for 56% -> 60%
where the time goes in v4:
time: 1090 us; the launch traced here: 1080 us
  Pallas kernels  881 us (81%)
  waiting for transfers between devices  130 us (12%)
  other arithmetic  40.6 us (4%)
  between operations  15 us (1%)
  local copies, waits for them, and re-layouts  12.6 us (1%)
    pallas_call x3, Pallas kernels, enter_call(): line_call(kernel, name, ident, outs, specs, scratch, 0, LINK_COST)(*args)  242 us
    pallas_call x2, Pallas kernels, leave_call(): line_call(kernel, name, ident, outs, specs, scratch, 0, LINK_COST)(*args)  172 us
    pallas_call x2, Pallas kernels, back_call(): return call(dy, weight, base, middle, norm_rows, outs_z)  151 us
    pallas_call x2, Pallas kernels, forward_call(): return call(*args)  145 us
    reduce_scatter x5, waiting for transfers between devices, gather_sum(): summed = lax.psum_scatter(piece, 'dp', scatter_dimension=0, tiled=True)  128 us
    pallas_call x1, Pallas kernels, last_call(): return call(dy, weight, base, tokens, norm_rows, branch, middle)  85 us
    sub x6, other arithmetic, adamw_update(): weight - rate * (first_hat / (jnp.sqrt(second_hat) + adam_eps) + decay *...  38.3 us
    pallas_call x1, Pallas kernels, ffn(): local_call(ffn_kernel, 'ffn', 4, (shape((tokens, 4 * share), bf16), shape...  30.3 us
  transfers between devices with their start and end apart: 10, of which 2 were waited for; matrix products, arithmetic and copies ran while one was open for 1% of the time, Pallas kernels for 60%

profile of v4, /device:TPU:0, one launch (start us, length us, event | category | flops | bytes accessed | tf_op | source)
XLA Modules:
  0.0 1079.8 jit_solution(17631343233888883891)
XLA Ops:
  10.4 54.3 %enter_query.1 = (bf16[4,64,2048]{2,1,0:T(8,128)(2,1)}, s32[4,8,256]{2,1,0:T(8,128)S(1)}, f32[8,2048]{1,0:T(8,128)S(1)}) custom-call(s32[2,288]{1,0:T(2,128)S(1)} %pad_add_fusion.refs_0_, f32[512,2048]{1,0:T(8,128)} %refs_1_.3, s32[8,256]{1,0:T(8,128)S(1)} %pad.8.refs_2_, f32[8,256]{1,0:T(8,128)S(1)} %pad.9.refs_3_), custom_call_target="tpu_custom_call" | custom-call | bytes 120000000 | tf_op jit(solution)/shard_map/enter_query/pallas_call | solution.py:817
  64.9 106.9 %enter_text.1 = (bf16[1,64,4096]{2,1,0:T(8,128)(2,1)}, bf16[4,64,2048]{2,1,0:T(8,128)(2,1)}, bf16[4,128,2048]{2,1,0:T(8,128)(2,1)}, bf16[4,32,4096]{2,1,0:T(8,128)(2,1)}) custom-call(s32[2,288]{1,0:T(2,128)S(1)} %pad_add_fusion.refs_0_, f32[512,1024]{1,0:T(8,128)} %refs_1_.4, f32[512,2048]{1,0:T(8,128)} %refs_2_.2, bf16[128,2048]{1,0:T(8,128)(2,1)S(1)} %copy-done, ...), custom_call_target="tpu_custom_call" | custom-call | bytes 120000000 | tf_op jit(solution)/shard_map/enter_text/pallas_call | solution.py:817
  172.9 13.0 %self_forward.1 = (bf16[3,512,512]{2,1,0:T(8,128)(2,1)}, bf16[512,512]{1,0:T(8,128)(2,1)S(1)}, f32[16,128,128]{2,1,0:T(8,128)S(1)}) custom-call(bf16[512,2048]{1,0:T(8,128)(2,1)} %bitcast.116, bf16[2048,2048]{1,0:T(8,128)(2,1)} %all-gather.8.cloned.1.call-done.w_ref.rest_0_.w_hbm, s32[4,128,128]{2,1,0:T(8,128)S(1)} %get-tuple-element.152.mask_ref), custom_call_target="tpu_custom_call" | custom-call | flops 3221225472 | bytes 20000000 | tf_op jit(solution)/shard_map/self_forward/pallas_call | solution.py:1129
  186.9 80.4 %enter_up.1 = (bf16[4,64,2048]{2,1,0:T(8,128)(2,1)}, bf16[1,64,8192]{2,1,0:T(8,128)(2,1)}, bf16[4,128,2048]{2,1,0:T(8,128)(2,1)}) custom-call(s32[2,288]{1,0:T(2,128)S(1)} %pad_add_fusion.refs_0_, f32[512,2048]{1,0:T(8,128)} %refs_1_.5, f32[512,2048]{1,0:T(8,128)} %refs_2_.3, bf16[128,2048]{1,0:T(8,128)(2,1)S(1)} %copy-done.2), custom_call_target="tpu_custom_call" | custom-call | bytes 120000000 | tf_op jit(solution)/shard_map/enter_up/pallas_call | solution.py:817
  268.0 70.7 %forward0.1 = (f32[128,2048]{1,0:T(8,128)}, bf16[4,128,2048]{2,1,0:T(8,128)(2,1)}, bf16[512,512]{1,0:T(8,128)(2,1)S(1)}) custom-call(bf16[512,512]{1,0:T(8,128)(2,1)S(1)} %get-tuple-element.74.att_ref.att1_ref, bf16[512,4096]{1,0:T(8,128)(2,1)} %bitcast.86, bf16[128,2048]{1,0:T(8,128)(2,1)S(1)} %copy-done, f32[2,2048]{1,0:T(2,128)S(1)} %get-tuple-element.78.norm_ref, ...), custom_call_target="tpu_custom_call" | custom-call | bytes 120000000 | tf_op jit(solution)/shard_map/forward0/pallas_call | solution.py:870
  338.7 11.5 %cross_forward.1 = (bf16[2,128,512]{2,1,0:T(8,128)(2,1)S(1)}, bf16[512,512]{1,0:T(8,128)(2,1)S(1)}, f32[16,128,128]{2,1,0:T(8,128)}) custom-call(bf16[512,512]{1,0:T(8,128)(2,1)S(1)} %get-tuple-element.79.cq_ref, bf16[128,4096]{1,0:T(8,128)(2,1)} %bitcast.95, bf16[2048,2048]{1,0:T(8,128)(2,1)} %all-gather.10.cloned.1.call-done.w_ref, ...), custom_call_target="tpu_custom_call" | custom-call | flops 1073741824 | bytes 20000000 | tf_op jit(solution)/shard_map/cross_forward/pallas_call | solution.py:1148
  350.2 74.3 %forward1.1 = (f32[128,2048]{1,0:T(8,128)S(1)}, bf16[4,128,2048]{2,1,0:T(8,128)(2,1)}) custom-call(bf16[512,512]{1,0:T(8,128)(2,1)S(1)} %get-tuple-element.82.att_ref.att2_ref, bf16[512,4096]{1,0:T(8,128)(2,1)} %bitcast.87, f32[128,2048]{1,0:T(8,128)} %get-tuple-element.83.base_ref.middle_ref, f32[2,2048]{1,0:T(2,128)S(1)} %get-tuple-element.148.norm_ref), custom_call_target="tpu_custom_call" | custom-call | bytes 120000000 | tf_op jit(solution)/shard_map/forward1/pallas_call | solution.py:870
  425.5 30.3 %ffn.1 = (bf16[512,2048]{1,0:T(8,128)(2,1)}, bf16[512,2048]{1,0:T(8,128)(2,1)}, bf16[2048,2048]{1,0:T(8,128)(2,1)}, bf16[512,8192]{1,0:T(8,128)(2,1)}) custom-call(bf16[512,2048]{1,0:T(8,128)(2,1)} %bitcast.120, bf16[2048,2048]{1,0:T(8,128)(2,1)} %all-gather.12.cloned.1.call-done.up_ref.w_hbm, bf16[512,8192]{1,0:T(8,128)(2,1)} %bitcast.115, ...), custom_call_target="tpu_custom_call" | custom-call | flops 21474836480 | bytes 60000000 | tf_op jit(solution)/shard_map/ffn/pallas_call | solution.py:1169
  455.8 77.7 %back1.1 = (f32[128,2048]{1,0:T(8,128)}, bf16[4,128,2048]{2,1,0:T(8,128)(2,1)}, bf16[512,512]{1,0:T(8,128)(2,1)S(1)}, f32[8,2048]{1,0:T(8,128)S(1)}) custom-call(bf16[512,2048]{1,0:T(8,128)(2,1)} %get-tuple-element.87.dy_ref, bf16[2048,2048]{1,0:T(8,128)(2,1)} %all-gather.12.cloned.1.call-done.up_ref.w_hbm, bf16[128,2048]{1,0:T(8,128)(2,1)S(1)} %copy-done.2, ...), custom_call_target="tpu_custom_call" | custom-call | bytes 120000000 | tf_op jit(solution)/shard_map/back1/pallas_call | solution.py:904
  533.5 9.9 cross_back.1
  544.9 73.3 %back0.1 = (f32[128,2048]{1,0:T(8,128)}, bf16[4,128,2048]{2,1,0:T(8,128)(2,1)}, bf16[512,512]{1,0:T(8,128)(2,1)S(1)}, f32[8,2048]{1,0:T(8,128)S(1)}) custom-call(bf16[512,512]{1,0:T(8,128)(2,1)S(1)} %get-tuple-element.92.dy_ref.dcq_ref, bf16[2048,2048]{1,0:T(8,128)(2,1)} %all-gather.8.cloned.1.call-done.w_ref.rest_0_.w_hbm, ...), custom_call_target="tpu_custom_call" | custom-call | bytes 120000000 | tf_op jit(solution)/shard_map/back0/pallas_call | solution.py:904
  618.2 6.2 outs_grad.1
  624.4 15.0 %self_back.1 = (bf16[512,1536]{1,0:T(8,128)(2,1)}, bf16[2048,2048]{1,0:T(8,128)(2,1)}) custom-call(bf16[512,512]{1,0:T(8,128)(2,1)S(1)} %get-tuple-element.94.back_ref, bf16[3,512,512]{2,1,0:T(8,128)(2,1)} %get-tuple-element.95.proj_ref, f32[16,128,128]{2,1,0:T(8,128)} %copy-done.6, bf16[512,2048]{1,0:T(8,128)(2,1)} %bitcast.117, ...), custom_call_target="tpu_custom_call" | custom-call | flops 4294967296 | bytes 25000000 | tf_op jit(solution)/shard_map/self_back/pallas_call | solution.py:1239
  640.8 52.9 %reduce-scatter.8.cloned.1.call-done = bf16[256,2048]{1,0:T(8,128)(2,1)} async-done(((bf16[2048,2048]{1,0:T(8,128)(2,1)}), bf16[256,2048]{1,0:T(8,128)(2,1)}) %reduce-scatter.8.cloned.1.call-update) | async-done | bytes 1048592 | tf_op jit(solution)/shard_map/reduce_scatter | solution.py:1357
  693.7 74.7 %reduce-scatter.10.cloned.1.call-done = bf16[64,8192]{1,0:T(8,128)(2,1)} async-done(((bf16[512,8192]{1,0:T(8,128)(2,1)}), bf16[64,8192]{1,0:T(8,128)(2,1)}) %reduce-scatter.10.cloned.1.call-update) | async-done | bytes 1048592 | tf_op jit(solution)/shard_map/reduce_scatter | solution.py:1357
  769.7 112.3 %leave_up.1 = (bf16[8,64,2048]{2,1,0:T(8,128)(2,1)}, bf16[8,64,2048]{2,1,0:T(8,128)(2,1)}, bf16[8,64,2048]{2,1,0:T(8,128)(2,1)}) custom-call(s32[2,576]{1,0:T(2,128)S(1)} %concatenate.22.refs_0_, bf16[4,64,2048]{2,1,0:T(8,128)(2,1)S(1)} %bitcast.84, bf16[4,64,2048]{2,1,0:T(8,128)(2,1)} %bitcast.93, bf16[1,64,8192]{2,1,0:T(8,128)(2,1)} %bitcast.94), custom_call_target="tpu_custom_call" | custom-call | bytes 120000000 | tf_op jit(solution)/shard_map/leave_up/pallas_call | solution.py:845
  882.0 85.0 %last.1 = (bf16[128,2048]{1,0:T(8,128)(2,1)S(1)}, bf16[128,2048]{1,0:T(8,128)(2,1)S(1)}, f32[8,2048]{1,0:T(8,128)S(1)}) custom-call(bf16[512,1536]{1,0:T(8,128)(2,1)} %get-tuple-element.98.dy_ref, bf16[2048,2048]{1,0:T(8,128)(2,1)} %all-gather.8.cloned.1.call-done.w_ref.rest_0_.w_hbm, f32[128,2048]{1,0:T(8,128)} %get-tuple-element.99.base_ref, ...), custom_call_target="tpu_custom_call" | custom-call | bytes 120000000 | tf_op jit(solution)/shard_map/last/pallas_call | solution.py:928
  967.1 7.8 multiply_subtract_fusion.1
  976.0 60.2 %leave_query.1 = (bf16[8,64,2048]{2,1,0:T(8,128)(2,1)}, bf16[8,64,1024]{2,1,0:T(8,128)(2,1)S(1)}, f32[8,256]{1,0:T(8,128)S(1)}) custom-call(s32[2,576]{1,0:T(2,128)S(1)} %concatenate.22.refs_0_, bf16[4,64,2048]{2,1,0:T(8,128)(2,1)} %bitcast.97, bf16[1,64,4096]{2,1,0:T(8,128)(2,1)S(1)} %bitcast.85, f32[8,2048]{1,0:T(8,128)S(1)} %pad_maximum_fusion.refs_3_), custom_call_target="tpu_custom_call" | custom-call | bytes 120000000 | tf_op jit(solution)/shard_map/leave_query/pallas_call | solution.py:845
  1036.2 10.3 multiply_subtract_fusion.3
  1047.7 4.1 multiply_subtract_fusion.4
  1051.8 1.7 copy-done.12
  1054.6 8.0 multiply_subtract_fusion.2
  1062.9 7.5 multiply_subtract_fusion
  (122 shorter events, 17.0 us)
Async XLA Ops:
  7.2 57.6 %copy-start = (bf16[128,2048]{1,0:T(8,128)(2,1)S(1)}, bf16[128,2048]{1,0:T(8,128)(2,1)}, u32[]{:S(2)}) copy-start(bf16[128,2048]{1,0:T(8,128)(2,1)} %tokens.1) | copy-start | bytes 1572868
  7.2 57.6 %copy-start.5 = (bf16[32,4096]{1,0:T(8,128)(2,1)S(1)}, bf16[32,4096]{1,0:T(8,128)(2,1)}, u32[]{:S(2)}) copy-start(bf16[32,4096]{1,0:T(8,128)(2,1)} %refs_4_.1) | copy-start | bytes 786436
  7.2 165.7 %all-gather.8.cloned.1.call-start = ((), (), s32[]{:S(2)}) async-start(), calls=%async_computation.5 | async-start | bytes 9437184 | tf_op jit(solution)/shard_map/all_gather | solution.py:1354
  64.8 203.2 %all-gather.14.cloned.1.call-start = ((), (), s32[]{:S(2)}) async-start(), calls=%async_computation.13 | async-start | bytes 4718592 | tf_op jit(solution)/shard_map/all_gather | solution.py:1354
  171.8 167.0 %all-gather.10.cloned.1.call-start = ((), (), s32[]{:S(2)}) async-start(), calls=%async_computation.6 | async-start | bytes 9437184 | tf_op jit(solution)/shard_map/all_gather | solution.py:1354
  172.5 253.0 %all-gather.12.cloned.1.call-start = ((), (), s32[]{:S(2)}) async-start(), calls=%async_computation.7 | async-start | bytes 9437184 | tf_op jit(solution)/shard_map/all_gather | solution.py:1354
  172.9 13.9 %copy-start.2 = (bf16[128,2048]{1,0:T(8,128)(2,1)S(1)}, bf16[128,2048]{1,0:T(8,128)(2,1)}, u32[]{:S(2)}) copy-start(bf16[128,2048]{1,0:T(8,128)(2,1)} %base_ref.3) | copy-start | bytes 1572868
  267.3 158.2 %all-gather.16.cloned.1.call-start = ((), (), s32[]{:S(2)}) async-start(), calls=%async_computation.14 | async-start | bytes 9437184 | tf_op jit(solution)/shard_map/all_gather | solution.py:1354
  267.9 372.9 %reduce-scatter.6.cloned.1.call-start = ((), (), s32[]{:S(2)}) async-start(), calls=%async_computation.8 | async-start | bytes 9437184 | tf_op jit(solution)/shard_map/reduce_scatter | solution.py:1357
  543.4 150.4 %reduce-scatter.8.cloned.1.call-start = ((), (), s32[]{:S(2)}) async-start(), calls=%async_computation.9 | async-start | bytes 9437184 | tf_op jit(solution)/shard_map/reduce_scatter | solution.py:1357
  544.1 224.4 %reduce-scatter.10.cloned.1.call-start = ((), (), s32[]{:S(2)}) async-start(), calls=%async_computation.10 | async-start | bytes 9437184 | tf_op jit(solution)/shard_map/reduce_scatter | solution.py:1357
  544.9 430.0 %reduce-scatter.14.cloned.1.call-start = ((), (), s32[]{:S(2)}) async-start(), calls=%async_computation.12 | async-start | bytes 4718592 | tf_op jit(solution)/shard_map/reduce_scatter | solution.py:1357
  624.4 350.5 %reduce-scatter.12.cloned.1.call-start = ((), (), s32[]{:S(2)}) async-start(), calls=%async_computation.11 | async-start | bytes 9437184 | tf_op jit(solution)/shard_map/reduce_scatter | solution.py:1357
  882.0 85.1 %copy-start.7 = (f32[512,2048]{1,0:T(8,128)S(1)}, f32[512,2048]{1,0:T(8,128)}, u32[]{:S(2)}) copy-start(f32[512,2048]{1,0:T(8,128)} %refs_2_.2) | copy-start | bytes 12582916
  882.0 85.1 %copy-start.11 = (f32[512,2048]{1,0:T(8,128)S(1)}, f32[512,2048]{1,0:T(8,128)}, u32[]{:S(2)}) copy-start(f32[512,2048]{1,0:T(8,128)} %param.49) | copy-start | bytes 12582916
  1036.2 10.4 copy-start.10
  1036.2 10.4 copy-start.15
  1036.2 11.5 %copy-start.16 = (f32[512,1024]{1,0:T(8,128)S(1)}, f32[512,1024]{1,0:T(8,128)}, u32[]{:S(2)}) copy-start(f32[512,1024]{1,0:T(8,128)} %param.45) | copy-start | bytes 6291460
  1054.6 8.0 copy-start.9
  1054.6 8.0 copy-start.14
  1054.6 8.3 copy-start.17
  1062.9 7.5 copy-start.18
  1062.9 7.5 copy-start.19
  1062.9 7.5 copy-start.20
  (12 other events, 24.7 us)
Sparse Core Ops, SparseCore 0:
  64.9 75.1 all-gather.7
  171.9 57.0 all-gather.13
  230.9 59.9 all-gather.9
  292.6 54.4 all-gather.11
  348.9 54.3 all-gather.15
  543.5 75.0 reduce-scatter.5
  622.4 71.2 reduce-scatter.7
  697.2 71.2 reduce-scatter.9
  772.8 87.6 reduce-scatter.13
  863.8 78.2 reduce-scatter.11

commit v5 on v4

--- a/solution.py
+++ b/solution.py
@@ -483,14 +483,17 @@
     reorder(load, store, rows, width, orders)
 
 
-def leave_kernel(weights, summed, *refs):
+def leave_kernel(weights, summed, inner, inner_counts, *refs):
     refs = Refs(refs)
     n_dp = lax.axis_size("dp")
     slots_ref = refs.take()
     row_refs = refs.take(len(weights))
     term_ref = refs.take() if summed else None
+    inner_refs = refs.take(inner_counts[0])
     out_refs = refs.take(len(weights))
     sum_ref = refs.take() if summed else None
+    inner_refs += refs.take(inner_counts[1])
+    inner_refs += refs.take(inner_counts[2])
     greet_all()
     if summed:
         cut, parts, send, recv, total, others, send2, recv2 = refs.take(8)
@@ -539,6 +542,8 @@
         swap.start()
         swap.keep()
         swaps.append(swap)
+    if inner is not None:
+        inner(*inner_refs)
     if summed:
         total_spread.wait()
         sum_ref[...] = jnp.sum(others[...], axis=0)
@@ -695,7 +700,6 @@
     load_w = fetch_columns(w_hbm, 0, w_ref, w_sem)
     load_w.start()
     line = Line(n, rows, step)
-    line.greet()
     load_w.wait()
     sums = Sums(line, part, held, s_send, s_recv)
     results = Sums(line, branch, held2, r_send, r_recv)
@@ -762,7 +766,7 @@
     return jax.ShapeDtypeStruct(dims, kind)
 
 
-LINK_COST = 120_000_000
+LINK_COST = 4_000_000
 
 
 class Order:
@@ -817,7 +821,7 @@
     return line_call(kernel, name, ident, outs, specs, scratch, 0, LINK_COST)(*args)
 
 
-def leave_call(name, ident, slots, weights, term, n, n_dp):
+def leave_call(name, ident, slots, weights, term, n, n_dp, inner=None):
     outs, scratch = [], []
     specs = [pl.BlockSpec(memory_space=pltpu.SMEM)] + [whole_vmem()] * len(weights)
     args = [slots, *(weight[0] for weight in weights)]
@@ -826,6 +830,15 @@
         args.append(term)
         specs.append(whole_vmem())
         block = (term.shape[0], term.shape[1] // n_dp)
+    counts = (0, 0, 0)
+    run = None
+    if inner is not None:
+        run, inner_args, inner_specs, inner_outs, inner_scratch = inner
+        counts = (len(inner_args), len(inner_outs), len(inner_scratch))
+        args += inner_args
+        specs += inner_specs
+        scratch += inner_scratch
+    if term is not None:
         scratch += [pltpu.VMEM((n_dp, *block), f32)] * 2 + swap_sems(n_dp)
         scratch += [pltpu.VMEM(block, f32), pltpu.VMEM((n, *block), f32), *swap_sems(n)]
     for rows, split, _, _ in weights:
@@ -839,8 +852,10 @@
         scratch.append(pltpu.VMEM((blocks, chunk, BLK), bf16))
     if term is not None:
         outs.append(shape(block, f32))
+    if inner is not None:
+        outs += inner_outs
     kernel = functools.partial(
-        leave_kernel, [weight[1:] for weight in weights], term is not None
+        leave_kernel, [weight[1:] for weight in weights], term is not None, run, counts
     )
     return line_call(kernel, name, ident, outs, specs, scratch, 0, LINK_COST)(*args)
 
@@ -904,7 +919,7 @@
     return call(dy, weight, base, middle, norm_rows, outs_z)
 
 
-def last_call(dy, weight, base, tokens, norm_rows, branch, middle, n, n_dp, ident):
+def last_parts(dy, weight, base, tokens, norm_rows, branch, middle, n, n_dp):
     rows, width = base.shape
     outs = [
         shape((rows, width), bf16),
@@ -924,8 +939,7 @@
         pltpu.SemaphoreType.DMA,
     ]
     kernel = functools.partial(last_kernel, n, unshuffle_order(n, n_dp))
-    call = line_call(kernel, "last", ident, outs, specs, scratch, 0, LINK_COST)
-    return call(dy, weight, base, tokens, norm_rows, branch, middle)
+    return kernel, [dy, weight, base, tokens, norm_rows, branch, middle], specs, outs, scratch
 
 
 def attend_forward(query, keys, values, mask_ref, keyed, att_ref, share_ref):
@@ -1117,7 +1131,9 @@
         out_specs=out_specs,
         scratch_shapes=scratch,
         compiler_params=pltpu.CompilerParams(vmem_limit_bytes=VMEM_CAP),
-        cost_estimate=pl.CostEstimate(flops=flops, bytes_accessed=moved, transcendentals=0),
+        cost_estimate=pl.CostEstimate(
+            flops=flops // 8, bytes_accessed=moved // 8, transcendentals=0
+        ),
     )
 
 
@@ -1374,11 +1390,11 @@
         n_dp,
         width,
     )
-    outs_rows, text_rows, hidden1, text_all = enter_call(
-        "enter_text",
+    outs_rows, hidden1, text_all = enter_call(
+        "enter_outs",
         6,
         slots,
-        [(w_outs, out_places, False, firsts[1]), (w_text, split_places, True, firsts[2])],
+        [(w_outs, out_places, False, firsts[1])],
         [(tokens_in, True), (text_in, True)],
         norm_full[0:2],
         False,
@@ -1387,7 +1403,7 @@
         n_dp,
         width,
     )
-    query_z, outs_z, text_z = spread(query_rows), spread(outs_rows), spread(text_rows)
+    query_z, outs_z = spread(query_rows), spread(outs_rows)
     hidden1 = hidden1.reshape(-1, width)
     text_all = text_all.reshape(-1, text_in.shape[1])
     segment = marks[:, 0, :token_count]
@@ -1400,11 +1416,15 @@
     ).astype(jnp.int32)
 
     projected, attended1, shares1 = self_forward(hidden1, query_z, self_mask)
-    up_rows, down_rows, grad_all = enter_call(
-        "enter_up",
+    text_rows, up_rows, down_rows, grad_all = enter_call(
+        "enter_rest",
         7,
         after(slots, attended1),
-        [(w_up, split_places, True, firsts[3]), (w_down, big_places, False, firsts[4])],
+        [
+            (w_text, split_places, True, firsts[2]),
+            (w_up, split_places, True, firsts[3]),
+            (w_down, big_places, False, firsts[4]),
+        ],
         [(grad_out, False)],
         None,
         False,
@@ -1414,7 +1434,7 @@
         width,
     )
     grad_all = grad_all.reshape(-1, width)
-    up_z, down_z = spread(up_rows), spread(down_rows)
+    text_z, up_z, down_z = spread(text_rows), spread(up_rows), spread(down_rows)
     middle1, hidden2, cross_query = forward_call(
         attended1, outs_z, 0, tokens_in, after(norm_full[2:4], up_rows), query_z, n_z, n_dp, 1
     )
@@ -1445,36 +1465,49 @@
         back_att1, projected, shares1, hidden1, hidden2, back_cross, token_count
     )
     query_sum = gather_sum(query_part, n_z)
-    text_grad, up_grad, down_grad = leave_call(
+    down_grad, up_grad, grad_in, result, term1 = leave_call(
         "leave_up",
         8,
-        after(contents, back_projected),
+        contents,
         [
-            (text_sum, True, cap_big, slot_firsts[2]),
+            (down_sum, False, cap_big, slot_firsts[4]),
             (up_sum, True, cap_big, slot_firsts[3]),
-            (down_sum, False, cap_big, slot_firsts[4]),
         ],
         None,
         n_z,
         n_dp,
-    )
-    grad_in, result, term1 = last_call(
-        back_projected,
-        query_z,
-        at_middle1,
-        tokens_in,
-        after(norm_full[0:2], text_grad),
-        branch3,
-        middle2,
+        last_parts(
+            back_projected,
+            query_z,
+            at_middle1,
+            tokens_in,
+            norm_full[0:2],
+            branch3,
+            middle2,
+            n_z,
+            n_dp,
+        ),
+    )
+    (text_grad,) = leave_call(
+        "leave_text",
+        5,
+        after(contents, term1),
+        [(text_sum, True, cap_big, slot_firsts[2])],
+        None,
         n_z,
         n_dp,
-        5,
-    )
+    )
+    text_grad, up_grad, down_grad = (
+        grad.reshape(own_rows, -1).astype(f32) for grad in (text_grad, up_grad, down_grad)
+    )
+    up_new = adamw_update(w_up, m_up, v_up, up_grad, rate_up, decay_rate)
+    text_new = adamw_update(w_text, m_text, v_text, text_grad, rate_text, decay_rate)
+    down_new = adamw_update(w_down, m_down, v_down, down_grad, rate_down, decay_rate)
     norm_term = jnp.concatenate([term1[:2], term2[:2], term3[:4]], axis=0)
     query_grad, outs_slots, norm_grad = leave_call(
         "leave_query",
         9,
-        contents,
+        after(contents, (up_new, down_new, text_new)),
         [
             (query_sum, True, cap_big, slot_firsts[0]),
             (outs_sum, False, cap_out, slot_firsts[1]),
@@ -1484,15 +1517,11 @@
         n_dp,
     )
     norm_grad = norm_grad[:6]
-    query_grad, outs_slots, text_grad, up_grad, down_grad = (
-        grad.reshape(own_rows, -1).astype(f32)
-        for grad in (query_grad, outs_slots, text_grad, up_grad, down_grad)
+    query_grad, outs_slots = (
+        grad.reshape(own_rows, -1).astype(f32) for grad in (query_grad, outs_slots)
     )
     query_new = adamw_update(w_query, m_query, v_query, query_grad, rate_query, decay_rate)
-    up_new = adamw_update(w_up, m_up, v_up, up_grad, rate_up, decay_rate)
     outs_new = adamw_update(w_outs, m_outs, v_outs, outs_slots, rate_outs, decay_rate)
-    text_new = adamw_update(w_text, m_text, v_text, text_grad, rate_text, decay_rate)
-    down_new = adamw_update(w_down, m_down, v_down, down_grad, rate_down, decay_rate)
     norm_new = adamw_update(norm_weight, m_norm, v_norm, norm_grad, rate_norm, 0.0)
     return (
         result,

time: 1090 us -> 936 us (0.86)
  waiting for transfers between devices: 130 us -> 23.6 us
  Pallas kernels: 881 us -> 827 us
    reduce_scatter x5, waiting for transfers between devices: 128 us -> 14.2 us  [gather_sum(): summed = lax.psum_scatter(piece, 'dp', scatter_dimension=0, tiled=True)]
    pallas_call x1 -> x0, Pallas kernels: 85 us -> none  [last_call(): return call(dy, weight, base, tokens, norm_rows, branch, middle)]
    pallas_call x2 -> x3, Pallas kernels: 172 us -> 219 us  [leave_call(): line_call(kernel, name, ident, outs, specs, scratch, 0, LINK_COST)(*args)]
    pallas_call x3, Pallas kernels: 242 us -> 221 us  [enter_call(): line_call(kernel, name, ident, outs, specs, scratch, 0, LINK_COST)(*args)]
  transfers between devices with their start and end apart: 10 -> 10, of which waited for: 2 -> 2; matrix products, arithmetic and copies ran while one was open for 1% -> 3% of each run, Pallas kernels for 60% -> 74%
where the time goes in v5:
time: 936 us; the launch traced here: 923 us
  Pallas kernels  827 us (88%)
  other arithmetic  43.9 us (5%)
  waiting for transfers between devices  23.6 us (3%)
  between operations  15 us (2%)
  local copies, waits for them, and re-layouts  12.5 us (1%)
    pallas_call x3, Pallas kernels, enter_call(): line_call(kernel, name, ident, outs, specs, scratch, 0, LINK_COST)(*args)  221 us
    pallas_call x3, Pallas kernels, leave_call(): line_call(kernel, name, ident, outs, specs, scratch, 0, LINK_COST)(*args)  219 us
    pallas_call x2, Pallas kernels, back_call(): return call(dy, weight, base, middle, norm_rows, outs_z)  154 us
    pallas_call x2, Pallas kernels, forward_call(): return call(*args)  146 us
    sub x6, other arithmetic, adamw_update(): weight - rate * (first_hat / (jnp.sqrt(second_hat) + adam_eps) + decay *...  41.6 us
    pallas_call x1, Pallas kernels, ffn(): local_call(ffn_kernel, 'ffn', 4, (shape((tokens, 4 * share), bf16), shape...  30.3 us
  transfers between devices with their start and end apart: 10, of which 2 were waited for; matrix products, arithmetic and copies ran while one was open for 3% of the time, Pallas kernels for 74%

profile of v5, /device:TPU:0, one launch (start us, length us, event | category | flops | bytes accessed | tf_op | source)
XLA Modules:
  0.0 923.3 jit_solution(13586362660227909900)
XLA Ops:
  10.4 54.3 %enter_query.1 = (bf16[4,64,2048]{2,1,0:T(8,128)(2,1)}, s32[4,8,256]{2,1,0:T(8,128)S(1)}, f32[8,2048]{1,0:T(8,128)S(1)}) custom-call(s32[2,288]{1,0:T(2,128)S(1)} %pad_add_fusion.refs_0_, f32[512,2048]{1,0:T(8,128)} %refs_1_.3, s32[8,256]{1,0:T(8,128)S(1)} %pad.8.refs_2_, f32[8,256]{1,0:T(8,128)S(1)} %pad.9.refs_3_), custom_call_target="tpu_custom_call" | custom-call | bytes 4000000 | tf_op jit(solution)/shard_map/enter_query/pallas_call | solution.py:821
  64.8 57.7 %enter_outs.1 = (bf16[1,64,4096]{2,1,0:T(8,128)(2,1)}, bf16[4,128,2048]{2,1,0:T(8,128)(2,1)}, bf16[4,32,4096]{2,1,0:T(8,128)(2,1)}) custom-call(s32[2,288]{1,0:T(2,128)S(1)} %pad_add_fusion.refs_0_, f32[512,1024]{1,0:T(8,128)} %refs_1_.4, bf16[128,2048]{1,0:T(8,128)(2,1)S(1)} %copy-done, bf16[32,4096]{1,0:T(8,128)(2,1)S(1)} %copy-done.6, ...), custom_call_target="tpu_custom_call" | custom-call | bytes 4000000 | tf_op jit(solution)/shard_map/enter_outs/pallas_call | solution.py:821
  123.1 12.8 %self_forward.1 = (bf16[3,512,512]{2,1,0:T(8,128)(2,1)}, bf16[512,512]{1,0:T(8,128)(2,1)S(1)}, f32[16,128,128]{2,1,0:T(8,128)S(1)}) custom-call(bf16[512,2048]{1,0:T(8,128)(2,1)} %bitcast.91, bf16[2048,2048]{1,0:T(8,128)(2,1)} %all-gather.8.cloned.1.call-done.w_ref.rest_0_.w_hbm.refs_4_, s32[4,128,128]{2,1,0:T(8,128)S(1)} %get-tuple-element.150.mask_ref), custom_call_target="tpu_custom_call" | custom-call | flops 402653184 | bytes 2500000 | tf_op jit(solution)/shard_map/self_forward/pallas_call | solution.py:1145
  135.9 108.8 %enter_rest.1 = (bf16[4,64,2048]{2,1,0:T(8,128)(2,1)}, bf16[4,64,2048]{2,1,0:T(8,128)(2,1)}, bf16[1,64,8192]{2,1,0:T(8,128)(2,1)}, bf16[4,128,2048]{2,1,0:T(8,128)(2,1)}) custom-call(s32[2,288]{1,0:T(2,128)S(1)} %pad_add_fusion.refs_0_, f32[512,2048]{1,0:T(8,128)} %refs_1_.5, f32[512,2048]{1,0:T(8,128)} %refs_2_.3, f32[512,2048]{1,0:T(8,128)} %refs_3_.3, ...), custom_call_target="tpu_custom_call" | custom-call | bytes 4000000 | tf_op jit(solution)/shard_map/enter_rest/pallas_call | solution.py:821
  245.9 72.4 %forward0.1 = (f32[128,2048]{1,0:T(8,128)}, bf16[4,128,2048]{2,1,0:T(8,128)(2,1)}, bf16[512,512]{1,0:T(8,128)(2,1)S(1)}) custom-call(bf16[512,512]{1,0:T(8,128)(2,1)S(1)} %get-tuple-element.73.att_ref.att1_ref, bf16[512,4096]{1,0:T(8,128)(2,1)} %bitcast.86, bf16[128,2048]{1,0:T(8,128)(2,1)S(1)} %copy-done, f32[2,2048]{1,0:T(2,128)S(1)} %get-tuple-element.77.norm_ref, ...), custom_call_target="tpu_custom_call" | custom-call | bytes 4000000 | tf_op jit(solution)/shard_map/forward0/pallas_call | solution.py:885
  318.3 11.5 %cross_forward.1 = (bf16[2,128,512]{2,1,0:T(8,128)(2,1)S(1)}, bf16[512,512]{1,0:T(8,128)(2,1)S(1)}, f32[16,128,128]{2,1,0:T(8,128)}) custom-call(bf16[512,512]{1,0:T(8,128)(2,1)S(1)} %get-tuple-element.78.cq_ref, bf16[128,4096]{1,0:T(8,128)(2,1)} %bitcast.93, bf16[2048,2048]{1,0:T(8,128)(2,1)} %all-gather.10.cloned.1.call-done.w_ref, ...), custom_call_target="tpu_custom_call" | custom-call | flops 134217728 | bytes 2500000 | tf_op jit(solution)/shard_map/cross_forward/pallas_call | solution.py:1164
  329.8 74.1 %forward1.1 = (f32[128,2048]{1,0:T(8,128)S(1)}, bf16[4,128,2048]{2,1,0:T(8,128)(2,1)}) custom-call(bf16[512,512]{1,0:T(8,128)(2,1)S(1)} %get-tuple-element.81.att_ref.att2_ref, bf16[512,4096]{1,0:T(8,128)(2,1)} %bitcast.87, f32[128,2048]{1,0:T(8,128)} %get-tuple-element.82.base_ref.middle_ref, f32[2,2048]{1,0:T(2,128)S(1)} %get-tuple-element.146.norm_ref), custom_call_target="tpu_custom_call" | custom-call | bytes 4000000 | tf_op jit(solution)/shard_map/forward1/pallas_call | solution.py:885
  404.9 7.5 all-gather.16.cloned.1.call-done
  412.4 30.3 %ffn.1 = (bf16[512,2048]{1,0:T(8,128)(2,1)}, bf16[512,2048]{1,0:T(8,128)(2,1)}, bf16[2048,2048]{1,0:T(8,128)(2,1)}, bf16[512,8192]{1,0:T(8,128)(2,1)}) custom-call(bf16[512,2048]{1,0:T(8,128)(2,1)} %bitcast.96, bf16[2048,2048]{1,0:T(8,128)(2,1)} %all-gather.12.cloned.1.call-done.up_ref.w_hbm, bf16[512,8192]{1,0:T(8,128)(2,1)} %bitcast.90, ...), custom_call_target="tpu_custom_call" | custom-call | flops 2684354560 | bytes 7500000 | tf_op jit(solution)/shard_map/ffn/pallas_call | solution.py:1185
  443.9 82.3 %back1.1 = (f32[128,2048]{1,0:T(8,128)}, bf16[4,128,2048]{2,1,0:T(8,128)(2,1)}, bf16[512,512]{1,0:T(8,128)(2,1)S(1)}, f32[8,2048]{1,0:T(8,128)S(1)}) custom-call(bf16[512,2048]{1,0:T(8,128)(2,1)} %get-tuple-element.88.dy_ref, bf16[2048,2048]{1,0:T(8,128)(2,1)} %all-gather.12.cloned.1.call-done.up_ref.w_hbm, bf16[128,2048]{1,0:T(8,128)(2,1)S(1)} %copy-done.2, ...), custom_call_target="tpu_custom_call" | custom-call | bytes 4000000 | tf_op jit(solution)/shard_map/back1/pallas_call | solution.py:919
  526.2 10.3 %cross_back.1 = (bf16[512,512]{1,0:T(8,128)(2,1)S(1)}, bf16[2048,2048]{1,0:T(8,128)(2,1)}) custom-call(bf16[512,512]{1,0:T(8,128)(2,1)S(1)} %get-tuple-element.90.back_ref, bf16[512,512]{1,0:T(8,128)(2,1)S(1)} %get-tuple-element.78.cq_ref, bf16[2,128,512]{2,1,0:T(8,128)(2,1)S(1)} %get-tuple-element.91.kv_ref, f32[16,128,128]{2,1,0:T(8,128)} %get-tuple-element.92.share_ref, ...), custom_call_target="tpu_custom_call" | custom-call | flops 134217728 | bytes 2500000 | tf_op jit(solution)/shard_map/cross_back/pallas_call | solution.py:1217
  536.6 72.1 %back0.1 = (f32[128,2048]{1,0:T(8,128)}, bf16[4,128,2048]{2,1,0:T(8,128)(2,1)}, bf16[512,512]{1,0:T(8,128)(2,1)S(1)}, f32[8,2048]{1,0:T(8,128)S(1)}) custom-call(bf16[512,512]{1,0:T(8,128)(2,1)S(1)} %get-tuple-element.93.dy_ref.dcq_ref, bf16[2048,2048]{1,0:T(8,128)(2,1)} %all-gather.8.cloned.1.call-done.w_ref.rest_0_.w_hbm.refs_4_, ...), custom_call_target="tpu_custom_call" | custom-call | bytes 4000000 | tf_op jit(solution)/shard_map/back0/pallas_call | solution.py:919
  608.6 6.4 outs_grad.1
  615.1 15.3 %self_back.1 = (bf16[512,1536]{1,0:T(8,128)(2,1)}, bf16[2048,2048]{1,0:T(8,128)(2,1)}) custom-call(bf16[512,512]{1,0:T(8,128)(2,1)S(1)} %get-tuple-element.95.back_ref, bf16[3,512,512]{2,1,0:T(8,128)(2,1)} %get-tuple-element.96.proj_ref, f32[16,128,128]{2,1,0:T(8,128)} %copy-done.3, bf16[512,2048]{1,0:T(8,128)(2,1)} %bitcast.92, bf16[512,2048]{1,0:T(8,128)(2,1)} %bitcast.97, ...), custom_call_target="tpu_custom_call" | custom-call | flops 536870912 | bytes 3125000 | tf_op jit(solution)/shard_map/self_back/pallas_call | solution.py:1255
  631.7 108.3 %leave_up.1 = (bf16[8,64,2048]{2,1,0:T(8,128)(2,1)}, bf16[8,64,2048]{2,1,0:T(8,128)(2,1)}, bf16[128,2048]{1,0:T(8,128)(2,1)S(1)}, bf16[128,2048]{1,0:T(8,128)(2,1)S(1)}, f32[8,2048]{1,0:T(8,128)S(1)}) custom-call(s32[2,576]{1,0:T(2,128)S(1)} %concatenate.36.refs_0_, bf16[1,64,8192]{2,1,0:T(8,128)(2,1)} %bitcast.101, bf16[4,64,2048]{2,1,0:T(8,128)(2,1)} %bitcast.102, ...), custom_call_target="tpu_custom_call" | custom-call | bytes 4000000 | tf_op jit(solution)/shard_map/leave_up/pallas_call | solution.py:860
  741.4 51.2 %leave_text.1 = bf16[8,64,2048]{2,1,0:T(8,128)(2,1)} custom-call(s32[2,576]{1,0:T(2,128)S(1)} %concatenate.36.refs_0_, bf16[4,64,2048]{2,1,0:T(8,128)(2,1)S(1)} %bitcast.84), custom_call_target="tpu_custom_call" | custom-call | bytes 4000000 | tf_op jit(solution)/shard_map/leave_text/pallas_call | solution.py:860
  792.6 11.2 %multiply_subtract_fusion.1 = (f32[512,2048]{1,0:T(8,128)}, f32[512,2048]{1,0:T(8,128)}, f32[512,2048]{1,0:T(8,128)}) fusion(f32[512,2048]{1,0:T(8,128)} %refs_1_.5, bf16[8,64,2048]{2,1,0:T(8,128)(2,1)} %leave_text.1, f32[512,2048]{1,0:T(8,128)} %param.49, f32[512,2048]{1,0:T(8,128)} %param.48), kind=kLoop, calls=%fused_computation.21 | loop fusion | flops 16777216 | bytes 27262976 | tf_op jit(solution)/shard_map/sub | solution.py:52
  803.8 1.6 copy-done.10
  806.5 8.4 multiply_subtract_fusion.3
  816.3 7.1 multiply_subtract_fusion.2
  823.4 14.1 %reduce-scatter.12.cloned.1.call-done = bf16[256,2048]{1,0:T(8,128)(2,1)} async-done(((bf16[2048,2048]{1,0:T(8,128)(2,1)}), bf16[256,2048]{1,0:T(8,128)(2,1)}) %reduce-scatter.12.cloned.1.call-update) | async-done | bytes 1048592 | tf_op jit(solution)/shard_map/reduce_scatter | solution.py:1373
  838.6 59.8 %leave_query.1 = (bf16[8,64,2048]{2,1,0:T(8,128)(2,1)}, bf16[8,64,1024]{2,1,0:T(8,128)(2,1)S(1)}, f32[8,256]{1,0:T(8,128)S(1)}) custom-call(s32[2,576]{1,0:T(2,128)S(1)} %concatenate.36.refs_0_, bf16[4,64,2048]{2,1,0:T(8,128)(2,1)} %bitcast.103, bf16[1,64,4096]{2,1,0:T(8,128)(2,1)S(1)} %bitcast.85, f32[8,2048]{1,0:T(8,128)S(1)} %pad_maximum_fusion.refs_3_), custom_call_target="tpu_custom_call" | custom-call | bytes 4000000 | tf_op jit(solution)/shard_map/leave_query/pallas_call | solution.py:860
  898.4 10.3 %multiply_subtract_fusion = (f32[512,2048]{1,0:T(8,128)}, f32[512,2048]{1,0:T(8,128)}, f32[512,2048]{1,0:T(8,128)}) fusion(f32[512,2048]{1,0:T(8,128)} %refs_1_.3, bf16[8,64,2048]{2,1,0:T(8,128)(2,1)} %get-tuple-element.115, f32[512,2048]{1,0:T(8,128)} %param.40, f32[512,2048]{1,0:T(8,128)} %param.39), kind=kLoop, calls=%fused_computation.20 | loop fusion | flops 16777216 | bytes 27262976 | tf_op jit(solution)/shard_map/sub | solution.py:52
  909.9 4.0 multiply_subtract_fusion.4
  (118 shorter events, 16.7 us)
Async XLA Ops:
  7.2 57.6 %copy-start = (bf16[128,2048]{1,0:T(8,128)(2,1)S(1)}, bf16[128,2048]{1,0:T(8,128)(2,1)}, u32[]{:S(2)}) copy-start(bf16[128,2048]{1,0:T(8,128)(2,1)} %refs_6_.1) | copy-start | bytes 1572868
  7.2 57.6 %copy-start.6 = (bf16[32,4096]{1,0:T(8,128)(2,1)S(1)}, bf16[32,4096]{1,0:T(8,128)(2,1)}, u32[]{:S(2)}) copy-start(bf16[32,4096]{1,0:T(8,128)(2,1)} %refs_3_.2) | copy-start | bytes 786436
  7.2 115.9 %all-gather.8.cloned.1.call-start = ((), (), s32[]{:S(2)}) async-start(), calls=%async_computation.5 | async-start | bytes 9437184 | tf_op jit(solution)/shard_map/all_gather | solution.py:1370
  64.8 181.2 %all-gather.14.cloned.1.call-start = ((), (), s32[]{:S(2)}) async-start(), calls=%async_computation.13 | async-start | bytes 4718592 | tf_op jit(solution)/shard_map/all_gather | solution.py:1370
  122.6 195.7 %all-gather.10.cloned.1.call-start = ((), (), s32[]{:S(2)}) async-start(), calls=%async_computation.6 | async-start | bytes 9437184 | tf_op jit(solution)/shard_map/all_gather | solution.py:1370
  123.1 12.8 %copy-start.2 = (bf16[128,2048]{1,0:T(8,128)(2,1)S(1)}, bf16[128,2048]{1,0:T(8,128)(2,1)}, u32[]{:S(2)}) copy-start(bf16[128,2048]{1,0:T(8,128)(2,1)} %base_ref.3) | copy-start | bytes 1572868
  135.9 108.8 %copy-start.3 = (f32[16,128,128]{2,1,0:T(8,128)}, f32[16,128,128]{2,1,0:T(8,128)S(1)}, u32[]{:S(2)}) copy-start(f32[16,128,128]{2,1,0:T(8,128)S(1)} %get-tuple-element.97.share_ref) | copy-start | bytes 3145732
  244.7 160.2 %all-gather.12.cloned.1.call-start = ((), (), s32[]{:S(2)}) async-start(), calls=%async_computation.7 | async-start | bytes 9437184 | tf_op jit(solution)/shard_map/all_gather | solution.py:1370
  245.3 167.1 %all-gather.16.cloned.1.call-start = ((), (), s32[]{:S(2)}) async-start(), calls=%async_computation.14 | async-start | bytes 9437184 | tf_op jit(solution)/shard_map/all_gather | solution.py:1370
  245.8 385.9 %reduce-scatter.6.cloned.1.call-start = ((), (), s32[]{:S(2)}) async-start(), calls=%async_computation.8 | async-start | bytes 9437184 | tf_op jit(solution)/shard_map/reduce_scatter | solution.py:1373
  442.7 189.0 %reduce-scatter.8.cloned.1.call-start = ((), (), s32[]{:S(2)}) async-start(), calls=%async_computation.9 | async-start | bytes 9437184 | tf_op jit(solution)/shard_map/reduce_scatter | solution.py:1373
  443.4 296.7 %reduce-scatter.10.cloned.1.call-start = ((), (), s32[]{:S(2)}) async-start(), calls=%async_computation.10 | async-start | bytes 9437184 | tf_op jit(solution)/shard_map/reduce_scatter | solution.py:1373
  536.5 286.9 %reduce-scatter.14.cloned.1.call-start = ((), (), s32[]{:S(2)}) async-start(), calls=%async_computation.12 | async-start | bytes 4718592 | tf_op jit(solution)/shard_map/reduce_scatter | solution.py:1373
  615.0 222.5 %reduce-scatter.12.cloned.1.call-start = ((), (), s32[]{:S(2)}) async-start(), calls=%async_computation.11 | async-start | bytes 9437184 | tf_op jit(solution)/shard_map/reduce_scatter | solution.py:1373
  792.6 11.2 %copy-start.7 = (f32[512,2048]{1,0:T(8,128)S(1)}, f32[512,2048]{1,0:T(8,128)}, u32[]{:S(2)}) copy-start(f32[512,2048]{1,0:T(8,128)} %refs_2_.3) | copy-start | bytes 12582916
  792.6 12.8 %copy-start.10 = (f32[512,2048]{1,0:T(8,128)S(1)}, f32[512,2048]{1,0:T(8,128)}, u32[]{:S(2)}) copy-start(f32[512,2048]{1,0:T(8,128)} %param.43) | copy-start | bytes 12582916
  792.6 13.9 %copy-start.11 = (f32[512,2048]{1,0:T(8,128)S(1)}, f32[512,2048]{1,0:T(8,128)}, u32[]{:S(2)}) copy-start(f32[512,2048]{1,0:T(8,128)} %param.42) | copy-start | bytes 12582916
  806.5 8.4 copy-start.8
  806.5 8.4 copy-start.12
  806.5 9.7 %copy-start.13 = (f32[512,2048]{1,0:T(8,128)S(1)}, f32[512,2048]{1,0:T(8,128)}, u32[]{:S(2)}) copy-start(f32[512,2048]{1,0:T(8,128)} %param.51) | copy-start | bytes 12582916
  898.4 10.4 %copy-start.9 = (f32[512,1024]{1,0:T(8,128)S(1)}, f32[512,1024]{1,0:T(8,128)}, u32[]{:S(2)}) copy-start(f32[512,1024]{1,0:T(8,128)} %refs_1_.4) | copy-start | bytes 6291460
  898.4 10.4 %copy-start.14 = (f32[512,1024]{1,0:T(8,128)S(1)}, f32[512,1024]{1,0:T(8,128)}, u32[]{:S(2)}) copy-start(f32[512,1024]{1,0:T(8,128)} %param.46) | copy-start | bytes 6291460
  898.4 11.5 %copy-start.15 = (f32[512,1024]{1,0:T(8,128)S(1)}, f32[512,1024]{1,0:T(8,128)}, u32[]{:S(2)}) copy-start(f32[512,1024]{1,0:T(8,128)} %param.45) | copy-start | bytes 6291460
  909.9 4.0 copy-start.18
  (10 other events, 15.0 us)
Sparse Core Ops, SparseCore 0:
  64.9 58.0 all-gather.7
  124.8 53.4 all-gather.13
  244.8 55.1 all-gather.9
  301.7 54.4 all-gather.11
  358.0 54.3 all-gather.15
  442.8 71.2 reduce-scatter.5
  518.0 71.3 reduce-scatter.7
  592.8 107.2 reduce-scatter.9
  704.4 50.3 reduce-scatter.13
  758.1 79.3 reduce-scatter.11

commit v6 on v5

--- a/solution.py
+++ b/solution.py
@@ -360,16 +360,19 @@
         return taken[0] if count is None else taken
 
 
-def enter_kernel(weights, gathers, order, normed, hidden, *refs):
+def enter_kernel(weights, gathers, order, normed, hidden, inner, inner_counts, *refs):
     refs = Refs(refs)
     n_dp, n_z = lax.axis_size("dp"), lax.axis_size("fsdp")
     slots_ref = refs.take()
     w_refs = refs.take(len(weights))
     in_refs = refs.take(len(gathers))
     norm_in = refs.take() if normed or hidden else None
+    inner_refs = refs.take(inner_counts[0])
     row_refs = refs.take(len(weights))
     full_refs = refs.take(len(gathers))
     norm_out = refs.take() if normed else None
+    inner_refs += refs.take(inner_counts[1])
+    inner_refs += refs.take(inner_counts[2])
     loads = []
     for w_ref in w_refs:
         stage, sem = refs.take(2)
@@ -384,7 +387,7 @@
     lines = []
     for in_ref, full_ref in zip(in_refs, full_refs):
         rows = in_ref.shape[0]
-        step = rows // SUBS if rows >= 16 * SUBS else rows
+        step = rows // pieces_of(rows)
         lines.append(Blocks(Line(n_z, rows, step), full_ref, *refs.take(2)))
     swaps = []
     for (stage, load), (places, split, _) in zip(loads, weights):
@@ -402,7 +405,8 @@
             if jump:
                 swap.copy(jump).start()
         swaps.append(swap)
-    work = refs.take()
+    if hidden:
+        work = refs.take()
     for index, (in_ref, full_ref, blocks) in enumerate(zip(in_refs, full_refs, lines)):
         line = blocks.line
         if hidden and index == 0:
@@ -428,7 +432,12 @@
         share = norm_in.shape[1]
         for index in range(n_dp):
             norm_out[:, index * share : (index + 1) * share] = parts[index]
+    if inner is not None:
+        inner(*inner_refs)
     shares = []
+    for blocks in lines:
+        for sub in range(blocks.line.rows // blocks.line.step):
+            blocks.forward_all(sub)
     for swap, row_ref, (places, split, first) in zip(swaps, row_refs, weights):
         swap.wait()
         if split:
@@ -443,9 +452,6 @@
         if split:
             share.start()
             share.keep()
-    for blocks in lines:
-        for sub in range(blocks.line.rows // blocks.line.step):
-            blocks.forward_all(sub)
     for share in shares:
         share.wait()
     for one in [*swaps, *shares, *lines]:
@@ -562,7 +568,7 @@
     return pltpu.make_async_copy(source.at[:, pl.ds(index * columns, columns)], target, sem)
 
 
-def forward_kernel(n, order, half, wide, att_ref, outs_hbm, base_ref, norm_ref, *rest):
+def forward_kernel(n, order, half, wide, alone, att_ref, outs_hbm, base_ref, norm_ref, *rest):
     if wide:
         next_hbm, middle_ref, full_ref, result_ref = rest[:4]
         *rest, next_ref, next_sem = rest[4:]
@@ -578,7 +584,8 @@
         load_next = fetch_columns(next_hbm, 3, next_ref, next_sem)
         load_next.start()
     line = Line(n, rows, step)
-    line.greet()
+    if alone:
+        line.greet()
     load_outs.wait()
     sums = Sums(line, part, held, s_send, s_recv)
     blocks = Blocks(line, full_ref, b_send, b_recv)
@@ -769,6 +776,10 @@
 LINK_COST = 4_000_000
 
 
+def pieces_of(rows):
+    return max(1, rows * SUBS // 128)
+
+
 class Order:
     def __init__(self, pieces, width):
         self.pieces, self.width = pieces, width
@@ -778,9 +789,13 @@
     return [pltpu.SemaphoreType.DMA((n,)), pltpu.SemaphoreType.DMA((n,))]
 
 
-def enter_call(name, ident, slots, weights, gathers, norms, normed, hidden, n, n_dp, width):
+def enter_call(
+    name, ident, slots, weights, gathers, norms, normed, hidden, n, n_dp, width, inner=None
+):
     chunk = weights[0][0].shape[0] // n_dp
-    outs, scratch = [], []
+    run, inner_args, inner_specs, inner_outs, scratch = inner or (None, [], [], [], [])
+    counts = (len(inner_args), len(inner_outs), len(scratch))
+    outs, scratch = [], list(scratch)
     for array, places, split, _ in weights:
         parts = n if split else 1
         outs.append(shape((parts, chunk, len(places) // parts * BLK), bf16))
@@ -790,14 +805,14 @@
     for array, _ in gathers:
         rows = array.shape[0]
         outs.append(shape((n, *array.shape), array.dtype))
-        scratch += sem_pair(n, SUBS if rows >= 16 * SUBS else 1)
+        scratch += sem_pair(n, pieces_of(rows))
     if normed:
         outs.append(shape((norms.shape[0], n_dp * norms.shape[1]), f32))
     for array, _, _, _ in weights:
         slots_shape = (n_dp, array.shape[1] // BLK, chunk, BLK)
         scratch += [pltpu.VMEM(slots_shape, bf16)] * 2 + swap_sems(n_dp)
-    rows = gathers[0][0].shape[0]
-    scratch.append(pltpu.VMEM((rows // SUBS if hidden else 8, width), f32))
+    if hidden:
+        scratch.append(pltpu.VMEM((gathers[0][0].shape[0] // SUBS, width), f32))
     for array, moved in gathers[1 if hidden else 0 :]:
         if moved:
             scratch.append(pltpu.VMEM(array.shape, f32))
@@ -810,6 +825,9 @@
     if normed or hidden:
         args.append(norms)
         specs.append(whole_vmem())
+    args += inner_args
+    specs += inner_specs
+    outs += inner_outs
     kernel = functools.partial(
         enter_kernel,
         [weight[1:] for weight in weights],
@@ -817,6 +835,8 @@
         Order(shuffle_order(n, n_dp), width),
         normed,
         hidden,
+        run,
+        counts,
     )
     return line_call(kernel, name, ident, outs, specs, scratch, 0, LINK_COST)(*args)
 
@@ -860,7 +880,7 @@
     return line_call(kernel, name, ident, outs, specs, scratch, 0, LINK_COST)(*args)
 
 
-def forward_call(attended, outs_z, half, base, norm_rows, after, n, n_dp, ident):
+def forward_parts(attended, outs_z, half, base, norm_rows, after, n, n_dp, alone):
     rows, width = base.shape
     share = outs_z.shape[0]
     outs = [shape((rows, width), f32), shape((n, rows, width), bf16)]
@@ -880,7 +900,16 @@
         specs.append(in_place())
         args.append(after)
         scratch += [pltpu.VMEM((width, share), bf16), pltpu.SemaphoreType.DMA]
-    kernel = functools.partial(forward_kernel, n, shuffle_order(n, n_dp), half, after is not None)
+    kernel = functools.partial(
+        forward_kernel, n, shuffle_order(n, n_dp), half, after is not None, alone
+    )
+    return kernel, args, specs, outs, scratch
+
+
+def forward_call(attended, outs_z, half, base, norm_rows, after, n, n_dp, ident):
+    kernel, args, specs, outs, scratch = forward_parts(
+        attended, outs_z, half, base, norm_rows, after, n, n_dp, True
+    )
     call = line_call(kernel, f"forward{half}", ident, outs, specs, scratch, 0, LINK_COST)
     return call(*args)
 
@@ -1013,25 +1042,32 @@
         attend_forward(cq_ref, kv_ref.at[0], kv_ref.at[1], mask_ref, False, att_ref, share_ref)
 
 
-def ffn_kernel(h_ref, up_ref, down_ref, grad_ref, du_ref, branch_ref, gup_ref, gdown_ref, total):
-    tile = pl.program_id(0)
+def ffn_kernel(h_ref, up_ref, grad_ref, act_ref, slope_ref, gdown_ref):
     up_values = dot(h_ref[...], up_ref[...])
     chance = 0.5 * (1.0 + lax.erf(up_values * 0.5**0.5))
     density = jnp.exp(-0.5 * up_values * up_values) * 0.3989422804014327
     activated = (up_values * chance).astype(bf16)
+    act_ref[...] = activated
+    slope_ref[...] = chance + up_values * density
+    gdown_ref[...] = dot_tn(activated, grad_ref[...]).astype(bf16)
+
+
+def ffn_back_kernel(
+    h_ref, down_ref, grad_ref, act_ref, slope_ref, du_ref, branch_ref, gup_ref, total
+):
+    tile = pl.program_id(0)
     back_act = dot_nt(grad_ref[...], down_ref[...])
-    back_up = (back_act * (chance + up_values * density)).astype(bf16)
+    back_up = (back_act * slope_ref[...]).astype(bf16)
     du_ref[...] = back_up
     gup_ref[...] = dot_tn(h_ref[...], back_up).astype(bf16)
-    gdown_ref[...] = dot_tn(activated, grad_ref[...]).astype(bf16)
 
     @pl.when(tile == 0)
     def _():
-        total[...] = dot(activated, down_ref[...])
+        total[...] = dot(act_ref[...], down_ref[...])
 
     @pl.when(tile > 0)
     def _():
-        total[...] += dot(activated, down_ref[...])
+        total[...] += dot(act_ref[...], down_ref[...])
 
     @pl.when(tile == 3)
     def _():
@@ -1179,35 +1215,58 @@
     )(cross_query, text_all, text_z, mask)
 
 
-def ffn(hidden, up_z, down_z, grad_all):
+def ffn(hidden, up_z, grad_all):
     tokens, width = hidden.shape
-    share = down_z.shape[0]
+    share = up_z.shape[1] // 4
     return local_call(
         ffn_kernel,
         "ffn",
         4,
         (
             shape((tokens, 4 * share), bf16),
+            shape((tokens, 4 * share), f32),
+            shape((share, 4 * width), bf16),
+        ),
+        [fixed(hidden.shape), moving((width, share), lambda t: t), fixed(grad_all.shape)],
+        (
+            moving((tokens, share), lambda t: t),
+            moving((tokens, share), lambda t: t),
+            moving((share, width), lambda t: t),
+        ),
+        [],
+        16 * tokens * width * share,
+        30_000_000,
+    )(hidden, up_z, grad_all)
+
+
+def ffn_back(hidden, down_z, grad_all, activated, slope):
+    tokens, width = hidden.shape
+    share = down_z.shape[0]
+    return local_call(
+        ffn_back_kernel,
+        "ffn_back",
+        4,
+        (
+            shape((tokens, 4 * share), bf16),
             shape((tokens, width), bf16),
-            shape(up_z.shape, bf16),
-            shape(down_z.shape, bf16),
+            shape((width, 4 * share), bf16),
         ),
         [
             fixed(hidden.shape),
-            moving((width, share), lambda t: t),
             moving((share, width), lambda t: t),
             fixed(grad_all.shape),
+            moving((tokens, share), lambda t: t),
+            moving((tokens, share), lambda t: t),
         ],
         (
             moving((tokens, share), lambda t: t),
             fixed((tokens, width)),
             moving((width, share), lambda t: t),
-            moving((share, width), lambda t: t),
         ),
         [pltpu.VMEM((tokens, width), f32)],
-        40 * tokens * width * share,
-        60_000_000,
-    )(hidden, up_z, down_z, grad_all)
+        24 * tokens * width * share,
+        40_000_000,
+    )(hidden, down_z, grad_all, activated, slope)
 
 
 def cross_back(back_attended, cross_query, text_pairs, shares, text_all, rows):
@@ -1377,12 +1436,13 @@
     marks = jnp.concatenate([seg_ids, capt_ids], axis=1)
     marks = jnp.pad(marks, ((0, 7), (0, 256 - marks.shape[1])))
     norms = jnp.pad(norm_weight, ((0, 2), (0, 0)))
-    query_rows, marks, norm_full = enter_call(
+    half = token_count // 2
+    query_rows, grad_low, marks, norm_full = enter_call(
         "enter_query",
         0,
         slots,
         [(w_query, split_places, True, firsts[0])],
-        [(marks, False)],
+        [(grad_out[:half], False), (marks, False)],
         norms,
         True,
         False,
@@ -1390,12 +1450,12 @@
         n_dp,
         width,
     )
-    outs_rows, hidden1, text_all = enter_call(
+    outs_rows, hidden1, text_all, grad_high = enter_call(
         "enter_outs",
         6,
         slots,
         [(w_outs, out_places, False, firsts[1])],
-        [(tokens_in, True), (text_in, True)],
+        [(tokens_in, True), (text_in, True), (grad_out[half:], False)],
         norm_full[0:2],
         False,
         True,
@@ -1404,6 +1464,7 @@
         width,
     )
     query_z, outs_z = spread(query_rows), spread(outs_rows)
+    grad_all = jnp.concatenate([grad_low, grad_high], axis=1).reshape(-1, width)
     hidden1 = hidden1.reshape(-1, width)
     text_all = text_all.reshape(-1, text_in.shape[1])
     segment = marks[:, 0, :token_count]
@@ -1416,16 +1477,15 @@
     ).astype(jnp.int32)
 
     projected, attended1, shares1 = self_forward(hidden1, query_z, self_mask)
-    text_rows, up_rows, down_rows, grad_all = enter_call(
-        "enter_rest",
+    text_rows, up_rows = enter_call(
+        "enter_text",
         7,
         after(slots, attended1),
         [
             (w_text, split_places, True, firsts[2]),
             (w_up, split_places, True, firsts[3]),
-            (w_down, big_places, False, firsts[4]),
         ],
-        [(grad_out, False)],
+        [],
         None,
         False,
         False,
@@ -1433,20 +1493,41 @@
         n_dp,
         width,
     )
-    grad_all = grad_all.reshape(-1, width)
+    down_rows, middle1, hidden2, cross_query = enter_call(
+        "forward0",
+        1,
+        slots,
+        [(w_down, big_places, False, firsts[4])],
+        [],
+        None,
+        False,
+        False,
+        n_z,
+        n_dp,
+        width,
+        forward_parts(
+            attended1,
+            outs_z,
+            0,
+            tokens_in,
+            after(norm_full[2:4], up_rows),
+            query_z,
+            n_z,
+            n_dp,
+            False,
+        ),
+    )
+    hidden2 = hidden2.reshape(-1, width)
     text_z, up_z, down_z = spread(text_rows), spread(up_rows), spread(down_rows)
-    middle1, hidden2, cross_query = forward_call(
-        attended1, outs_z, 0, tokens_in, after(norm_full[2:4], up_rows), query_z, n_z, n_dp, 1
-    )
-    hidden2 = hidden2.reshape(-1, width)
     text_pairs, attended2, shares2 = cross_forward(cross_query, text_all, text_z, cross_mask)
     middle2, hidden3 = forward_call(
         attended2, outs_z, 1, middle1, norm_full[4:6], None, n_z, n_dp, 2
     )
     hidden3 = hidden3.reshape(-1, width)
-    back_up, branch3, up_part, down_part = ffn(hidden3, up_z, down_z, grad_all)
+    activated, slope, down_part = ffn(hidden3, up_z, grad_all)
+    down_sum = gather_sum(down_part, 1)
+    back_up, branch3, up_part = ffn_back(hidden3, down_z, grad_all, activated, slope)
     branch3 = branch3.reshape(n_z, token_count, width)
-    down_sum = gather_sum(down_part, 1)
     up_sum = gather_sum(up_part, n_z)
     at_middle2, carry2, back_att2, term3 = back_call(
         back_up, up_z, 0, grad_out, middle2, norm_full[4:6], outs_z, 1, n_z, n_dp, 3
@@ -1460,11 +1541,11 @@
         back_cross, query_z, 3, at_middle2, middle1, norm_full[2:4], outs_z, 0, n_z, n_dp, 4
     )
     carry1 = carry1.reshape(-1, width)
-    outs_sum = gather_sum(outs_grad(attended1, carry1, attended2, carry2), 1)
     back_projected, query_part = self_back(
         back_att1, projected, shares1, hidden1, hidden2, back_cross, token_count
     )
     query_sum = gather_sum(query_part, n_z)
+    outs_sum = gather_sum(outs_grad(after(attended1, query_part), carry1, attended2, carry2), 1)
     down_grad, up_grad, grad_in, result, term1 = leave_call(
         "leave_up",
         8,
@@ -1504,15 +1585,21 @@
     text_new = adamw_update(w_text, m_text, v_text, text_grad, rate_text, decay_rate)
     down_new = adamw_update(w_down, m_down, v_down, down_grad, rate_down, decay_rate)
     norm_term = jnp.concatenate([term1[:2], term2[:2], term3[:4]], axis=0)
-    query_grad, outs_slots, norm_grad = leave_call(
+    query_grad, norm_grad = leave_call(
         "leave_query",
         9,
         after(contents, (up_new, down_new, text_new)),
-        [
-            (query_sum, True, cap_big, slot_firsts[0]),
-            (outs_sum, False, cap_out, slot_firsts[1]),
-        ],
+        [(query_sum, True, cap_big, slot_firsts[0])],
         norm_term,
+        n_z,
+        n_dp,
+    )
+    (outs_slots,) = leave_call(
+        "leave_outs",
+        10,
+        after(contents, query_grad),
+        [(outs_sum, False, cap_out, slot_firsts[1])],
+        None,
         n_z,
         n_dp,
     )

time: 936 us -> 935 us (level)
  waiting for transfers between devices: 23.6 us -> 0.82 us
  Pallas kernels: 827 us -> 844 us
    pallas_call x2 -> x1, Pallas kernels: 146 us -> 72.7 us  [forward_call(): return call(*args)]
    pallas_call x3 -> x4, Pallas kernels: 221 us -> 291 us  [enter_call(): line_call(kernel, name, ident, outs, specs, scratch, 0, LINK_COST)(*args)]
    pallas_call x0 -> x1, Pallas kernels: none -> 21 us  [ffn_back(): local_call(ffn_back_kernel, 'ffn_back', 4, (shape((tokens, 4 * share), bf...]
    pallas_call x1, Pallas kernels: 30.3 us -> 15.1 us  [ffn(): local_call(ffn_kernel, 'ffn', 4, (shape((tokens, 4 * share), bf16), shape...]
    reduce_scatter x5, waiting for transfers between devices: 14.2 us -> 0.08 us  [gather_sum(): summed = lax.psum_scatter(piece, 'dp', scatter_dimension=0, tiled=True)]
    pallas_call x3 -> x4, Pallas kernels: 219 us -> 232 us  [leave_call(): line_call(kernel, name, ident, outs, specs, scratch, 0, LINK_COST)(*args)]
  transfers between devices with their start and end apart: 10 -> 10, of which waited for: 2 -> 0; matrix products, arithmetic and copies ran while one was open for 3% -> 4% of each run, Pallas kernels for 74% -> 84%
where the time goes in v6:
time: 935 us; the launch traced here: 925 us
  Pallas kernels  844 us (90%)
  other arithmetic  47.4 us (5%)
  local copies, waits for them, and re-layouts  16.5 us (2%)
  between operations  15 us (2%)
    pallas_call x4, Pallas kernels, enter_call(): line_call(kernel, name, ident, outs, specs, scratch, 0, LINK_COST)(*args)  291 us
    pallas_call x4, Pallas kernels, leave_call(): line_call(kernel, name, ident, outs, specs, scratch, 0, LINK_COST)(*args)  232 us
    pallas_call x2, Pallas kernels, back_call(): return call(dy, weight, base, middle, norm_rows, outs_z)  157 us
    pallas_call x1, Pallas kernels, forward_call(): return call(*args)  72.7 us
    sub x6, other arithmetic, adamw_update(): weight - rate * (first_hat / (jnp.sqrt(second_hat) + adam_eps) + decay *...  42.3 us
    pallas_call x1, Pallas kernels, ffn_back(): local_call(ffn_back_kernel, 'ffn_back', 4, (shape((tokens, 4 * share), bf...  21 us
  transfers between devices with their start and end apart: 10, of which 0 were waited for; matrix products, arithmetic and copies ran while one was open for 4% of the time, Pallas kernels for 84%

profile of v6, /device:TPU:0, one launch (start us, length us, event | category | flops | bytes accessed | tf_op | source)
XLA Modules:
  0.0 924.9 jit_solution(8231220922715624201)
XLA Ops:
  11.5 47.0 %enter_query.1 = (bf16[4,64,2048]{2,1,0:T(8,128)(2,1)}, bf16[4,64,2048]{2,1,0:T(8,128)(2,1)}, s32[4,8,256]{2,1,0:T(8,128)S(1)}, f32[8,2048]{1,0:T(8,128)S(1)}) custom-call(s32[2,288]{1,0:T(2,128)S(1)} %pad_add_fusion.refs_0_, f32[512,2048]{1,0:T(8,128)} %refs_1_.4, bf16[64,2048]{1,0:T(8,128)(2,1)S(1)} %get-tuple-element.154.refs_2_, ...), custom_call_target="tpu_custom_call" | custom-call | bytes 4000000 | tf_op jit(solution)/shard_map/enter_query/pallas_call | solution.py:841
  58.7 82.5 %enter_outs.1 = (bf16[1,64,4096]{2,1,0:T(8,128)(2,1)}, bf16[4,128,2048]{2,1,0:T(8,128)(2,1)}, bf16[4,32,4096]{2,1,0:T(8,128)(2,1)}, bf16[4,64,2048]{2,1,0:T(8,128)(2,1)}) custom-call(s32[2,288]{1,0:T(2,128)S(1)} %pad_add_fusion.refs_0_, f32[512,1024]{1,0:T(8,128)} %refs_1_.5, bf16[128,2048]{1,0:T(8,128)(2,1)S(1)} %copy-done, bf16[32,4096]{1,0:T(8,128)(2,1)S(1)} %copy-done.7, ...), custom_call_target="tpu_custom_call" | custom-call | bytes 4000000 | tf_op jit(solution)/shard_map/enter_outs/pallas_call | solution.py:841
  141.6 12.7 %self_forward.1 = (bf16[3,512,512]{2,1,0:T(8,128)(2,1)}, bf16[512,512]{1,0:T(8,128)(2,1)S(1)}, f32[16,128,128]{2,1,0:T(8,128)S(1)}) custom-call(bf16[512,2048]{1,0:T(8,128)(2,1)} %bitcast.96, bf16[2048,2048]{1,0:T(8,128)(2,1)} %all-gather.8.cloned.1.call-done.w_ref.refs_6_.w_hbm.refs_4_, s32[4,128,128]{2,1,0:T(8,128)S(1)} %get-tuple-element.160.mask_ref), custom_call_target="tpu_custom_call" | custom-call | flops 402653184 | bytes 2500000 | tf_op jit(solution)/shard_map/self_forward/pallas_call | solution.py:1181
  155.3 76.3 %enter_text.1 = (bf16[4,64,2048]{2,1,0:T(8,128)(2,1)}, bf16[4,64,2048]{2,1,0:T(8,128)(2,1)}) custom-call(s32[2,288]{1,0:T(2,128)S(1)} %pad_add_fusion.refs_0_, f32[512,2048]{1,0:T(8,128)} %refs_1_.6, f32[512,2048]{1,0:T(8,128)} %refs_2_.3), custom_call_target="tpu_custom_call" | custom-call | bytes 4000000 | tf_op jit(solution)/shard_map/enter_text/pallas_call | solution.py:841
  232.4 85.3 %forward0.1 = (bf16[1,64,8192]{2,1,0:T(8,128)(2,1)}, f32[128,2048]{1,0:T(8,128)}, bf16[4,128,2048]{2,1,0:T(8,128)(2,1)}, bf16[512,512]{1,0:T(8,128)(2,1)S(1)}) custom-call(s32[2,288]{1,0:T(2,128)S(1)} %pad_add_fusion.refs_0_, f32[512,2048]{1,0:T(8,128)} %refs_1_.7, bf16[512,512]{1,0:T(8,128)(2,1)S(1)} %get-tuple-element.122.refs_2_.att1_ref, ...), custom_call_target="tpu_custom_call" | custom-call | bytes 4000000 | tf_op jit(solution)/shard_map/forward0/pallas_call | solution.py:841
  318.0 2.8 pad_maximum_fusion
  320.8 11.5 %cross_forward.1 = (bf16[2,128,512]{2,1,0:T(8,128)(2,1)S(1)}, bf16[512,512]{1,0:T(8,128)(2,1)S(1)}, f32[16,128,128]{2,1,0:T(8,128)}) custom-call(bf16[512,512]{1,0:T(8,128)(2,1)S(1)} %get-tuple-element.82.cq_ref, bf16[128,4096]{1,0:T(8,128)(2,1)} %bitcast.98, bf16[2048,2048]{1,0:T(8,128)(2,1)} %all-gather.10.cloned.1.call-done.w_ref, ...), custom_call_target="tpu_custom_call" | custom-call | flops 134217728 | bytes 2500000 | tf_op jit(solution)/shard_map/cross_forward/pallas_call | solution.py:1200
  332.3 72.7 %forward1.1 = (f32[128,2048]{1,0:T(8,128)S(1)}, bf16[4,128,2048]{2,1,0:T(8,128)(2,1)}) custom-call(bf16[512,512]{1,0:T(8,128)(2,1)S(1)} %get-tuple-element.85.att_ref.att2_ref, bf16[512,4096]{1,0:T(8,128)(2,1)} %bitcast.88, f32[128,2048]{1,0:T(8,128)} %get-tuple-element.86.base_ref.middle_ref, f32[2,2048]{1,0:T(2,128)S(1)} %get-tuple-element.156.norm_ref), custom_call_target="tpu_custom_call" | custom-call | bytes 4000000 | tf_op jit(solution)/shard_map/forward1/pallas_call | solution.py:914
  406.0 15.1 %ffn.1 = (bf16[512,2048]{1,0:T(8,128)(2,1)}, f32[512,2048]{1,0:T(8,128)}, bf16[512,8192]{1,0:T(8,128)(2,1)}) custom-call(bf16[512,2048]{1,0:T(8,128)(2,1)} %bitcast.94, bf16[2048,2048]{1,0:T(8,128)(2,1)} %all-gather.12.cloned.1.call-done.up_ref.w_hbm, bf16[512,2048]{1,0:T(8,128)(2,1)} %bitcast.91), custom_call_target="tpu_custom_call" | custom-call | flops 1073741824 | bytes 3750000 | tf_op jit(solution)/shard_map/ffn/pallas_call | solution.py:1221
  421.1 21.0 %ffn_back.1 = (bf16[512,2048]{1,0:T(8,128)(2,1)}, bf16[512,2048]{1,0:T(8,128)(2,1)}, bf16[2048,2048]{1,0:T(8,128)(2,1)}) custom-call(bf16[512,2048]{1,0:T(8,128)(2,1)} %bitcast.95, bf16[512,8192]{1,0:T(8,128)(2,1)} %bitcast.93, bf16[512,2048]{1,0:T(8,128)(2,1)} %bitcast.92, bf16[512,2048]{1,0:T(8,128)(2,1)} %get-tuple-element.92.act_ref, ...), custom_call_target="tpu_custom_call" | custom-call | flops 1610612736 | bytes 5000000 | tf_op jit(solution)/shard_map/ffn_back/pallas_call | solution.py:1245
  443.2 81.9 %back1.1 = (f32[128,2048]{1,0:T(8,128)}, bf16[4,128,2048]{2,1,0:T(8,128)(2,1)}, bf16[512,512]{1,0:T(8,128)(2,1)S(1)}, f32[8,2048]{1,0:T(8,128)S(1)}) custom-call(bf16[512,2048]{1,0:T(8,128)(2,1)} %get-tuple-element.95.dy_ref, bf16[2048,2048]{1,0:T(8,128)(2,1)} %all-gather.12.cloned.1.call-done.up_ref.w_hbm, bf16[128,2048]{1,0:T(8,128)(2,1)S(1)} %copy-done.2, ...), custom_call_target="tpu_custom_call" | custom-call | bytes 4000000 | tf_op jit(solution)/shard_map/back1/pallas_call | solution.py:948
  525.1 9.9 %cross_back.1 = (bf16[512,512]{1,0:T(8,128)(2,1)S(1)}, bf16[2048,2048]{1,0:T(8,128)(2,1)}) custom-call(bf16[512,512]{1,0:T(8,128)(2,1)S(1)} %get-tuple-element.97.back_ref, bf16[512,512]{1,0:T(8,128)(2,1)S(1)} %get-tuple-element.82.cq_ref, bf16[2,128,512]{2,1,0:T(8,128)(2,1)S(1)} %get-tuple-element.98.kv_ref, f32[16,128,128]{2,1,0:T(8,128)} %get-tuple-element.99.share_ref, ...), custom_call_target="tpu_custom_call" | custom-call | flops 134217728 | bytes 2500000 | tf_op jit(solution)/shard_map/cross_back/pallas_call | solution.py:1276
  535.1 75.4 %back0.1 = (f32[128,2048]{1,0:T(8,128)}, bf16[4,128,2048]{2,1,0:T(8,128)(2,1)}, bf16[512,512]{1,0:T(8,128)(2,1)S(1)}, f32[8,2048]{1,0:T(8,128)S(1)}) custom-call(bf16[512,512]{1,0:T(8,128)(2,1)S(1)} %get-tuple-element.100.dy_ref.dcq_ref, bf16[2048,2048]{1,0:T(8,128)(2,1)} %all-gather.8.cloned.1.call-done.w_ref.refs_6_.w_hbm.refs_4_, ...), custom_call_target="tpu_custom_call" | custom-call | bytes 4000000 | tf_op jit(solution)/shard_map/back0/pallas_call | solution.py:948
  610.6 15.2 %self_back.1 = (bf16[512,1536]{1,0:T(8,128)(2,1)}, bf16[2048,2048]{1,0:T(8,128)(2,1)}) custom-call(bf16[512,512]{1,0:T(8,128)(2,1)S(1)} %get-tuple-element.102.back_ref, bf16[3,512,512]{2,1,0:T(8,128)(2,1)} %get-tuple-element.103.proj_ref, f32[16,128,128]{2,1,0:T(8,128)} %copy-done.3, bf16[512,2048]{1,0:T(8,128)(2,1)} %bitcast.97, ...), custom_call_target="tpu_custom_call" | custom-call | flops 536870912 | bytes 3125000 | tf_op jit(solution)/shard_map/self_back/pallas_call | solution.py:1314
  626.6 6.1 outs_grad.1
  633.8 108.1 %leave_up.1 = (bf16[8,64,2048]{2,1,0:T(8,128)(2,1)}, bf16[8,64,2048]{2,1,0:T(8,128)(2,1)}, bf16[128,2048]{1,0:T(8,128)(2,1)S(1)}, bf16[128,2048]{1,0:T(8,128)(2,1)S(1)}, f32[8,2048]{1,0:T(8,128)S(1)}) custom-call(s32[2,576]{1,0:T(2,128)S(1)} %concatenate.39.refs_0_, bf16[1,64,8192]{2,1,0:T(8,128)(2,1)} %bitcast.104, bf16[4,64,2048]{2,1,0:T(8,128)(2,1)} %bitcast.105, ...), custom_call_target="tpu_custom_call" | custom-call | bytes 4000000 | tf_op jit(solution)/shard_map/leave_up/pallas_call | solution.py:880
  743.1 52.8 %leave_text.1 = bf16[8,64,2048]{2,1,0:T(8,128)(2,1)} custom-call(s32[2,576]{1,0:T(2,128)S(1)} %concatenate.39.refs_0_, bf16[4,64,2048]{2,1,0:T(8,128)(2,1)S(1)} %bitcast.84), custom_call_target="tpu_custom_call" | custom-call | bytes 4000000 | tf_op jit(solution)/shard_map/leave_text/pallas_call | solution.py:880
  796.0 10.1 %multiply_subtract_fusion.3 = (f32[512,2048]{1,0:T(8,128)}, f32[512,2048]{1,0:T(8,128)}, f32[512,2048]{1,0:T(8,128)}) fusion(f32[512,2048]{1,0:T(8,128)} %refs_2_.3, bf16[8,64,2048]{2,1,0:T(8,128)(2,1)S(1)} %copy-done.15, f32[512,2048]{1,0:T(8,128)} %param.43, f32[512,2048]{1,0:T(8,128)} %param.42), kind=kLoop, calls=%fused_computation.23 | loop fusion | flops 16777216 | bytes 27262976 | tf_op jit(solution)/shard_map/sub | solution.py:52
  809.5 7.2 multiply_subtract_fusion.2
  817.9 7.5 multiply_subtract_fusion.1
  826.7 49.2 %leave_query.1 = (bf16[8,64,2048]{2,1,0:T(8,128)(2,1)}, f32[8,256]{1,0:T(8,128)S(1)}) custom-call(s32[2,576]{1,0:T(2,128)S(1)} %concatenate.39.refs_0_, bf16[4,64,2048]{2,1,0:T(8,128)(2,1)S(1)} %bitcast.85, f32[8,2048]{1,0:T(8,128)S(1)} %pad_maximum_fusion.1.refs_2_), custom_call_target="tpu_custom_call" | custom-call | bytes 4000000 | tf_op jit(solution)/shard_map/leave_query/pallas_call | solution.py:880
  875.9 10.0 %multiply_subtract_fusion = (f32[512,2048]{1,0:T(8,128)}, f32[512,2048]{1,0:T(8,128)}, f32[512,2048]{1,0:T(8,128)}) fusion(f32[512,2048]{1,0:T(8,128)} %refs_1_.4, bf16[8,64,2048]{2,1,0:T(8,128)(2,1)} %get-tuple-element.120, f32[512,2048]{1,0:T(8,128)} %param.40, f32[512,2048]{1,0:T(8,128)} %param.39), kind=kLoop, calls=%fused_computation.20 | loop fusion | flops 16777216 | bytes 27262976 | tf_op jit(solution)/shard_map/sub | solution.py:52
  886.9 21.6 %leave_outs.1 = bf16[8,64,1024]{2,1,0:T(8,128)(2,1)S(1)} custom-call(s32[2,576]{1,0:T(2,128)S(1)} %concatenate.39.refs_0_, bf16[1,64,4096]{2,1,0:T(8,128)(2,1)S(1)} %bitcast.86), custom_call_target="tpu_custom_call" | custom-call | bytes 4000000 | tf_op jit(solution)/shard_map/leave_outs/pallas_call | solution.py:880
  908.5 6.9 multiply_subtract_fusion.4
  (124 shorter events, 20.9 us)
Async XLA Ops:
  7.2 51.5 %copy-start = (bf16[128,2048]{1,0:T(8,128)(2,1)S(1)}, bf16[128,2048]{1,0:T(8,128)(2,1)}, u32[]{:S(2)}) copy-start(bf16[128,2048]{1,0:T(8,128)(2,1)} %refs_6_.1) | copy-start | bytes 1572868
  7.2 51.5 %copy-start.7 = (bf16[32,4096]{1,0:T(8,128)(2,1)S(1)}, bf16[32,4096]{1,0:T(8,128)(2,1)}, u32[]{:S(2)}) copy-start(bf16[32,4096]{1,0:T(8,128)(2,1)} %refs_3_.1) | copy-start | bytes 786436
  7.2 134.4 %all-gather.8.cloned.1.call-start = ((), (), s32[]{:S(2)}) async-start(), calls=%async_computation.5 | async-start | bytes 9437184 | tf_op jit(solution)/shard_map/all_gather | solution.py:1429
  58.6 173.8 %all-gather.14.cloned.1.call-start = ((), (), s32[]{:S(2)}) async-start(), calls=%async_computation.13 | async-start | bytes 4718592 | tf_op jit(solution)/shard_map/all_gather | solution.py:1429
  141.2 179.6 %all-gather.10.cloned.1.call-start = ((), (), s32[]{:S(2)}) async-start(), calls=%async_computation.6 | async-start | bytes 9437184 | tf_op jit(solution)/shard_map/all_gather | solution.py:1429
  231.7 174.2 %all-gather.12.cloned.1.call-start = ((), (), s32[]{:S(2)}) async-start(), calls=%async_computation.7 | async-start | bytes 9437184 | tf_op jit(solution)/shard_map/all_gather | solution.py:1429
  232.3 188.8 %all-gather.16.cloned.1.call-start = ((), (), s32[]{:S(2)}) async-start(), calls=%async_computation.14 | async-start | bytes 9437184 | tf_op jit(solution)/shard_map/all_gather | solution.py:1429
  232.4 85.6 %copy-start.16 = (bf16[4,64,2048]{2,1,0:T(8,128)(2,1)S(1)}, bf16[4,64,2048]{2,1,0:T(8,128)(2,1)}, u32[]{:S(2)}) copy-start(bf16[4,64,2048]{2,1,0:T(8,128)(2,1)} %get-tuple-element.88) | copy-start | bytes 3145732
  317.7 316.0 %reduce-scatter.6.cloned.1.call-start = ((), (), s32[]{:S(2)}) async-start(), calls=%async_computation.8 | async-start | bytes 9437184 | tf_op jit(solution)/shard_map/reduce_scatter | solution.py:1432
  421.1 212.7 %reduce-scatter.8.cloned.1.call-start = ((), (), s32[]{:S(2)}) async-start(), calls=%async_computation.9 | async-start | bytes 9437184 | tf_op jit(solution)/shard_map/reduce_scatter | solution.py:1432
  442.2 299.7 %reduce-scatter.10.cloned.1.call-start = ((), (), s32[]{:S(2)}) async-start(), calls=%async_computation.10 | async-start | bytes 9437184 | tf_op jit(solution)/shard_map/reduce_scatter | solution.py:1432
  535.1 290.4 %reduce-scatter.12.cloned.1.call-start = ((), (), s32[]{:S(2)}) async-start(), calls=%async_computation.11 | async-start | bytes 9437184 | tf_op jit(solution)/shard_map/reduce_scatter | solution.py:1432
  625.9 260.0 %reduce-scatter.14.cloned.1.call-start = ((), (), s32[]{:S(2)}) async-start(), calls=%async_computation.12 | async-start | bytes 4718592 | tf_op jit(solution)/shard_map/reduce_scatter | solution.py:1432
  743.1 52.8 %copy-start.15 = (bf16[8,64,2048]{2,1,0:T(8,128)(2,1)S(1)}, bf16[8,64,2048]{2,1,0:T(8,128)(2,1)}, u32[]{:S(2)}) copy-start(bf16[8,64,2048]{2,1,0:T(8,128)(2,1)} %get-tuple-element.111) | copy-start | bytes 6291460
  795.9 10.2 %copy-start.9 = (f32[512,2048]{1,0:T(8,128)S(1)}, f32[512,2048]{1,0:T(8,128)}, u32[]{:S(2)}) copy-start(f32[512,2048]{1,0:T(8,128)} %refs_1_.7) | copy-start | bytes 12582916
  796.0 11.7 %copy-start.11 = (f32[512,2048]{1,0:T(8,128)S(1)}, f32[512,2048]{1,0:T(8,128)}, u32[]{:S(2)}) copy-start(f32[512,2048]{1,0:T(8,128)} %param.52) | copy-start | bytes 12582916
  796.0 12.9 %copy-start.12 = (f32[512,2048]{1,0:T(8,128)S(1)}, f32[512,2048]{1,0:T(8,128)}, u32[]{:S(2)}) copy-start(f32[512,2048]{1,0:T(8,128)} %param.51) | copy-start | bytes 12582916
  796.0 13.5 %copy-start.14 = (bf16[8,64,2048]{2,1,0:T(8,128)(2,1)S(1)}, bf16[8,64,2048]{2,1,0:T(8,128)(2,1)}, u32[]{:S(2)}) copy-start(bf16[8,64,2048]{2,1,0:T(8,128)(2,1)} %get-tuple-element.112) | copy-start | bytes 6291460
  809.5 7.2 copy-start.8
  809.5 7.2 copy-start.10
  809.5 8.4 copy-start.13
  908.5 6.9 copy-start.17
  908.5 6.9 copy-start.18
  908.5 6.9 copy-start.19
  (11 other events, 9.8 us)
Sparse Core Ops, SparseCore 0:
  58.7 64.5 all-gather.7
  141.3 64.5 all-gather.13
  231.8 76.6 all-gather.9
  310.3 54.4 all-gather.11
  366.5 54.3 all-gather.15
  424.2 71.2 reduce-scatter.5
  499.4 71.2 reduce-scatter.7
  574.1 85.2 reduce-scatter.9
  663.3 71.8 reduce-scatter.11
  738.4 70.6 reduce-scatter.13

commit v7 on v6

--- a/solution.py
+++ b/solution.py
@@ -192,9 +192,11 @@
                         self.move(way, target, sub, held).wait_send()
 
 
-def relay(n, sums, blocks, settle):
+def relay(n, sums, blocks, settle, hook=None):
     for slot in range((SUBS + 2) * (n - 1)):
         sub, time = divmod(slot, n - 1)
+        if hook is not None and slot == SUBS * (n - 1):
+            hook()
         if sub < SUBS:
             for one in sums:
                 one.forward(sub, time)
@@ -244,10 +246,6 @@
                 @pl.when(line.has(way))
                 def _():
                     self.move(way, source, sub).start()
-
-    def forward_all(self, sub):
-        for step in range(1, self.line.n):
-            self.forward(sub, step)
 
     def finish(self):
         line = self.line
@@ -432,13 +430,10 @@
         share = norm_in.shape[1]
         for index in range(n_dp):
             norm_out[:, index * share : (index + 1) * share] = parts[index]
-    if inner is not None:
-        inner(*inner_refs)
     shares = []
-    for blocks in lines:
-        for sub in range(blocks.line.rows // blocks.line.step):
-            blocks.forward_all(sub)
-    for swap, row_ref, (places, split, first) in zip(swaps, row_refs, weights):
+
+    def compact(index):
+        swap, row_ref, (places, split, first) = swaps[index], row_refs[index], weights[index]
         swap.wait()
         if split:
             cut, *sems = refs.take(3)
@@ -452,6 +447,17 @@
         if split:
             share.start()
             share.keep()
+
+    ahead = 0
+    if inner is not None:
+        ahead = 1
+        inner(*inner_refs, hook=lambda: compact(0))
+    for step in range(1, n_z):
+        for blocks in lines:
+            for sub in range(blocks.line.rows // blocks.line.step):
+                blocks.forward(sub, step)
+    for index in range(ahead, len(weights)):
+        compact(index)
     for share in shares:
         share.wait()
     for one in [*swaps, *shares, *lines]:
@@ -487,6 +493,38 @@
         full_ref[line.at, here, group * BLK : (group + 1) * BLK] = value.astype(bf16)
 
     reorder(load, store, rows, width, orders)
+
+
+def expand_slots(slots_ref, rows, cut, blocks, capacity, first):
+    columns = rows.shape[2] // BLK
+    for part in range(rows.shape[0]):
+        for column in range(columns):
+            blocks[part * columns + column] = rows[part, :, column * BLK : (column + 1) * BLK]
+    for owner in range(cut.shape[0]):
+        for position in range(capacity):
+            slot = first + owner * capacity + position
+            value = blocks[slots_ref[0, slot]].astype(f32)
+            live = slots_ref[1, slot].astype(f32)
+            cut[owner, :, position * BLK : (position + 1) * BLK] = (value * live).astype(bf16)
+
+
+def expand_call(slots, rows, capacity, first, n_dp):
+    chunk = rows.shape[1]
+    blocks = rows.shape[0] * rows.shape[2] // BLK
+
+    def kernel(slots_ref, row_ref, cut, blocks):
+        expand_slots(slots_ref, row_ref, cut, blocks, capacity, first)
+
+    return pl.pallas_call(
+        kernel,
+        name="expand",
+        out_shape=shape((n_dp, chunk, capacity * BLK), bf16),
+        in_specs=[pl.BlockSpec(memory_space=pltpu.SMEM), whole_vmem()],
+        out_specs=whole_vmem(),
+        scratch_shapes=[pltpu.VMEM((blocks, chunk, BLK), bf16)],
+        compiler_params=pltpu.CompilerParams(vmem_limit_bytes=VMEM_CAP),
+        cost_estimate=pl.CostEstimate(flops=0, bytes_accessed=1_000_000, transcendentals=0),
+    )(slots, rows)
 
 
 def leave_kernel(weights, summed, inner, inner_counts, *refs):
@@ -510,7 +548,7 @@
         term_swap.start()
         term_swap.keep()
     shares = []
-    for row_ref, (split, _, _) in zip(row_refs, weights):
+    for row_ref, (split, _, _, _) in zip(row_refs, weights):
         if split:
             held, *sems = refs.take(3)
             share = Swap("fsdp", row_ref, held, *sems)
@@ -526,25 +564,18 @@
         total_spread.start()
         others[total_spread.me] = total[...]
     swaps = []
-    for row_ref, out_ref, share, (split, capacity, first) in zip(
+    for row_ref, out_ref, share, (split, capacity, first, whole) in zip(
         row_refs, out_refs, shares, weights
     ):
         if split:
             share.wait()
         rows = share.target if split else row_ref
+        if not whole:
+            expand_slots(slots_ref, rows, out_ref, refs.take(), capacity, first)
+            continue
         cut, *sems, blocks = refs.take(4)
-        columns = rows.shape[2] // BLK
-        for part in range(rows.shape[0]):
-            for column in range(columns):
-                blocks[part * columns + column] = rows[part, :, column * BLK : (column + 1) * BLK]
+        expand_slots(slots_ref, rows, cut, blocks, capacity, first)
         swap = Swap("dp", cut, out_ref, *sems)
-        for owner in range(n_dp):
-
-            for position in range(capacity):
-                slot = first + owner * capacity + position
-                value = blocks[slots_ref[0, slot]].astype(f32)
-                live = slots_ref[1, slot].astype(f32)
-                cut[owner, :, position * BLK : (position + 1) * BLK] = (value * live).astype(bf16)
         swap.start()
         swap.keep()
         swaps.append(swap)
@@ -568,7 +599,9 @@
     return pltpu.make_async_copy(source.at[:, pl.ds(index * columns, columns)], target, sem)
 
 
-def forward_kernel(n, order, half, wide, alone, att_ref, outs_hbm, base_ref, norm_ref, *rest):
+def forward_kernel(
+    n, order, half, wide, alone, att_ref, outs_hbm, base_ref, norm_ref, *rest, hook=None
+):
     if wide:
         next_hbm, middle_ref, full_ref, result_ref = rest[:4]
         *rest, next_ref, next_sem = rest[4:]
@@ -613,7 +646,7 @@
         reorder(load, store, step, width, order)
         blocks.start(sub)
 
-    relay(n, [sums], blocks, settle)
+    relay(n, [sums], blocks, settle, hook)
     if wide:
         load_next.wait()
 
@@ -647,7 +680,7 @@
 
 
 def back_kernel(
-    n, order, column, half, dy_ref, w_hbm, base_ref, middle_ref, norm_ref, outs_hbm, *rest
+    n, order, column, half, alone, dy_ref, w_hbm, base_ref, middle_ref, norm_ref, outs_hbm, *rest
 ):
     carry_ref, full_ref, att_ref, term_ref = rest[:4]
     part, held, work, plain, s_send, s_recv, b_send, b_recv = rest[4:12]
@@ -659,7 +692,8 @@
     load_outs = fetch_columns(outs_hbm, half, outs_ref, outs_sem)
     load_outs.start()
     line = Line(n, rows, step)
-    line.greet()
+    if alone:
+        line.greet()
     load_w.wait()
     sums = Sums(line, part, held, s_send, s_recv)
     blocks = Blocks(line, full_ref, b_send, b_recv)
@@ -861,13 +895,14 @@
     if term is not None:
         scratch += [pltpu.VMEM((n_dp, *block), f32)] * 2 + swap_sems(n_dp)
         scratch += [pltpu.VMEM(block, f32), pltpu.VMEM((n, *block), f32), *swap_sems(n)]
-    for rows, split, _, _ in weights:
+    for rows, split, _, _, _ in weights:
         if split:
             scratch += [pltpu.VMEM(rows.shape, bf16), *swap_sems(n)]
-    for rows, _, capacity, _ in weights:
+    for rows, _, capacity, _, whole in weights:
         slots_shape = (n_dp, chunk, capacity * BLK)
         outs.append(shape(slots_shape, bf16))
-        scratch += [pltpu.VMEM(slots_shape, bf16), *swap_sems(n_dp)]
+        if whole:
+            scratch += [pltpu.VMEM(slots_shape, bf16), *swap_sems(n_dp)]
         blocks = rows.shape[0] * rows.shape[2] // BLK
         scratch.append(pltpu.VMEM((blocks, chunk, BLK), bf16))
     if term is not None:
@@ -914,7 +949,7 @@
     return call(*args)
 
 
-def back_call(dy, weight, column, base, middle, norm_rows, outs_z, half, n, n_dp, ident):
+def back_parts(dy, weight, column, base, middle, norm_rows, outs_z, half, n, n_dp, alone):
     rows, width = base.shape
     share = outs_z.shape[0]
     outs = [
@@ -943,9 +978,16 @@
         pltpu.VMEM((share, width), bf16),
         pltpu.SemaphoreType.DMA,
     ]
-    kernel = functools.partial(back_kernel, n, unshuffle_order(n, n_dp), column, half)
+    kernel = functools.partial(back_kernel, n, unshuffle_order(n, n_dp), column, half, alone)
+    return kernel, [dy, weight, base, middle, norm_rows, outs_z], specs, outs, scratch
+
+
+def back_call(dy, weight, column, base, middle, norm_rows, outs_z, half, n, n_dp, ident):
+    kernel, args, specs, outs, scratch = back_parts(
+        dy, weight, column, base, middle, norm_rows, outs_z, half, n, n_dp, True
+    )
     call = line_call(kernel, f"back{half}", ident, outs, specs, scratch, 0, LINK_COST)
-    return call(dy, weight, base, middle, norm_rows, outs_z)
+    return call(*args)
 
 
 def last_parts(dy, weight, base, tokens, norm_rows, branch, middle, n, n_dp):
@@ -1477,14 +1519,11 @@
     ).astype(jnp.int32)
 
     projected, attended1, shares1 = self_forward(hidden1, query_z, self_mask)
-    text_rows, up_rows = enter_call(
+    (text_rows,) = enter_call(
         "enter_text",
         7,
         after(slots, attended1),
-        [
-            (w_text, split_places, True, firsts[2]),
-            (w_up, split_places, True, firsts[3]),
-        ],
+        [(w_text, split_places, True, firsts[2])],
         [],
         None,
         False,
@@ -1493,11 +1532,11 @@
         n_dp,
         width,
     )
-    down_rows, middle1, hidden2, cross_query = enter_call(
+    up_rows, down_rows, middle1, hidden2, cross_query = enter_call(
         "forward0",
         1,
         slots,
-        [(w_down, big_places, False, firsts[4])],
+        [(w_up, split_places, True, firsts[3]), (w_down, big_places, False, firsts[4])],
         [],
         None,
         False,
@@ -1510,7 +1549,7 @@
             outs_z,
             0,
             tokens_in,
-            after(norm_full[2:4], up_rows),
+            after(norm_full[2:4], text_rows),
             query_z,
             n_z,
             n_dp,
@@ -1537,8 +1576,27 @@
         back_att2, cross_query, text_pairs, shares2, text_all, token_count
     )
     text_sum = gather_sum(text_part, n_z)
-    at_middle1, carry1, back_att1, term2 = back_call(
-        back_cross, query_z, 3, at_middle2, middle1, norm_full[2:4], outs_z, 0, n_z, n_dp, 4
+    down_grad, at_middle1, carry1, back_att1, term2 = leave_call(
+        "back0",
+        4,
+        contents,
+        [(down_sum, False, cap_big, slot_firsts[4], True)],
+        None,
+        n_z,
+        n_dp,
+        back_parts(
+            back_cross,
+            query_z,
+            3,
+            at_middle2,
+            middle1,
+            after(norm_full[2:4], back_cross),
+            outs_z,
+            0,
+            n_z,
+            n_dp,
+            False,
+        ),
     )
     carry1 = carry1.reshape(-1, width)
     back_projected, query_part = self_back(
@@ -1546,14 +1604,11 @@
     )
     query_sum = gather_sum(query_part, n_z)
     outs_sum = gather_sum(outs_grad(after(attended1, query_part), carry1, attended2, carry2), 1)
-    down_grad, up_grad, grad_in, result, term1 = leave_call(
+    up_grad, grad_in, result, term1 = leave_call(
         "leave_up",
         8,
         contents,
-        [
-            (down_sum, False, cap_big, slot_firsts[4]),
-            (up_sum, True, cap_big, slot_firsts[3]),
-        ],
+        [(up_sum, True, cap_big, slot_firsts[3], True)],
         None,
         n_z,
         n_dp,
@@ -1569,14 +1624,25 @@
             n_dp,
         ),
     )
-    (text_grad,) = leave_call(
-        "leave_text",
-        5,
-        after(contents, term1),
-        [(text_sum, True, cap_big, slot_firsts[2])],
-        None,
+    norm_term = jnp.concatenate([term1[:2], term2[:2], term3[:4]], axis=0)
+    text_grad, query_slots, norm_grad = leave_call(
+        "leave_query",
+        9,
+        contents,
+        [
+            (text_sum, True, cap_big, slot_firsts[2], True),
+            (query_sum, True, cap_big, slot_firsts[0], False),
+        ],
+        norm_term,
         n_z,
         n_dp,
+    )
+    query_grad = lax.all_to_all(query_slots, "dp", 0, 0, tiled=True)
+    outs_slots = expand_call(after(contents, query_slots), outs_sum, cap_out, slot_firsts[1], n_dp)
+    outs_slots = lax.all_to_all(outs_slots, "dp", 0, 0, tiled=True)
+    norm_grad = norm_grad[:6]
+    query_grad, outs_slots = (
+        grad.reshape(own_rows, -1).astype(f32) for grad in (query_grad, outs_slots)
     )
     text_grad, up_grad, down_grad = (
         grad.reshape(own_rows, -1).astype(f32) for grad in (text_grad, up_grad, down_grad)
@@ -1584,29 +1650,6 @@
     up_new = adamw_update(w_up, m_up, v_up, up_grad, rate_up, decay_rate)
     text_new = adamw_update(w_text, m_text, v_text, text_grad, rate_text, decay_rate)
     down_new = adamw_update(w_down, m_down, v_down, down_grad, rate_down, decay_rate)
-    norm_term = jnp.concatenate([term1[:2], term2[:2], term3[:4]], axis=0)
-    query_grad, norm_grad = leave_call(
-        "leave_query",
-        9,
-        after(contents, (up_new, down_new, text_new)),
-        [(query_sum, True, cap_big, slot_firsts[0])],
-        norm_term,
-        n_z,
-        n_dp,
-    )
-    (outs_slots,) = leave_call(
-        "leave_outs",
-        10,
-        after(contents, query_grad),
-        [(outs_sum, False, cap_out, slot_firsts[1])],
-        None,
-        n_z,
-        n_dp,
-    )
-    norm_grad = norm_grad[:6]
-    query_grad, outs_slots = (
-        grad.reshape(own_rows, -1).astype(f32) for grad in (query_grad, outs_slots)
-    )
     query_new = adamw_update(w_query, m_query, v_query, query_grad, rate_query, decay_rate)
     outs_new = adamw_update(w_outs, m_outs, v_outs, outs_slots, rate_outs, decay_rate)
     norm_new = adamw_update(norm_weight, m_norm, v_norm, norm_grad, rate_norm, 0.0)

time: 935 us -> 908 us (0.971)
  Pallas kernels: 844 us -> 780 us
  waiting for transfers between devices: 0.82 us -> 31.8 us
    pallas_call x2, Pallas kernels: 157 us -> 83.2 us  [the longest x1 81.3 us: back_call(): return call(*args)]
    all_to_all x0 -> x2, waiting for transfers between devices: none -> 15.9 us  [the longest x1 11.2 us: body(): query_grad = lax.all_to_all(query_slots, 'dp', 0, 0, tiled=True)]
    reduce_scatter x5, waiting for transfers between devices: 0.08 us -> 11.5 us  [gather_sum(): summed = lax.psum_scatter(piece, 'dp', scatter_dimension=0, tiled=True)]
    pallas_call x4 -> x3, Pallas kernels: 232 us -> 241 us  [leave_call(): line_call(kernel, name, ident, outs, specs, scratch, 0, LINK_COST)(*args)]
  transfers between devices with their start and end apart: 10 -> 12, of which waited for: 0 -> 4; matrix products, arithmetic and copies ran while one was open for 4% -> 4% of each run, Pallas kernels for 84% -> 82%
where the time goes in v7:
time: 908 us; the launch traced here: 895 us
  Pallas kernels  780 us (86%)
  other arithmetic  47.7 us (5%)
  waiting for transfers between devices  31.8 us (4%)
  between operations  15.1 us (2%)
  local copies, waits for them, and re-layouts  11.4 us (1%)
    pallas_call x4, Pallas kernels, enter_call(): line_call(kernel, name, ident, outs, specs, scratch, 0, LINK_COST)(*args)  291 us
    pallas_call x3, Pallas kernels, leave_call(): line_call(kernel, name, ident, outs, specs, scratch, 0, LINK_COST)(*args)  241 us
    pallas_call x1, Pallas kernels, back_call(): return call(*args)  81.3 us
    pallas_call x1, Pallas kernels, forward_call(): return call(*args)  71.7 us
    sub x6, other arithmetic, adamw_update(): weight - rate * (first_hat / (jnp.sqrt(second_hat) + adam_eps) + decay *...  42.6 us
    pallas_call x1, Pallas kernels, ffn_back(): local_call(ffn_back_kernel, 'ffn_back', 4, (shape((tokens, 4 * share), bf...  20.9 us
  transfers between devices with their start and end apart: 12, of which 4 were waited for; matrix products, arithmetic and copies ran while one was open for 4% of the time, Pallas kernels for 82%

profile of v7, /device:TPU:0, one launch (start us, length us, event | category | flops | bytes accessed | tf_op | source)
XLA Modules:
  0.0 894.9 jit_solution(11351412438895266214)
XLA Ops:
  11.5 46.9 %enter_query.1 = (bf16[4,64,2048]{2,1,0:T(8,128)(2,1)}, bf16[4,64,2048]{2,1,0:T(8,128)(2,1)}, s32[4,8,256]{2,1,0:T(8,128)S(1)}, f32[8,2048]{1,0:T(8,128)S(1)}) custom-call(s32[2,288]{1,0:T(2,128)S(1)} %pad_add_fusion.refs_0_, f32[512,2048]{1,0:T(8,128)} %refs_1_.4, bf16[64,2048]{1,0:T(8,128)(2,1)S(1)} %get-tuple-element.152.refs_2_, ...), custom_call_target="tpu_custom_call" | custom-call | bytes 4000000 | tf_op jit(solution)/shard_map/enter_query/pallas_call | solution.py:875
  58.6 81.8 %enter_outs.1 = (bf16[1,64,4096]{2,1,0:T(8,128)(2,1)}, bf16[4,128,2048]{2,1,0:T(8,128)(2,1)}, bf16[4,32,4096]{2,1,0:T(8,128)(2,1)}, bf16[4,64,2048]{2,1,0:T(8,128)(2,1)}) custom-call(s32[2,288]{1,0:T(2,128)S(1)} %pad_add_fusion.refs_0_, f32[512,1024]{1,0:T(8,128)} %refs_1_.5, bf16[128,2048]{1,0:T(8,128)(2,1)S(1)} %copy-done, bf16[32,4096]{1,0:T(8,128)(2,1)S(1)} %copy-done.6, ...), custom_call_target="tpu_custom_call" | custom-call | bytes 4000000 | tf_op jit(solution)/shard_map/enter_outs/pallas_call | solution.py:875
  140.8 12.9 %self_forward.1 = (bf16[3,512,512]{2,1,0:T(8,128)(2,1)}, bf16[512,512]{1,0:T(8,128)(2,1)S(1)}, f32[16,128,128]{2,1,0:T(8,128)S(1)}) custom-call(bf16[512,2048]{1,0:T(8,128)(2,1)} %bitcast.95, bf16[2048,2048]{1,0:T(8,128)(2,1)} %all-gather.8.cloned.1.call-done.w_ref.refs_7_.refs_3_, s32[4,128,128]{2,1,0:T(8,128)S(1)} %get-tuple-element.158.mask_ref), custom_call_target="tpu_custom_call" | custom-call | flops 402653184 | bytes 2500000 | tf_op jit(solution)/shard_map/self_forward/pallas_call | solution.py:1223
  154.7 53.2 %enter_text.1 = bf16[4,64,2048]{2,1,0:T(8,128)(2,1)} custom-call(s32[2,288]{1,0:T(2,128)S(1)} %pad_add_fusion.refs_0_, f32[512,2048]{1,0:T(8,128)} %refs_1_.6), custom_call_target="tpu_custom_call" | custom-call | bytes 4000000 | tf_op jit(solution)/shard_map/enter_text/pallas_call | solution.py:875
  208.0 109.3 %forward0.1 = (bf16[4,64,2048]{2,1,0:T(8,128)(2,1)}, bf16[1,64,8192]{2,1,0:T(8,128)(2,1)}, f32[128,2048]{1,0:T(8,128)}, bf16[4,128,2048]{2,1,0:T(8,128)(2,1)}, bf16[512,512]{1,0:T(8,128)(2,1)S(1)}) custom-call(s32[2,288]{1,0:T(2,128)S(1)} %pad_add_fusion.refs_0_, f32[512,2048]{1,0:T(8,128)} %refs_1_.7, f32[512,2048]{1,0:T(8,128)} %refs_2_.3, ...), custom_call_target="tpu_custom_call" | custom-call | bytes 4000000 | tf_op jit(solution)/shard_map/forward0/pallas_call | solution.py:875
  320.9 11.8 %cross_forward.1 = (bf16[2,128,512]{2,1,0:T(8,128)(2,1)S(1)}, bf16[512,512]{1,0:T(8,128)(2,1)S(1)}, f32[16,128,128]{2,1,0:T(8,128)}) custom-call(bf16[512,512]{1,0:T(8,128)(2,1)S(1)} %get-tuple-element.80.cq_ref, bf16[128,4096]{1,0:T(8,128)(2,1)} %bitcast.97, bf16[2048,2048]{1,0:T(8,128)(2,1)} %all-gather.10.cloned.1.call-done.w_ref, ...), custom_call_target="tpu_custom_call" | custom-call | flops 134217728 | bytes 2500000 | tf_op jit(solution)/shard_map/cross_forward/pallas_call | solution.py:1242
  332.8 71.7 %forward1.1 = (f32[128,2048]{1,0:T(8,128)S(1)}, bf16[4,128,2048]{2,1,0:T(8,128)(2,1)}) custom-call(bf16[512,512]{1,0:T(8,128)(2,1)S(1)} %get-tuple-element.82.att_ref.att2_ref, bf16[512,4096]{1,0:T(8,128)(2,1)} %bitcast.87, f32[128,2048]{1,0:T(8,128)} %get-tuple-element.83.base_ref.refs_5_, f32[2,2048]{1,0:T(2,128)S(1)} %get-tuple-element.154.norm_ref), custom_call_target="tpu_custom_call" | custom-call | bytes 4000000 | tf_op jit(solution)/shard_map/forward1/pallas_call | solution.py:949
  405.4 15.3 %ffn.1 = (bf16[512,2048]{1,0:T(8,128)(2,1)}, f32[512,2048]{1,0:T(8,128)}, bf16[512,8192]{1,0:T(8,128)(2,1)}) custom-call(bf16[512,2048]{1,0:T(8,128)(2,1)} %bitcast.93, bf16[2048,2048]{1,0:T(8,128)(2,1)} %all-gather.12.cloned.1.call-done.up_ref.w_hbm, bf16[512,2048]{1,0:T(8,128)(2,1)} %bitcast.90), custom_call_target="tpu_custom_call" | custom-call | flops 1073741824 | bytes 3750000 | tf_op jit(solution)/shard_map/ffn/pallas_call | solution.py:1263
  424.5 20.9 %ffn_back.1 = (bf16[512,2048]{1,0:T(8,128)(2,1)}, bf16[512,2048]{1,0:T(8,128)(2,1)}, bf16[2048,2048]{1,0:T(8,128)(2,1)}) custom-call(bf16[512,2048]{1,0:T(8,128)(2,1)} %bitcast.94, bf16[512,8192]{1,0:T(8,128)(2,1)} %bitcast.92, bf16[512,2048]{1,0:T(8,128)(2,1)} %bitcast.91, bf16[512,2048]{1,0:T(8,128)(2,1)} %get-tuple-element.89.act_ref, ...), custom_call_target="tpu_custom_call" | custom-call | flops 1610612736 | bytes 5000000 | tf_op jit(solution)/shard_map/ffn_back/pallas_call | solution.py:1287
  446.5 81.3 %back1.1 = (f32[128,2048]{1,0:T(8,128)}, bf16[4,128,2048]{2,1,0:T(8,128)(2,1)}, bf16[512,512]{1,0:T(8,128)(2,1)S(1)}, f32[8,2048]{1,0:T(8,128)S(1)}) custom-call(bf16[512,2048]{1,0:T(8,128)(2,1)} %get-tuple-element.93.dy_ref, bf16[2048,2048]{1,0:T(8,128)(2,1)} %all-gather.12.cloned.1.call-done.up_ref.w_hbm, bf16[128,2048]{1,0:T(8,128)(2,1)S(1)} %copy-done.2, ...), custom_call_target="tpu_custom_call" | custom-call | bytes 4000000 | tf_op jit(solution)/shard_map/back1/pallas_call | solution.py:990
  527.7 10.3 %cross_back.1 = (bf16[512,512]{1,0:T(8,128)(2,1)S(1)}, bf16[2048,2048]{1,0:T(8,128)(2,1)}) custom-call(bf16[512,512]{1,0:T(8,128)(2,1)S(1)} %get-tuple-element.95.back_ref, bf16[512,512]{1,0:T(8,128)(2,1)S(1)} %get-tuple-element.80.cq_ref, bf16[2,128,512]{2,1,0:T(8,128)(2,1)S(1)} %get-tuple-element.96.kv_ref, f32[16,128,128]{2,1,0:T(8,128)} %get-tuple-element.97.share_ref, ...), custom_call_target="tpu_custom_call" | custom-call | flops 134217728 | bytes 2500000 | tf_op jit(solution)/shard_map/cross_back/pallas_call | solution.py:1318
  539.3 80.9 %back0.1 = (bf16[8,64,2048]{2,1,0:T(8,128)(2,1)}, f32[128,2048]{1,0:T(8,128)}, bf16[4,128,2048]{2,1,0:T(8,128)(2,1)}, bf16[512,512]{1,0:T(8,128)(2,1)S(1)}, f32[8,2048]{1,0:T(8,128)S(1)}) custom-call(s32[2,576]{1,0:T(2,128)S(1)} %concatenate.39.refs_0_.slots_ref, bf16[1,64,8192]{2,1,0:T(8,128)(2,1)} %bitcast.106, ...), custom_call_target="tpu_custom_call" | custom-call | bytes 4000000 | tf_op jit(solution)/shard_map/back0/pallas_call | solution.py:915
  620.3 15.7 %self_back.1 = (bf16[512,1536]{1,0:T(8,128)(2,1)}, bf16[2048,2048]{1,0:T(8,128)(2,1)}) custom-call(bf16[512,512]{1,0:T(8,128)(2,1)S(1)} %get-tuple-element.101.back_ref, bf16[3,512,512]{2,1,0:T(8,128)(2,1)} %get-tuple-element.102.proj_ref, f32[16,128,128]{2,1,0:T(8,128)} %copy-done.3, bf16[512,2048]{1,0:T(8,128)(2,1)} %bitcast.96, ...), custom_call_target="tpu_custom_call" | custom-call | flops 536870912 | bytes 3125000 | tf_op jit(solution)/shard_map/self_back/pallas_call | solution.py:1356
  636.1 6.3 outs_grad.1
  642.4 104.3 %leave_up.1 = (bf16[8,64,2048]{2,1,0:T(8,128)(2,1)}, bf16[128,2048]{1,0:T(8,128)(2,1)S(1)}, bf16[128,2048]{1,0:T(8,128)(2,1)S(1)}, f32[8,2048]{1,0:T(8,128)S(1)}) custom-call(s32[2,576]{1,0:T(2,128)S(1)} %concatenate.39.refs_0_.slots_ref, bf16[4,64,2048]{2,1,0:T(8,128)(2,1)} %bitcast.105, bf16[512,1536]{1,0:T(8,128)(2,1)} %get-tuple-element.105.refs_2_, ...), custom_call_target="tpu_custom_call" | custom-call | bytes 4000000 | tf_op jit(solution)/shard_map/leave_up/pallas_call | solution.py:915
  746.8 7.8 multiply_subtract_fusion.2
  755.8 55.6 %leave_query.1 = (bf16[8,64,2048]{2,1,0:T(8,128)(2,1)}, bf16[8,64,2048]{2,1,0:T(8,128)(2,1)}, f32[8,256]{1,0:T(8,128)S(1)}) custom-call(s32[2,576]{1,0:T(2,128)S(1)} %concatenate.39.refs_0_.slots_ref, bf16[4,64,2048]{2,1,0:T(8,128)(2,1)S(1)} %bitcast.84, bf16[4,64,2048]{2,1,0:T(8,128)(2,1)} %bitcast.104, f32[8,2048]{1,0:T(8,128)S(1)} %pad_maximum_fusion.1.refs_3_), custom_call_target="tpu_custom_call" | custom-call | bytes 4000000 | tf_op jit(solution)/shard_map/leave_query/pallas_call | solution.py:915
  811.5 11.5 %reduce-scatter.14.cloned.1.call-done = bf16[64,4096]{1,0:T(8,128)(2,1)} async-done(((bf16[512,4096]{1,0:T(8,128)(2,1)}), bf16[64,4096]{1,0:T(8,128)(2,1)}) %reduce-scatter.14.cloned.1.call-update) | async-done | bytes 524304 | tf_op jit(solution)/shard_map/reduce_scatter | solution.py:1474
  829.5 10.0 %multiply_subtract_fusion = (f32[512,2048]{1,0:T(8,128)}, f32[512,2048]{1,0:T(8,128)}, f32[512,2048]{1,0:T(8,128)}) fusion(f32[512,2048]{1,0:T(8,128)} %refs_2_.3, bf16[8,64,2048]{2,1,0:T(8,128)(2,1)} %get-tuple-element.122, f32[512,2048]{1,0:T(8,128)} %param.52, f32[512,2048]{1,0:T(8,128)} %param.51), kind=kLoop, calls=%fused_computation.20 | loop fusion | flops 16777216 | bytes 27262976 | tf_op jit(solution)/shard_map/sub | solution.py:52
  840.1 4.7 all-to-all-done.1
  844.8 4.6 all-to-all-start
  849.4 10.3 %multiply_subtract_fusion.1 = (f32[512,2048]{1,0:T(8,128)}, f32[512,2048]{1,0:T(8,128)}, f32[512,2048]{1,0:T(8,128)}) fusion(f32[512,2048]{1,0:T(8,128)} %refs_1_.6, bf16[8,64,2048]{2,1,0:T(8,128)(2,1)} %get-tuple-element.121, f32[512,2048]{1,0:T(8,128)} %param.49, f32[512,2048]{1,0:T(8,128)} %param.48), kind=kLoop, calls=%fused_computation.21 | loop fusion | flops 16777216 | bytes 27262976 | tf_op jit(solution)/shard_map/sub | solution.py:52
  864.9 11.2 %all-to-all-done = bf16[8,64,2048]{2,1,0:T(8,128)(2,1)} async-done(((bf16[8,64,2048]{2,1,0:T(8,128)(2,1)}), bf16[8,64,2048]{2,1,0:T(8,128)(2,1)}, u32[]{:S(2)}, u32[]{:S(2)}) %all-to-all-start) | async-done | bytes 2097184 | tf_op jit(solution)/shard_map/all_to_all | solution.py:1640
  876.1 9.9 %multiply_subtract_fusion.3 = (f32[512,2048]{1,0:T(8,128)}, f32[512,2048]{1,0:T(8,128)}, f32[512,2048]{1,0:T(8,128)}) fusion(f32[512,2048]{1,0:T(8,128)} %refs_1_.4, bf16[8,64,2048]{2,1,0:T(8,128)(2,1)} %all-to-all-done, f32[512,2048]{1,0:T(8,128)} %param.40, f32[512,2048]{1,0:T(8,128)} %param.39), kind=kLoop, calls=%fused_computation.23 | loop fusion | flops 16777216 | bytes 27262976 | tf_op jit(solution)/shard_map/sub | solution.py:52
  (119 shorter events, 31.7 us)
Async XLA Ops:
  7.2 51.4 %copy-start = (bf16[128,2048]{1,0:T(8,128)(2,1)S(1)}, bf16[128,2048]{1,0:T(8,128)(2,1)}, u32[]{:S(2)}) copy-start(bf16[128,2048]{1,0:T(8,128)(2,1)} %refs_5_.3) | copy-start | bytes 1572868
  7.2 51.4 %copy-start.6 = (bf16[32,4096]{1,0:T(8,128)(2,1)S(1)}, bf16[32,4096]{1,0:T(8,128)(2,1)}, u32[]{:S(2)}) copy-start(bf16[32,4096]{1,0:T(8,128)(2,1)} %refs_3_.1) | copy-start | bytes 786436
  7.2 133.6 %all-gather.8.cloned.1.call-start = ((), (), s32[]{:S(2)}) async-start(), calls=%async_computation.7 | async-start | bytes 9437184 | tf_op jit(solution)/shard_map/all_gather | solution.py:1471
  58.5 149.5 %all-gather.14.cloned.1.call-start = ((), (), s32[]{:S(2)}) async-start(), calls=%async_computation.15 | async-start | bytes 4718592 | tf_op jit(solution)/shard_map/all_gather | solution.py:1471
  140.4 180.5 %all-gather.10.cloned.1.call-start = ((), (), s32[]{:S(2)}) async-start(), calls=%async_computation.8 | async-start | bytes 9437184 | tf_op jit(solution)/shard_map/all_gather | solution.py:1471
  207.9 197.6 %all-gather.12.cloned.1.call-start = ((), (), s32[]{:S(2)}) async-start(), calls=%async_computation.9 | async-start | bytes 9437184 | tf_op jit(solution)/shard_map/all_gather | solution.py:1471
  208.0 110.2 %copy-start.12 = (bf16[4,64,2048]{2,1,0:T(8,128)(2,1)S(1)}, bf16[4,64,2048]{2,1,0:T(8,128)(2,1)}, u32[]{:S(2)}) copy-start(bf16[4,64,2048]{2,1,0:T(8,128)(2,1)} %get-tuple-element.86) | copy-start | bytes 3145732
  317.3 107.2 %all-gather.16.cloned.1.call-start = ((), (), s32[]{:S(2)}) async-start(), calls=%async_computation.16 | async-start | bytes 9437184 | tf_op jit(solution)/shard_map/all_gather | solution.py:1471
  317.8 221.5 %reduce-scatter.8.cloned.1.call-start = ((), (), s32[]{:S(2)}) async-start(), calls=%async_computation.11 | async-start | bytes 9437184 | tf_op jit(solution)/shard_map/reduce_scatter | solution.py:1474
  420.7 221.7 %reduce-scatter.6.cloned.1.call-start = ((), (), s32[]{:S(2)}) async-start(), calls=%async_computation.10 | async-start | bytes 9437184 | tf_op jit(solution)/shard_map/reduce_scatter | solution.py:1474
  445.4 309.2 %reduce-scatter.10.cloned.1.call-start = ((), (), s32[]{:S(2)}) async-start(), calls=%async_computation.12 | async-start | bytes 9437184 | tf_op jit(solution)/shard_map/reduce_scatter | solution.py:1474
  538.1 216.5 %reduce-scatter.12.cloned.1.call-start = ((), (), s32[]{:S(2)}) async-start(), calls=%async_computation.13 | async-start | bytes 9437184 | tf_op jit(solution)/shard_map/reduce_scatter | solution.py:1474
  636.0 186.9 %reduce-scatter.14.cloned.1.call-start = ((), (), s32[]{:S(2)}) async-start(), calls=%async_computation.14 | async-start | bytes 4718592 | tf_op jit(solution)/shard_map/reduce_scatter | solution.py:1474
  642.4 104.4 %copy-start.7 = (f32[512,2048]{1,0:T(8,128)S(1)}, f32[512,2048]{1,0:T(8,128)}, u32[]{:S(2)}) copy-start(f32[512,2048]{1,0:T(8,128)} %refs_1_.7) | copy-start | bytes 12582916
  642.4 104.4 %copy-start.9 = (f32[512,2048]{1,0:T(8,128)S(1)}, f32[512,2048]{1,0:T(8,128)}, u32[]{:S(2)}) copy-start(f32[512,2048]{1,0:T(8,128)} %param.43) | copy-start | bytes 12582916
  754.6 1.2 copy-start.4
  825.9 18.9 %all-to-all-start.1 = ((bf16[8,64,1024]{2,1,0:T(8,128)(2,1)}), bf16[8,64,1024]{2,1,0:T(8,128)(2,1)S(1)}, u32[]{:S(2)}, u32[]{:S(2)}) async-start(bf16[8,64,1024]{2,1,0:T(8,128)(2,1)} %expand.1), calls=%async_computation.6 | async-start | bytes 2097152 | tf_op jit(solution)/shard_map/all_to_all | solution.py:1642
  829.4 10.0 %copy-start.13 = (f32[6,256]{1,0:T(8,128)S(1)}, f32[6,256]{1,0:T(8,128)}, u32[]{:S(2)}) copy-start(f32[6,256]{1,0:T(8,128)} %param.53) | copy-start | bytes 18436
  829.5 10.0 %copy-start.14 = (f32[6,256]{1,0:T(8,128)S(1)}, f32[6,256]{1,0:T(8,128)}, u32[]{:S(2)}) copy-start(f32[6,256]{1,0:T(8,128)} %param.55) | copy-start | bytes 18436
  829.5 10.0 %copy-start.15 = (f32[6,256]{1,0:T(8,128)S(1)}, f32[6,256]{1,0:T(8,128)}, u32[]{:S(2)}) copy-start(f32[6,256]{1,0:T(8,128)} %param.54) | copy-start | bytes 18436
  844.8 31.3 %all-to-all-start = ((bf16[8,64,2048]{2,1,0:T(8,128)(2,1)}), bf16[8,64,2048]{2,1,0:T(8,128)(2,1)}, u32[]{:S(2)}, u32[]{:S(2)}) async-start(bf16[8,64,2048]{2,1,0:T(8,128)(2,1)} %get-tuple-element.115), calls=%async_computation.4 | async-start | bytes 4194304 | tf_op jit(solution)/shard_map/all_to_all | solution.py:1640
  849.4 10.4 %copy-start.8 = (f32[512,1024]{1,0:T(8,128)S(1)}, f32[512,1024]{1,0:T(8,128)}, u32[]{:S(2)}) copy-start(f32[512,1024]{1,0:T(8,128)} %refs_1_.5) | copy-start | bytes 6291460
  849.4 10.4 %copy-start.10 = (f32[512,1024]{1,0:T(8,128)S(1)}, f32[512,1024]{1,0:T(8,128)}, u32[]{:S(2)}) copy-start(f32[512,1024]{1,0:T(8,128)} %param.46) | copy-start | bytes 6291460
  849.4 11.5 %copy-start.11 = (f32[512,1024]{1,0:T(8,128)S(1)}, f32[512,1024]{1,0:T(8,128)}, u32[]{:S(2)}) copy-start(f32[512,1024]{1,0:T(8,128)} %param.45) | copy-start | bytes 6291460
  (9 other events, 7.7 us)
Sparse Core Ops, SparseCore 0:
  58.6 64.5 all-gather.7
  140.5 54.2 all-gather.13
  208.0 90.3 all-gather.9
  317.4 50.9 all-gather.11
  370.1 54.3 all-gather.15
  427.8 71.2 reduce-scatter.7
  503.0 89.8 reduce-scatter.5
  596.3 81.8 reduce-scatter.9
  682.0 67.1 reduce-scatter.11
  753.0 69.8 reduce-scatter.13

commit v8 on v7

--- a/solution.py
+++ b/solution.py
@@ -495,7 +495,7 @@
     reorder(load, store, rows, width, orders)
 
 
-def expand_slots(slots_ref, rows, cut, blocks, capacity, first):
+def expand_slots(slots_ref, rows, cut, blocks, capacity, first, offset):
     columns = rows.shape[2] // BLK
     for part in range(rows.shape[0]):
         for column in range(columns):
@@ -505,26 +505,8 @@
             slot = first + owner * capacity + position
             value = blocks[slots_ref[0, slot]].astype(f32)
             live = slots_ref[1, slot].astype(f32)
-            cut[owner, :, position * BLK : (position + 1) * BLK] = (value * live).astype(bf16)
-
-
-def expand_call(slots, rows, capacity, first, n_dp):
-    chunk = rows.shape[1]
-    blocks = rows.shape[0] * rows.shape[2] // BLK
-
-    def kernel(slots_ref, row_ref, cut, blocks):
-        expand_slots(slots_ref, row_ref, cut, blocks, capacity, first)
-
-    return pl.pallas_call(
-        kernel,
-        name="expand",
-        out_shape=shape((n_dp, chunk, capacity * BLK), bf16),
-        in_specs=[pl.BlockSpec(memory_space=pltpu.SMEM), whole_vmem()],
-        out_specs=whole_vmem(),
-        scratch_shapes=[pltpu.VMEM((blocks, chunk, BLK), bf16)],
-        compiler_params=pltpu.CompilerParams(vmem_limit_bytes=VMEM_CAP),
-        cost_estimate=pl.CostEstimate(flops=0, bytes_accessed=1_000_000, transcendentals=0),
-    )(slots, rows)
+            start = offset + position * BLK
+            cut[owner, :, start : start + BLK] = (value * live).astype(bf16)
 
 
 def leave_kernel(weights, summed, inner, inner_counts, *refs):
@@ -534,7 +516,9 @@
     row_refs = refs.take(len(weights))
     term_ref = refs.take() if summed else None
     inner_refs = refs.take(inner_counts[0])
-    out_refs = refs.take(len(weights))
+    gone = sum(1 for weight in weights if weight[3])
+    out_refs = refs.take(gone)
+    loose_ref = refs.take() if gone < len(weights) else None
     sum_ref = refs.take() if summed else None
     inner_refs += refs.take(inner_counts[1])
     inner_refs += refs.take(inner_counts[2])
@@ -564,17 +548,18 @@
         total_spread.start()
         others[total_spread.me] = total[...]
     swaps = []
-    for row_ref, out_ref, share, (split, capacity, first, whole) in zip(
-        row_refs, out_refs, shares, weights
-    ):
+    offset = 0
+    for row_ref, share, (split, capacity, first, whole) in zip(row_refs, shares, weights):
         if split:
             share.wait()
         rows = share.target if split else row_ref
         if not whole:
-            expand_slots(slots_ref, rows, out_ref, refs.take(), capacity, first)
+            expand_slots(slots_ref, rows, loose_ref, refs.take(), capacity, first, offset)
+            offset += capacity * BLK
             continue
+        out_ref = out_refs.pop(0)
         cut, *sems, blocks = refs.take(4)
-        expand_slots(slots_ref, rows, cut, blocks, capacity, first)
+        expand_slots(slots_ref, rows, cut, blocks, capacity, first, 0)
         swap = Swap("dp", cut, out_ref, *sems)
         swap.start()
         swap.keep()
@@ -683,26 +668,30 @@
     n, order, column, half, alone, dy_ref, w_hbm, base_ref, middle_ref, norm_ref, outs_hbm, *rest
 ):
     carry_ref, full_ref, att_ref, term_ref = rest[:4]
-    part, held, work, plain, s_send, s_recv, b_send, b_recv = rest[4:12]
-    w_ref, w_sem, outs_ref, outs_sem = rest[12:]
+    held, work, plain, s_send, s_recv, b_send, b_recv, outs_ref, outs_sem = rest[4:13]
     rows, width = base_ref.shape
     step = rows // SUBS
-    load_w = fetch_columns(w_hbm, column, w_ref, w_sem)
-    load_w.start()
+    if column is not None:
+        part, w_ref, w_sem = rest[13:]
+        load_w = fetch_columns(w_hbm, column, w_ref, w_sem)
+        load_w.start()
+    else:
+        part = dy_ref
     load_outs = fetch_columns(outs_hbm, half, outs_ref, outs_sem)
     load_outs.start()
     line = Line(n, rows, step)
     if alone:
         line.greet()
-    load_w.wait()
     sums = Sums(line, part, held, s_send, s_recv)
     blocks = Blocks(line, full_ref, b_send, b_recv)
-
-    def multiply(columns):
-        product = dot_nt(dy_ref[...], w_ref[columns]).astype(bf16)
-        part[:, :, columns] = product.reshape(n, rows, -1)
-
-    by_tiles(width, 256, multiply)
+    if column is not None:
+        load_w.wait()
+
+        def multiply(columns):
+            product = dot_nt(dy_ref[...], w_ref[columns]).astype(bf16)
+            part[:, :, columns] = product.reshape(n, rows, -1)
+
+        by_tiles(width, 256, multiply)
 
     def settle(sub):
         here = line.part(sub)
@@ -900,11 +889,14 @@
             scratch += [pltpu.VMEM(rows.shape, bf16), *swap_sems(n)]
     for rows, _, capacity, _, whole in weights:
         slots_shape = (n_dp, chunk, capacity * BLK)
-        outs.append(shape(slots_shape, bf16))
         if whole:
+            outs.append(shape(slots_shape, bf16))
             scratch += [pltpu.VMEM(slots_shape, bf16), *swap_sems(n_dp)]
         blocks = rows.shape[0] * rows.shape[2] // BLK
         scratch.append(pltpu.VMEM((blocks, chunk, BLK), bf16))
+    loose = sum(capacity * BLK for _, _, capacity, _, whole in weights if not whole)
+    if loose:
+        outs.append(shape((n_dp, chunk, loose), bf16))
     if term is not None:
         outs.append(shape(block, f32))
     if inner is not None:
@@ -967,17 +959,20 @@
         in_place(),
     ]
     scratch = [
-        pltpu.VMEM((n, rows, width), bf16),
         pltpu.VMEM((2, n, rows, width), bf16),
         pltpu.VMEM((rows // SUBS, width), f32),
         pltpu.VMEM((rows // SUBS, width), f32),
         *sem_pair(n, SUBS),
         *sem_pair(n, SUBS),
-        pltpu.VMEM((width, dy.shape[1]), bf16),
-        pltpu.SemaphoreType.DMA,
         pltpu.VMEM((share, width), bf16),
         pltpu.SemaphoreType.DMA,
     ]
+    if column is not None:
+        scratch += [
+            pltpu.VMEM((n, rows, width), bf16),
+            pltpu.VMEM((width, dy.shape[1]), bf16),
+            pltpu.SemaphoreType.DMA,
+        ]
     kernel = functools.partial(back_kernel, n, unshuffle_order(n, n_dp), column, half, alone)
     return kernel, [dy, weight, base, middle, norm_rows, outs_z], specs, outs, scratch
 
@@ -1091,29 +1086,48 @@
     activated = (up_values * chance).astype(bf16)
     act_ref[...] = activated
     slope_ref[...] = chance + up_values * density
-    gdown_ref[...] = dot_tn(activated, grad_ref[...]).astype(bf16)
+    gradient = dot_tn(activated, grad_ref[...]).astype(bf16)
+    n_dp, rows, columns = gdown_ref.shape
+    chunk = gradient.shape[0] // n_dp
+    for piece in range(rows // chunk):
+        cut = gradient[:, piece * columns : (piece + 1) * columns]
+        gdown_ref[:, piece * chunk : (piece + 1) * chunk] = cut.reshape(n_dp, chunk, columns)
 
 
 def ffn_back_kernel(
-    h_ref, down_ref, grad_ref, act_ref, slope_ref, du_ref, branch_ref, gup_ref, total
+    h_ref,
+    down_ref,
+    up_ref,
+    grad_ref,
+    act_ref,
+    slope_ref,
+    both_ref,
+    branch_ref,
+    part_ref,
+    gup_ref,
+    total,
+    part,
 ):
+    del both_ref
     tile = pl.program_id(0)
     back_act = dot_nt(grad_ref[...], down_ref[...])
     back_up = (back_act * slope_ref[...]).astype(bf16)
-    du_ref[...] = back_up
-    gup_ref[...] = dot_tn(h_ref[...], back_up).astype(bf16)
+    gup_ref[...] = dot_tn(h_ref[...], back_up).astype(bf16).reshape(gup_ref.shape)
 
     @pl.when(tile == 0)
     def _():
         total[...] = dot(act_ref[...], down_ref[...])
+        part[...] = dot_nt(back_up, up_ref[...])
 
     @pl.when(tile > 0)
     def _():
         total[...] += dot(act_ref[...], down_ref[...])
+        part[...] += dot_nt(back_up, up_ref[...])
 
     @pl.when(tile == 3)
     def _():
         branch_ref[...] = total[...].astype(bf16)
+        part_ref[...] = part[...].astype(bf16)
 
 
 def cross_back_kernel(
@@ -1199,11 +1213,14 @@
     return pl.BlockSpec(dims, lambda t: (0, index(t)))
 
 
-def local_call(kernel, name, tiles, outs, specs, out_specs, scratch, flops, moved):
+def local_call(
+    kernel, name, tiles, outs, specs, out_specs, scratch, flops, moved, aliases=None
+):
     return pl.pallas_call(
         kernel,
         name=name,
         grid=(tiles,),
+        input_output_aliases=aliases or {},
         out_shape=outs,
         in_specs=specs,
         out_specs=out_specs,
@@ -1257,9 +1274,10 @@
     )(cross_query, text_all, text_z, mask)
 
 
-def ffn(hidden, up_z, grad_all):
+def ffn(hidden, up_z, grad_all, n, n_dp):
     tokens, width = hidden.shape
     share = up_z.shape[1] // 4
+    chunk = share // n_dp
     return local_call(
         ffn_kernel,
         "ffn",
@@ -1267,13 +1285,13 @@
         (
             shape((tokens, 4 * share), bf16),
             shape((tokens, 4 * share), f32),
-            shape((share, 4 * width), bf16),
+            shape((n_dp, 2 * n * chunk, 4 * share), bf16),
         ),
         [fixed(hidden.shape), moving((width, share), lambda t: t), fixed(grad_all.shape)],
         (
             moving((tokens, share), lambda t: t),
             moving((tokens, share), lambda t: t),
-            moving((share, width), lambda t: t),
+            pl.BlockSpec((n_dp, n * chunk // 4, 4 * share), lambda t: (0, 4 + t, 0)),
         ),
         [],
         16 * tokens * width * share,
@@ -1281,34 +1299,33 @@
     )(hidden, up_z, grad_all)
 
 
-def ffn_back(hidden, down_z, grad_all, activated, slope):
+def ffn_back(hidden, down_z, up_z, grad_all, activated, slope, both):
     tokens, width = hidden.shape
     share = down_z.shape[0]
     return local_call(
         ffn_back_kernel,
         "ffn_back",
         4,
-        (
-            shape((tokens, 4 * share), bf16),
-            shape((tokens, width), bf16),
-            shape((width, 4 * share), bf16),
-        ),
+        (shape((tokens, width), bf16), shape((tokens, width), bf16), shape(both.shape, bf16)),
         [
             fixed(hidden.shape),
             moving((share, width), lambda t: t),
+            moving((width, share), lambda t: t),
             fixed(grad_all.shape),
             moving((tokens, share), lambda t: t),
             moving((tokens, share), lambda t: t),
+            in_place(),
         ],
         (
-            moving((tokens, share), lambda t: t),
             fixed((tokens, width)),
-            moving((width, share), lambda t: t),
+            fixed((tokens, width)),
+            pl.BlockSpec((both.shape[0], both.shape[1] // 2, share), lambda t: (0, 0, t)),
         ),
-        [pltpu.VMEM((tokens, width), f32)],
-        24 * tokens * width * share,
-        40_000_000,
-    )(hidden, down_z, grad_all, activated, slope)
+        [pltpu.VMEM((tokens, width), f32)] * 2,
+        32 * tokens * width * share,
+        50_000_000,
+        {6: 2},
+    )(hidden, down_z, up_z, grad_all, activated, slope, both)
 
 
 def cross_back(back_attended, cross_query, text_pairs, shares, text_all, rows):
@@ -1492,12 +1509,12 @@
         n_dp,
         width,
     )
-    outs_rows, hidden1, text_all, grad_high = enter_call(
+    outs_rows, hidden1, text_all = enter_call(
         "enter_outs",
         6,
         slots,
         [(w_outs, out_places, False, firsts[1])],
-        [(tokens_in, True), (text_in, True), (grad_out[half:], False)],
+        [(tokens_in, True), (text_in, True)],
         norm_full[0:2],
         False,
         True,
@@ -1506,7 +1523,6 @@
         width,
     )
     query_z, outs_z = spread(query_rows), spread(outs_rows)
-    grad_all = jnp.concatenate([grad_low, grad_high], axis=1).reshape(-1, width)
     hidden1 = hidden1.reshape(-1, width)
     text_all = text_all.reshape(-1, text_in.shape[1])
     segment = marks[:, 0, :token_count]
@@ -1519,12 +1535,12 @@
     ).astype(jnp.int32)
 
     projected, attended1, shares1 = self_forward(hidden1, query_z, self_mask)
-    (text_rows,) = enter_call(
+    text_rows, grad_high = enter_call(
         "enter_text",
         7,
         after(slots, attended1),
         [(w_text, split_places, True, firsts[2])],
-        [],
+        [(grad_out[half:], False)],
         None,
         False,
         False,
@@ -1532,6 +1548,7 @@
         n_dp,
         width,
     )
+    grad_all = jnp.concatenate([grad_low, grad_high], axis=1).reshape(-1, width)
     up_rows, down_rows, middle1, hidden2, cross_query = enter_call(
         "forward0",
         1,
@@ -1563,40 +1580,22 @@
         attended2, outs_z, 1, middle1, norm_full[4:6], None, n_z, n_dp, 2
     )
     hidden3 = hidden3.reshape(-1, width)
-    activated, slope, down_part = ffn(hidden3, up_z, grad_all)
-    down_sum = gather_sum(down_part, 1)
-    back_up, branch3, up_part = ffn_back(hidden3, down_z, grad_all, activated, slope)
+    activated, slope, both = ffn(hidden3, up_z, grad_all, n_z, n_dp)
+    branch3, part3, both = ffn_back(hidden3, down_z, up_z, grad_all, activated, slope, both)
     branch3 = branch3.reshape(n_z, token_count, width)
-    up_sum = gather_sum(up_part, n_z)
+    part3 = part3.reshape(n_z, token_count, width)
+    up_down_sum = gather_sum(both.reshape(-1, 4 * share), 2 * n_z)
+    up_sum, down_sum = up_down_sum[:n_z], up_down_sum[n_z:]
     at_middle2, carry2, back_att2, term3 = back_call(
-        back_up, up_z, 0, grad_out, middle2, norm_full[4:6], outs_z, 1, n_z, n_dp, 3
+        part3, after(slots, part3), None, grad_out, middle2, norm_full[4:6], outs_z, 1, n_z, n_dp, 3
     )
     carry2 = carry2.reshape(-1, width)
     back_cross, text_part = cross_back(
         back_att2, cross_query, text_pairs, shares2, text_all, token_count
     )
     text_sum = gather_sum(text_part, n_z)
-    down_grad, at_middle1, carry1, back_att1, term2 = leave_call(
-        "back0",
-        4,
-        contents,
-        [(down_sum, False, cap_big, slot_firsts[4], True)],
-        None,
-        n_z,
-        n_dp,
-        back_parts(
-            back_cross,
-            query_z,
-            3,
-            at_middle2,
-            middle1,
-            after(norm_full[2:4], back_cross),
-            outs_z,
-            0,
-            n_z,
-            n_dp,
-            False,
-        ),
+    at_middle1, carry1, back_att1, term2 = back_call(
+        back_cross, query_z, 3, at_middle2, middle1, norm_full[2:4], outs_z, 0, n_z, n_dp, 4
     )
     carry1 = carry1.reshape(-1, width)
     back_projected, query_part = self_back(
@@ -1604,11 +1603,15 @@
     )
     query_sum = gather_sum(query_part, n_z)
     outs_sum = gather_sum(outs_grad(after(attended1, query_part), carry1, attended2, carry2), 1)
-    up_grad, grad_in, result, term1 = leave_call(
+    down_grad, up_grad, text_grad, grad_in, result, term1 = leave_call(
         "leave_up",
         8,
         contents,
-        [(up_sum, True, cap_big, slot_firsts[3], True)],
+        [
+            (down_sum, False, cap_big, slot_firsts[4], True),
+            (up_sum, True, cap_big, slot_firsts[3], True),
+            (text_sum, True, cap_big, slot_firsts[2], True),
+        ],
         None,
         n_z,
         n_dp,
@@ -1625,25 +1628,22 @@
         ),
     )
     norm_term = jnp.concatenate([term1[:2], term2[:2], term3[:4]], axis=0)
-    text_grad, query_slots, norm_grad = leave_call(
+    loose, norm_grad = leave_call(
         "leave_query",
         9,
         contents,
         [
-            (text_sum, True, cap_big, slot_firsts[2], True),
+            (outs_sum, False, cap_out, slot_firsts[1], False),
             (query_sum, True, cap_big, slot_firsts[0], False),
         ],
         norm_term,
         n_z,
         n_dp,
     )
-    query_grad = lax.all_to_all(query_slots, "dp", 0, 0, tiled=True)
-    outs_slots = expand_call(after(contents, query_slots), outs_sum, cap_out, slot_firsts[1], n_dp)
-    outs_slots = lax.all_to_all(outs_slots, "dp", 0, 0, tiled=True)
+    loose = lax.all_to_all(loose, "dp", 0, 0, tiled=True).reshape(own_rows, -1)
+    outs_slots = loose[:, : cap_out * BLK].astype(f32)
+    query_grad = loose[:, cap_out * BLK :].astype(f32)
     norm_grad = norm_grad[:6]
-    query_grad, outs_slots = (
-        grad.reshape(own_rows, -1).astype(f32) for grad in (query_grad, outs_slots)
-    )
     text_grad, up_grad, down_grad = (
         grad.reshape(own_rows, -1).astype(f32) for grad in (text_grad, up_grad, down_grad)
     )

time: 908 us -> 898 us (0.989)
  Pallas kernels: 780 us -> 752 us
  waiting for transfers between devices: 31.8 us -> 52 us
    pallas_call x3 -> x2, Pallas kernels: 241 us -> 164 us  [leave_call(): line_call(kernel, name, ident, outs, specs, scratch, 0, LINK_COST)(*args)]
    pallas_call x1 -> x2, Pallas kernels: 81.3 us -> 147 us  [back_call(): return call(*args)]
    reduce_scatter x5 -> x4, waiting for transfers between devices: 11.5 us -> 36.9 us  [gather_sum(): summed = lax.psum_scatter(piece, 'dp', scatter_dimension=0, tiled=True)]
    pallas_call x4, Pallas kernels: 291 us -> 269 us  [enter_call(): line_call(kernel, name, ident, outs, specs, scratch, 0, LINK_COST)(*args)]
    pallas_call x2 -> x1, Pallas kernels: 22.8 us -> 27 us  [ffn_back(): local_call(ffn_back_kernel, 'ffn_back', 4, (shape((tokens, width), bf16),...]
  transfers between devices with their start and end apart: 12 -> 10, of which waited for: 4 -> 4; matrix products, arithmetic and copies ran while one was open for 4% -> 4% of each run, Pallas kernels for 82% -> 73%
where the time goes in v8:
time: 898 us; the launch traced here: 889 us
  Pallas kernels  752 us (84%)
  waiting for transfers between devices  52 us (6%)
  other arithmetic  47 us (5%)
  local copies, waits for them, and re-layouts  17.6 us (2%)
  between operations  14.7 us (2%)
    pallas_call x4, Pallas kernels, enter_call(): line_call(kernel, name, ident, outs, specs, scratch, 0, LINK_COST)(*args)  269 us
    pallas_call x2, Pallas kernels, leave_call(): line_call(kernel, name, ident, outs, specs, scratch, 0, LINK_COST)(*args)  164 us
    pallas_call x2, Pallas kernels, back_call(): return call(*args)  147 us
    pallas_call x1, Pallas kernels, forward_call(): return call(*args)  74.9 us
    sub x6, other arithmetic, adamw_update(): weight - rate * (first_hat / (jnp.sqrt(second_hat) + adam_eps) + decay *...  41.9 us
    reduce_scatter x4, waiting for transfers between devices, gather_sum(): summed = lax.psum_scatter(piece, 'dp', scatter_dimension=0, tiled=True)  36.9 us
    pallas_call x1, Pallas kernels, ffn_back(): local_call(ffn_back_kernel, 'ffn_back', 4, (shape((tokens, width), bf16),...  27 us
  transfers between devices with their start and end apart: 10, of which 4 were waited for; matrix products, arithmetic and copies ran while one was open for 4% of the time, Pallas kernels for 73%

profile of v8, /device:TPU:0, one launch (start us, length us, event | category | flops | bytes accessed | tf_op | source)
XLA Modules:
  0.0 888.8 jit_solution(14773475338518714895)
XLA Ops:
  11.5 47.0 %enter_query.1 = (bf16[4,64,2048]{2,1,0:T(8,128)(2,1)}, bf16[4,64,2048]{2,1,0:T(8,128)(2,1)}, s32[4,8,256]{2,1,0:T(8,128)S(1)}, f32[8,2048]{1,0:T(8,128)S(1)}) custom-call(s32[2,288]{1,0:T(2,128)S(1)} %pad_add_fusion.refs_0_.w_hbm, f32[512,2048]{1,0:T(8,128)} %refs_1_.4, bf16[64,2048]{1,0:T(8,128)(2,1)S(1)} %get-tuple-element.155.refs_2_, ...), custom_call_target="tpu_custom_call" | custom-call | bytes 4000000 | tf_op jit(solution)/shard_map/enter_query/pallas_call | solution.py:864
  58.6 64.3 %enter_outs.1 = (bf16[1,64,4096]{2,1,0:T(8,128)(2,1)}, bf16[4,128,2048]{2,1,0:T(8,128)(2,1)}, bf16[4,32,4096]{2,1,0:T(8,128)(2,1)}) custom-call(s32[2,288]{1,0:T(2,128)S(1)} %pad_add_fusion.refs_0_.w_hbm, f32[512,1024]{1,0:T(8,128)} %refs_1_.5, bf16[128,2048]{1,0:T(8,128)(2,1)S(1)} %copy-done, bf16[32,4096]{1,0:T(8,128)(2,1)S(1)} %copy-done.6, ...), custom_call_target="tpu_custom_call" | custom-call | bytes 4000000 | tf_op jit(solution)/shard_map/enter_outs/pallas_call | solution.py:864
  123.4 12.7 %self_forward.1 = (bf16[3,512,512]{2,1,0:T(8,128)(2,1)}, bf16[512,512]{1,0:T(8,128)(2,1)S(1)}, f32[16,128,128]{2,1,0:T(8,128)S(1)}) custom-call(bf16[512,2048]{1,0:T(8,128)(2,1)} %bitcast.85, bf16[2048,2048]{1,0:T(8,128)(2,1)} %all-gather.8.cloned.1.call-done.w_ref.refs_7_.w_hbm.refs_5_, s32[4,128,128]{2,1,0:T(8,128)S(1)} %get-tuple-element.160.mask_ref), custom_call_target="tpu_custom_call" | custom-call | flops 402653184 | bytes 2500000 | tf_op jit(solution)/shard_map/self_forward/pallas_call | solution.py:1240
  137.1 55.0 %enter_text.1 = (bf16[4,64,2048]{2,1,0:T(8,128)(2,1)}, bf16[4,64,2048]{2,1,0:T(8,128)(2,1)}) custom-call(s32[2,288]{1,0:T(2,128)S(1)} %pad_add_fusion.refs_0_.w_hbm, f32[512,2048]{1,0:T(8,128)} %refs_1_.6, bf16[64,2048]{1,0:T(8,128)(2,1)S(1)} %get-tuple-element.154.refs_2_), custom_call_target="tpu_custom_call" | custom-call | bytes 4000000 | tf_op jit(solution)/shard_map/enter_text/pallas_call | solution.py:864
  192.2 102.8 %forward0.1 = (bf16[4,64,2048]{2,1,0:T(8,128)(2,1)}, bf16[1,64,8192]{2,1,0:T(8,128)(2,1)}, f32[128,2048]{1,0:T(8,128)}, bf16[4,128,2048]{2,1,0:T(8,128)(2,1)}, bf16[512,512]{1,0:T(8,128)(2,1)S(1)}) custom-call(s32[2,288]{1,0:T(2,128)S(1)} %pad_add_fusion.refs_0_.w_hbm, f32[512,2048]{1,0:T(8,128)} %refs_1_.7, f32[512,2048]{1,0:T(8,128)} %refs_2_.3, ...), custom_call_target="tpu_custom_call" | custom-call | bytes 4000000 | tf_op jit(solution)/shard_map/forward0/pallas_call | solution.py:864
  298.7 11.6 %cross_forward.1 = (bf16[2,128,512]{2,1,0:T(8,128)(2,1)S(1)}, bf16[512,512]{1,0:T(8,128)(2,1)S(1)}, f32[16,128,128]{2,1,0:T(8,128)}) custom-call(bf16[512,512]{1,0:T(8,128)(2,1)S(1)} %get-tuple-element.81.cq_ref, bf16[128,4096]{1,0:T(8,128)(2,1)} %bitcast.89, bf16[2048,2048]{1,0:T(8,128)(2,1)} %all-gather.10.cloned.1.call-done.w_ref, ...), custom_call_target="tpu_custom_call" | custom-call | flops 134217728 | bytes 2500000 | tf_op jit(solution)/shard_map/cross_forward/pallas_call | solution.py:1259
  310.2 74.9 %forward1.1 = (f32[128,2048]{1,0:T(8,128)S(1)}, bf16[4,128,2048]{2,1,0:T(8,128)(2,1)}) custom-call(bf16[512,512]{1,0:T(8,128)(2,1)S(1)} %get-tuple-element.83.att_ref.att2_ref, bf16[512,4096]{1,0:T(8,128)(2,1)} %bitcast.78, f32[128,2048]{1,0:T(8,128)} %get-tuple-element.84.base_ref.middle_ref, f32[2,2048]{1,0:T(2,128)S(1)} %get-tuple-element.156.norm_ref), custom_call_target="tpu_custom_call" | custom-call | bytes 4000000 | tf_op jit(solution)/shard_map/forward1/pallas_call | solution.py:941
  386.1 15.2 %ffn.1 = (bf16[512,2048]{1,0:T(8,128)(2,1)}, f32[512,2048]{1,0:T(8,128)}, bf16[8,512,2048]{2,1,0:T(8,128)(2,1)}) custom-call(bf16[512,2048]{1,0:T(8,128)(2,1)} %bitcast.87, bf16[2048,2048]{1,0:T(8,128)(2,1)} %all-gather.12.cloned.1.call-done.up_ref, bf16[512,2048]{1,0:T(8,128)(2,1)} %bitcast.82), custom_call_target="tpu_custom_call" | custom-call | flops 1073741824 | bytes 3750000 | tf_op jit(solution)/shard_map/ffn/pallas_call | solution.py:1281
  401.3 6.0 all-gather.16.cloned.1.call-done
  407.3 27.0 %ffn_back.1 = (bf16[512,2048]{1,0:T(8,128)(2,1)}, bf16[512,2048]{1,0:T(8,128)(2,1)}, bf16[8,512,2048]{2,1,0:T(8,128)(2,1)}) custom-call(bf16[512,2048]{1,0:T(8,128)(2,1)} %bitcast.88, bf16[512,8192]{1,0:T(8,128)(2,1)} %bitcast.84, bf16[2048,2048]{1,0:T(8,128)(2,1)} %all-gather.12.cloned.1.call-done.up_ref, ...), custom_call_target="tpu_custom_call", output_to_operand_aliasing={{2}: (6, {})} | custom-call | flops 2147483648 | bytes 6250000 | tf_op jit(solution)/shard_map/ffn_back/pallas_call | solution.py:1305
  435.4 72.6 %back1.1 = (f32[128,2048]{1,0:T(8,128)}, bf16[4,128,2048]{2,1,0:T(8,128)(2,1)}, bf16[512,512]{1,0:T(8,128)(2,1)S(1)}, f32[8,2048]{1,0:T(8,128)S(1)}) custom-call(bf16[4,128,2048]{2,1,0:T(8,128)(2,1)} %bitcast.94, s32[2,288]{1,0:T(2,128)S(1)} %pad_add_fusion.refs_0_.w_hbm, bf16[128,2048]{1,0:T(8,128)(2,1)S(1)} %copy-done.2, f32[128,2048]{1,0:T(8,128)} %copy-done.1, ...), custom_call_target="tpu_custom_call" | custom-call | bytes 4000000 | tf_op jit(solution)/shard_map/back1/pallas_call | solution.py:985
  508.0 10.0 %cross_back.1 = (bf16[512,512]{1,0:T(8,128)(2,1)S(1)}, bf16[2048,2048]{1,0:T(8,128)(2,1)}) custom-call(bf16[512,512]{1,0:T(8,128)(2,1)S(1)} %get-tuple-element.97.back_ref, bf16[512,512]{1,0:T(8,128)(2,1)S(1)} %get-tuple-element.81.cq_ref, bf16[2,128,512]{2,1,0:T(8,128)(2,1)S(1)} %get-tuple-element.98.kv_ref, f32[16,128,128]{2,1,0:T(8,128)} %get-tuple-element.99.share_ref, ...), custom_call_target="tpu_custom_call" | custom-call | flops 134217728 | bytes 2500000 | tf_op jit(solution)/shard_map/cross_back/pallas_call | solution.py:1335
  518.0 74.0 %back0.1 = (f32[128,2048]{1,0:T(8,128)}, bf16[4,128,2048]{2,1,0:T(8,128)(2,1)}, bf16[512,512]{1,0:T(8,128)(2,1)S(1)}, f32[8,2048]{1,0:T(8,128)S(1)}) custom-call(bf16[512,512]{1,0:T(8,128)(2,1)S(1)} %get-tuple-element.101.dy_ref.dcq_ref, bf16[2048,2048]{1,0:T(8,128)(2,1)} %all-gather.8.cloned.1.call-done.w_ref.refs_7_.w_hbm.refs_5_, ...), custom_call_target="tpu_custom_call" | custom-call | bytes 4000000 | tf_op jit(solution)/shard_map/back0/pallas_call | solution.py:985
  592.0 15.4 %self_back.1 = (bf16[512,1536]{1,0:T(8,128)(2,1)}, bf16[2048,2048]{1,0:T(8,128)(2,1)}) custom-call(bf16[512,512]{1,0:T(8,128)(2,1)S(1)} %get-tuple-element.103.back_ref, bf16[3,512,512]{2,1,0:T(8,128)(2,1)} %get-tuple-element.104.proj_ref, f32[16,128,128]{2,1,0:T(8,128)} %copy-done.3, bf16[512,2048]{1,0:T(8,128)(2,1)} %bitcast.86, ...), custom_call_target="tpu_custom_call" | custom-call | flops 536870912 | bytes 3125000 | tf_op jit(solution)/shard_map/self_back/pallas_call | solution.py:1373
  607.4 6.2 outs_grad.1
  618.3 7.0 reduce-scatter.7.cloned.1.call-done
  625.3 133.2 %leave_up.1 = (bf16[8,64,2048]{2,1,0:T(8,128)(2,1)}, bf16[8,64,2048]{2,1,0:T(8,128)(2,1)}, bf16[8,64,2048]{2,1,0:T(8,128)(2,1)}, bf16[128,2048]{1,0:T(8,128)(2,1...) custom-call(s32[2,576]{1,0:T(2,128)S(1)} %concatenate.39.refs_0_, bf16[4,64,2048]{2,1,0:T(8,128)(2,1)} %bitcast.92, ...), custom_call_target="tpu_custom_call" | custom-call | bytes 4000000 | tf_op jit(solution)/shard_map/leave_up/pallas_call | solution.py:907
  758.6 29.9 %reduce-scatter.11.cloned.1.call-done = bf16[256,2048]{1,0:T(8,128)(2,1)} async-done(((bf16[2048,2048]{1,0:T(8,128)(2,1)}), bf16[256,2048]{1,0:T(8,128)(2,1)}) %reduce-scatter.11.cloned.1.call-update) | async-done | bytes 1048592 | tf_op jit(solution)/shard_map/reduce_scatter | solution.py:1491
  790.7 30.6 %leave_query.1 = (bf16[8,64,3072]{2,1,0:T(8,128)(2,1)}, f32[8,256]{1,0:T(8,128)S(1)}) custom-call(s32[2,576]{1,0:T(2,128)S(1)} %concatenate.39.refs_0_, bf16[1,64,4096]{2,1,0:T(8,128)(2,1)S(1)} %bitcast.76, bf16[4,64,2048]{2,1,0:T(8,128)(2,1)S(1)} %bitcast.75, f32[8,2048]{1,0:T(8,128)S(1)} %pad_maximum_fusion.1.refs_3_), custom_call_target="tpu_custom_call" | custom-call | bytes 4000000 | tf_op jit(solution)/shard_map/leave_query/pallas_call | solution.py:907
  825.9 10.3 %multiply_subtract_fusion.2 = (f32[512,2048]{1,0:T(8,128)}, f32[512,2048]{1,0:T(8,128)}, f32[512,2048]{1,0:T(8,128)}) fusion(f32[512,2048]{1,0:T(8,128)} %refs_1_.7, bf16[8,64,2048]{2,1,0:T(8,128)(2,1)} %get-tuple-element.120, f32[512,2048]{1,0:T(8,128)} %param.43, f32[512,2048]{1,0:T(8,128)} %param.42), kind=kLoop, calls=%fused_computation.21 | loop fusion | flops 16777216 | bytes 27262976 | tf_op jit(solution)/shard_map/sub | solution.py:52
  839.2 8.4 multiply_subtract_fusion.1
  848.8 7.1 multiply_subtract_fusion
  855.9 7.8 all-to-all-done
  863.7 10.3 %multiply_subtract_fusion.3 = (f32[512,2048]{1,0:T(8,128)}, f32[512,2048]{1,0:T(8,128)}, f32[512,2048]{1,0:T(8,128)}) fusion(f32[512,2048]{1,0:T(8,128)} %refs_1_.4, bf16[512,3072]{1,0:T(8,128)(2,1)} %bitcast.46, f32[512,2048]{1,0:T(8,128)} %param.40, f32[512,2048]{1,0:T(8,128)} %param.39), kind=kLoop, calls=%fused_computation.22 | loop fusion | flops 16777216 | bytes 27262976 | tf_op jit(solution)/shard_map/sub | solution.py:52
  (122 shorter events, 34.8 us)
Async XLA Ops:
  7.2 51.4 %copy-start = (bf16[128,2048]{1,0:T(8,128)(2,1)S(1)}, bf16[128,2048]{1,0:T(8,128)(2,1)}, u32[]{:S(2)}) copy-start(bf16[128,2048]{1,0:T(8,128)(2,1)} %refs_7_.1) | copy-start | bytes 1572868
  7.2 51.4 %copy-start.6 = (bf16[32,4096]{1,0:T(8,128)(2,1)S(1)}, bf16[32,4096]{1,0:T(8,128)(2,1)}, u32[]{:S(2)}) copy-start(bf16[32,4096]{1,0:T(8,128)(2,1)} %refs_3_.1) | copy-start | bytes 786436
  7.2 116.2 %all-gather.8.cloned.1.call-start = ((), (), s32[]{:S(2)}) async-start(), calls=%async_computation.5 | async-start | bytes 9437184 | tf_op jit(solution)/shard_map/all_gather | solution.py:1488
  58.5 133.7 %all-gather.14.cloned.1.call-start = ((), (), s32[]{:S(2)}) async-start(), calls=%async_computation.12 | async-start | bytes 4718592 | tf_op jit(solution)/shard_map/all_gather | solution.py:1488
  122.9 175.7 %all-gather.10.cloned.1.call-start = ((), (), s32[]{:S(2)}) async-start(), calls=%async_computation.6 | async-start | bytes 9437184 | tf_op jit(solution)/shard_map/all_gather | solution.py:1488
  192.1 194.1 %all-gather.12.cloned.1.call-start = ((), (), s32[]{:S(2)}) async-start(), calls=%async_computation.7 | async-start | bytes 9437184 | tf_op jit(solution)/shard_map/all_gather | solution.py:1488
  192.2 103.7 %copy-start.16 = (bf16[4,64,2048]{2,1,0:T(8,128)(2,1)S(1)}, bf16[4,64,2048]{2,1,0:T(8,128)(2,1)}, u32[]{:S(2)}) copy-start(bf16[4,64,2048]{2,1,0:T(8,128)(2,1)} %get-tuple-element.88) | copy-start | bytes 3145732
  295.1 112.2 %all-gather.16.cloned.1.call-start = ((), (), s32[]{:S(2)}) async-start(), calls=%async_computation.13 | async-start | bytes 9437184 | tf_op jit(solution)/shard_map/all_gather | solution.py:1488
  295.7 319.5 %reduce-scatter.5.cloned.1.call-start = ((), (), s32[]{:S(2)}) async-start(), calls=%async_computation.8 | async-start | bytes 18874368 | tf_op jit(solution)/shard_map/reduce_scatter | solution.py:1491
  434.4 190.9 %reduce-scatter.7.cloned.1.call-start = ((), (), s32[]{:S(2)}) async-start(), calls=%async_computation.9 | async-start | bytes 9437184 | tf_op jit(solution)/shard_map/reduce_scatter | solution.py:1491
  518.0 240.6 %reduce-scatter.9.cloned.1.call-start = ((), (), s32[]{:S(2)}) async-start(), calls=%async_computation.10 | async-start | bytes 4718592 | tf_op jit(solution)/shard_map/reduce_scatter | solution.py:1491
  613.7 174.8 %reduce-scatter.11.cloned.1.call-start = ((), (), s32[]{:S(2)}) async-start(), calls=%async_computation.11 | async-start | bytes 9437184 | tf_op jit(solution)/shard_map/reduce_scatter | solution.py:1491
  821.4 42.3 %all-to-all-start = ((bf16[8,64,3072]{2,1,0:T(8,128)(2,1)}), bf16[8,64,3072]{2,1,0:T(8,128)(2,1)}, u32[]{:S(2)}, u32[]{:S(2)}) async-start(bf16[8,64,3072]{2,1,0:T(8,128)(2,1)} %get-tuple-element.119), calls=%async_computation.4 | async-start | bytes 6291456 | tf_op jit(solution)/shard_map/all_to_all | solution.py:1643
  825.8 10.4 %copy-start.17 = (f32[6,256]{1,0:T(8,128)S(1)}, f32[6,256]{1,0:T(8,128)}, u32[]{:S(2)}) copy-start(f32[6,256]{1,0:T(8,128)} %param.53) | copy-start | bytes 18436
  825.8 10.4 %copy-start.18 = (f32[6,256]{1,0:T(8,128)S(1)}, f32[6,256]{1,0:T(8,128)}, u32[]{:S(2)}) copy-start(f32[6,256]{1,0:T(8,128)} %param.55) | copy-start | bytes 18436
  825.9 10.4 %copy-start.19 = (f32[6,256]{1,0:T(8,128)S(1)}, f32[6,256]{1,0:T(8,128)}, u32[]{:S(2)}) copy-start(f32[6,256]{1,0:T(8,128)} %param.54) | copy-start | bytes 18436
  825.9 11.0 %copy-start.8 = (f32[512,2048]{1,0:T(8,128)S(1)}, f32[512,2048]{1,0:T(8,128)}, u32[]{:S(2)}) copy-start(f32[512,2048]{1,0:T(8,128)} %refs_1_.6) | copy-start | bytes 12582916
  825.9 12.1 %copy-start.10 = (f32[512,2048]{1,0:T(8,128)S(1)}, f32[512,2048]{1,0:T(8,128)}, u32[]{:S(2)}) copy-start(f32[512,2048]{1,0:T(8,128)} %param.49) | copy-start | bytes 12582916
  825.9 13.3 %copy-start.11 = (f32[512,2048]{1,0:T(8,128)S(1)}, f32[512,2048]{1,0:T(8,128)}, u32[]{:S(2)}) copy-start(f32[512,2048]{1,0:T(8,128)} %param.48) | copy-start | bytes 12582916
  839.2 8.4 copy-start.12
  839.2 9.6 %copy-start.13 = (f32[512,2048]{1,0:T(8,128)S(1)}, f32[512,2048]{1,0:T(8,128)}, u32[]{:S(2)}) copy-start(f32[512,2048]{1,0:T(8,128)} %param.51) | copy-start | bytes 12582916
  863.7 10.3 %copy-start.9 = (f32[512,1024]{1,0:T(8,128)S(1)}, f32[512,1024]{1,0:T(8,128)}, u32[]{:S(2)}) copy-start(f32[512,1024]{1,0:T(8,128)} %refs_1_.5) | copy-start | bytes 6291460
  863.7 10.3 %copy-start.14 = (f32[512,1024]{1,0:T(8,128)S(1)}, f32[512,1024]{1,0:T(8,128)}, u32[]{:S(2)}) copy-start(f32[512,1024]{1,0:T(8,128)} %param.46) | copy-start | bytes 6291460
  863.7 11.5 %copy-start.15 = (f32[512,1024]{1,0:T(8,128)S(1)}, f32[512,1024]{1,0:T(8,128)}, u32[]{:S(2)}) copy-start(f32[512,1024]{1,0:T(8,128)} %param.45) | copy-start | bytes 6291460
  (11 other events, 18.5 us)
Sparse Core Ops, SparseCore 0:
  58.6 64.6 all-gather.7
  125.2 53.2 all-gather.13
  192.2 89.5 all-gather.9
  295.2 55.8 all-gather.11
  352.8 54.4 all-gather.15
  434.5 115.9 reduce-scatter.4
  553.9 71.2 reduce-scatter.6
  629.6 85.2 reduce-scatter.8
  718.3 70.0 reduce-scatter.10

commit v9 on v8

--- a/solution.py
+++ b/solution.py
@@ -192,9 +192,12 @@
                         self.move(way, target, sub, held).wait_send()
 
 
-def relay(n, sums, blocks, settle, hook=None):
+def relay(n, sums, blocks, settle, hook=None, later=None):
+    lag = 2 * (n - 1)
     for slot in range((SUBS + 2) * (n - 1)):
         sub, time = divmod(slot, n - 1)
+        if later is not None and slot >= lag:
+            later.forward(*divmod(slot - lag, n - 1))
         if hook is not None and slot == SUBS * (n - 1):
             hook()
         if sub < SUBS:
@@ -667,16 +670,21 @@
 def back_kernel(
     n, order, column, half, alone, dy_ref, w_hbm, base_ref, middle_ref, norm_ref, outs_hbm, *rest
 ):
-    carry_ref, full_ref, att_ref, term_ref = rest[:4]
-    held, work, plain, s_send, s_recv, b_send, b_recv, outs_ref, outs_sem = rest[4:13]
+    if column is None:
+        branch, *rest = rest
+    carry_ref, full_ref, att_ref, term_ref, *rest = rest
+    if column is None:
+        result_ref, *rest = rest
+    held, work, plain, s_send, s_recv, b_send, b_recv, outs_ref, outs_sem = rest[:9]
     rows, width = base_ref.shape
     step = rows // SUBS
     if column is not None:
-        part, w_ref, w_sem = rest[13:]
+        part, w_ref, w_sem = rest[9:]
         load_w = fetch_columns(w_hbm, column, w_ref, w_sem)
         load_w.start()
     else:
         part = dy_ref
+        held2, r_send, r_recv = rest[9:]
     load_outs = fetch_columns(outs_hbm, half, outs_ref, outs_sem)
     load_outs.start()
     line = Line(n, rows, step)
@@ -684,6 +692,9 @@
         line.greet()
     sums = Sums(line, part, held, s_send, s_recv)
     blocks = Blocks(line, full_ref, b_send, b_recv)
+    results = None
+    if column is None:
+        results = Sums(line, branch, held2, r_send, r_recv)
     if column is not None:
         load_w.wait()
 
@@ -712,7 +723,13 @@
         full_ref[line.at, here] = carry.astype(bf16)
         blocks.start(sub)
 
-    relay(n, [sums], blocks, settle)
+    relay(n, [sums], blocks, settle, None, results)
+    if results is not None:
+        for sub in range(SUBS):
+            here = line.part(sub)
+            results.total(sub, work)
+            result_ref[here] = (middle_ref[here] + work[...]).astype(bf16)
+        results.finish()
     load_outs.wait()
 
     def multiply_next(columns):
@@ -722,9 +739,9 @@
     by_tiles(att_ref.shape[1], 256, multiply_next)
 
 
-def last_kernel(n, order, dy_ref, w_hbm, base_ref, tokens, norm_ref, branch, middle, *rest):
-    grad_ref, result_ref, term_ref = rest[:3]
-    part, held, held2, work, plain, s_send, s_recv, r_send, r_recv, w_ref, w_sem = rest[3:]
+def last_kernel(n, order, dy_ref, w_hbm, base_ref, tokens, norm_ref, *rest):
+    grad_ref, term_ref = rest[:2]
+    part, held, work, plain, s_send, s_recv, w_ref, w_sem = rest[2:]
     rows, width = base_ref.shape
     step = rows // SUBS
     load_w = fetch_columns(w_hbm, 0, w_ref, w_sem)
@@ -732,7 +749,6 @@
     line = Line(n, rows, step)
     load_w.wait()
     sums = Sums(line, part, held, s_send, s_recv)
-    results = Sums(line, branch, held2, r_send, r_recv)
 
     def multiply(columns):
         product = dot_nt(dy_ref[...], w_ref[columns]).astype(bf16)
@@ -756,10 +772,8 @@
             sub == 0,
         )
         grad_ref[here] = carry.astype(bf16)
-        results.total(sub, work)
-        result_ref[here] = (middle[here] + work[...]).astype(bf16)
-
-    relay(n, [sums, results], None, settle)
+
+    relay(n, [sums], None, settle)
 
 
 VMEM_CAP = 52 * 1024 * 1024
@@ -941,7 +955,7 @@
     return call(*args)
 
 
-def back_parts(dy, weight, column, base, middle, norm_rows, outs_z, half, n, n_dp, alone):
+def back_parts(dy, weight, column, base, middle, norm_rows, outs_z, half, branch, n, n_dp, alone):
     rows, width = base.shape
     share = outs_z.shape[0]
     outs = [
@@ -973,39 +987,42 @@
             pltpu.VMEM((width, dy.shape[1]), bf16),
             pltpu.SemaphoreType.DMA,
         ]
+    args = [dy, weight, base, middle, norm_rows, outs_z]
+    if branch is not None:
+        args.append(branch)
+        specs.append(whole_vmem())
+        outs.append(shape((rows, width), bf16))
+        scratch += [pltpu.VMEM((2, n, rows, width), bf16), *sem_pair(n, SUBS)]
     kernel = functools.partial(back_kernel, n, unshuffle_order(n, n_dp), column, half, alone)
-    return kernel, [dy, weight, base, middle, norm_rows, outs_z], specs, outs, scratch
-
-
-def back_call(dy, weight, column, base, middle, norm_rows, outs_z, half, n, n_dp, ident):
+    return kernel, args, specs, outs, scratch
+
+
+def back_call(dy, weight, column, base, middle, norm_rows, outs_z, half, branch, n, n_dp, ident):
     kernel, args, specs, outs, scratch = back_parts(
-        dy, weight, column, base, middle, norm_rows, outs_z, half, n, n_dp, True
+        dy, weight, column, base, middle, norm_rows, outs_z, half, branch, n, n_dp, True
     )
     call = line_call(kernel, f"back{half}", ident, outs, specs, scratch, 0, LINK_COST)
     return call(*args)
 
 
-def last_parts(dy, weight, base, tokens, norm_rows, branch, middle, n, n_dp):
+def last_parts(dy, weight, base, tokens, norm_rows, n, n_dp):
     rows, width = base.shape
     outs = [
         shape((rows, width), bf16),
-        shape((rows, width), bf16),
         shape((8, width), f32),
     ]
-    specs = [whole_vmem(), in_place()] + [whole_vmem()] * 5
+    specs = [whole_vmem(), in_place()] + [whole_vmem()] * 3
     scratch = [
         pltpu.VMEM((n, rows, width), bf16),
         pltpu.VMEM((2, n, rows, width), bf16),
-        pltpu.VMEM((2, n, rows, width), bf16),
         pltpu.VMEM((rows // SUBS, width), f32),
         pltpu.VMEM((rows // SUBS, width), f32),
-        *sem_pair(n, SUBS),
         *sem_pair(n, SUBS),
         pltpu.VMEM((width, dy.shape[1]), bf16),
         pltpu.SemaphoreType.DMA,
     ]
     kernel = functools.partial(last_kernel, n, unshuffle_order(n, n_dp))
-    return kernel, [dy, weight, base, tokens, norm_rows, branch, middle], specs, outs, scratch
+    return kernel, [dy, weight, base, tokens, norm_rows], specs, outs, scratch
 
 
 def attend_forward(query, keys, values, mask_ref, keyed, att_ref, share_ref):
@@ -1086,12 +1103,7 @@
     activated = (up_values * chance).astype(bf16)
     act_ref[...] = activated
     slope_ref[...] = chance + up_values * density
-    gradient = dot_tn(activated, grad_ref[...]).astype(bf16)
-    n_dp, rows, columns = gdown_ref.shape
-    chunk = gradient.shape[0] // n_dp
-    for piece in range(rows // chunk):
-        cut = gradient[:, piece * columns : (piece + 1) * columns]
-        gdown_ref[:, piece * chunk : (piece + 1) * chunk] = cut.reshape(n_dp, chunk, columns)
+    store_pieces(dot_tn(activated, grad_ref[...]), gdown_ref)
 
 
 def ffn_back_kernel(
@@ -1157,16 +1169,36 @@
 
     @pl.when(tile == 0)
     def _():
-        grad_ref[...] = dot_tn(att1_ref[...], carry1_ref[...]).astype(bf16)
+        store_pieces(dot_tn(att1_ref[...], carry1_ref[...]), grad_ref)
 
     @pl.when(tile == 1)
     def _():
-        grad_ref[...] = dot_tn(att2_ref[...], carry2_ref[...]).astype(bf16)
+        store_pieces(dot_tn(att2_ref[...], carry2_ref[...]), grad_ref)
+
+
+def store_pieces(gradient, target):
+    n_dp, rows, columns = target.shape
+    gradient = gradient.astype(bf16)
+    chunk = gradient.shape[0] // n_dp
+    for piece in range(rows // chunk):
+        cut = gradient[:, piece * columns : (piece + 1) * columns]
+        target[:, piece * chunk : (piece + 1) * chunk] = cut.reshape(n_dp, chunk, columns)
 
 
 def self_back_kernel(
-    rows, back_ref, proj_ref, share_ref, h1_ref, h2_ref, dcq_ref, dproj_ref, grad_ref, parts
+    rows,
+    back_ref,
+    proj_ref,
+    share_ref,
+    h1_ref,
+    h2_ref,
+    dcq_ref,
+    both_ref,
+    dproj_ref,
+    grad_ref,
+    parts,
 ):
+    del both_ref
     tile = pl.program_id(0)
     share = dcq_ref.shape[1]
 
@@ -1198,11 +1230,11 @@
 
     @pl.when(tile < 3)
     def _():
-        grad_ref[...] = dot_tn(h1_ref[...], parts[tile]).astype(bf16)
+        grad_ref[...] = dot_tn(h1_ref[...], parts[tile]).astype(bf16).reshape(grad_ref.shape)
 
     @pl.when(tile == 3)
     def _():
-        grad_ref[...] = dot_tn(h2_ref[...], dcq_ref[...]).astype(bf16)
+        grad_ref[...] = dot_tn(h2_ref[...], dcq_ref[...]).astype(bf16).reshape(grad_ref.shape)
 
 
 def fixed(dims):
@@ -1351,30 +1383,31 @@
     )(back_attended, cross_query, text_pairs, shares, text_all)
 
 
-def outs_grad(attended1, carry1, attended2, carry2):
+def outs_grad(attended1, carry1, attended2, carry2, n, n_dp):
     tokens, share = attended1.shape
     width = carry1.shape[1]
+    chunk = share // n_dp
     return local_call(
         outs_grad_kernel,
         "outs_grad",
         2,
-        shape((share, 2 * width), bf16),
+        shape((n_dp, n * chunk * 3 // 2, 4 * share), bf16),
         [fixed((tokens, share)), fixed((tokens, width))] * 2,
-        moving((share, width), lambda t: t),
+        pl.BlockSpec((n_dp, n * chunk // 4, 4 * share), lambda t: (0, 4 + t, 0)),
         [],
         4 * tokens * width * share,
         10_000_000,
     )(attended1, carry1, attended2, carry2)
 
 
-def self_back(back_attended, projected, shares, hidden1, hidden2, back_cross, rows):
+def self_back(back_attended, projected, shares, hidden1, hidden2, back_cross, both, rows):
     tokens, width = hidden1.shape
     share = back_cross.shape[1]
     return local_call(
         functools.partial(self_back_kernel, rows),
         "self_back",
         4,
-        (shape((tokens, 3 * share), bf16), shape((width, 4 * share), bf16)),
+        (shape((tokens, 3 * share), bf16), shape(both.shape, bf16)),
         [
             fixed(back_attended.shape),
             fixed(projected.shape),
@@ -1382,12 +1415,17 @@
             fixed(hidden1.shape),
             fixed(hidden2.shape),
             fixed(back_cross.shape),
+            in_place(),
         ],
-        (fixed((tokens, 3 * share)), moving((width, share), lambda t: t)),
+        (
+            fixed((tokens, 3 * share)),
+            pl.BlockSpec((both.shape[0], both.shape[1] * 2 // 3, share), lambda t: (0, 0, t)),
+        ),
         [pltpu.VMEM((3, tokens, share), bf16)],
         8 * tokens * width * share,
         25_000_000,
-    )(back_attended, projected, shares, hidden1, hidden2, back_cross)
+        {6: 1},
+    )(back_attended, projected, shares, hidden1, hidden2, back_cross, both)
 
 
 def block_slots(owners):
@@ -1586,8 +1624,8 @@
     part3 = part3.reshape(n_z, token_count, width)
     up_down_sum = gather_sum(both.reshape(-1, 4 * share), 2 * n_z)
     up_sum, down_sum = up_down_sum[:n_z], up_down_sum[n_z:]
-    at_middle2, carry2, back_att2, term3 = back_call(
-        part3, after(slots, part3), None, grad_out, middle2, norm_full[4:6], outs_z, 1, n_z, n_dp, 3
+    at_middle2, carry2, back_att2, term3, result = back_call(
+        part3, after(slots, part3), None, grad_out, middle2, norm_full[4:6], outs_z, 1, branch3, n_z, n_dp, 3
     )
     carry2 = carry2.reshape(-1, width)
     back_cross, text_part = cross_back(
@@ -1595,15 +1633,15 @@
     )
     text_sum = gather_sum(text_part, n_z)
     at_middle1, carry1, back_att1, term2 = back_call(
-        back_cross, query_z, 3, at_middle2, middle1, norm_full[2:4], outs_z, 0, n_z, n_dp, 4
+        back_cross, query_z, 3, at_middle2, middle1, norm_full[2:4], outs_z, 0, None, n_z, n_dp, 4
     )
     carry1 = carry1.reshape(-1, width)
-    back_projected, query_part = self_back(
-        back_att1, projected, shares1, hidden1, hidden2, back_cross, token_count
-    )
-    query_sum = gather_sum(query_part, n_z)
-    outs_sum = gather_sum(outs_grad(after(attended1, query_part), carry1, attended2, carry2), 1)
-    down_grad, up_grad, text_grad, grad_in, result, term1 = leave_call(
+    both = outs_grad(after(attended1, up_down_sum), carry1, attended2, carry2, n_z, n_dp)
+    back_projected, both = self_back(
+        back_att1, projected, shares1, hidden1, hidden2, back_cross, both, token_count
+    )
+    query_outs_sum = gather_sum(both.reshape(-1, 4 * share), 3 * n_z // 2)
+    down_grad, up_grad, text_grad, grad_in, term1 = leave_call(
         "leave_up",
         8,
         contents,
@@ -1621,12 +1659,12 @@
             at_middle1,
             tokens_in,
             norm_full[0:2],
-            branch3,
-            middle2,
             n_z,
             n_dp,
         ),
     )
+    query_outs_sum = after(query_outs_sum, term1)
+    query_sum, outs_sum = query_outs_sum[:n_z], query_outs_sum[n_z:]
     norm_term = jnp.concatenate([term1[:2], term2[:2], term3[:4]], axis=0)
     loose, norm_grad = leave_call(
         "leave_query",

time: 898 us -> 887 us (0.988)
  waiting for transfers between devices: 52 us -> 36.6 us
    pallas_call x2, Pallas kernels: 147 us -> 171 us  [back_call(): return call(*args)]
    pallas_call x2, Pallas kernels: 164 us -> 143 us  [leave_call(): line_call(kernel, name, ident, outs, specs, scratch, 0, LINK_COST)(*args)]
    reduce_scatter x4 -> x3, waiting for transfers between devices: 36.9 us -> 22.2 us  [gather_sum(): summed = lax.psum_scatter(piece, 'dp', scatter_dimension=0, tiled=True)]
  transfers between devices with their start and end apart: 10 -> 9, of which waited for: 4 -> 3; matrix products, arithmetic and copies ran while one was open for 4% -> 4% of each run, Pallas kernels for 73% -> 74%
where the time goes in v9:
time: 887 us; the launch traced here: 878 us
  Pallas kernels  756 us (85%)
  other arithmetic  47 us (5%)
  waiting for transfers between devices  36.6 us (4%)
  local copies, waits for them, and re-layouts  18.3 us (2%)
  between operations  15 us (2%)
    pallas_call x4, Pallas kernels, enter_call(): line_call(kernel, name, ident, outs, specs, scratch, 0, LINK_COST)(*args)  269 us
    pallas_call x2, Pallas kernels, back_call(): return call(*args)  171 us
    pallas_call x2, Pallas kernels, leave_call(): line_call(kernel, name, ident, outs, specs, scratch, 0, LINK_COST)(*args)  143 us
    pallas_call x1, Pallas kernels, forward_call(): return call(*args)  74.9 us
    sub x6, other arithmetic, adamw_update(): weight - rate * (first_hat / (jnp.sqrt(second_hat) + adam_eps) + decay *...  41.9 us
    pallas_call x1, Pallas kernels, ffn_back(): local_call(ffn_back_kernel, 'ffn_back', 4, (shape((tokens, width), bf16),...  27.1 us
    reduce_scatter x3, waiting for transfers between devices, gather_sum(): summed = lax.psum_scatter(piece, 'dp', scatter_dimension=0, tiled=True)  22.2 us
  transfers between devices with their start and end apart: 9, of which 3 were waited for; matrix products, arithmetic and copies ran while one was open for 4% of the time, Pallas kernels for 74%

profile of v9, /device:TPU:0, one launch (start us, length us, event | category | flops | bytes accessed | tf_op | source)
XLA Modules:
  0.0 877.9 jit_solution(1777219583967820808)
XLA Ops:
  11.5 46.9 %enter_query.1 = (bf16[4,64,2048]{2,1,0:T(8,128)(2,1)}, bf16[4,64,2048]{2,1,0:T(8,128)(2,1)}, s32[4,8,256]{2,1,0:T(8,128)S(1)}, f32[8,2048]{1,0:T(8,128)S(1)}) custom-call(s32[2,288]{1,0:T(2,128)S(1)} %pad_add_fusion.refs_0_.w_hbm, f32[512,2048]{1,0:T(8,128)} %refs_1_.4, bf16[64,2048]{1,0:T(8,128)(2,1)S(1)} %get-tuple-element.155.refs_2_, ...), custom_call_target="tpu_custom_call" | custom-call | bytes 4000000 | tf_op jit(solution)/shard_map/enter_query/pallas_call | solution.py:878
  58.6 64.3 %enter_outs.1 = (bf16[1,64,4096]{2,1,0:T(8,128)(2,1)}, bf16[4,128,2048]{2,1,0:T(8,128)(2,1)}, bf16[4,32,4096]{2,1,0:T(8,128)(2,1)}) custom-call(s32[2,288]{1,0:T(2,128)S(1)} %pad_add_fusion.refs_0_.w_hbm, f32[512,1024]{1,0:T(8,128)} %refs_1_.5, bf16[128,2048]{1,0:T(8,128)(2,1)S(1)} %copy-done, bf16[32,4096]{1,0:T(8,128)(2,1)S(1)} %copy-done.4, ...), custom_call_target="tpu_custom_call" | custom-call | bytes 4000000 | tf_op jit(solution)/shard_map/enter_outs/pallas_call | solution.py:878
  123.4 12.7 %self_forward.1 = (bf16[3,512,512]{2,1,0:T(8,128)(2,1)}, bf16[512,512]{1,0:T(8,128)(2,1)S(1)}, f32[16,128,128]{2,1,0:T(8,128)S(1)}) custom-call(bf16[512,2048]{1,0:T(8,128)(2,1)} %bitcast.83, bf16[2048,2048]{1,0:T(8,128)(2,1)} %all-gather.8.cloned.1.call-done.w_ref.refs_7_.w_hbm.refs_5_, s32[4,128,128]{2,1,0:T(8,128)S(1)} %get-tuple-element.160.mask_ref), custom_call_target="tpu_custom_call" | custom-call | flops 402653184 | bytes 2500000 | tf_op jit(solution)/shard_map/self_forward/pallas_call | solution.py:1272
  137.1 55.0 %enter_text.1 = (bf16[4,64,2048]{2,1,0:T(8,128)(2,1)}, bf16[4,64,2048]{2,1,0:T(8,128)(2,1)}) custom-call(s32[2,288]{1,0:T(2,128)S(1)} %pad_add_fusion.refs_0_.w_hbm, f32[512,2048]{1,0:T(8,128)} %refs_1_.6, bf16[64,2048]{1,0:T(8,128)(2,1)S(1)} %get-tuple-element.154.refs_2_), custom_call_target="tpu_custom_call" | custom-call | bytes 4000000 | tf_op jit(solution)/shard_map/enter_text/pallas_call | solution.py:878
  192.2 102.8 %forward0.1 = (bf16[4,64,2048]{2,1,0:T(8,128)(2,1)}, bf16[1,64,8192]{2,1,0:T(8,128)(2,1)}, f32[128,2048]{1,0:T(8,128)}, bf16[4,128,2048]{2,1,0:T(8,128)(2,1)}, bf16[512,512]{1,0:T(8,128)(2,1)S(1)}) custom-call(s32[2,288]{1,0:T(2,128)S(1)} %pad_add_fusion.refs_0_.w_hbm, f32[512,2048]{1,0:T(8,128)} %refs_1_.7, f32[512,2048]{1,0:T(8,128)} %refs_2_.3, ...), custom_call_target="tpu_custom_call" | custom-call | bytes 4000000 | tf_op jit(solution)/shard_map/forward0/pallas_call | solution.py:878
  298.8 11.6 %cross_forward.1 = (bf16[2,128,512]{2,1,0:T(8,128)(2,1)S(1)}, bf16[512,512]{1,0:T(8,128)(2,1)S(1)}, f32[16,128,128]{2,1,0:T(8,128)}) custom-call(bf16[512,512]{1,0:T(8,128)(2,1)S(1)} %get-tuple-element.81.cq_ref, bf16[128,4096]{1,0:T(8,128)(2,1)} %bitcast.88, bf16[2048,2048]{1,0:T(8,128)(2,1)} %all-gather.10.cloned.1.call-done.w_ref, ...), custom_call_target="tpu_custom_call" | custom-call | flops 134217728 | bytes 2500000 | tf_op jit(solution)/shard_map/cross_forward/pallas_call | solution.py:1291
  310.4 74.9 %forward1.1 = (f32[128,2048]{1,0:T(8,128)S(1)}, bf16[4,128,2048]{2,1,0:T(8,128)(2,1)}) custom-call(bf16[512,512]{1,0:T(8,128)(2,1)S(1)} %get-tuple-element.83.att_ref.att2_ref, bf16[512,4096]{1,0:T(8,128)(2,1)} %bitcast.77, f32[128,2048]{1,0:T(8,128)} %get-tuple-element.84.base_ref.middle_ref, f32[2,2048]{1,0:T(2,128)S(1)} %get-tuple-element.156.norm_ref), custom_call_target="tpu_custom_call" | custom-call | bytes 4000000 | tf_op jit(solution)/shard_map/forward1/pallas_call | solution.py:955
  386.2 15.2 %ffn.1 = (bf16[512,2048]{1,0:T(8,128)(2,1)}, f32[512,2048]{1,0:T(8,128)}, bf16[8,512,2048]{2,1,0:T(8,128)(2,1)}) custom-call(bf16[512,2048]{1,0:T(8,128)(2,1)} %bitcast.86, bf16[2048,2048]{1,0:T(8,128)(2,1)} %all-gather.12.cloned.1.call-done.up_ref, bf16[512,2048]{1,0:T(8,128)(2,1)} %bitcast.81), custom_call_target="tpu_custom_call" | custom-call | flops 1073741824 | bytes 3750000 | tf_op jit(solution)/shard_map/ffn/pallas_call | solution.py:1313
  401.4 6.0 all-gather.16.cloned.1.call-done
  407.4 27.1 %ffn_back.1 = (bf16[512,2048]{1,0:T(8,128)(2,1)}, bf16[512,2048]{1,0:T(8,128)(2,1)}, bf16[8,512,2048]{2,1,0:T(8,128)(2,1)}) custom-call(bf16[512,2048]{1,0:T(8,128)(2,1)} %bitcast.87, bf16[512,8192]{1,0:T(8,128)(2,1)} %bitcast.85, bf16[2048,2048]{1,0:T(8,128)(2,1)} %all-gather.12.cloned.1.call-done.up_ref, ...), custom_call_target="tpu_custom_call", output_to_operand_aliasing={{2}: (6, {})} | custom-call | flops 2147483648 | bytes 6250000 | tf_op jit(solution)/shard_map/ffn_back/pallas_call | solution.py:1337
  435.5 95.7 %back1.1 = (f32[128,2048]{1,0:T(8,128)}, bf16[4,128,2048]{2,1,0:T(8,128)(2,1)}, bf16[512,512]{1,0:T(8,128)(2,1)S(1)}, f32[8,2048]{1,0:T(8,128)S(1)}, bf16[128,2048]{1,0:T(8,128)(2,1)S(1)}) custom-call(bf16[4,128,2048]{2,1,0:T(8,128)(2,1)} %bitcast.96, s32[2,288]{1,0:T(2,128)S(1)} %pad_add_fusion.refs_0_.w_hbm, bf16[128,2048]{1,0:T(8,128)(2,1)S(1)} %copy-done.1, ...), custom_call_target="tpu_custom_call" | custom-call | bytes 4000000 | tf_op jit(solution)/shard_map/back1/pallas_call | solution.py:1005
  531.1 10.0 %cross_back.1 = (bf16[512,512]{1,0:T(8,128)(2,1)S(1)}, bf16[2048,2048]{1,0:T(8,128)(2,1)}) custom-call(bf16[512,512]{1,0:T(8,128)(2,1)S(1)} %get-tuple-element.99.back_ref, bf16[512,512]{1,0:T(8,128)(2,1)S(1)} %get-tuple-element.81.cq_ref, bf16[2,128,512]{2,1,0:T(8,128)(2,1)S(1)} %get-tuple-element.100.kv_ref, f32[16,128,128]{2,1,0:T(8,128)} %get-tuple-element.101.share_ref, ...), custom_call_target="tpu_custom_call" | custom-call | flops 134217728 | bytes 2500000 | tf_op jit(solution)/shard_map/cross_back/pallas_call | solution.py:1367
  541.2 74.9 %back0.1 = (f32[128,2048]{1,0:T(8,128)}, bf16[4,128,2048]{2,1,0:T(8,128)(2,1)}, bf16[512,512]{1,0:T(8,128)(2,1)S(1)}, f32[8,2048]{1,0:T(8,128)S(1)}) custom-call(bf16[512,512]{1,0:T(8,128)(2,1)S(1)} %get-tuple-element.103.dy_ref.dcq_ref, bf16[2048,2048]{1,0:T(8,128)(2,1)} %all-gather.8.cloned.1.call-done.w_ref.refs_7_.w_hbm.refs_5_, ...), custom_call_target="tpu_custom_call" | custom-call | bytes 4000000 | tf_op jit(solution)/shard_map/back0/pallas_call | solution.py:1005
  616.1 6.3 outs_grad.1.both_ref
  622.4 15.1 %self_back.1 = (bf16[512,1536]{1,0:T(8,128)(2,1)}, bf16[8,384,2048]{2,1,0:T(8,128)(2,1)}) custom-call(bf16[512,512]{1,0:T(8,128)(2,1)S(1)} %get-tuple-element.105.back_ref, bf16[3,512,512]{2,1,0:T(8,128)(2,1)} %get-tuple-element.106.proj_ref, f32[16,128,128]{2,1,0:T(8,128)} %copy-done.2, ...), custom_call_target="tpu_custom_call", output_to_operand_aliasing={{1}: (6, {})} | custom-call | flops 536870912 | bytes 3125000 | tf_op jit(solution)/shard_map/self_back/pallas_call | solution.py:1406
  642.0 112.8 %leave_up.1 = (bf16[8,64,2048]{2,1,0:T(8,128)(2,1)}, bf16[8,64,2048]{2,1,0:T(8,128)(2,1)}, bf16[8,64,2048]{2,1,0:T(8,128)(2,1)}, bf16[128,2048]{1,0:T(8,128)(2,1)S(1)}, f32[8,2048]{1,0:T(8,128)S(1)}) custom-call(s32[2,576]{1,0:T(2,128)S(1)} %concatenate.26.refs_0_, bf16[4,64,2048]{2,1,0:T(8,128)(2,1)} %bitcast.91, bf16[4,64,2048]{2,1,0:T(8,128)(2,1)} %bitcast.90, ...), custom_call_target="tpu_custom_call" | custom-call | bytes 4000000 | tf_op jit(solution)/shard_map/leave_up/pallas_call | solution.py:921
  754.8 22.1 %reduce-scatter.8.cloned.1.call-done = bf16[384,2048]{1,0:T(8,128)(2,1)} async-done(((bf16[3072,2048]{1,0:T(8,128)(2,1)}), bf16[384,2048]{1,0:T(8,128)(2,1)}) %reduce-scatter.8.cloned.1.call-update) | async-done | bytes 1572880 | tf_op jit(solution)/shard_map/reduce_scatter | solution.py:1529
  779.4 30.7 %leave_query.1 = (bf16[8,64,3072]{2,1,0:T(8,128)(2,1)}, f32[8,256]{1,0:T(8,128)S(1)}) custom-call(s32[2,576]{1,0:T(2,128)S(1)} %concatenate.26.refs_0_, bf16[2,64,2048]{2,1,0:T(8,128)(2,1)S(1)} %slice.91.refs_1_, bf16[4,64,2048]{2,1,0:T(8,128)(2,1)S(1)} %slice.92.refs_2_, f32[8,2048]{1,0:T(8,128)S(1)} %pad_maximum_fusion.1.refs_3_), custom_call_target="tpu_custom_call" | custom-call | bytes 4000000 | tf_op jit(solution)/shard_map/leave_query/pallas_call | solution.py:921
  814.6 10.3 %multiply_subtract_fusion.2 = (f32[512,2048]{1,0:T(8,128)}, f32[512,2048]{1,0:T(8,128)}, f32[512,2048]{1,0:T(8,128)}) fusion(f32[512,2048]{1,0:T(8,128)} %refs_1_.7, bf16[8,64,2048]{2,1,0:T(8,128)(2,1)} %get-tuple-element.120, f32[512,2048]{1,0:T(8,128)} %param.43, f32[512,2048]{1,0:T(8,128)} %param.42), kind=kLoop, calls=%fused_computation.21 | loop fusion | flops 16777216 | bytes 27262976 | tf_op jit(solution)/shard_map/sub | solution.py:52
  827.9 8.4 multiply_subtract_fusion.1
  837.5 7.1 multiply_subtract_fusion
  844.6 7.8 all-to-all-done
  852.4 10.3 %multiply_subtract_fusion.3 = (f32[512,2048]{1,0:T(8,128)}, f32[512,2048]{1,0:T(8,128)}, f32[512,2048]{1,0:T(8,128)}) fusion(f32[512,2048]{1,0:T(8,128)} %refs_1_.4, bf16[512,3072]{1,0:T(8,128)(2,1)} %bitcast.46, f32[512,2048]{1,0:T(8,128)} %param.40, f32[512,2048]{1,0:T(8,128)} %param.39), kind=kLoop, calls=%fused_computation.22 | loop fusion | flops 16777216 | bytes 27262976 | tf_op jit(solution)/shard_map/sub | solution.py:52
  863.9 5.1 multiply_subtract_fusion.4
  (117 shorter events, 29.8 us)
Async XLA Ops:
  7.2 51.4 %copy-start = (bf16[128,2048]{1,0:T(8,128)(2,1)S(1)}, bf16[128,2048]{1,0:T(8,128)(2,1)}, u32[]{:S(2)}) copy-start(bf16[128,2048]{1,0:T(8,128)(2,1)} %refs_7_.1) | copy-start | bytes 1572868
  7.2 51.4 %copy-start.4 = (bf16[32,4096]{1,0:T(8,128)(2,1)S(1)}, bf16[32,4096]{1,0:T(8,128)(2,1)}, u32[]{:S(2)}) copy-start(bf16[32,4096]{1,0:T(8,128)(2,1)} %refs_3_.1) | copy-start | bytes 786436
  7.2 116.1 %all-gather.8.cloned.1.call-start = ((), (), s32[]{:S(2)}) async-start(), calls=%async_computation.4 | async-start | bytes 9437184 | tf_op jit(solution)/shard_map/all_gather | solution.py:1526
  58.5 133.7 %all-gather.14.cloned.1.call-start = ((), (), s32[]{:S(2)}) async-start(), calls=%async_computation.10 | async-start | bytes 4718592 | tf_op jit(solution)/shard_map/all_gather | solution.py:1526
  122.9 175.9 %all-gather.10.cloned.1.call-start = ((), (), s32[]{:S(2)}) async-start(), calls=%async_computation.5 | async-start | bytes 9437184 | tf_op jit(solution)/shard_map/all_gather | solution.py:1526
  192.1 194.1 %all-gather.12.cloned.1.call-start = ((), (), s32[]{:S(2)}) async-start(), calls=%async_computation.6 | async-start | bytes 9437184 | tf_op jit(solution)/shard_map/all_gather | solution.py:1526
  192.2 103.8 %copy-start.14 = (bf16[4,64,2048]{2,1,0:T(8,128)(2,1)S(1)}, bf16[4,64,2048]{2,1,0:T(8,128)(2,1)}, u32[]{:S(2)}) copy-start(bf16[4,64,2048]{2,1,0:T(8,128)(2,1)} %get-tuple-element.88) | copy-start | bytes 3145732
  295.0 112.3 %all-gather.16.cloned.1.call-start = ((), (), s32[]{:S(2)}) async-start(), calls=%async_computation.11 | async-start | bytes 9437184 | tf_op jit(solution)/shard_map/all_gather | solution.py:1526
  295.6 343.2 %reduce-scatter.4.cloned.1.call-start = ((), (), s32[]{:S(2)}) async-start(), calls=%async_computation.7 | async-start | bytes 18874368 | tf_op jit(solution)/shard_map/reduce_scatter | solution.py:1529
  434.5 207.5 %reduce-scatter.6.cloned.1.call-start = ((), (), s32[]{:S(2)}) async-start(), calls=%async_computation.8 | async-start | bytes 9437184 | tf_op jit(solution)/shard_map/reduce_scatter | solution.py:1529
  541.1 235.8 %reduce-scatter.8.cloned.1.call-start = ((), (), s32[]{:S(2)}) async-start(), calls=%async_computation.9 | async-start | bytes 14155776 | tf_op jit(solution)/shard_map/reduce_scatter | solution.py:1529
  810.1 42.4 %all-to-all-start = ((bf16[8,64,3072]{2,1,0:T(8,128)(2,1)}), bf16[8,64,3072]{2,1,0:T(8,128)(2,1)}, u32[]{:S(2)}, u32[]{:S(2)}) async-start(bf16[8,64,3072]{2,1,0:T(8,128)(2,1)} %get-tuple-element.119), calls=%async_computation.3 | async-start | bytes 6291456 | tf_op jit(solution)/shard_map/all_to_all | solution.py:1681
  814.5 10.4 %copy-start.15 = (f32[6,256]{1,0:T(8,128)S(1)}, f32[6,256]{1,0:T(8,128)}, u32[]{:S(2)}) copy-start(f32[6,256]{1,0:T(8,128)} %param.53) | copy-start | bytes 18436
  814.6 10.4 %copy-start.16 = (f32[6,256]{1,0:T(8,128)S(1)}, f32[6,256]{1,0:T(8,128)}, u32[]{:S(2)}) copy-start(f32[6,256]{1,0:T(8,128)} %param.55) | copy-start | bytes 18436
  814.6 10.4 %copy-start.17 = (f32[6,256]{1,0:T(8,128)S(1)}, f32[6,256]{1,0:T(8,128)}, u32[]{:S(2)}) copy-start(f32[6,256]{1,0:T(8,128)} %param.54) | copy-start | bytes 18436
  814.6 11.0 %copy-start.6 = (f32[512,2048]{1,0:T(8,128)S(1)}, f32[512,2048]{1,0:T(8,128)}, u32[]{:S(2)}) copy-start(f32[512,2048]{1,0:T(8,128)} %refs_1_.6) | copy-start | bytes 12582916
  814.6 12.1 %copy-start.8 = (f32[512,2048]{1,0:T(8,128)S(1)}, f32[512,2048]{1,0:T(8,128)}, u32[]{:S(2)}) copy-start(f32[512,2048]{1,0:T(8,128)} %param.49) | copy-start | bytes 12582916
  814.6 13.3 %copy-start.9 = (f32[512,2048]{1,0:T(8,128)S(1)}, f32[512,2048]{1,0:T(8,128)}, u32[]{:S(2)}) copy-start(f32[512,2048]{1,0:T(8,128)} %param.48) | copy-start | bytes 12582916
  827.9 8.4 copy-start.5
  827.9 8.4 copy-start.10
  827.9 9.6 %copy-start.11 = (f32[512,2048]{1,0:T(8,128)S(1)}, f32[512,2048]{1,0:T(8,128)}, u32[]{:S(2)}) copy-start(f32[512,2048]{1,0:T(8,128)} %param.51) | copy-start | bytes 12582916
  852.4 10.3 %copy-start.7 = (f32[512,1024]{1,0:T(8,128)S(1)}, f32[512,1024]{1,0:T(8,128)}, u32[]{:S(2)}) copy-start(f32[512,1024]{1,0:T(8,128)} %refs_1_.5) | copy-start | bytes 6291460
  852.4 10.3 %copy-start.12 = (f32[512,1024]{1,0:T(8,128)S(1)}, f32[512,1024]{1,0:T(8,128)}, u32[]{:S(2)}) copy-start(f32[512,1024]{1,0:T(8,128)} %param.46) | copy-start | bytes 6291460
  852.4 11.5 %copy-start.13 = (f32[512,1024]{1,0:T(8,128)S(1)}, f32[512,1024]{1,0:T(8,128)}, u32[]{:S(2)}) copy-start(f32[512,1024]{1,0:T(8,128)} %param.45) | copy-start | bytes 6291460
  (8 other events, 6.7 us)
Sparse Core Ops, SparseCore 0:
  58.6 64.6 all-gather.7
  125.2 53.2 all-gather.13
  192.2 89.5 all-gather.9
  295.1 55.9 all-gather.11
  352.9 54.4 all-gather.15
  434.6 115.9 reduce-scatter.3
  554.1 71.2 reduce-scatter.5
  637.7 139.2 reduce-scatter.7

commit v10 on v9

--- a/solution.py
+++ b/solution.py
@@ -1113,14 +1113,12 @@
     grad_ref,
     act_ref,
     slope_ref,
-    both_ref,
     branch_ref,
     part_ref,
     gup_ref,
     total,
     part,
 ):
-    del both_ref
     tile = pl.program_id(0)
     back_act = dot_nt(grad_ref[...], down_ref[...])
     back_up = (back_act * slope_ref[...]).astype(bf16)
@@ -1317,13 +1315,13 @@
         (
             shape((tokens, 4 * share), bf16),
             shape((tokens, 4 * share), f32),
-            shape((n_dp, 2 * n * chunk, 4 * share), bf16),
+            shape((n_dp, n * chunk, 4 * share), bf16),
         ),
         [fixed(hidden.shape), moving((width, share), lambda t: t), fixed(grad_all.shape)],
         (
             moving((tokens, share), lambda t: t),
             moving((tokens, share), lambda t: t),
-            pl.BlockSpec((n_dp, n * chunk // 4, 4 * share), lambda t: (0, 4 + t, 0)),
+            pl.BlockSpec((n_dp, n * chunk // 4, 4 * share), lambda t: (0, t, 0)),
         ),
         [],
         16 * tokens * width * share,
@@ -1331,14 +1329,18 @@
     )(hidden, up_z, grad_all)
 
 
-def ffn_back(hidden, down_z, up_z, grad_all, activated, slope, both):
+def ffn_back(hidden, down_z, up_z, grad_all, activated, slope, n_dp):
     tokens, width = hidden.shape
     share = down_z.shape[0]
     return local_call(
         ffn_back_kernel,
         "ffn_back",
         4,
-        (shape((tokens, width), bf16), shape((tokens, width), bf16), shape(both.shape, bf16)),
+        (
+            shape((tokens, width), bf16),
+            shape((tokens, width), bf16),
+            shape((n_dp, width // n_dp, 4 * share), bf16),
+        ),
         [
             fixed(hidden.shape),
             moving((share, width), lambda t: t),
@@ -1346,18 +1348,16 @@
             fixed(grad_all.shape),
             moving((tokens, share), lambda t: t),
             moving((tokens, share), lambda t: t),
-            in_place(),
         ],
         (
             fixed((tokens, width)),
             fixed((tokens, width)),
-            pl.BlockSpec((both.shape[0], both.shape[1] // 2, share), lambda t: (0, 0, t)),
+            pl.BlockSpec((n_dp, width // n_dp, share), lambda t: (0, 0, t)),
         ),
         [pltpu.VMEM((tokens, width), f32)] * 2,
         32 * tokens * width * share,
         50_000_000,
-        {6: 2},
-    )(hidden, down_z, up_z, grad_all, activated, slope, both)
+    )(hidden, down_z, up_z, grad_all, activated, slope)
 
 
 def cross_back(back_attended, cross_query, text_pairs, shares, text_all, rows):
@@ -1618,12 +1618,12 @@
         attended2, outs_z, 1, middle1, norm_full[4:6], None, n_z, n_dp, 2
     )
     hidden3 = hidden3.reshape(-1, width)
-    activated, slope, both = ffn(hidden3, up_z, grad_all, n_z, n_dp)
-    branch3, part3, both = ffn_back(hidden3, down_z, up_z, grad_all, activated, slope, both)
+    activated, slope, down_part = ffn(hidden3, up_z, grad_all, n_z, n_dp)
+    down_sum = gather_sum(down_part.reshape(-1, 4 * share), n_z)
+    branch3, part3, up_part = ffn_back(hidden3, down_z, up_z, grad_all, activated, slope, n_dp)
     branch3 = branch3.reshape(n_z, token_count, width)
     part3 = part3.reshape(n_z, token_count, width)
-    up_down_sum = gather_sum(both.reshape(-1, 4 * share), 2 * n_z)
-    up_sum, down_sum = up_down_sum[:n_z], up_down_sum[n_z:]
+    up_sum = gather_sum(up_part.reshape(-1, 4 * share), n_z)
     at_middle2, carry2, back_att2, term3, result = back_call(
         part3, after(slots, part3), None, grad_out, middle2, norm_full[4:6], outs_z, 1, branch3, n_z, n_dp, 3
     )
@@ -1632,21 +1632,40 @@
         back_att2, cross_query, text_pairs, shares2, text_all, token_count
     )
     text_sum = gather_sum(text_part, n_z)
-    at_middle1, carry1, back_att1, term2 = back_call(
-        back_cross, query_z, 3, at_middle2, middle1, norm_full[2:4], outs_z, 0, None, n_z, n_dp, 4
+    down_grad, at_middle1, carry1, back_att1, term2 = leave_call(
+        "back0",
+        4,
+        contents,
+        [(down_sum, False, cap_big, slot_firsts[4], True)],
+        None,
+        n_z,
+        n_dp,
+        back_parts(
+            back_cross,
+            query_z,
+            3,
+            at_middle2,
+            middle1,
+            norm_full[2:4],
+            outs_z,
+            0,
+            None,
+            n_z,
+            n_dp,
+            False,
+        ),
     )
     carry1 = carry1.reshape(-1, width)
-    both = outs_grad(after(attended1, up_down_sum), carry1, attended2, carry2, n_z, n_dp)
+    both = outs_grad(attended1, after(carry1, up_sum), attended2, carry2, n_z, n_dp)
     back_projected, both = self_back(
         back_att1, projected, shares1, hidden1, hidden2, back_cross, both, token_count
     )
     query_outs_sum = gather_sum(both.reshape(-1, 4 * share), 3 * n_z // 2)
-    down_grad, up_grad, text_grad, grad_in, term1 = leave_call(
+    up_grad, text_grad, grad_in, term1 = leave_call(
         "leave_up",
         8,
         contents,
         [
-            (down_sum, False, cap_big, slot_firsts[4], True),
             (up_sum, True, cap_big, slot_firsts[3], True),
             (text_sum, True, cap_big, slot_firsts[2], True),
         ],

time: 887 us -> 897 us (1.011)
  waiting for transfers between devices: 36.6 us -> 49.7 us
    pallas_call x2 -> x1, Pallas kernels: 171 us -> 96.4 us  [back_call(): return call(*args)]
    pallas_call x2 -> x3, Pallas kernels: 143 us -> 217 us  [leave_call(): line_call(kernel, name, ident, outs, specs, scratch, 0, LINK_COST)(*args)]
    reduce_scatter x3 -> x4, waiting for transfers between devices: 22.2 us -> 36.1 us  [gather_sum(): summed = lax.psum_scatter(piece, 'dp', scatter_dimension=0, tiled=True)]
  transfers between devices with their start and end apart: 9 -> 10, of which waited for: 3 -> 4; matrix products, arithmetic and copies ran while one was open for 4% -> 3% of each run, Pallas kernels for 74% -> 76%
where the time goes in v10:
time: 897 us; the launch traced here: 888 us
  Pallas kernels  755 us (84%)
  waiting for transfers between devices  49.7 us (6%)
  other arithmetic  47 us (5%)
  local copies, waits for them, and re-layouts  15.7 us (2%)
  between operations  14.7 us (2%)
    pallas_call x4, Pallas kernels, enter_call(): line_call(kernel, name, ident, outs, specs, scratch, 0, LINK_COST)(*args)  269 us
    pallas_call x3, Pallas kernels, leave_call(): line_call(kernel, name, ident, outs, specs, scratch, 0, LINK_COST)(*args)  217 us
    pallas_call x1, Pallas kernels, back_call(): return call(*args)  96.4 us
    pallas_call x1, Pallas kernels, forward_call(): return call(*args)  74.9 us
    sub x6, other arithmetic, adamw_update(): weight - rate * (first_hat / (jnp.sqrt(second_hat) + adam_eps) + decay *...  42 us
    reduce_scatter x4, waiting for transfers between devices, gather_sum(): summed = lax.psum_scatter(piece, 'dp', scatter_dimension=0, tiled=True)  36.1 us
    pallas_call x1, Pallas kernels, ffn_back(): local_call(ffn_back_kernel, 'ffn_back', 4, (shape((tokens, width), bf16),...  27.1 us
  transfers between devices with their start and end apart: 10, of which 4 were waited for; matrix products, arithmetic and copies ran while one was open for 3% of the time, Pallas kernels for 76%

profile of v10, /device:TPU:0, one launch (start us, length us, event | category | flops | bytes accessed | tf_op | source)
XLA Modules:
  0.0 888.0 jit_solution(7719332884547097357)
XLA Ops:
  11.5 46.9 %enter_query.1 = (bf16[4,64,2048]{2,1,0:T(8,128)(2,1)}, bf16[4,64,2048]{2,1,0:T(8,128)(2,1)}, s32[4,8,256]{2,1,0:T(8,128)S(1)}, f32[8,2048]{1,0:T(8,128)S(1)}) custom-call(s32[2,288]{1,0:T(2,128)S(1)} %pad_add_fusion.refs_0_.w_hbm, f32[512,2048]{1,0:T(8,128)} %refs_1_.4, bf16[64,2048]{1,0:T(8,128)(2,1)S(1)} %get-tuple-element.155.refs_2_, ...), custom_call_target="tpu_custom_call" | custom-call | bytes 4000000 | tf_op jit(solution)/shard_map/enter_query/pallas_call | solution.py:878
  58.6 64.3 %enter_outs.1 = (bf16[1,64,4096]{2,1,0:T(8,128)(2,1)}, bf16[4,128,2048]{2,1,0:T(8,128)(2,1)}, bf16[4,32,4096]{2,1,0:T(8,128)(2,1)}) custom-call(s32[2,288]{1,0:T(2,128)S(1)} %pad_add_fusion.refs_0_.w_hbm, f32[512,1024]{1,0:T(8,128)} %refs_1_.5, bf16[128,2048]{1,0:T(8,128)(2,1)S(1)} %copy-done, bf16[32,4096]{1,0:T(8,128)(2,1)S(1)} %copy-done.4, ...), custom_call_target="tpu_custom_call" | custom-call | bytes 4000000 | tf_op jit(solution)/shard_map/enter_outs/pallas_call | solution.py:878
  123.3 12.7 %self_forward.1 = (bf16[3,512,512]{2,1,0:T(8,128)(2,1)}, bf16[512,512]{1,0:T(8,128)(2,1)S(1)}, f32[16,128,128]{2,1,0:T(8,128)S(1)}) custom-call(bf16[512,2048]{1,0:T(8,128)(2,1)} %bitcast.86, bf16[2048,2048]{1,0:T(8,128)(2,1)} %all-gather.8.cloned.1.call-done.w_ref.refs_7_.refs_3_.refs_4_, s32[4,128,128]{2,1,0:T(8,128)S(1)} %get-tuple-element.160.mask_ref), custom_call_target="tpu_custom_call" | custom-call | flops 402653184 | bytes 2500000 | tf_op jit(solution)/shard_map/self_forward/pallas_call | solution.py:1270
  137.1 55.0 %enter_text.1 = (bf16[4,64,2048]{2,1,0:T(8,128)(2,1)}, bf16[4,64,2048]{2,1,0:T(8,128)(2,1)}) custom-call(s32[2,288]{1,0:T(2,128)S(1)} %pad_add_fusion.refs_0_.w_hbm, f32[512,2048]{1,0:T(8,128)} %refs_1_.6, bf16[64,2048]{1,0:T(8,128)(2,1)S(1)} %get-tuple-element.154.refs_2_), custom_call_target="tpu_custom_call" | custom-call | bytes 4000000 | tf_op jit(solution)/shard_map/enter_text/pallas_call | solution.py:878
  192.2 102.9 %forward0.1 = (bf16[4,64,2048]{2,1,0:T(8,128)(2,1)}, bf16[1,64,8192]{2,1,0:T(8,128)(2,1)}, f32[128,2048]{1,0:T(8,128)}, bf16[4,128,2048]{2,1,0:T(8,128)(2,1)}, bf16[512,512]{1,0:T(8,128)(2,1)S(1)}) custom-call(s32[2,288]{1,0:T(2,128)S(1)} %pad_add_fusion.refs_0_.w_hbm, f32[512,2048]{1,0:T(8,128)} %refs_1_.7, f32[512,2048]{1,0:T(8,128)} %refs_2_.3, ...), custom_call_target="tpu_custom_call" | custom-call | bytes 4000000 | tf_op jit(solution)/shard_map/forward0/pallas_call | solution.py:878
  298.7 11.5 %cross_forward.1 = (bf16[2,128,512]{2,1,0:T(8,128)(2,1)S(1)}, bf16[512,512]{1,0:T(8,128)(2,1)S(1)}, f32[16,128,128]{2,1,0:T(8,128)}) custom-call(bf16[512,512]{1,0:T(8,128)(2,1)S(1)} %get-tuple-element.82.cq_ref, bf16[128,4096]{1,0:T(8,128)(2,1)} %bitcast.90, bf16[2048,2048]{1,0:T(8,128)(2,1)} %all-gather.10.cloned.1.call-done.w_ref, ...), custom_call_target="tpu_custom_call" | custom-call | flops 134217728 | bytes 2500000 | tf_op jit(solution)/shard_map/cross_forward/pallas_call | solution.py:1289
  310.2 74.9 %forward1.1 = (f32[128,2048]{1,0:T(8,128)S(1)}, bf16[4,128,2048]{2,1,0:T(8,128)(2,1)}) custom-call(bf16[512,512]{1,0:T(8,128)(2,1)S(1)} %get-tuple-element.84.att_ref.att2_ref, bf16[512,4096]{1,0:T(8,128)(2,1)} %bitcast.78, f32[128,2048]{1,0:T(8,128)} %get-tuple-element.85.base_ref.refs_5_, f32[2,2048]{1,0:T(2,128)S(1)} %get-tuple-element.156.norm_ref), custom_call_target="tpu_custom_call" | custom-call | bytes 4000000 | tf_op jit(solution)/shard_map/forward1/pallas_call | solution.py:955
  386.1 15.2 %ffn.1 = (bf16[512,2048]{1,0:T(8,128)(2,1)}, f32[512,2048]{1,0:T(8,128)}, bf16[8,256,2048]{2,1,0:T(8,128)(2,1)}) custom-call(bf16[512,2048]{1,0:T(8,128)(2,1)} %bitcast.88, bf16[2048,2048]{1,0:T(8,128)(2,1)} %all-gather.12.cloned.1.call-done.up_ref, bf16[512,2048]{1,0:T(8,128)(2,1)} %bitcast.81), custom_call_target="tpu_custom_call" | custom-call | flops 1073741824 | bytes 3750000 | tf_op jit(solution)/shard_map/ffn/pallas_call | solution.py:1311
  401.8 5.7 all-gather.16.cloned.1.call-done
  407.5 27.1 %ffn_back.1 = (bf16[512,2048]{1,0:T(8,128)(2,1)}, bf16[512,2048]{1,0:T(8,128)(2,1)}, bf16[8,256,2048]{2,1,0:T(8,128)(2,1)}) custom-call(bf16[512,2048]{1,0:T(8,128)(2,1)} %bitcast.89, bf16[512,8192]{1,0:T(8,128)(2,1)} %bitcast.85, bf16[2048,2048]{1,0:T(8,128)(2,1)} %all-gather.12.cloned.1.call-done.up_ref, bf16[512,2048]{1,0:T(8,128)(2,1)} %bitcast.82, ...), custom_call_target="tpu_custom_call" | custom-call | flops 2147483648 | bytes 6250000 | tf_op jit(solution)/shard_map/ffn_back/pallas_call | solution.py:1335
  435.6 96.4 %back1.1 = (f32[128,2048]{1,0:T(8,128)}, bf16[4,128,2048]{2,1,0:T(8,128)(2,1)}, bf16[512,512]{1,0:T(8,128)(2,1)S(1)}, f32[8,2048]{1,0:T(8,128)S(1)}, bf16[128,2048]{1,0:T(8,128)(2,1)S(1)}) custom-call(bf16[4,128,2048]{2,1,0:T(8,128)(2,1)} %bitcast.96, s32[2,288]{1,0:T(2,128)S(1)} %pad_add_fusion.refs_0_.w_hbm, bf16[128,2048]{1,0:T(8,128)(2,1)S(1)} %copy-done.1, ...), custom_call_target="tpu_custom_call" | custom-call | bytes 4000000 | tf_op jit(solution)/shard_map/back1/pallas_call | solution.py:1005
  532.0 9.9 %cross_back.1 = (bf16[512,512]{1,0:T(8,128)(2,1)S(1)}, bf16[2048,2048]{1,0:T(8,128)(2,1)}) custom-call(bf16[512,512]{1,0:T(8,128)(2,1)S(1)} %get-tuple-element.99.back_ref, bf16[512,512]{1,0:T(8,128)(2,1)S(1)} %get-tuple-element.82.cq_ref, bf16[2,128,512]{2,1,0:T(8,128)(2,1)S(1)} %get-tuple-element.100.kv_ref, f32[16,128,128]{2,1,0:T(8,128)} %get-tuple-element.101.share_ref, ...), custom_call_target="tpu_custom_call" | custom-call | flops 134217728 | bytes 2500000 | tf_op jit(solution)/shard_map/cross_back/pallas_call | solution.py:1367
  543.3 80.4 %back0.1 = (bf16[8,64,2048]{2,1,0:T(8,128)(2,1)}, f32[128,2048]{1,0:T(8,128)}, bf16[4,128,2048]{2,1,0:T(8,128)(2,1)}, bf16[512,512]{1,0:T(8,128)(2,1)S(1)}, f32[8,2048]{1,0:T(8,128)S(1)}) custom-call(s32[2,576]{1,0:T(2,128)S(1)} %concatenate.26.refs_0_, bf16[4,64,2048]{2,1,0:T(8,128)(2,1)} %bitcast.102, ...), custom_call_target="tpu_custom_call" | custom-call | bytes 4000000 | tf_op jit(solution)/shard_map/back0/pallas_call | solution.py:921
  623.8 6.2 outs_grad.1.both_ref
  629.9 14.9 %self_back.1 = (bf16[512,1536]{1,0:T(8,128)(2,1)}, bf16[8,384,2048]{2,1,0:T(8,128)(2,1)}) custom-call(bf16[512,512]{1,0:T(8,128)(2,1)S(1)} %get-tuple-element.106.back_ref, bf16[3,512,512]{2,1,0:T(8,128)(2,1)} %get-tuple-element.107.proj_ref, f32[16,128,128]{2,1,0:T(8,128)} %copy-done.2, ...), custom_call_target="tpu_custom_call", output_to_operand_aliasing={{1}: (6, {})} | custom-call | flops 536870912 | bytes 3125000 | tf_op jit(solution)/shard_map/self_back/pallas_call | solution.py:1406
  649.0 106.3 %leave_up.1 = (bf16[8,64,2048]{2,1,0:T(8,128)(2,1)}, bf16[8,64,2048]{2,1,0:T(8,128)(2,1)}, bf16[128,2048]{1,0:T(8,128)(2,1)S(1)}, f32[8,2048]{1,0:T(8,128)S(1)}) custom-call(s32[2,576]{1,0:T(2,128)S(1)} %concatenate.26.refs_0_, bf16[4,64,2048]{2,1,0:T(8,128)(2,1)} %bitcast.99, bf16[4,64,2048]{2,1,0:T(8,128)(2,1)} %bitcast.100, ...), custom_call_target="tpu_custom_call" | custom-call | bytes 4000000 | tf_op jit(solution)/shard_map/leave_up/pallas_call | solution.py:921
  755.4 31.9 %reduce-scatter.11.cloned.1.call-done = bf16[384,2048]{1,0:T(8,128)(2,1)} async-done(((bf16[3072,2048]{1,0:T(8,128)(2,1)}), bf16[384,2048]{1,0:T(8,128)(2,1)}) %reduce-scatter.11.cloned.1.call-update) | async-done | bytes 1572880 | tf_op jit(solution)/shard_map/reduce_scatter | solution.py:1529
  789.7 30.7 %leave_query.1 = (bf16[8,64,3072]{2,1,0:T(8,128)(2,1)}, f32[8,256]{1,0:T(8,128)S(1)}) custom-call(s32[2,576]{1,0:T(2,128)S(1)} %concatenate.26.refs_0_, bf16[2,64,2048]{2,1,0:T(8,128)(2,1)S(1)} %slice.75.refs_1_, bf16[4,64,2048]{2,1,0:T(8,128)(2,1)S(1)} %slice.76.refs_2_, f32[8,2048]{1,0:T(8,128)S(1)} %pad_maximum_fusion.1.refs_3_), custom_call_target="tpu_custom_call" | custom-call | bytes 4000000 | tf_op jit(solution)/shard_map/leave_query/pallas_call | solution.py:921
  824.9 10.3 %multiply_subtract_fusion.2 = (f32[512,2048]{1,0:T(8,128)}, f32[512,2048]{1,0:T(8,128)}, f32[512,2048]{1,0:T(8,128)}) fusion(f32[512,2048]{1,0:T(8,128)} %refs_1_.7, bf16[8,64,2048]{2,1,0:T(8,128)(2,1)} %get-tuple-element.122, f32[512,2048]{1,0:T(8,128)} %param.43, f32[512,2048]{1,0:T(8,128)} %param.42), kind=kLoop, calls=%fused_computation.21 | loop fusion | flops 16777216 | bytes 27262976 | tf_op jit(solution)/shard_map/sub | solution.py:52
  838.2 8.4 multiply_subtract_fusion.1
  847.8 7.1 multiply_subtract_fusion
  855.6 7.2 all-to-all-done
  862.8 10.3 %multiply_subtract_fusion.3 = (f32[512,2048]{1,0:T(8,128)}, f32[512,2048]{1,0:T(8,128)}, f32[512,2048]{1,0:T(8,128)}) fusion(f32[512,2048]{1,0:T(8,128)} %refs_1_.4, bf16[512,3072]{1,0:T(8,128)(2,1)} %bitcast.47, f32[512,2048]{1,0:T(8,128)} %param.40, f32[512,2048]{1,0:T(8,128)} %param.39), kind=kLoop, calls=%fused_computation.22 | loop fusion | flops 16777216 | bytes 27262976 | tf_op jit(solution)/shard_map/sub | solution.py:52
  874.3 5.1 multiply_subtract_fusion.4
  (119 shorter events, 31.7 us)
Async XLA Ops:
  7.2 51.3 %copy-start = (bf16[128,2048]{1,0:T(8,128)(2,1)S(1)}, bf16[128,2048]{1,0:T(8,128)(2,1)}, u32[]{:S(2)}) copy-start(bf16[128,2048]{1,0:T(8,128)(2,1)} %refs_6_.1) | copy-start | bytes 1572868
  7.2 51.3 %copy-start.4 = (bf16[32,4096]{1,0:T(8,128)(2,1)S(1)}, bf16[32,4096]{1,0:T(8,128)(2,1)}, u32[]{:S(2)}) copy-start(bf16[32,4096]{1,0:T(8,128)(2,1)} %refs_3_.1) | copy-start | bytes 786436
  7.2 116.1 %all-gather.8.cloned.1.call-start = ((), (), s32[]{:S(2)}) async-start(), calls=%async_computation.5 | async-start | bytes 9437184 | tf_op jit(solution)/shard_map/all_gather | solution.py:1526
  58.5 133.7 %all-gather.14.cloned.1.call-start = ((), (), s32[]{:S(2)}) async-start(), calls=%async_computation.12 | async-start | bytes 4718592 | tf_op jit(solution)/shard_map/all_gather | solution.py:1526
  122.9 175.8 %all-gather.10.cloned.1.call-start = ((), (), s32[]{:S(2)}) async-start(), calls=%async_computation.6 | async-start | bytes 9437184 | tf_op jit(solution)/shard_map/all_gather | solution.py:1526
  192.1 194.0 %all-gather.12.cloned.1.call-start = ((), (), s32[]{:S(2)}) async-start(), calls=%async_computation.7 | async-start | bytes 9437184 | tf_op jit(solution)/shard_map/all_gather | solution.py:1526
  192.1 103.8 %copy-start.14 = (bf16[4,64,2048]{2,1,0:T(8,128)(2,1)S(1)}, bf16[4,64,2048]{2,1,0:T(8,128)(2,1)}, u32[]{:S(2)}) copy-start(bf16[4,64,2048]{2,1,0:T(8,128)(2,1)} %get-tuple-element.89) | copy-start | bytes 3145732
  295.1 112.4 %all-gather.16.cloned.1.call-start = ((), (), s32[]{:S(2)}) async-start(), calls=%async_computation.13 | async-start | bytes 9437184 | tf_op jit(solution)/shard_map/all_gather | solution.py:1526
  295.7 247.6 %reduce-scatter.9.cloned.1.call-start = ((), (), s32[]{:S(2)}) async-start(), calls=%async_computation.10 | async-start | bytes 9437184 | tf_op jit(solution)/shard_map/reduce_scatter | solution.py:1529
  401.4 222.4 %reduce-scatter.5.cloned.1.call-start = ((), (), s32[]{:S(2)}) async-start(), calls=%async_computation.8 | async-start | bytes 9437184 | tf_op jit(solution)/shard_map/reduce_scatter | solution.py:1529
  434.6 214.4 %reduce-scatter.7.cloned.1.call-start = ((), (), s32[]{:S(2)}) async-start(), calls=%async_computation.9 | async-start | bytes 9437184 | tf_op jit(solution)/shard_map/reduce_scatter | solution.py:1529
  542.0 245.4 %reduce-scatter.11.cloned.1.call-start = ((), (), s32[]{:S(2)}) async-start(), calls=%async_computation.11 | async-start | bytes 14155776 | tf_op jit(solution)/shard_map/reduce_scatter | solution.py:1529
  820.4 42.4 %all-to-all-start = ((bf16[8,64,3072]{2,1,0:T(8,128)(2,1)}), bf16[8,64,3072]{2,1,0:T(8,128)(2,1)}, u32[]{:S(2)}, u32[]{:S(2)}) async-start(bf16[8,64,3072]{2,1,0:T(8,128)(2,1)} %get-tuple-element.121), calls=%async_computation.4 | async-start | bytes 6291456 | tf_op jit(solution)/shard_map/all_to_all | solution.py:1700
  824.9 10.4 %copy-start.6 = (f32[512,2048]{1,0:T(8,128)S(1)}, f32[512,2048]{1,0:T(8,128)}, u32[]{:S(2)}) copy-start(f32[512,2048]{1,0:T(8,128)} %refs_1_.6) | copy-start | bytes 12582916
  824.9 12.1 %copy-start.8 = (f32[512,2048]{1,0:T(8,128)S(1)}, f32[512,2048]{1,0:T(8,128)}, u32[]{:S(2)}) copy-start(f32[512,2048]{1,0:T(8,128)} %param.49) | copy-start | bytes 12582916
  824.9 13.3 %copy-start.9 = (f32[512,2048]{1,0:T(8,128)S(1)}, f32[512,2048]{1,0:T(8,128)}, u32[]{:S(2)}) copy-start(f32[512,2048]{1,0:T(8,128)} %param.48) | copy-start | bytes 12582916
  838.2 8.4 copy-start.5
  838.2 8.4 copy-start.10
  838.2 9.6 %copy-start.11 = (f32[512,2048]{1,0:T(8,128)S(1)}, f32[512,2048]{1,0:T(8,128)}, u32[]{:S(2)}) copy-start(f32[512,2048]{1,0:T(8,128)} %param.51) | copy-start | bytes 12582916
  847.8 7.1 copy-start.16
  847.8 7.1 copy-start.17
  862.8 10.3 %copy-start.7 = (f32[512,1024]{1,0:T(8,128)S(1)}, f32[512,1024]{1,0:T(8,128)}, u32[]{:S(2)}) copy-start(f32[512,1024]{1,0:T(8,128)} %refs_1_.5) | copy-start | bytes 6291460
  862.8 10.3 %copy-start.12 = (f32[512,1024]{1,0:T(8,128)S(1)}, f32[512,1024]{1,0:T(8,128)}, u32[]{:S(2)}) copy-start(f32[512,1024]{1,0:T(8,128)} %param.46) | copy-start | bytes 6291460
  862.8 11.5 %copy-start.13 = (f32[512,1024]{1,0:T(8,128)S(1)}, f32[512,1024]{1,0:T(8,128)}, u32[]{:S(2)}) copy-start(f32[512,1024]{1,0:T(8,128)} %param.45) | copy-start | bytes 6291460
  (9 other events, 14.0 us)
Sparse Core Ops, SparseCore 0:
  58.6 64.6 all-gather.7
  125.2 53.1 all-gather.13
  192.2 89.5 all-gather.9
  295.2 56.0 all-gather.11
  353.1 54.3 all-gather.15
  410.8 71.2 reduce-scatter.8
  486.0 88.1 reduce-scatter.4
  577.7 71.3 reduce-scatter.6
  652.9 134.3 reduce-scatter.10

commit v11 on v8

--- a/solution.py
+++ b/solution.py
@@ -1086,12 +1086,7 @@
     activated = (up_values * chance).astype(bf16)
     act_ref[...] = activated
     slope_ref[...] = chance + up_values * density
-    gradient = dot_tn(activated, grad_ref[...]).astype(bf16)
-    n_dp, rows, columns = gdown_ref.shape
-    chunk = gradient.shape[0] // n_dp
-    for piece in range(rows // chunk):
-        cut = gradient[:, piece * columns : (piece + 1) * columns]
-        gdown_ref[:, piece * chunk : (piece + 1) * chunk] = cut.reshape(n_dp, chunk, columns)
+    store_pieces(dot_tn(activated, grad_ref[...]), gdown_ref)
 
 
 def ffn_back_kernel(
@@ -1157,16 +1152,36 @@
 
     @pl.when(tile == 0)
     def _():
-        grad_ref[...] = dot_tn(att1_ref[...], carry1_ref[...]).astype(bf16)
+        store_pieces(dot_tn(att1_ref[...], carry1_ref[...]), grad_ref)
 
     @pl.when(tile == 1)
     def _():
-        grad_ref[...] = dot_tn(att2_ref[...], carry2_ref[...]).astype(bf16)
+        store_pieces(dot_tn(att2_ref[...], carry2_ref[...]), grad_ref)
+
+
+def store_pieces(gradient, target):
+    n_dp, rows, columns = target.shape
+    gradient = gradient.astype(bf16)
+    chunk = gradient.shape[0] // n_dp
+    for piece in range(rows // chunk):
+        cut = gradient[:, piece * columns : (piece + 1) * columns]
+        target[:, piece * chunk : (piece + 1) * chunk] = cut.reshape(n_dp, chunk, columns)
 
 
 def self_back_kernel(
-    rows, back_ref, proj_ref, share_ref, h1_ref, h2_ref, dcq_ref, dproj_ref, grad_ref, parts
+    rows,
+    back_ref,
+    proj_ref,
+    share_ref,
+    h1_ref,
+    h2_ref,
+    dcq_ref,
+    both_ref,
+    dproj_ref,
+    grad_ref,
+    parts,
 ):
+    del both_ref
     tile = pl.program_id(0)
     share = dcq_ref.shape[1]
 
@@ -1198,11 +1213,11 @@
 
     @pl.when(tile < 3)
     def _():
-        grad_ref[...] = dot_tn(h1_ref[...], parts[tile]).astype(bf16)
+        grad_ref[...] = dot_tn(h1_ref[...], parts[tile]).astype(bf16).reshape(grad_ref.shape)
 
     @pl.when(tile == 3)
     def _():
-        grad_ref[...] = dot_tn(h2_ref[...], dcq_ref[...]).astype(bf16)
+        grad_ref[...] = dot_tn(h2_ref[...], dcq_ref[...]).astype(bf16).reshape(grad_ref.shape)
 
 
 def fixed(dims):
@@ -1351,30 +1366,31 @@
     )(back_attended, cross_query, text_pairs, shares, text_all)
 
 
-def outs_grad(attended1, carry1, attended2, carry2):
+def outs_grad(attended1, carry1, attended2, carry2, n, n_dp):
     tokens, share = attended1.shape
     width = carry1.shape[1]
+    chunk = share // n_dp
     return local_call(
         outs_grad_kernel,
         "outs_grad",
         2,
-        shape((share, 2 * width), bf16),
+        shape((n_dp, n * chunk * 3 // 2, 4 * share), bf16),
         [fixed((tokens, share)), fixed((tokens, width))] * 2,
-        moving((share, width), lambda t: t),
+        pl.BlockSpec((n_dp, n * chunk // 4, 4 * share), lambda t: (0, 4 + t, 0)),
         [],
         4 * tokens * width * share,
         10_000_000,
     )(attended1, carry1, attended2, carry2)
 
 
-def self_back(back_attended, projected, shares, hidden1, hidden2, back_cross, rows):
+def self_back(back_attended, projected, shares, hidden1, hidden2, back_cross, both, rows):
     tokens, width = hidden1.shape
     share = back_cross.shape[1]
     return local_call(
         functools.partial(self_back_kernel, rows),
         "self_back",
         4,
-        (shape((tokens, 3 * share), bf16), shape((width, 4 * share), bf16)),
+        (shape((tokens, 3 * share), bf16), shape(both.shape, bf16)),
         [
             fixed(back_attended.shape),
             fixed(projected.shape),
@@ -1382,12 +1398,17 @@
             fixed(hidden1.shape),
             fixed(hidden2.shape),
             fixed(back_cross.shape),
+            in_place(),
         ],
-        (fixed((tokens, 3 * share)), moving((width, share), lambda t: t)),
+        (
+            fixed((tokens, 3 * share)),
+            pl.BlockSpec((both.shape[0], both.shape[1] * 2 // 3, share), lambda t: (0, 0, t)),
+        ),
         [pltpu.VMEM((3, tokens, share), bf16)],
         8 * tokens * width * share,
         25_000_000,
-    )(back_attended, projected, shares, hidden1, hidden2, back_cross)
+        {6: 1},
+    )(back_attended, projected, shares, hidden1, hidden2, back_cross, both)
 
 
 def block_slots(owners):
@@ -1598,11 +1619,11 @@
         back_cross, query_z, 3, at_middle2, middle1, norm_full[2:4], outs_z, 0, n_z, n_dp, 4
     )
     carry1 = carry1.reshape(-1, width)
-    back_projected, query_part = self_back(
-        back_att1, projected, shares1, hidden1, hidden2, back_cross, token_count
-    )
-    query_sum = gather_sum(query_part, n_z)
-    outs_sum = gather_sum(outs_grad(after(attended1, query_part), carry1, attended2, carry2), 1)
+    both = outs_grad(attended1, after(carry1, up_down_sum), attended2, carry2, n_z, n_dp)
+    back_projected, both = self_back(
+        back_att1, projected, shares1, hidden1, hidden2, back_cross, both, token_count
+    )
+    query_outs_sum = gather_sum(both.reshape(-1, 4 * share), 3 * n_z // 2)
     down_grad, up_grad, text_grad, grad_in, result, term1 = leave_call(
         "leave_up",
         8,
@@ -1627,6 +1648,8 @@
             n_dp,
         ),
     )
+    query_outs_sum = after(query_outs_sum, term1)
+    query_sum, outs_sum = query_outs_sum[:n_z], query_outs_sum[n_z:]
     norm_term = jnp.concatenate([term1[:2], term2[:2], term3[:4]], axis=0)
     loose, norm_grad = leave_call(
         "leave_query",

time: 898 us -> 874 us (0.973)
  waiting for transfers between devices: 52 us -> 26.3 us
    reduce_scatter x4 -> x3, waiting for transfers between devices: 36.9 us -> 11.7 us  [gather_sum(): summed = lax.psum_scatter(piece, 'dp', scatter_dimension=0, tiled=True)]
  transfers between devices with their start and end apart: 10 -> 9, of which waited for: 4 -> 4; matrix products, arithmetic and copies ran while one was open for 4% -> 4% of each run, Pallas kernels for 73% -> 75%
where the time goes in v11:
time: 874 us; the launch traced here: 865 us
  Pallas kernels  753 us (86%)
  other arithmetic  47 us (5%)
  waiting for transfers between devices  26.3 us (3%)
  local copies, waits for them, and re-layouts  18.2 us (2%)
  between operations  15 us (2%)
    pallas_call x4, Pallas kernels, enter_call(): line_call(kernel, name, ident, outs, specs, scratch, 0, LINK_COST)(*args)  269 us
    pallas_call x2, Pallas kernels, leave_call(): line_call(kernel, name, ident, outs, specs, scratch, 0, LINK_COST)(*args)  165 us
    pallas_call x2, Pallas kernels, back_call(): return call(*args)  147 us
    pallas_call x1, Pallas kernels, forward_call(): return call(*args)  74.9 us
    sub x6, other arithmetic, adamw_update(): weight - rate * (first_hat / (jnp.sqrt(second_hat) + adam_eps) + decay *...  41.9 us
    pallas_call x1, Pallas kernels, ffn_back(): local_call(ffn_back_kernel, 'ffn_back', 4, (shape((tokens, width), bf16),...  27.1 us
  transfers between devices with their start and end apart: 9, of which 4 were waited for; matrix products, arithmetic and copies ran while one was open for 4% of the time, Pallas kernels for 75%

profile of v11, /device:TPU:0, one launch (start us, length us, event | category | flops | bytes accessed | tf_op | source)
XLA Modules:
  0.0 864.6 jit_solution(14366229974883296145)
XLA Ops:
  11.5 46.9 %enter_query.1 = (bf16[4,64,2048]{2,1,0:T(8,128)(2,1)}, bf16[4,64,2048]{2,1,0:T(8,128)(2,1)}, s32[4,8,256]{2,1,0:T(8,128)S(1)}, f32[8,2048]{1,0:T(8,128)S(1)}) custom-call(s32[2,288]{1,0:T(2,128)S(1)} %pad_add_fusion.refs_0_.w_hbm, f32[512,2048]{1,0:T(8,128)} %refs_1_.4, bf16[64,2048]{1,0:T(8,128)(2,1)S(1)} %get-tuple-element.155.refs_2_, ...), custom_call_target="tpu_custom_call" | custom-call | bytes 4000000 | tf_op jit(solution)/shard_map/enter_query/pallas_call | solution.py:864
  58.6 64.3 %enter_outs.1 = (bf16[1,64,4096]{2,1,0:T(8,128)(2,1)}, bf16[4,128,2048]{2,1,0:T(8,128)(2,1)}, bf16[4,32,4096]{2,1,0:T(8,128)(2,1)}) custom-call(s32[2,288]{1,0:T(2,128)S(1)} %pad_add_fusion.refs_0_.w_hbm, f32[512,1024]{1,0:T(8,128)} %refs_1_.5, bf16[128,2048]{1,0:T(8,128)(2,1)S(1)} %copy-done, bf16[32,4096]{1,0:T(8,128)(2,1)S(1)} %copy-done.4, ...), custom_call_target="tpu_custom_call" | custom-call | bytes 4000000 | tf_op jit(solution)/shard_map/enter_outs/pallas_call | solution.py:864
  123.4 12.7 %self_forward.1 = (bf16[3,512,512]{2,1,0:T(8,128)(2,1)}, bf16[512,512]{1,0:T(8,128)(2,1)S(1)}, f32[16,128,128]{2,1,0:T(8,128)S(1)}) custom-call(bf16[512,2048]{1,0:T(8,128)(2,1)} %bitcast.83, bf16[2048,2048]{1,0:T(8,128)(2,1)} %all-gather.8.cloned.1.call-done.w_ref.refs_7_.w_hbm.refs_5_, s32[4,128,128]{2,1,0:T(8,128)S(1)} %get-tuple-element.160.mask_ref), custom_call_target="tpu_custom_call" | custom-call | flops 402653184 | bytes 2500000 | tf_op jit(solution)/shard_map/self_forward/pallas_call | solution.py:1255
  137.1 55.0 %enter_text.1 = (bf16[4,64,2048]{2,1,0:T(8,128)(2,1)}, bf16[4,64,2048]{2,1,0:T(8,128)(2,1)}) custom-call(s32[2,288]{1,0:T(2,128)S(1)} %pad_add_fusion.refs_0_.w_hbm, f32[512,2048]{1,0:T(8,128)} %refs_1_.6, bf16[64,2048]{1,0:T(8,128)(2,1)S(1)} %get-tuple-element.154.refs_2_), custom_call_target="tpu_custom_call" | custom-call | bytes 4000000 | tf_op jit(solution)/shard_map/enter_text/pallas_call | solution.py:864
  192.2 102.8 %forward0.1 = (bf16[4,64,2048]{2,1,0:T(8,128)(2,1)}, bf16[1,64,8192]{2,1,0:T(8,128)(2,1)}, f32[128,2048]{1,0:T(8,128)}, bf16[4,128,2048]{2,1,0:T(8,128)(2,1)}, bf16[512,512]{1,0:T(8,128)(2,1)S(1)}) custom-call(s32[2,288]{1,0:T(2,128)S(1)} %pad_add_fusion.refs_0_.w_hbm, f32[512,2048]{1,0:T(8,128)} %refs_1_.7, f32[512,2048]{1,0:T(8,128)} %refs_2_.3, ...), custom_call_target="tpu_custom_call" | custom-call | bytes 4000000 | tf_op jit(solution)/shard_map/forward0/pallas_call | solution.py:864
  298.6 11.5 %cross_forward.1 = (bf16[2,128,512]{2,1,0:T(8,128)(2,1)S(1)}, bf16[512,512]{1,0:T(8,128)(2,1)S(1)}, f32[16,128,128]{2,1,0:T(8,128)}) custom-call(bf16[512,512]{1,0:T(8,128)(2,1)S(1)} %get-tuple-element.81.cq_ref, bf16[128,4096]{1,0:T(8,128)(2,1)} %bitcast.88, bf16[2048,2048]{1,0:T(8,128)(2,1)} %all-gather.10.cloned.1.call-done.w_ref, ...), custom_call_target="tpu_custom_call" | custom-call | flops 134217728 | bytes 2500000 | tf_op jit(solution)/shard_map/cross_forward/pallas_call | solution.py:1274
  310.2 74.9 %forward1.1 = (f32[128,2048]{1,0:T(8,128)S(1)}, bf16[4,128,2048]{2,1,0:T(8,128)(2,1)}) custom-call(bf16[512,512]{1,0:T(8,128)(2,1)S(1)} %get-tuple-element.83.att_ref.att2_ref, bf16[512,4096]{1,0:T(8,128)(2,1)} %bitcast.77, f32[128,2048]{1,0:T(8,128)} %get-tuple-element.84.base_ref.middle_ref, f32[2,2048]{1,0:T(2,128)S(1)} %get-tuple-element.156.norm_ref), custom_call_target="tpu_custom_call" | custom-call | bytes 4000000 | tf_op jit(solution)/shard_map/forward1/pallas_call | solution.py:941
  386.1 15.2 %ffn.1 = (bf16[512,2048]{1,0:T(8,128)(2,1)}, f32[512,2048]{1,0:T(8,128)}, bf16[8,512,2048]{2,1,0:T(8,128)(2,1)}) custom-call(bf16[512,2048]{1,0:T(8,128)(2,1)} %bitcast.86, bf16[2048,2048]{1,0:T(8,128)(2,1)} %all-gather.12.cloned.1.call-done.up_ref, bf16[512,2048]{1,0:T(8,128)(2,1)} %bitcast.81), custom_call_target="tpu_custom_call" | custom-call | flops 1073741824 | bytes 3750000 | tf_op jit(solution)/shard_map/ffn/pallas_call | solution.py:1296
  401.3 6.1 all-gather.16.cloned.1.call-done
  407.3 27.1 %ffn_back.1 = (bf16[512,2048]{1,0:T(8,128)(2,1)}, bf16[512,2048]{1,0:T(8,128)(2,1)}, bf16[8,512,2048]{2,1,0:T(8,128)(2,1)}) custom-call(bf16[512,2048]{1,0:T(8,128)(2,1)} %bitcast.87, bf16[512,8192]{1,0:T(8,128)(2,1)} %bitcast.85, bf16[2048,2048]{1,0:T(8,128)(2,1)} %all-gather.12.cloned.1.call-done.up_ref, ...), custom_call_target="tpu_custom_call", output_to_operand_aliasing={{2}: (6, {})} | custom-call | flops 2147483648 | bytes 6250000 | tf_op jit(solution)/shard_map/ffn_back/pallas_call | solution.py:1320
  435.5 72.5 %back1.1 = (f32[128,2048]{1,0:T(8,128)}, bf16[4,128,2048]{2,1,0:T(8,128)(2,1)}, bf16[512,512]{1,0:T(8,128)(2,1)S(1)}, f32[8,2048]{1,0:T(8,128)S(1)}) custom-call(bf16[4,128,2048]{2,1,0:T(8,128)(2,1)} %bitcast.95, s32[2,288]{1,0:T(2,128)S(1)} %pad_add_fusion.refs_0_.w_hbm, bf16[128,2048]{1,0:T(8,128)(2,1)S(1)} %copy-done.2, f32[128,2048]{1,0:T(8,128)} %copy-done.1, ...), custom_call_target="tpu_custom_call" | custom-call | bytes 4000000 | tf_op jit(solution)/shard_map/back1/pallas_call | solution.py:985
  508.0 10.0 %cross_back.1 = (bf16[512,512]{1,0:T(8,128)(2,1)S(1)}, bf16[2048,2048]{1,0:T(8,128)(2,1)}) custom-call(bf16[512,512]{1,0:T(8,128)(2,1)S(1)} %get-tuple-element.97.back_ref, bf16[512,512]{1,0:T(8,128)(2,1)S(1)} %get-tuple-element.81.cq_ref, bf16[2,128,512]{2,1,0:T(8,128)(2,1)S(1)} %get-tuple-element.98.kv_ref, f32[16,128,128]{2,1,0:T(8,128)} %get-tuple-element.99.share_ref, ...), custom_call_target="tpu_custom_call" | custom-call | flops 134217728 | bytes 2500000 | tf_op jit(solution)/shard_map/cross_back/pallas_call | solution.py:1350
  518.0 74.0 %back0.1 = (f32[128,2048]{1,0:T(8,128)}, bf16[4,128,2048]{2,1,0:T(8,128)(2,1)}, bf16[512,512]{1,0:T(8,128)(2,1)S(1)}, f32[8,2048]{1,0:T(8,128)S(1)}) custom-call(bf16[512,512]{1,0:T(8,128)(2,1)S(1)} %get-tuple-element.101.dy_ref.dcq_ref, bf16[2048,2048]{1,0:T(8,128)(2,1)} %all-gather.8.cloned.1.call-done.w_ref.refs_7_.w_hbm.refs_5_, ...), custom_call_target="tpu_custom_call" | custom-call | bytes 4000000 | tf_op jit(solution)/shard_map/back0/pallas_call | solution.py:985
  592.1 6.3 outs_grad.1.both_ref
  598.4 15.1 %self_back.1 = (bf16[512,1536]{1,0:T(8,128)(2,1)}, bf16[8,384,2048]{2,1,0:T(8,128)(2,1)}) custom-call(bf16[512,512]{1,0:T(8,128)(2,1)S(1)} %get-tuple-element.103.back_ref, bf16[3,512,512]{2,1,0:T(8,128)(2,1)} %get-tuple-element.104.proj_ref, f32[16,128,128]{2,1,0:T(8,128)} %copy-done.3, ...), custom_call_target="tpu_custom_call", output_to_operand_aliasing={{1}: (6, {})} | custom-call | flops 536870912 | bytes 3125000 | tf_op jit(solution)/shard_map/self_back/pallas_call | solution.py:1389
  618.0 7.4 reduce-scatter.6.cloned.1.call-done
  625.3 134.1 %leave_up.1 = (bf16[8,64,2048]{2,1,0:T(8,128)(2,1)}, bf16[8,64,2048]{2,1,0:T(8,128)(2,1)}, bf16[8,64,2048]{2,1,0:T(8,128)(2,1)}, bf16[128,2048]{1,0:T(8,128)(2,1...) custom-call(s32[2,576]{1,0:T(2,128)S(1)} %concatenate.39.refs_0_, bf16[4,64,2048]{2,1,0:T(8,128)(2,1)} %bitcast.91, ...), custom_call_target="tpu_custom_call" | custom-call | bytes 4000000 | tf_op jit(solution)/shard_map/leave_up/pallas_call | solution.py:907
  766.2 30.7 %leave_query.1 = (bf16[8,64,3072]{2,1,0:T(8,128)(2,1)}, f32[8,256]{1,0:T(8,128)S(1)}) custom-call(s32[2,576]{1,0:T(2,128)S(1)} %concatenate.39.refs_0_, bf16[2,64,2048]{2,1,0:T(8,128)(2,1)S(1)} %slice.91.refs_1_, bf16[4,64,2048]{2,1,0:T(8,128)(2,1)S(1)} %slice.92.refs_2_, f32[8,2048]{1,0:T(8,128)S(1)} %pad_maximum_fusion.1.refs_3_), custom_call_target="tpu_custom_call" | custom-call | bytes 4000000 | tf_op jit(solution)/shard_map/leave_query/pallas_call | solution.py:907
  801.4 10.3 %multiply_subtract_fusion.2 = (f32[512,2048]{1,0:T(8,128)}, f32[512,2048]{1,0:T(8,128)}, f32[512,2048]{1,0:T(8,128)}) fusion(f32[512,2048]{1,0:T(8,128)} %refs_1_.7, bf16[8,64,2048]{2,1,0:T(8,128)(2,1)} %get-tuple-element.120, f32[512,2048]{1,0:T(8,128)} %param.43, f32[512,2048]{1,0:T(8,128)} %param.42), kind=kLoop, calls=%fused_computation.21 | loop fusion | flops 16777216 | bytes 27262976 | tf_op jit(solution)/shard_map/sub | solution.py:52
  814.7 8.4 multiply_subtract_fusion.1
  824.3 7.1 multiply_subtract_fusion
  831.4 7.8 all-to-all-done
  839.2 10.3 %multiply_subtract_fusion.3 = (f32[512,2048]{1,0:T(8,128)}, f32[512,2048]{1,0:T(8,128)}, f32[512,2048]{1,0:T(8,128)}) fusion(f32[512,2048]{1,0:T(8,128)} %refs_1_.4, bf16[512,3072]{1,0:T(8,128)(2,1)} %bitcast.46, f32[512,2048]{1,0:T(8,128)} %param.40, f32[512,2048]{1,0:T(8,128)} %param.39), kind=kLoop, calls=%fused_computation.22 | loop fusion | flops 16777216 | bytes 27262976 | tf_op jit(solution)/shard_map/sub | solution.py:52
  850.7 5.1 multiply_subtract_fusion.4
  (117 shorter events, 33.9 us)
Async XLA Ops:
  7.2 51.4 %copy-start = (bf16[128,2048]{1,0:T(8,128)(2,1)S(1)}, bf16[128,2048]{1,0:T(8,128)(2,1)}, u32[]{:S(2)}) copy-start(bf16[128,2048]{1,0:T(8,128)(2,1)} %refs_7_.1) | copy-start | bytes 1572868
  7.2 51.4 %copy-start.4 = (bf16[32,4096]{1,0:T(8,128)(2,1)S(1)}, bf16[32,4096]{1,0:T(8,128)(2,1)}, u32[]{:S(2)}) copy-start(bf16[32,4096]{1,0:T(8,128)(2,1)} %refs_3_.1) | copy-start | bytes 786436
  7.2 116.1 %all-gather.8.cloned.1.call-start = ((), (), s32[]{:S(2)}) async-start(), calls=%async_computation.4 | async-start | bytes 9437184 | tf_op jit(solution)/shard_map/all_gather | solution.py:1509
  58.5 133.7 %all-gather.14.cloned.1.call-start = ((), (), s32[]{:S(2)}) async-start(), calls=%async_computation.10 | async-start | bytes 4718592 | tf_op jit(solution)/shard_map/all_gather | solution.py:1509
  122.9 175.7 %all-gather.10.cloned.1.call-start = ((), (), s32[]{:S(2)}) async-start(), calls=%async_computation.5 | async-start | bytes 9437184 | tf_op jit(solution)/shard_map/all_gather | solution.py:1509
  192.1 194.0 %all-gather.12.cloned.1.call-start = ((), (), s32[]{:S(2)}) async-start(), calls=%async_computation.6 | async-start | bytes 9437184 | tf_op jit(solution)/shard_map/all_gather | solution.py:1509
  192.2 103.7 %copy-start.14 = (bf16[4,64,2048]{2,1,0:T(8,128)(2,1)S(1)}, bf16[4,64,2048]{2,1,0:T(8,128)(2,1)}, u32[]{:S(2)}) copy-start(bf16[4,64,2048]{2,1,0:T(8,128)(2,1)} %get-tuple-element.88) | copy-start | bytes 3145732
  295.0 112.3 %all-gather.16.cloned.1.call-start = ((), (), s32[]{:S(2)}) async-start(), calls=%async_computation.11 | async-start | bytes 9437184 | tf_op jit(solution)/shard_map/all_gather | solution.py:1509
  295.6 319.2 %reduce-scatter.4.cloned.1.call-start = ((), (), s32[]{:S(2)}) async-start(), calls=%async_computation.7 | async-start | bytes 18874368 | tf_op jit(solution)/shard_map/reduce_scatter | solution.py:1512
  434.4 190.9 %reduce-scatter.6.cloned.1.call-start = ((), (), s32[]{:S(2)}) async-start(), calls=%async_computation.8 | async-start | bytes 9437184 | tf_op jit(solution)/shard_map/reduce_scatter | solution.py:1512
  518.0 245.8 %reduce-scatter.8.cloned.1.call-start = ((), (), s32[]{:S(2)}) async-start(), calls=%async_computation.9 | async-start | bytes 14155776 | tf_op jit(solution)/shard_map/reduce_scatter | solution.py:1512
  796.8 42.4 %all-to-all-start = ((bf16[8,64,3072]{2,1,0:T(8,128)(2,1)}), bf16[8,64,3072]{2,1,0:T(8,128)(2,1)}, u32[]{:S(2)}, u32[]{:S(2)}) async-start(bf16[8,64,3072]{2,1,0:T(8,128)(2,1)} %get-tuple-element.119), calls=%async_computation.3 | async-start | bytes 6291456 | tf_op jit(solution)/shard_map/all_to_all | solution.py:1666
  801.3 10.4 %copy-start.15 = (f32[6,256]{1,0:T(8,128)S(1)}, f32[6,256]{1,0:T(8,128)}, u32[]{:S(2)}) copy-start(f32[6,256]{1,0:T(8,128)} %param.53) | copy-start | bytes 18436
  801.3 10.4 %copy-start.16 = (f32[6,256]{1,0:T(8,128)S(1)}, f32[6,256]{1,0:T(8,128)}, u32[]{:S(2)}) copy-start(f32[6,256]{1,0:T(8,128)} %param.55) | copy-start | bytes 18436
  801.3 10.4 %copy-start.17 = (f32[6,256]{1,0:T(8,128)S(1)}, f32[6,256]{1,0:T(8,128)}, u32[]{:S(2)}) copy-start(f32[6,256]{1,0:T(8,128)} %param.54) | copy-start | bytes 18436
  801.4 11.0 %copy-start.6 = (f32[512,2048]{1,0:T(8,128)S(1)}, f32[512,2048]{1,0:T(8,128)}, u32[]{:S(2)}) copy-start(f32[512,2048]{1,0:T(8,128)} %refs_1_.6) | copy-start | bytes 12582916
  801.4 12.1 %copy-start.8 = (f32[512,2048]{1,0:T(8,128)S(1)}, f32[512,2048]{1,0:T(8,128)}, u32[]{:S(2)}) copy-start(f32[512,2048]{1,0:T(8,128)} %param.49) | copy-start | bytes 12582916
  801.4 13.3 %copy-start.9 = (f32[512,2048]{1,0:T(8,128)S(1)}, f32[512,2048]{1,0:T(8,128)}, u32[]{:S(2)}) copy-start(f32[512,2048]{1,0:T(8,128)} %param.48) | copy-start | bytes 12582916
  814.7 8.4 copy-start.5
  814.7 8.4 copy-start.10
  814.7 9.6 %copy-start.11 = (f32[512,2048]{1,0:T(8,128)S(1)}, f32[512,2048]{1,0:T(8,128)}, u32[]{:S(2)}) copy-start(f32[512,2048]{1,0:T(8,128)} %param.51) | copy-start | bytes 12582916
  839.2 10.3 %copy-start.7 = (f32[512,1024]{1,0:T(8,128)S(1)}, f32[512,1024]{1,0:T(8,128)}, u32[]{:S(2)}) copy-start(f32[512,1024]{1,0:T(8,128)} %refs_1_.5) | copy-start | bytes 6291460
  839.2 10.3 %copy-start.12 = (f32[512,1024]{1,0:T(8,128)S(1)}, f32[512,1024]{1,0:T(8,128)}, u32[]{:S(2)}) copy-start(f32[512,1024]{1,0:T(8,128)} %param.46) | copy-start | bytes 6291460
  839.2 11.5 %copy-start.13 = (f32[512,1024]{1,0:T(8,128)S(1)}, f32[512,1024]{1,0:T(8,128)}, u32[]{:S(2)}) copy-start(f32[512,1024]{1,0:T(8,128)} %param.45) | copy-start | bytes 6291460
  (8 other events, 6.7 us)
Sparse Core Ops, SparseCore 0:
  58.6 64.6 all-gather.7
  125.2 53.2 all-gather.13
  192.2 89.5 all-gather.9
  295.1 55.9 all-gather.11
  352.9 54.3 all-gather.15
  434.6 115.9 reduce-scatter.3
  554.0 71.2 reduce-scatter.5
  629.2 134.4 reduce-scatter.7

commit v12 on v11

--- a/solution.py
+++ b/solution.py
@@ -1651,12 +1651,12 @@
     query_outs_sum = after(query_outs_sum, term1)
     query_sum, outs_sum = query_outs_sum[:n_z], query_outs_sum[n_z:]
     norm_term = jnp.concatenate([term1[:2], term2[:2], term3[:4]], axis=0)
-    loose, norm_grad = leave_call(
+    outs_slots, loose, norm_grad = leave_call(
         "leave_query",
         9,
         contents,
         [
-            (outs_sum, False, cap_out, slot_firsts[1], False),
+            (outs_sum, False, cap_out, slot_firsts[1], True),
             (query_sum, True, cap_big, slot_firsts[0], False),
         ],
         norm_term,
@@ -1664,8 +1664,8 @@
         n_dp,
     )
     loose = lax.all_to_all(loose, "dp", 0, 0, tiled=True).reshape(own_rows, -1)
-    outs_slots = loose[:, : cap_out * BLK].astype(f32)
-    query_grad = loose[:, cap_out * BLK :].astype(f32)
+    outs_slots = outs_slots.reshape(own_rows, -1).astype(f32)
+    query_grad = loose.astype(f32)
     norm_grad = norm_grad[:6]
     text_grad, up_grad, down_grad = (
         grad.reshape(own_rows, -1).astype(f32) for grad in (text_grad, up_grad, down_grad)

time: 874 us -> 865 us (0.990)
  transfers between devices with their start and end apart: 9 -> 9, of which waited for: 4 -> 3; matrix products, arithmetic and copies ran while one was open for 4% -> 4% of each run, Pallas kernels for 75% -> 76%
where the time goes in v12:
time: 865 us; the launch traced here: 856 us
  Pallas kernels  753 us (87%)
  other arithmetic  42.9 us (5%)
  local copies, waits for them, and re-layouts  20.8 us (2%)
  waiting for transfers between devices  18.5 us (2%)
  between operations  15 us (2%)
    pallas_call x4, Pallas kernels, enter_call(): line_call(kernel, name, ident, outs, specs, scratch, 0, LINK_COST)(*args)  269 us
    pallas_call x2, Pallas kernels, leave_call(): line_call(kernel, name, ident, outs, specs, scratch, 0, LINK_COST)(*args)  165 us
    pallas_call x2, Pallas kernels, back_call(): return call(*args)  146 us
    pallas_call x1, Pallas kernels, forward_call(): return call(*args)  74.9 us
    sub x6, other arithmetic, adamw_update(): weight - rate * (first_hat / (jnp.sqrt(second_hat) + adam_eps) + decay *...  37.8 us
    pallas_call x1, Pallas kernels, ffn_back(): local_call(ffn_back_kernel, 'ffn_back', 4, (shape((tokens, width), bf16),...  27 us
  transfers between devices with their start and end apart: 9, of which 3 were waited for; matrix products, arithmetic and copies ran while one was open for 4% of the time, Pallas kernels for 76%

profile of v12, /device:TPU:0, one launch (start us, length us, event | category | flops | bytes accessed | tf_op | source)
XLA Modules:
  0.0 855.6 jit_solution(7654457626333703035)
XLA Ops:
  11.5 47.0 %enter_query.1 = (bf16[4,64,2048]{2,1,0:T(8,128)(2,1)}, bf16[4,64,2048]{2,1,0:T(8,128)(2,1)}, s32[4,8,256]{2,1,0:T(8,128)S(1)}, f32[8,2048]{1,0:T(8,128)S(1)}) custom-call(s32[2,288]{1,0:T(2,128)S(1)} %pad_add_fusion.refs_0_.w_hbm, f32[512,2048]{1,0:T(8,128)} %refs_1_.4, bf16[64,2048]{1,0:T(8,128)(2,1)S(1)} %get-tuple-element.157.refs_2_, ...), custom_call_target="tpu_custom_call" | custom-call | bytes 4000000 | tf_op jit(solution)/shard_map/enter_query/pallas_call | solution.py:864
  58.6 64.3 %enter_outs.1 = (bf16[1,64,4096]{2,1,0:T(8,128)(2,1)}, bf16[4,128,2048]{2,1,0:T(8,128)(2,1)}, bf16[4,32,4096]{2,1,0:T(8,128)(2,1)}) custom-call(s32[2,288]{1,0:T(2,128)S(1)} %pad_add_fusion.refs_0_.w_hbm, f32[512,1024]{1,0:T(8,128)} %refs_1_.5, bf16[128,2048]{1,0:T(8,128)(2,1)S(1)} %copy-done, bf16[32,4096]{1,0:T(8,128)(2,1)S(1)} %copy-done.4, ...), custom_call_target="tpu_custom_call" | custom-call | bytes 4000000 | tf_op jit(solution)/shard_map/enter_outs/pallas_call | solution.py:864
  123.4 12.7 %self_forward.1 = (bf16[3,512,512]{2,1,0:T(8,128)(2,1)}, bf16[512,512]{1,0:T(8,128)(2,1)S(1)}, f32[16,128,128]{2,1,0:T(8,128)S(1)}) custom-call(bf16[512,2048]{1,0:T(8,128)(2,1)} %bitcast.94, bf16[2048,2048]{1,0:T(8,128)(2,1)} %all-gather.8.cloned.1.call-done.w_ref.refs_7_.w_hbm.refs_5_, s32[4,128,128]{2,1,0:T(8,128)S(1)} %get-tuple-element.162.mask_ref), custom_call_target="tpu_custom_call" | custom-call | flops 402653184 | bytes 2500000 | tf_op jit(solution)/shard_map/self_forward/pallas_call | solution.py:1255
  137.1 55.0 %enter_text.1 = (bf16[4,64,2048]{2,1,0:T(8,128)(2,1)}, bf16[4,64,2048]{2,1,0:T(8,128)(2,1)}) custom-call(s32[2,288]{1,0:T(2,128)S(1)} %pad_add_fusion.refs_0_.w_hbm, f32[512,2048]{1,0:T(8,128)} %refs_1_.6, bf16[64,2048]{1,0:T(8,128)(2,1)S(1)} %get-tuple-element.156.refs_2_), custom_call_target="tpu_custom_call" | custom-call | bytes 4000000 | tf_op jit(solution)/shard_map/enter_text/pallas_call | solution.py:864
  192.2 102.8 %forward0.1 = (bf16[4,64,2048]{2,1,0:T(8,128)(2,1)}, bf16[1,64,8192]{2,1,0:T(8,128)(2,1)}, f32[128,2048]{1,0:T(8,128)}, bf16[4,128,2048]{2,1,0:T(8,128)(2,1)}, bf16[512,512]{1,0:T(8,128)(2,1)S(1)}) custom-call(s32[2,288]{1,0:T(2,128)S(1)} %pad_add_fusion.refs_0_.w_hbm, f32[512,2048]{1,0:T(8,128)} %refs_1_.7, f32[512,2048]{1,0:T(8,128)} %refs_2_.3, ...), custom_call_target="tpu_custom_call" | custom-call | bytes 4000000 | tf_op jit(solution)/shard_map/forward0/pallas_call | solution.py:864
  298.7 11.6 %cross_forward.1 = (bf16[2,128,512]{2,1,0:T(8,128)(2,1)S(1)}, bf16[512,512]{1,0:T(8,128)(2,1)S(1)}, f32[16,128,128]{2,1,0:T(8,128)}) custom-call(bf16[512,512]{1,0:T(8,128)(2,1)S(1)} %get-tuple-element.82.cq_ref, bf16[128,4096]{1,0:T(8,128)(2,1)} %bitcast.99, bf16[2048,2048]{1,0:T(8,128)(2,1)} %all-gather.10.cloned.1.call-done.w_ref, ...), custom_call_target="tpu_custom_call" | custom-call | flops 134217728 | bytes 2500000 | tf_op jit(solution)/shard_map/cross_forward/pallas_call | solution.py:1274
  310.2 74.9 %forward1.1 = (f32[128,2048]{1,0:T(8,128)S(1)}, bf16[4,128,2048]{2,1,0:T(8,128)(2,1)}) custom-call(bf16[512,512]{1,0:T(8,128)(2,1)S(1)} %get-tuple-element.84.att_ref.att2_ref, bf16[512,4096]{1,0:T(8,128)(2,1)} %bitcast.88, f32[128,2048]{1,0:T(8,128)} %get-tuple-element.85.base_ref.middle_ref, f32[2,2048]{1,0:T(2,128)S(1)} %get-tuple-element.158.norm_ref), custom_call_target="tpu_custom_call" | custom-call | bytes 4000000 | tf_op jit(solution)/shard_map/forward1/pallas_call | solution.py:941
  386.1 15.2 %ffn.1 = (bf16[512,2048]{1,0:T(8,128)(2,1)}, f32[512,2048]{1,0:T(8,128)}, bf16[8,512,2048]{2,1,0:T(8,128)(2,1)}) custom-call(bf16[512,2048]{1,0:T(8,128)(2,1)} %bitcast.97, bf16[2048,2048]{1,0:T(8,128)(2,1)} %all-gather.12.cloned.1.call-done.up_ref, bf16[512,2048]{1,0:T(8,128)(2,1)} %bitcast.92), custom_call_target="tpu_custom_call" | custom-call | flops 1073741824 | bytes 3750000 | tf_op jit(solution)/shard_map/ffn/pallas_call | solution.py:1296
  401.3 6.0 all-gather.16.cloned.1.call-done
  407.3 27.0 %ffn_back.1 = (bf16[512,2048]{1,0:T(8,128)(2,1)}, bf16[512,2048]{1,0:T(8,128)(2,1)}, bf16[8,512,2048]{2,1,0:T(8,128)(2,1)}) custom-call(bf16[512,2048]{1,0:T(8,128)(2,1)} %bitcast.98, bf16[512,8192]{1,0:T(8,128)(2,1)} %bitcast.96, bf16[2048,2048]{1,0:T(8,128)(2,1)} %all-gather.12.cloned.1.call-done.up_ref, ...), custom_call_target="tpu_custom_call", output_to_operand_aliasing={{2}: (6, {})} | custom-call | flops 2147483648 | bytes 6250000 | tf_op jit(solution)/shard_map/ffn_back/pallas_call | solution.py:1320
  435.4 72.5 %back1.1 = (f32[128,2048]{1,0:T(8,128)}, bf16[4,128,2048]{2,1,0:T(8,128)(2,1)}, bf16[512,512]{1,0:T(8,128)(2,1)S(1)}, f32[8,2048]{1,0:T(8,128)S(1)}) custom-call(bf16[4,128,2048]{2,1,0:T(8,128)(2,1)} %bitcast.106, s32[2,288]{1,0:T(2,128)S(1)} %pad_add_fusion.refs_0_.w_hbm, bf16[128,2048]{1,0:T(8,128)(2,1)S(1)} %copy-done.2, f32[128,2048]{1,0:T(8,128)} %copy-done.1, ...), custom_call_target="tpu_custom_call" | custom-call | bytes 4000000 | tf_op jit(solution)/shard_map/back1/pallas_call | solution.py:985
  507.9 10.0 %cross_back.1 = (bf16[512,512]{1,0:T(8,128)(2,1)S(1)}, bf16[2048,2048]{1,0:T(8,128)(2,1)}) custom-call(bf16[512,512]{1,0:T(8,128)(2,1)S(1)} %get-tuple-element.98.back_ref, bf16[512,512]{1,0:T(8,128)(2,1)S(1)} %get-tuple-element.82.cq_ref, bf16[2,128,512]{2,1,0:T(8,128)(2,1)S(1)} %get-tuple-element.99.kv_ref, f32[16,128,128]{2,1,0:T(8,128)} %get-tuple-element.100.share_ref, ...), custom_call_target="tpu_custom_call" | custom-call | flops 134217728 | bytes 2500000 | tf_op jit(solution)/shard_map/cross_back/pallas_call | solution.py:1350
  518.0 73.9 %back0.1 = (f32[128,2048]{1,0:T(8,128)}, bf16[4,128,2048]{2,1,0:T(8,128)(2,1)}, bf16[512,512]{1,0:T(8,128)(2,1)S(1)}, f32[8,2048]{1,0:T(8,128)S(1)}) custom-call(bf16[512,512]{1,0:T(8,128)(2,1)S(1)} %get-tuple-element.102.dy_ref.dcq_ref, bf16[2048,2048]{1,0:T(8,128)(2,1)} %all-gather.8.cloned.1.call-done.w_ref.refs_7_.w_hbm.refs_5_, ...), custom_call_target="tpu_custom_call" | custom-call | bytes 4000000 | tf_op jit(solution)/shard_map/back0/pallas_call | solution.py:985
  591.9 6.3 outs_grad.1.both_ref
  598.2 15.2 %self_back.1 = (bf16[512,1536]{1,0:T(8,128)(2,1)}, bf16[8,384,2048]{2,1,0:T(8,128)(2,1)}) custom-call(bf16[512,512]{1,0:T(8,128)(2,1)S(1)} %get-tuple-element.104.back_ref, bf16[3,512,512]{2,1,0:T(8,128)(2,1)} %get-tuple-element.105.proj_ref, f32[16,128,128]{2,1,0:T(8,128)} %copy-done.3, ...), custom_call_target="tpu_custom_call", output_to_operand_aliasing={{1}: (6, {})} | custom-call | flops 536870912 | bytes 3125000 | tf_op jit(solution)/shard_map/self_back/pallas_call | solution.py:1389
  617.8 7.4 reduce-scatter.6.cloned.1.call-done
  625.2 134.0 %leave_up.1 = (bf16[8,64,2048]{2,1,0:T(8,128)(2,1)}, bf16[8,64,2048]{2,1,0:T(8,128)(2,1)}, bf16[8,64,2048]{2,1,0:T(8,128)(2,1)}, bf16[128,2048]{1,0:T(8,128)(2,1...) custom-call(s32[2,576]{1,0:T(2,128)S(1)} %concatenate.39.refs_0_, bf16[4,64,2048]{2,1,0:T(8,128)(2,1)} %bitcast.102, ...), custom_call_target="tpu_custom_call" | custom-call | bytes 4000000 | tf_op jit(solution)/shard_map/leave_up/pallas_call | solution.py:907
  759.2 4.4 reduce-scatter.8.cloned.1.call-done
  767.0 31.1 %leave_query.1 = (bf16[8,64,1024]{2,1,0:T(8,128)(2,1)S(1)}, bf16[8,64,2048]{2,1,0:T(8,128)(2,1)}, f32[8,256]{1,0:T(8,128)S(1)}) custom-call(s32[2,576]{1,0:T(2,128)S(1)} %concatenate.39.refs_0_, bf16[2,64,2048]{2,1,0:T(8,128)(2,1)S(1)} %slice.85.refs_1_, bf16[4,64,2048]{2,1,0:T(8,128)(2,1)} %slice.86.refs_2_, f32[8,2048]{1,0:T(8,128)S(1)} %pad_maximum_fusion.1.refs_3_), custom_call_target="tpu_custom_call" | custom-call | bytes 4000000 | tf_op jit(solution)/shard_map/leave_query/pallas_call | solution.py:907
  798.2 4.4 all-to-all-start
  802.6 10.3 %multiply_subtract_fusion.2 = (f32[512,2048]{1,0:T(8,128)}, f32[512,2048]{1,0:T(8,128)}, f32[512,2048]{1,0:T(8,128)}) fusion(f32[512,2048]{1,0:T(8,128)} %refs_1_.7, bf16[8,64,2048]{2,1,0:T(8,128)(2,1)} %get-tuple-element.121, f32[512,2048]{1,0:T(8,128)} %param.43, f32[512,2048]{1,0:T(8,128)} %param.42), kind=kLoop, calls=%fused_computation.22 | loop fusion | flops 16777216 | bytes 27262976 | tf_op jit(solution)/shard_map/sub | solution.py:52
  816.5 6.7 multiply_subtract_fusion.1
  830.8 6.0 multiply_subtract_fusion
  836.9 9.9 %multiply_subtract_fusion.3 = (f32[512,2048]{1,0:T(8,128)}, f32[512,2048]{1,0:T(8,128)}, f32[512,2048]{1,0:T(8,128)}) fusion(f32[512,2048]{1,0:T(8,128)} %refs_1_.4, bf16[8,64,2048]{2,1,0:T(8,128)(2,1)} %all-to-all-done, f32[512,2048]{1,0:T(8,128)} %param.40, f32[512,2048]{1,0:T(8,128)} %param.39), kind=kLoop, calls=%fused_computation.23 | loop fusion | flops 16777216 | bytes 27262976 | tf_op jit(solution)/shard_map/sub | solution.py:52
  (121 shorter events, 31.9 us)
Async XLA Ops:
  7.2 51.4 %copy-start = (bf16[128,2048]{1,0:T(8,128)(2,1)S(1)}, bf16[128,2048]{1,0:T(8,128)(2,1)}, u32[]{:S(2)}) copy-start(bf16[128,2048]{1,0:T(8,128)(2,1)} %refs_7_.1) | copy-start | bytes 1572868
  7.2 51.4 %copy-start.4 = (bf16[32,4096]{1,0:T(8,128)(2,1)S(1)}, bf16[32,4096]{1,0:T(8,128)(2,1)}, u32[]{:S(2)}) copy-start(bf16[32,4096]{1,0:T(8,128)(2,1)} %refs_3_.1) | copy-start | bytes 786436
  7.2 116.2 %all-gather.8.cloned.1.call-start = ((), (), s32[]{:S(2)}) async-start(), calls=%async_computation.4 | async-start | bytes 9437184 | tf_op jit(solution)/shard_map/all_gather | solution.py:1509
  58.5 133.7 %all-gather.14.cloned.1.call-start = ((), (), s32[]{:S(2)}) async-start(), calls=%async_computation.10 | async-start | bytes 4718592 | tf_op jit(solution)/shard_map/all_gather | solution.py:1509
  122.9 175.7 %all-gather.10.cloned.1.call-start = ((), (), s32[]{:S(2)}) async-start(), calls=%async_computation.5 | async-start | bytes 9437184 | tf_op jit(solution)/shard_map/all_gather | solution.py:1509
  192.1 194.1 %all-gather.12.cloned.1.call-start = ((), (), s32[]{:S(2)}) async-start(), calls=%async_computation.6 | async-start | bytes 9437184 | tf_op jit(solution)/shard_map/all_gather | solution.py:1509
  192.2 103.7 %copy-start.16 = (bf16[4,64,2048]{2,1,0:T(8,128)(2,1)S(1)}, bf16[4,64,2048]{2,1,0:T(8,128)(2,1)}, u32[]{:S(2)}) copy-start(bf16[4,64,2048]{2,1,0:T(8,128)(2,1)} %get-tuple-element.89) | copy-start | bytes 3145732
  295.1 112.2 %all-gather.16.cloned.1.call-start = ((), (), s32[]{:S(2)}) async-start(), calls=%async_computation.11 | async-start | bytes 9437184 | tf_op jit(solution)/shard_map/all_gather | solution.py:1509
  295.7 319.0 %reduce-scatter.4.cloned.1.call-start = ((), (), s32[]{:S(2)}) async-start(), calls=%async_computation.7 | async-start | bytes 18874368 | tf_op jit(solution)/shard_map/reduce_scatter | solution.py:1512
  434.4 190.9 %reduce-scatter.6.cloned.1.call-start = ((), (), s32[]{:S(2)}) async-start(), calls=%async_computation.8 | async-start | bytes 9437184 | tf_op jit(solution)/shard_map/reduce_scatter | solution.py:1512
  517.9 245.7 %reduce-scatter.8.cloned.1.call-start = ((), (), s32[]{:S(2)}) async-start(), calls=%async_computation.9 | async-start | bytes 14155776 | tf_op jit(solution)/shard_map/reduce_scatter | solution.py:1512
  798.2 38.7 %all-to-all-start = ((bf16[8,64,2048]{2,1,0:T(8,128)(2,1)}), bf16[8,64,2048]{2,1,0:T(8,128)(2,1)}, u32[]{:S(2)}, u32[]{:S(2)}) async-start(bf16[8,64,2048]{2,1,0:T(8,128)(2,1)} %get-tuple-element.120), calls=%async_computation.3 | async-start | bytes 4194304 | tf_op jit(solution)/shard_map/all_to_all | solution.py:1666
  802.6 10.4 %copy-start.6 = (f32[512,2048]{1,0:T(8,128)S(1)}, f32[512,2048]{1,0:T(8,128)}, u32[]{:S(2)}) copy-start(f32[512,2048]{1,0:T(8,128)} %refs_1_.6) | copy-start | bytes 12582916
  802.6 12.1 %copy-start.8 = (f32[512,2048]{1,0:T(8,128)S(1)}, f32[512,2048]{1,0:T(8,128)}, u32[]{:S(2)}) copy-start(f32[512,2048]{1,0:T(8,128)} %param.49) | copy-start | bytes 12582916
  802.6 13.3 %copy-start.9 = (f32[512,2048]{1,0:T(8,128)S(1)}, f32[512,2048]{1,0:T(8,128)}, u32[]{:S(2)}) copy-start(f32[512,2048]{1,0:T(8,128)} %param.48) | copy-start | bytes 12582916
  802.6 13.8 %copy-start.15 = (bf16[8,64,2048]{2,1,0:T(8,128)(2,1)S(1)}, bf16[8,64,2048]{2,1,0:T(8,128)(2,1)}, u32[]{:S(2)}) copy-start(bf16[8,64,2048]{2,1,0:T(8,128)(2,1)} %get-tuple-element.123) | copy-start | bytes 6291460
  816.4 6.8 copy-start.17
  816.5 6.8 copy-start.18
  816.5 6.8 copy-start.19
  816.5 7.4 copy-start.7
  816.5 7.4 copy-start.12
  816.5 7.4 copy-start.13
  816.5 11.6 %copy-start.14 = (bf16[8,64,2048]{2,1,0:T(8,128)(2,1)S(1)}, bf16[8,64,2048]{2,1,0:T(8,128)(2,1)}, u32[]{:S(2)}) copy-start(bf16[8,64,2048]{2,1,0:T(8,128)(2,1)} %get-tuple-element.124) | copy-start | bytes 6291460
  823.9 6.9 copy-start.11
  (10 other events, 16.6 us)
Sparse Core Ops, SparseCore 0:
  58.6 64.6 all-gather.7
  125.2 53.2 all-gather.13
  192.2 89.5 all-gather.9
  295.2 55.8 all-gather.11
  352.8 54.4 all-gather.15
  434.5 115.9 reduce-scatter.3
  553.9 71.2 reduce-scatter.5
  629.1 134.4 reduce-scatter.7
